TPU v7x, 32 devices: a whole 2x2x4 slice. The times are simulated.
32 devices in a mesh: section: 8 (over z, x), head: 4 (over y, core).
Axes of the slice: x: 2, y: 2, z: 4, core: 2. Of those that a mesh axis runs over, the one named last changes fastest.
Arguments:
- entering: bfloat16 [8, 128, 4096], P('section', None, 'head'), may hold values from -6 to 6, as said below
- fresh_slice: bfloat16 [128, 4096], P(None, 'head'), may hold values from -6 to 6
- norm_gain: float32 [8, 4096], P('section'), may hold values from 0.5 to 1.5
- w_query: bfloat16 [8, 4096, 4096], P('section', None, 'head'), may hold values from -18.8125 to 18.8125
- w_key_value: bfloat16 [8, 4096, 1024], P('section', None, 'head'), may hold values from -0.0625 to 0.0625
- doc_lengths: int32 [9], replicated, may hold values from 1 to 512, 1152 in all
Outputs:
- leaving: bfloat16 [8, 128, 4096], P('section', None, 'head')
Inputs may be any that keep to these rules, and one draw needn't show every extreme that they name: `entering`: entries of the activations that enter.
All inputs are finite; a program needn't handle non-finite values.
Results may differ from a plain program's by a relative error of at most 0.01.
Values may be sent and summed in bfloat16 or wider, within the bound.
No kernel may reach another device: no remote copies, remote signals or barrier semaphores. Data moves between devices by JAX's collectives and lax.ppermute only.
A program may use at most 64 MiB of HBM per device.

v0:
```python
import math

import jax
import jax.numpy as jnp
from jax import lax
from jax.sharding import PartitionSpec as P

HD = 128
KVH = 4
GROUP = 8


epsilon = 1e-05
masked_score = -1e30


def passed_along(array, axis, by):
    peers = lax.axis_size(axis)
    pairs = [(i, i + by) for i in range(peers) if 0 <= i + by < peers]
    return lax.ppermute(array, axis, pairs)


def doc_index(position, doc_ends):
    return jnp.sum((doc_ends[None, :] <= position[:, None]).astype(jnp.int32), axis=1)


def attend_block(query_block, query_pos, query_doc, all_keys, all_values, key_pos, key_doc):
    scores = jnp.einsum(
        "qghd,kgd->ghqk", query_block, all_keys, preferred_element_type=jnp.float32
    ) / math.sqrt(HD)
    allowed = (key_pos[None, :] <= query_pos[:, None]) & (key_doc[None, :] == query_doc[:, None])
    scores = jnp.where(allowed[None, None], scores, masked_score)
    row_max = jnp.max(scores, axis=-1, keepdims=True)
    expon = jnp.exp(scores - row_max)
    weights = (expon / jnp.sum(expon, axis=-1, keepdims=True)).astype(jnp.bfloat16)
    mixed = jnp.einsum("ghqk,kgd->qghd", weights, all_values, preferred_element_type=jnp.float32)
    return mixed.astype(jnp.bfloat16)


def shards(entering, fresh_slice, norm_gain, w_query, w_key_value, doc_lengths):
    heads_here = w_query.shape[2] // HD
    slice_len = fresh_slice.shape[0]
    sections = lax.axis_size("section")
    section_index = lax.axis_index("section")
    head_index = lax.axis_index("head")
    local_groups = max(1, heads_here // GROUP)
    group_heads = heads_here // local_groups
    doc_ends = jnp.cumsum(doc_lengths)
    gain_row = norm_gain[0]
    w_q = w_query[0]
    w_kv = w_key_value[0]

    def section_layer(own_part, start, resident):
        full_rows = lax.all_gather(own_part, "head", axis=1, tiled=True)
        widened = full_rows.astype(jnp.float32)
        mean_sq = jnp.mean(widened * widened, axis=1, keepdims=True)
        normed = (widened * lax.rsqrt(mean_sq + epsilon) * gain_row[None, :]).astype(jnp.bfloat16)
        queries = jnp.dot(normed, w_q, preferred_element_type=jnp.float32).astype(jnp.bfloat16)
        kv_part = jnp.dot(normed, w_kv, preferred_element_type=jnp.float32).astype(jnp.bfloat16)
        every_column = lax.all_gather(kv_part, "head", axis=1, tiled=True)
        every_column = every_column.reshape(slice_len, HD, KVH, 2)
        first_group = head_index * heads_here // GROUP
        chosen = lax.dynamic_slice_in_dim(every_column, first_group, local_groups, 2)
        packed = jnp.transpose(chosen, (0, 2, 3, 1))
        new_keys = packed[:, :, 0, :]
        new_values = packed[:, :, 1, :]
        position = start + jnp.arange(slice_len, dtype=jnp.int32)
        if resident is None:
            all_keys, all_values, key_pos = (new_keys, new_values, position)
        else:
            all_keys = jnp.concatenate([resident[0], new_keys], axis=0)
            all_values = jnp.concatenate([resident[1], new_values], axis=0)
            key_pos = jnp.concatenate([resident[2], position], axis=0)
        key_doc = doc_index(key_pos, doc_ends)
        query_doc = doc_index(position, doc_ends)
        block_len = min(512, slice_len)
        count = slice_len // block_len
        query_groups = queries.reshape(count, block_len, local_groups, group_heads, HD)

        def one_block(block_args):
            return attend_block(
                block_args[0], block_args[1], block_args[2], all_keys, all_values, key_pos, key_doc
            )

        attended = lax.map(
            one_block,
            (query_groups, position.reshape(count, block_len), query_doc.reshape(count, block_len)),
        )
        attended = attended.reshape(slice_len, heads_here * HD)
        section_out = (own_part.astype(jnp.float32) + attended.astype(jnp.float32)).astype(
            jnp.bfloat16
        )
        return (section_out, new_keys, new_values, position)

    first_start = (sections - 1 - section_index) * slice_len
    first_out, keys_first, values_first, pos_first = section_layer(entering[0], first_start, None)
    passed = passed_along(first_out, "section", 1)
    second_in = jnp.where(section_index == 0, fresh_slice, passed)
    second_out = section_layer(
        second_in, first_start + slice_len, (keys_first, values_first, pos_first)
    )[0]
    return second_out[None]


def solution(mesh):
    placed = (
        P("section", None, "head"),
        P(None, "head"),
        P("section", None),
        P("section", None, "head"),
        P("section", None, "head"),
        P(),
    )
    return jax.shard_map(
        shards, mesh=mesh, in_specs=placed, out_specs=P("section", None, "head"), check_vma=False
    )
```

profile of v0, /device:TPU:0, one launch (start us, length us, event | category | flops | bytes accessed | tf_op | source)
XLA Modules:
  0.0 98.8 jit_solution(17825499482595579642)
XLA Ops:
  6.5 0.0 copy-start
  6.5 0.0 all-gather.6.cloned.1.call-start
  6.5 0.7 all-gather.6.cloned.1.call-update
  7.3 0.0 all-gather.4.cloned.1.call-start
  7.3 0.8 reduce-window.8
  8.2 0.1 convert_reduce_fusion.2
  8.3 0.1 compare_and_fusion.1
  8.4 20.0 %all-gather.6.cloned.1.call-done = bf16[1,128,4096]{2,1,0:T(8,128)(2,1)} async-done(((bf16[1,128,1024]{2,1,0:T(8,128)(2,1)}), bf16[1,128,4096]{2,1,0:T(8,128)(2,1)}) %all-gather.6.cloned.1.call-update) | async-done | bytes 1048592 | tf_op jit(solution)/shard_map/all_gather | solution.py:54
  28.4 1.5 %fusion.7 = f32[128]{0:T(128)S(1)} fusion(bf16[1,128,4096]{2,1,0:T(8,128)(2,1)} %all-gather.6.cloned.1.call-done), kind=kLoop, calls=%fused_computation.11 | loop fusion | flops 1572736 | bytes 1049088 | tf_op jit(solution)/shard_map/reduce_sum | solution.py:56
  29.9 0.0 copy-done
  29.9 0.0 copy-start.2
  29.9 0.0 copy-start.6
  29.9 1.8 %fusion.34 = bf16[128,256]{1,0:T(8,128)(2,1)S(1)} fusion(bf16[1,4096,256]{2,1,0:T(8,128)(2,1)S(1)} %copy-done, bf16[1,128,4096]{2,1,0:T(8,128)(2,1)} %all-gather.6.cloned.1.call-done, f32[4096]{0:T(1024)} %bitcast.129, f32[128]{0:T(128)S(1)} %add_rsqrt_fusion.1), kind=kOutput, calls=%fused_computation.34 | convolution fusion | flops 270565376 | bytes 3228160 | tf_op jit(solution)/shard_map/dot_general | solution.py:59
  31.7 5.8 %all_gather.13 = bf16[128,1024]{1,0:T(8,128)(2,1)S(1)} all-gather(bf16[128,256]{1,0:T(8,128)(2,1)S(1)} %fusion.34), channel_id=1, replica_groups=mesh['section'=8,'head'=4] {'head'}, dimensions={1}, use_global_device_ids=true | all-gather | bytes 327680 | tf_op jit(solution)/shard_map/all_gather | solution.py:60
  37.5 0.8 copy.28
  38.4 0.9 constant_dynamic-slice_fusion.1
  39.3 0.1 copy.46
  39.4 0.0 copy-done.2
  39.4 0.0 copy-done.6
  39.4 4.7 %fusion.31 = bf16[16,8,8,128]{3,2,1,0:T(8,128)(2,1)S(1)} fusion(bf16[1,4096,1024]{2,1,0:T(8,128)(2,1)} %param.9, bf16[1,128,4096]{2,1,0:T(8,128)(2,1)S(1)} %copy-done.2, f32[4096]{0:T(1024)S(1)} %bitcast.130, f32[128]{0:T(128)S(1)} %add_rsqrt_fusion.1), kind=kOutput, calls=%fused_computation.33 | convolution fusion | flops 1075970048 | bytes 9716224 | tf_op jit(solution)/shard_map/dot_general | solution.py:58
  44.1 0.0 copy-start.4
  44.1 0.2 fusion.65
  44.4 0.1 fusion.43
  44.5 0.2 fusion.27
  44.7 0.2 copy.33
  44.9 0.1 copy-done.4
  45.1 0.1 fusion.41
  45.1 3.4 %collective-permute-start = (bf16[128,1024]{1,0:T(8,128)(2,1)S(1)}, bf16[128,1024]{1,0:T(8,128)(2,1)S(1)}, u32[]{:S(2)}, u32[]{:S(2)}) collective-permute-start(bf16[128,1024]{1,0:T(8,128)(2,1)S(1)} %fusion.41), channel_id=1, source_target_pairs={{0,4},{4,8},{8,12},{12,16},{16,20},{20,24},{24,28},{1,5},{5,9},{9,... | collective-permute-start | bytes 786440 | tf_op jit(solution)/shard_map/ppermute | solution.py:20
  48.5 6.0 %collective-permute-done = bf16[128,1024]{1,0:T(8,128)(2,1)S(1)} collective-permute-done((bf16[128,1024]{1,0:T(8,128)(2,1)S(1)}, bf16[128,1024]{1,0:T(8,128)(2,1)S(1)}, u32[]{:S(2)}, u32[]{:S(2)}) %collective-permute-start) | collective-permute-done | bytes 262176 | tf_op jit(solution)/shard_map/ppermute | solution.py:20
  54.6 1.7 %broadcast_select_fusion = bf16[128,1024]{1,0:T(8,128)(2,1)} fusion(bf16[128,1024]{1,0:T(8,128)(2,1)} %param.7, bf16[128,1024]{1,0:T(8,128)(2,1)S(1)} %collective-permute-done, pred[]{:T(512)S(6)} %eq.51), kind=kLoop, calls=%fused_computation.53 | loop fusion | flops 131072 | bytes 786433 | tf_op jit(solution)/shard_map/jit(_where)/select_n | solution.py:98
  56.2 0.0 all-gather.4.cloned.1.call-update
  56.3 0.1 convert_reduce_fusion
  56.4 0.1 compare_and_fusion
  56.5 0.6 slice_bitcast_fusion.3
  57.1 16.1 %all-gather.4.cloned.1.call-done = bf16[128,4096]{1,0:T(8,128)(2,1)} async-done(((bf16[128,1024]{1,0:T(8,128)(2,1)}), bf16[128,4096]{1,0:T(8,128)(2,1)}) %all-gather.4.cloned.1.call-update) | async-done | bytes 1048592 | tf_op jit(solution)/shard_map/all_gather | solution.py:54
  73.2 1.5 %fusion.4 = f32[128]{0:T(128)S(1)} fusion(bf16[128,4096]{1,0:T(8,128)(2,1)} %all-gather.4.cloned.1.call-done), kind=kLoop, calls=%fused_computation.8 | loop fusion | flops 1572736 | bytes 1049088 | tf_op jit(solution)/shard_map/reduce_sum | solution.py:56
  74.7 0.0 copy-start.7
  74.7 0.6 copy-done.7
  75.3 0.0 copy-start.3
  75.3 1.8 %fusion.37 = bf16[128,256]{1,0:T(8,128)(2,1)S(1)} fusion(bf16[1,4096,256]{2,1,0:T(8,128)(2,1)S(1)} %copy-done, bf16[128,4096]{1,0:T(8,128)(2,1)} %all-gather.4.cloned.1.call-done, f32[128]{0:T(128)S(1)} %add_rsqrt_fusion, f32[4096]{0:T(1024)S(1)} %bitcast.131), kind=kOutput, calls=%fused_computation.35 | convolution fusion | flops 270565376 | bytes 3228160 | tf_op jit(solution)/shard_map/dot_general | solution.py:59
  77.1 5.8 %all_gather.15 = bf16[128,1024]{1,0:T(8,128)(2,1)S(1)} all-gather(bf16[128,256]{1,0:T(8,128)(2,1)S(1)} %fusion.37), channel_id=1, replica_groups=mesh['section'=8,'head'=4] {'head'}, dimensions={1}, use_global_device_ids=true | all-gather | bytes 327680 | tf_op jit(solution)/shard_map/all_gather | solution.py:60
  82.9 0.9 copy.34
  83.8 0.9 constant_dynamic-slice_fusion
  84.7 0.1 copy.47
  84.8 0.0 copy-done.3
  84.8 4.7 %fusion.28 = bf16[16,8,8,128]{3,2,1,0:T(8,128)(2,1)S(1)} fusion(bf16[1,4096,1024]{2,1,0:T(8,128)(2,1)} %param.9, bf16[128,4096]{1,0:T(8,128)(2,1)S(1)} %copy-done.3, f32[128]{0:T(128)} %copy-done.7, f32[4096]{0:T(1024)S(1)} %bitcast.132), kind=kOutput, calls=%fused_computation.32 | convolution fusion | flops 1075970048 | bytes 9716224 | tf_op jit(solution)/shard_map/dot_general | solution.py:58
  89.5 0.0 copy-start.5
  89.5 0.3 fusion.66
  89.8 0.2 fusion.40
  90.0 0.3 copy-done.5
  90.3 0.0 copy-start.1
  90.3 0.3 fusion.25
  90.6 0.2 copy.39
  90.8 0.4 copy-done.1
  91.2 0.8 fusion.48
  (6 shorter events, 0.0 us)
Async XLA Ops:
  6.5 23.4 %copy-start = (bf16[1,4096,256]{2,1,0:T(8,128)(2,1)S(1)}, bf16[1,4096,256]{2,1,0:T(8,128)(2,1)}, u32[]{:S(2)}) copy-start(bf16[1,4096,256]{2,1,0:T(8,128)(2,1)} %param.10) | copy-start | bytes 6291460
  6.5 21.8 %all-gather.6.cloned.1.call-start = ((), (), s32[]{:S(2)}) async-start(), calls=%async_computation.1 | async-start | bytes 1310720 | tf_op jit(solution)/shard_map/all_gather | solution.py:54
  7.3 65.9 %all-gather.4.cloned.1.call-start = ((), (), s32[]{:S(2)}) async-start(), calls=%async_computation | async-start | bytes 1310720 | tf_op jit(solution)/shard_map/all_gather | solution.py:54
  29.9 9.5 %copy-start.2 = (bf16[1,128,4096]{2,1,0:T(8,128)(2,1)S(1)}, bf16[1,128,4096]{2,1,0:T(8,128)(2,1)}, u32[]{:S(2)}) copy-start(bf16[1,128,4096]{2,1,0:T(8,128)(2,1)} %all-gather.6.cloned.1.call-done) | copy-start | bytes 3145732
  29.9 9.5 %copy-start.6 = (f32[1,4096]{1,0:T(1,128)S(1)}, f32[1,4096]{1,0:T(1,128)}, u32[]{:S(2)}) copy-start(f32[1,4096]{1,0:T(1,128)} %param.8) | copy-start | bytes 49156
  44.1 1.0 copy-start.4
  45.1 9.4 %collective-permute-start = (bf16[128,1024]{1,0:T(8,128)(2,1)S(1)}, bf16[128,1024]{1,0:T(8,128)(2,1)S(1)}, u32[]{:S(2)}, u32[]{:S(2)}) collective-permute-start(bf16[128,1024]{1,0:T(8,128)(2,1)S(1)} %fusion.41), channel_id=1, source_target_pairs={{0,4},{4,8},{8,12},{12,16},{16,20},{20,24},{24,28},{1,5},{5,9},{9,... | collective-permute-start | bytes 786440 | tf_op jit(solution)/shard_map/ppermute | solution.py:20
  74.7 0.6 copy-start.7
  75.3 9.5 %copy-start.3 = (bf16[128,4096]{1,0:T(8,128)(2,1)S(1)}, bf16[128,4096]{1,0:T(8,128)(2,1)}, u32[]{:S(2)}) copy-start(bf16[128,4096]{1,0:T(8,128)(2,1)} %all-gather.4.cloned.1.call-done) | copy-start | bytes 3145732
  89.5 0.8 copy-start.5
  90.3 0.9 copy-start.1
Sparse Core Ops, SparseCore 0:
  8.9 19.4 all-gather.5
  56.4 16.7 all-gather.3
where the time goes:
time: 99.4 us; the launch traced here: 98.8 us
  waiting for transfers between devices  42.9 us (43%)
  matrix products  14.1 us (14%)
  between operations  13.7 us (14%)
  blocking collectives  11.6 us (12%)
  other arithmetic  7.05 us (7%)
  local copies, waits for them, and re-layouts  6.13 us (6%)
  starting transfers between devices  3.43 us (3%)
    all_gather x2, waiting for transfers between devices, section_layer(): full_rows = lax.all_gather(own_part, 'head', axis=1, tiled=True)  36.1 us
    all_gather x2, blocking collectives, section_layer(): every_column = lax.all_gather(kv_part, 'head', axis=1, tiled=True)  11.6 us
    dot_general x2, matrix products, section_layer(): jnp.dot(normed, w_q, preferred_element_type=jnp.float32)  9.38 us
    ppermute x1, waiting for transfers between devices, passed_along(): return lax.ppermute(array, axis, pairs)  6.04 us
    dot_general x2, matrix products, section_layer(): jnp.dot(normed, w_kv, preferred_element_type=jnp.float32)  3.6 us
    ppermute x1, starting transfers between devices, passed_along(): return lax.ppermute(array, axis, pairs)  3.39 us
    reduce_sum x2, other arithmetic, section_layer(): mean_sq = jnp.mean(widened * widened, axis=1, keepdims=True)  3.03 us
  transfers between devices with their start and end apart: 3, of which 3 were waited for; matrix products, arithmetic and copies ran while one was open for 2% of the time, Pallas kernels for 0%

commit v1 on v0

v1 whole, which is shorter than its diff:
```python
import functools
import math

import jax
import jax.numpy as jnp
from jax import lax
from jax.experimental import pallas as pl
from jax.experimental.pallas import tpu as pltpu
from jax.sharding import PartitionSpec as P

HD = 128
KVH = 4
GROUP = 8

epsilon = 1e-05
masked_score = -1e30

VMEM = pltpu.VMEM
SMEM = pltpu.SMEM
f32 = jnp.float32
bf16 = jnp.bfloat16
vmem = pl.BlockSpec(memory_space=VMEM)
smem = pl.BlockSpec(memory_space=SMEM)
in_hbm = pl.BlockSpec(memory_space=pltpu.HBM)


params = pltpu.CompilerParams(vmem_limit_bytes=16 * 1024 * 1024)


def resident_in(*arrays):
    return [pltpu.with_memory_space_constraint(a, VMEM) for a in arrays]


def cost(flops, moved):
    return pl.CostEstimate(flops=flops, bytes_accessed=moved, transcendentals=0)


def rows_of(block, width):
    return pl.ds(pl.multiple_of(block * width, width), width)


def gained(x, gain_ref, block):
    width = x.shape[1]
    wide = x.astype(f32)
    squares = wide * wide
    ssq = squares[:, :HD]
    for c in range(HD, width, HD):
        ssq = ssq + squares[:, c : c + HD]
    return (wide * gain_ref[:, rows_of(block, width)]).astype(bf16), ssq


def first_block_kernel(
    x_ref, gain_ref, wq_hbm, wkv_hbm, accq_ref, acckv_ref, ssq_ref, wq_ref, wkv_ref, sems
):
    n = wq_hbm.shape[0] // x_ref.shape[1]
    width = x_ref.shape[1]
    me = lax.axis_index("head")

    def copies(step):
        rows = rows_of(lax.rem(me + step, n), width)
        return (
            pltpu.make_async_copy(wkv_hbm.at[rows], wkv_ref.at[rows], sems.at[step, 0]),
            pltpu.make_async_copy(wq_hbm.at[rows], wq_ref.at[rows], sems.at[step, 1]),
        )

    for step in range(n):
        for copy in copies(step):
            copy.start()
    normed, ssq = gained(x_ref[...], gain_ref, me)
    ssq_ref[...] = ssq
    for copy in copies(0):
        copy.wait()
    rows = rows_of(me, width)
    acckv_ref[...] = jnp.dot(normed, wkv_ref[rows, :], preferred_element_type=f32)
    accq_ref[...] = jnp.dot(normed, wq_ref[rows, :], preferred_element_type=f32)
    for step in range(1, n):
        for copy in copies(step):
            copy.wait()


def first_block(x, gain, wq, wkv):
    tokens, width = x.shape
    n = wq.shape[0] // width
    return pl.pallas_call(
        first_block_kernel,
        out_shape=(
            VMEM((tokens, wq.shape[1]), f32),
            VMEM((tokens, wkv.shape[1]), f32),
            VMEM((tokens, HD), f32),
            VMEM(wq.shape, bf16),
            VMEM(wkv.shape, bf16),
        ),
        in_specs=[vmem, vmem, in_hbm, in_hbm],
        out_specs=(vmem,) * 5,
        scratch_shapes=[pltpu.SemaphoreType.DMA((n, 2))],
        cost_estimate=cost(2 * tokens * width * (wq.shape[1] + wkv.shape[1]), 2 * (wq.size + wkv.size)),
        compiler_params=params,
        name="load_and_first_block",
    )(x, gain, *(pltpu.with_memory_space_constraint(w, pltpu.HBM) for w in (wq, wkv)))


def blocks_kernel(count, fresh_start, places, *refs):
    xs, rest = refs[:count], refs[count:]
    if fresh_start:
        gain_ref, wq_ref, wkv_ref, accq_out, acckv_out, ssq_out = rest
    else:
        gain_ref, wq_ref, wkv_ref, accq_ref, acckv_ref, ssq_ref, accq_out, acckv_out, ssq_out = rest
    width = xs[0].shape[1]
    me = lax.axis_index("head")
    for i, x_ref in enumerate(xs):
        block = places[i](me)
        normed, ssq = gained(x_ref[...], gain_ref, block)
        rows = rows_of(block, width)
        kv = jnp.dot(normed, wkv_ref[rows, :], preferred_element_type=f32)
        q = jnp.dot(normed, wq_ref[rows, :], preferred_element_type=f32)
        if i == 0 and fresh_start:
            accq_out[...], acckv_out[...], ssq_out[...] = q, kv, ssq
        elif i == 0:
            accq_out[...] = accq_ref[...] + q
            acckv_out[...] = acckv_ref[...] + kv
            ssq_out[...] = ssq_ref[...] + ssq
        else:
            accq_out[...] += q
            acckv_out[...] += kv
            ssq_out[...] += ssq


def more_blocks(xs, places, gain, wq, wkv, state):
    tokens, width = xs[0].shape
    operands = [*xs, *resident_in(gain, wq, wkv), *(state or ())]
    shapes = ((tokens, wq.shape[1]), (tokens, wkv.shape[1]), (tokens, HD))
    return pl.pallas_call(
        functools.partial(blocks_kernel, len(xs), state is None, places),
        out_shape=tuple(VMEM(s, f32) for s in shapes),
        in_specs=[vmem] * len(operands),
        out_specs=(vmem,) * 3,
        cost_estimate=cost(
            len(xs) * 2 * tokens * width * (wq.shape[1] + wkv.shape[1]), len(xs) * 2 * tokens * width
        ),
        compiler_params=params,
        name="more_blocks",
    )(*operands)


def last_kv_kernel(count, places, *refs):
    xs, rest = refs[:count], refs[count:]
    gain_ref, wkv_ref, acckv_ref, ssq_ref = rest[:4]
    scale_ref, pieces, turned = rest[4], rest[5:-1], rest[-1]
    width = xs[0].shape[1]
    n = lax.axis_size("head")
    me = lax.axis_index("head")
    total, ssq = acckv_ref[...], ssq_ref[...]
    for i, x_ref in enumerate(xs):
        block = places[i](me)
        normed, more = gained(x_ref[...], gain_ref, block)
        ssq = ssq + more
        total = total + jnp.dot(normed, wkv_ref[rows_of(block, width), :], preferred_element_type=f32)
    scale = lax.rsqrt(jnp.sum(ssq, axis=1, keepdims=True) / (n * width) + epsilon)
    scale_ref[...] = jnp.broadcast_to(scale, scale_ref.shape)
    kv = (total * scale).astype(bf16)
    columns = kv.shape[1]
    features = columns // (2 * KVH)
    row = lax.broadcasted_iota(jnp.int32, (columns, columns), 0)
    col = lax.broadcasted_iota(jnp.int32, (columns, columns), 1)
    group, which, feature = row // (2 * features), (row // features) % 2, row % features
    choose = jnp.where(col == (feature * KVH + group) * 2 + which, 1.0, 0.0).astype(bf16)
    turned[...] = lax.dot_general(choose, kv, (((1,), (1,)), ((), ())), preferred_element_type=f32)
    for k in range(n):
        group_there = group_of(lax.rem(me + k, n), n)
        rows = pl.ds(pl.multiple_of(group_there * 2 * features, 2 * features), 2 * features)
        pieces[k][...] = turned[rows, :].astype(bf16)


def group_of(head_index, n):
    return head_index * KVH // n


def last_kv(xs, places, gain, wkv, acckv, ssq, n):
    tokens, width = xs[0].shape
    columns = wkv.shape[1]
    operands = [*xs, *resident_in(gain, wkv), acckv, ssq]
    return pl.pallas_call(
        functools.partial(last_kv_kernel, len(xs), places),
        out_shape=(VMEM((tokens, HD), f32),) + tuple(VMEM((columns // KVH, tokens), bf16) for _ in range(n)),
        in_specs=[vmem] * len(operands),
        out_specs=(vmem,) * (1 + n),
        scratch_shapes=[VMEM((columns, tokens), f32)],
        cost_estimate=cost(len(xs) * 2 * tokens * width * columns, 2 * tokens * width),
        compiler_params=params,
        name="last_block_key_value",
    )(*operands)


def last_q_kernel(count, places, *refs):
    xs, rest = refs[:count], refs[count:]
    gain_ref, wq_ref, accq_ref, scale_ref, q_ref = rest
    width = xs[0].shape[1]
    me = lax.axis_index("head")
    total = accq_ref[...]
    for i, x_ref in enumerate(xs):
        block = places[i](me)
        normed, _ = gained(x_ref[...], gain_ref, block)
        total = total + jnp.dot(normed, wq_ref[rows_of(block, width), :], preferred_element_type=f32)
    q_ref[...] = (total * scale_ref[:, 0:1]).astype(bf16)


def last_q(xs, places, gain, wq, accq, scale):
    tokens, width = xs[0].shape
    operands = [*xs, *resident_in(gain, wq), accq, scale]
    return pl.pallas_call(
        functools.partial(last_q_kernel, len(xs), places),
        out_shape=VMEM((tokens, wq.shape[1]), bf16),
        in_specs=[vmem] * len(operands),
        out_specs=vmem,
        cost_estimate=cost(len(xs) * 2 * tokens * width * wq.shape[1], 2 * tokens * width),
        compiler_params=params,
        name="last_block_queries",
    )(*operands)


def attend_kernel(n, sections, turn, doc_ref, q_ref, x_ref, *refs):
    pieces, rest = refs[:n], refs[n:]
    tokens = q_ref.shape[0]
    me = lax.axis_index("head")
    section = lax.axis_index("section")
    first_start = (sections - 1 - section) * tokens
    features = pieces[0].shape[0] // 2
    if turn == 1:
        fresh_ref, out_ref, keys_ref, values_ref, gather = rest
        start, base = first_start, first_start
    else:
        old_keys, old_values, out_ref, gather = rest
        start, base = first_start + tokens, first_start
    for k in range(n):
        source = lax.rem(me + n - k, n)
        piece = pieces[k][...].astype(f32)
        rows = pl.ds(pl.multiple_of(source * features, features), features)
        gather[0, rows, :] = piece[:features]
        gather[1, rows, :] = piece[features:]
    keys, values = gather[0].astype(bf16), gather[1].astype(bf16)
    if turn == 1:
        keys_ref[...], values_ref[...] = keys, values
    else:
        keys = jnp.concatenate([old_keys[...], keys], axis=1)
        values = jnp.concatenate([old_values[...], values], axis=1)
    here = start + lax.broadcasted_iota(jnp.int32, (tokens, 1), 0)
    there = base + lax.broadcasted_iota(jnp.int32, (1, keys.shape[1]), 1)
    opened = jnp.zeros((tokens, 1), jnp.int32)
    end = jnp.int32(0)
    for d in range(doc_ref.shape[0]):
        end = end + doc_ref[d]
        opened = jnp.where(end <= here, end, opened)
    allowed = (there >= opened) & (there <= here)
    for h in range(q_ref.shape[1] // HD):
        columns = slice(h * HD, (h + 1) * HD)
        scores = jnp.dot(q_ref[:, columns], keys, preferred_element_type=f32) * (1.0 / math.sqrt(HD))
        scores = jnp.where(allowed, scores, masked_score)
        expon = jnp.exp(scores - jnp.max(scores, axis=1, keepdims=True))
        weights = (expon * (1.0 / jnp.sum(expon, axis=1, keepdims=True))).astype(bf16)
        mixed = lax.dot_general(weights, values, (((1,), (1,)), ((), ())), preferred_element_type=f32)
        out = (x_ref[:, columns].astype(f32) + mixed.astype(bf16).astype(f32)).astype(bf16)
        if turn == 1:
            out = jnp.where(section == sections - 1, fresh_ref[:, columns].astype(f32), out.astype(f32)).astype(bf16)
        out_ref[:, columns] = out


def attend(doc_lengths, q, x, pieces, turn, extra, sections):
    n = len(pieces)
    tokens = q.shape[0]
    out = (jax.ShapeDtypeStruct(q.shape, bf16),)
    if turn == 1:
        out = out + (VMEM((HD, tokens), bf16),) * 2
    operands = [doc_lengths, q, x, *pieces, *extra]
    return pl.pallas_call(
        functools.partial(attend_kernel, n, sections, turn),
        out_shape=out,
        in_specs=[smem] + [vmem] * (len(operands) - 1),
        out_specs=(vmem,) * len(out),
        scratch_shapes=[VMEM((2, HD, tokens), f32)],
        cost_estimate=cost(8 * tokens * tokens * q.shape[1], 2 * q.size),
        compiler_params=params,
        name="attend",
    )(*operands)


def shards(entering, fresh_slice, norm_gain, w_query, w_key_value, doc_lengths):
    n = lax.axis_size("head")
    sections = lax.axis_size("section")
    own = entering[0]
    w_q, w_kv = w_query[0], w_key_value[0]
    gain = norm_gain

    def moved(array, by, flip):
        pairs = [
            (s * n + h, ((s + by) % sections) * n + (h ^ flip)) for s in range(sections) for h in range(n)
        ]
        return lax.ppermute(array, ("section", "head"), pairs)

    def turned(array, by):
        return lax.ppermute(array, "head", [(h, (h + by) % n) for h in range(n)])

    def finish(xs, places, wq, wkv, state, x, turn, extra):
        accq, acckv, ssq = state
        scale, *pieces = last_kv(xs, places, gain, wkv, acckv, ssq, n)
        arrived = [pieces[0]] + [turned(pieces[k], k) for k in range(1, n)]
        q = last_q(xs, places, gain, wq, accq, scale)
        return attend(doc_lengths, q, x, arrived, turn, extra, sections)

    paired = n == 4
    xor = [functools.partial(lambda flip, me: lax.bitwise_xor(me, jnp.int32(flip)), flip) for flip in range(4)]
    others = [functools.partial(lambda k, me: lax.rem(me + k, jnp.int32(n)), k) for k in range(n)]

    def rest_of(array):
        every = lax.all_gather(array, "head", axis=0)
        me = lax.axis_index("head")
        return [lax.dynamic_index_in_dim(every, (me + k) % n, 0, False) for k in range(1, n)]

    if paired:
        over = moved(own, 0, 2)
        beside = moved(own, 0, 1)
    *state, wq, wkv = first_block(own, gain, w_q, w_kv)
    if paired:
        over, *state = lax.optimization_barrier((over, *state))
        passed = moved(over, 0, 1)
        state = more_blocks([beside, over], [xor[1], xor[2]], gain, wq, wkv, state)
        last, places = [passed], [xor[3]]
    else:
        last, places = rest_of(own), others[1:]
    sent, keys, values = finish(last, places, wq, wkv, state, own, 1, [fresh_slice])

    if paired:
        mine = moved(sent, 1, 0)
        over = moved(sent, 1, 2)
        beside = moved(mine, 0, 1)
        passed = moved(over, 0, 1)
        state = more_blocks([mine], [xor[0]], gain, wq, wkv, None)
        state = more_blocks([over, beside], [xor[2], xor[1]], gain, wq, wkv, state)
        last, places = [passed], [xor[3]]
    else:
        mine = moved(sent, 1, 0)
        state = more_blocks([mine], [others[0]], gain, wq, wkv, None)
        last, places = rest_of(mine), others[1:]
    return finish(last, places, wq, wkv, state, mine, 2, [keys, values])[0][None]


def solution(mesh):
    placed = (
        P("section", None, "head"),
        P(None, "head"),
        P("section", None),
        P("section", None, "head"),
        P("section", None, "head"),
        P(),
    )
    return jax.shard_map(
        shards, mesh=mesh, in_specs=placed, out_specs=P("section", None, "head"), check_vma=False
    )
```

time: 99.4 us -> 44.9 us (0.45)
  waiting for transfers between devices: 42.9 us -> 17.6 us
  matrix products: 14.1 us -> 0 us
  between operations: 13.7 us -> 0.14 us
  Pallas kernels: 0 us -> 12.5 us
  blocking collectives: 11.6 us -> 0 us
  starting transfers between devices: 3.43 us -> 12.4 us
  other arithmetic: 7.05 us -> 0 us
  local copies, waits for them, and re-layouts: 6.13 us -> 1.69 us
    all_gather x2 -> x0, waiting for transfers between devices: 36.1 us -> none  [section_layer(): full_rows = lax.all_gather(own_part, 'head', axis=1, tiled=True)]
    dot_general x8 -> x0, matrix products: 14.1 us -> none  [the longest x2 9.38 us: section_layer(): jnp.dot(normed, w_q, preferred_element_type=jnp.float32)]
    pallas_call x0 -> x10, Pallas kernels: none -> 12.5 us  [the longest x1 4.17 us: first_block(): pl.pallas_call(first_block_kernel, out_shape=(VMEM((tokens, wq.shape[1]),...]
    all_gather x2 -> x0, blocking collectives: 11.6 us -> none  [section_layer(): every_column = lax.all_gather(kv_part, 'head', axis=1, tiled=True)]
    ppermute x1 -> x13, waiting for transfers between devices: 6.04 us -> 17.6 us  [the longest x7 15.4 us: moved(): return lax.ppermute(array, ('section', 'head'), pairs)]
    ppermute x1 -> x13, starting transfers between devices: 3.39 us -> 12.4 us  [the longest x7 6.6 us: moved(): return lax.ppermute(array, ('section', 'head'), pairs)]
    reduce_sum x6 -> x0, other arithmetic: 3.45 us -> none  [the longest x2 3.03 us: section_layer(): mean_sq = jnp.mean(widened * widened, axis=1, keepdims=True)]
    dynamic_slice x2 -> x0, local copies, waits for them, and re-layouts: 1.77 us -> none  [section_layer(): lax.dynamic_slice_in_dim(every_column, first_group, local_groups, 2)]
  transfers between devices with their start and end apart: 3 -> 13, of which waited for: 3 -> 8; matrix products, arithmetic and copies ran while one was open for 2% -> 0% of each run, Pallas kernels for 0% -> 17%
where the time goes in v1:
time: 44.9 us; the launch traced here: 44.2 us
  waiting for transfers between devices  17.6 us (39%)
  Pallas kernels  12.5 us (28%)
  starting transfers between devices  12.4 us (28%)
  local copies, waits for them, and re-layouts  1.69 us (4%)
    ppermute x7, waiting for transfers between devices, moved(): return lax.ppermute(array, ('section', 'head'), pairs)  15.4 us
    ppermute x7, starting transfers between devices, moved(): return lax.ppermute(array, ('section', 'head'), pairs)  6.6 us
    ppermute x6, starting transfers between devices, turned(): return lax.ppermute(array, 'head', [(h, (h + by) % n) for h in range(n)])  5.79 us
    pallas_call x1, Pallas kernels, first_block(): pl.pallas_call(first_block_kernel, out_shape=(VMEM((tokens, wq.shape[1]),...  4.17 us
    pallas_call x2, Pallas kernels, attend(): pl.pallas_call(functools.partial(attend_kernel, n, sections, turn), out_s...  4.12 us
    pallas_call x3, Pallas kernels, more_blocks(): pl.pallas_call(functools.partial(blocks_kernel, len(xs), state is None, p...  2.32 us
    ppermute x6, waiting for transfers between devices, turned(): return lax.ppermute(array, 'head', [(h, (h + by) % n) for h in range(n)])  2.16 us
    unnamed x12, local copies, waits for them, and re-layouts  1.69 us
  transfers between devices with their start and end apart: 13, of which 8 were waited for; matrix products, arithmetic and copies ran while one was open for 0% of the time, Pallas kernels for 17%

profile of v1, /device:TPU:0, one launch (start us, length us, event | category | flops | bytes accessed | tf_op | source)
XLA Modules:
  0.0 44.2 jit_solution(9731857718311536400)
XLA Ops:
  0.0 3.0 %collective-permute-start = (bf16[128,1024]{1,0:T(8,128)(2,1)}, bf16[128,1024]{1,0:T(8,128)(2,1)S(1)}, u32[]{:S(2)}, u32[]{:S(2)}) collective-permute-start(bf16[128,1024]{1,0:T(8,128)(2,1)} %bitcast.4), channel_id=1, source_target_pairs={{0,2},{1,3},{2,0},{3,1},{4,6},{5,7},{6,4},{7,5},{8,10},{9,11},{10,... | collective-permute-start | bytes 786440 | tf_op jit(solution)/shard_map/ppermute | solution.py:297
  3.0 0.0 collective-permute-start.2
  3.0 0.0 copy-start
  3.0 0.7 %copy-done = f32[1,4096]{1,0:T(1,128)S(1)} copy-done((f32[1,4096]{1,0:T(1,128)S(1)}, f32[1,4096]{1,0:T(1,128)}, u32[]{:S(2)}) %copy-start) | copy-done | bytes 16408
  3.7 0.0 copy-start.2
  3.7 0.9 %copy-done.2 = bf16[1,128,1024]{2,1,0:T(8,128)(2,1)S(1)} copy-done((bf16[1,128,1024]{2,1,0:T(8,128)(2,1)S(1)}, bf16[1,128,1024]{2,1,0:T(8,128)(2,1)}, u32[]{:S(2)}) %copy-start.2) | copy-done | bytes 262168
  4.6 0.0 copy-start.1
  4.6 4.2 %load_and_first_block.1 = (f32[128,1024]{1,0:T(8,128)S(1)}, f32[128,256]{1,0:T(8,128)S(1)}, f32[128,128]{1,0:T(8,128)S(1)}, bf16[4096,1024]{1,0:T(8,128)(2,1)S(1)}, bf16[4096,256]{1,0:T(8,128)(2,1)S(1)}) custom-call(bf16[128,1024]{1,0:T(8,128)(2,1)S(1)} %bitcast.6, f32[1,4096]{1,0:T(1,128)S(1)} %copy-done, bf16[4096,1024]{1,0:T(8,128)(2,1)} %bitcast.8, ...), custom_call_target="tpu_custom_call" | custom-call | flops 335544320 | bytes 10485760 | tf_op jit(solution)/shard_map/load_and_first_block/pallas_call | solution.py:84
  8.8 0.7 %collective-permute-done.refs_1_ = bf16[128,1024]{1,0:T(8,128)(2,1)S(1)} collective-permute-done((bf16[128,1024]{1,0:T(8,128)(2,1)}, bf16[128,1024]{1,0:T(8,128)(2,1)S(1)}, u32[]{:S(2)}, u32[]{:S(2)}) %collective-permute-start) | collective-permute-done | bytes 262176 | tf_op jit(solution)/shard_map/ppermute | solution.py:297
  9.5 0.0 collective-permute-start.1
  9.5 0.0 collective-permute-done.2.refs_0_
  9.5 0.0 copy-done.1
  9.5 0.9 %more_blocks.3 = (f32[128,1024]{1,0:T(8,128)S(1)}, f32[128,256]{1,0:T(8,128)S(1)}, f32[128,128]{1,0:T(8,128)S(1)}) custom-call(bf16[128,1024]{1,0:T(8,128)(2,1)S(1)} %collective-permute-done.2.refs_0_, bf16[128,1024]{1,0:T(8,128)(2,1)S(1)} %collective-permute-done.refs_1_, f32[1,4096]{1,0:T(1,128)S(1)} %copy-done.1, ...), custom_call_target="tpu_custom_call" | custom-call | flops 671088640 | bytes 524288 | tf_op jit(solution)/shard_map/more_blocks/pallas_call | solution.py:132
  10.4 0.0 copy-start.3
  10.4 0.0 copy-start.4
  10.4 0.0 copy-start.5
  10.4 0.6 %collective-permute-done.1.refs_0_ = bf16[128,1024]{1,0:T(8,128)(2,1)S(1)} collective-permute-done((bf16[128,1024]{1,0:T(8,128)(2,1)S(1)}, bf16[128,1024]{1,0:T(8,128)(2,1)S(1)}, u32[]{:S(2)}, u32[]{:S(2)}) %collective-permute-start.1) | collective-permute-done | bytes 262176 | tf_op jit(solution)/shard_map/ppermute | solution.py:297
  11.0 0.5 %last_block_key_value.2 = (f32[128,128]{1,0:T(8,128)S(1)}, bf16[64,128]{1,0:T(8,128)(2,1)S(1)}, bf16[64,128]{1,0:T(8,128)(2,1)S(1)}, bf16[64,128]{1,0:T(8,128)(2,1)S(1)}, bf16[64,128]{1,0:T(8,128)(2,1)S(1)}) custom-call(bf16[128,1024]{1,0:T(8,128)(2,1)S(1)} %collective-permute-done.1.refs_0_, f32[1,4096]{1,0:T(1,128)S(1)} %copy-done.1, ...), custom_call_target="tpu_custom_call" | custom-call | flops 67108864 | bytes 262144 | tf_op jit(solution)/shard_map/last_block_key_value/pallas_call | solution.py:182
  11.5 0.2 collective-permute-start.3
  11.7 1.7 %collective-permute-start.4 = (bf16[64,128]{1,0:T(8,128)(2,1)S(1)}, bf16[64,128]{1,0:T(8,128)(2,1)S(1)}, u32[]{:S(2)}, u32[]{:S(2)}) collective-permute-start(bf16[64,128]{1,0:T(8,128)(2,1)S(1)} %get-tuple-element.51), channel_id=1, source_target_pairs={{0,2},{1,3},{2,0},{3,1},{4,6},{5,7},{6,4},{7,5},{8,10},{9,11},{10,... | collective-permute-start | bytes 49160 | tf_op jit(solution)/shard_map/ppermute | solution.py:300
  13.4 1.3 %collective-permute-start.5 = (bf16[64,128]{1,0:T(8,128)(2,1)S(1)}, bf16[64,128]{1,0:T(8,128)(2,1)S(1)}, u32[]{:S(2)}, u32[]{:S(2)}) collective-permute-start(bf16[64,128]{1,0:T(8,128)(2,1)S(1)} %get-tuple-element.52), channel_id=1, source_target_pairs={{0,3},{1,0},{2,1},{3,2},{4,7},{5,4},{6,5},{7,6},{8,11},{9,8},{10,9... | collective-permute-start | bytes 49160 | tf_op jit(solution)/shard_map/ppermute | solution.py:300
  14.7 0.5 %last_block_queries.2.q_ref = bf16[128,1024]{1,0:T(8,128)(2,1)S(1)} custom-call(bf16[128,1024]{1,0:T(8,128)(2,1)S(1)} %collective-permute-done.1.refs_0_, f32[1,4096]{1,0:T(1,128)S(1)} %copy-done.1, bf16[4096,1024]{1,0:T(8,128)(2,1)S(1)} %get-tuple-element.40.refs_3_.refs_2_, f32[128,1024]{1,0:T(8,128)S(1)} %get-tuple-element.45.refs_3_, ...), custom_call_target="tpu_custom_call" | custom-call | flops 268435456 | bytes 262144 | tf_op jit(solution)/shard_map/last_block_queries/pallas_call | solution.py:210
  15.2 0.0 collective-permute-done.3.refs_1_
  15.2 0.2 collective-permute-done.4.refs_2_
  15.4 0.8 %collective-permute-done.5.refs_3_ = bf16[64,128]{1,0:T(8,128)(2,1)S(1)} collective-permute-done((bf16[64,128]{1,0:T(8,128)(2,1)S(1)}, bf16[64,128]{1,0:T(8,128)(2,1)S(1)}, u32[]{:S(2)}, u32[]{:S(2)}) %collective-permute-start.5) | collective-permute-done | bytes 16416 | tf_op jit(solution)/shard_map/ppermute | solution.py:300
  16.2 0.0 copy-done.3
  16.2 0.0 copy-done.4
  16.2 0.0 copy-done.5
  16.2 2.0 %attend.2 = (bf16[128,1024]{1,0:T(8,128)(2,1)S(1)}, bf16[128,128]{1,0:T(8,128)(2,1)S(1)}, bf16[128,128]{1,0:T(8,128)(2,1)S(1)}) custom-call(s32[9]{0:T(128)S(1)} %copy-done.5, bf16[128,1024]{1,0:T(8,128)(2,1)S(1)} %last_block_queries.2.q_ref, bf16[128,1024]{1,0:T(8,128)(2,1)S(1)} %bitcast.7, bf16[64,128]{1,0:T(8,128)(2,1)S(1)} %get-tuple-element.49.refs_0_, ...), custom_call_target="tpu_custom_call" | custom-call | flops 134217728 | bytes 262144 | tf_op jit(solution)/shard_map/attend/pallas_call | solution.py:274
  18.2 1.6 %collective-permute-start.8 = (bf16[128,1024]{1,0:T(8,128)(2,1)S(1)}, bf16[128,1024]{1,0:T(8,128)(2,1)S(1)}, u32[]{:S(2)}, u32[]{:S(2)}) collective-permute-start(bf16[128,1024]{1,0:T(8,128)(2,1)S(1)} %get-tuple-element.53), channel_id=1, source_target_pairs={{0,4},{1,5},{2,6},{3,7},{4,8},{5,9},{6,10},{7,11},{8,12},{9,13},{1... | collective-permute-start | bytes 786440 | tf_op jit(solution)/shard_map/ppermute | solution.py:297
  19.8 2.0 %collective-permute-start.6 = (bf16[128,1024]{1,0:T(8,128)(2,1)S(1)}, bf16[128,1024]{1,0:T(8,128)(2,1)S(1)}, u32[]{:S(2)}, u32[]{:S(2)}) collective-permute-start(bf16[128,1024]{1,0:T(8,128)(2,1)S(1)} %get-tuple-element.53), channel_id=1, source_target_pairs={{0,6},{1,7},{2,4},{3,5},{4,10},{5,11},{6,8},{7,9},{8,14},{9,15},{1... | collective-permute-start | bytes 786440 | tf_op jit(solution)/shard_map/ppermute | solution.py:297
  21.7 8.4 %collective-permute-done.8.refs_0_.x_ref = bf16[128,1024]{1,0:T(8,128)(2,1)S(1)} collective-permute-done((bf16[128,1024]{1,0:T(8,128)(2,1)S(1)}, bf16[128,1024]{1,0:T(8,128)(2,1)S(1)}, u32[]{:S(2)}, u32[]{:S(2)}) %collective-permute-start.8) | collective-permute-done | bytes 262176 | tf_op jit(solution)/shard_map/ppermute | solution.py:297
  30.1 0.0 collective-permute-start.9
  30.1 5.8 %collective-permute-done.6.refs_0_ = bf16[128,1024]{1,0:T(8,128)(2,1)S(1)} collective-permute-done((bf16[128,1024]{1,0:T(8,128)(2,1)S(1)}, bf16[128,1024]{1,0:T(8,128)(2,1)S(1)}, u32[]{:S(2)}, u32[]{:S(2)}) %collective-permute-start.6) | collective-permute-done | bytes 262176 | tf_op jit(solution)/shard_map/ppermute | solution.py:297
  35.9 0.1 collective-permute-start.7
  36.0 0.5 %more_blocks.4 = (f32[128,1024]{1,0:T(8,128)S(1)}, f32[128,256]{1,0:T(8,128)S(1)}, f32[128,128]{1,0:T(8,128)S(1)}) custom-call(bf16[128,1024]{1,0:T(8,128)(2,1)S(1)} %collective-permute-done.8.refs_0_.x_ref, f32[1,4096]{1,0:T(1,128)S(1)} %copy-done.1, bf16[4096,1024]{1,0:T(8,128)(2,1)S(1)} %get-tuple-element.40.refs_3_.refs_2_, ...), custom_call_target="tpu_custom_call" | custom-call | flops 335544320 | bytes 262144 | tf_op jit(solution)/shard_map/more_blocks/pallas_call | solution.py:132
  36.6 0.0 collective-permute-done.9.refs_1_
  36.6 0.9 %more_blocks.5 = (f32[128,1024]{1,0:T(8,128)S(1)}, f32[128,256]{1,0:T(8,128)S(1)}, f32[128,128]{1,0:T(8,128)S(1)}) custom-call(bf16[128,1024]{1,0:T(8,128)(2,1)S(1)} %collective-permute-done.6.refs_0_, bf16[128,1024]{1,0:T(8,128)(2,1)S(1)} %collective-permute-done.9.refs_1_, f32[1,4096]{1,0:T(1,128)S(1)} %copy-done.1, ...), custom_call_target="tpu_custom_call" | custom-call | flops 671088640 | bytes 524288 | tf_op jit(solution)/shard_map/more_blocks/pallas_call | solution.py:132
  37.5 0.0 collective-permute-done.7.refs_0_
  37.5 0.5 %last_block_key_value.3 = (f32[128,128]{1,0:T(8,128)S(1)}, bf16[64,128]{1,0:T(8,128)(2,1)S(1)}, bf16[64,128]{1,0:T(8,128)(2,1)S(1)}, bf16[64,128]{1,0:T(8,128)(2,1)S(1)}, bf16[64,128]{1,0:T(8,128)(2,1)S(1)}) custom-call(bf16[128,1024]{1,0:T(8,128)(2,1)S(1)} %collective-permute-done.7.refs_0_, f32[1,4096]{1,0:T(1,128)S(1)} %copy-done.1, ...), custom_call_target="tpu_custom_call" | custom-call | flops 67108864 | bytes 262144 | tf_op jit(solution)/shard_map/last_block_key_value/pallas_call | solution.py:182
  37.9 0.4 %collective-permute-start.10 = (bf16[64,128]{1,0:T(8,128)(2,1)S(1)}, bf16[64,128]{1,0:T(8,128)(2,1)S(1)}, u32[]{:S(2)}, u32[]{:S(2)}) collective-permute-start(bf16[64,128]{1,0:T(8,128)(2,1)S(1)} %get-tuple-element.62), channel_id=1, source_target_pairs={{0,1},{1,2},{2,3},{3,0},{4,5},{5,6},{6,7},{7,4},{8,9},{9,10},{10,1... | collective-permute-start | bytes 49160 | tf_op jit(solution)/shard_map/ppermute | solution.py:300
  38.4 1.0 %collective-permute-start.11 = (bf16[64,128]{1,0:T(8,128)(2,1)S(1)}, bf16[64,128]{1,0:T(8,128)(2,1)S(1)}, u32[]{:S(2)}, u32[]{:S(2)}) collective-permute-start(bf16[64,128]{1,0:T(8,128)(2,1)S(1)} %get-tuple-element.63), channel_id=1, source_target_pairs={{0,2},{1,3},{2,0},{3,1},{4,6},{5,7},{6,4},{7,5},{8,10},{9,11},{10,... | collective-permute-start | bytes 49160 | tf_op jit(solution)/shard_map/ppermute | solution.py:300
  39.4 1.0 %collective-permute-start.12 = (bf16[64,128]{1,0:T(8,128)(2,1)S(1)}, bf16[64,128]{1,0:T(8,128)(2,1)S(1)}, u32[]{:S(2)}, u32[]{:S(2)}) collective-permute-start(bf16[64,128]{1,0:T(8,128)(2,1)S(1)} %get-tuple-element.64), channel_id=1, source_target_pairs={{0,3},{1,0},{2,1},{3,2},{4,7},{5,4},{6,5},{7,6},{8,11},{9,8},{10,9... | collective-permute-start | bytes 49160 | tf_op jit(solution)/shard_map/ppermute | solution.py:300
  40.5 0.5 %last_block_queries.3.q_ref = bf16[128,1024]{1,0:T(8,128)(2,1)S(1)} custom-call(bf16[128,1024]{1,0:T(8,128)(2,1)S(1)} %collective-permute-done.7.refs_0_, f32[1,4096]{1,0:T(1,128)S(1)} %copy-done.1, bf16[4096,1024]{1,0:T(8,128)(2,1)S(1)} %get-tuple-element.40.refs_3_.refs_2_, f32[128,1024]{1,0:T(8,128)S(1)} %get-tuple-element.57.refs_3_, ...), custom_call_target="tpu_custom_call" | custom-call | flops 268435456 | bytes 262144 | tf_op jit(solution)/shard_map/last_block_queries/pallas_call | solution.py:210
  40.9 0.2 collective-permute-done.10.refs_1_
  41.2 1.0 %collective-permute-done.11.refs_2_ = bf16[64,128]{1,0:T(8,128)(2,1)S(1)} collective-permute-done((bf16[64,128]{1,0:T(8,128)(2,1)S(1)}, bf16[64,128]{1,0:T(8,128)(2,1)S(1)}, u32[]{:S(2)}, u32[]{:S(2)}) %collective-permute-start.11) | collective-permute-done | bytes 16416 | tf_op jit(solution)/shard_map/ppermute | solution.py:300
  42.1 0.0 collective-permute-done.12.refs_3_
  42.1 2.1 %attend.3 = bf16[128,1024]{1,0:T(8,128)(2,1)} custom-call(s32[9]{0:T(128)S(1)} %copy-done.5, bf16[128,1024]{1,0:T(8,128)(2,1)S(1)} %last_block_queries.3.q_ref, bf16[128,1024]{1,0:T(8,128)(2,1)S(1)} %collective-permute-done.8.refs_0_.x_ref, bf16[64,128]{1,0:T(8,128)(2,1)S(1)} %get-tuple-element.61.refs_0_, ...), custom_call_target="tpu_custom_call" | custom-call | flops 134217728 | bytes 262144 | tf_op jit(solution)/shard_map/attend/pallas_call | solution.py:274
Async XLA Ops:
  0.0 9.5 %collective-permute-start = (bf16[128,1024]{1,0:T(8,128)(2,1)}, bf16[128,1024]{1,0:T(8,128)(2,1)S(1)}, u32[]{:S(2)}, u32[]{:S(2)}) collective-permute-start(bf16[128,1024]{1,0:T(8,128)(2,1)} %bitcast.4), channel_id=1, source_target_pairs={{0,2},{1,3},{2,0},{3,1},{4,6},{5,7},{6,4},{7,5},{8,10},{9,11},{10,... | collective-permute-start | bytes 786440 | tf_op jit(solution)/shard_map/ppermute | solution.py:297
  3.0 6.5 %collective-permute-start.2 = (bf16[128,1024]{1,0:T(8,128)(2,1)}, bf16[128,1024]{1,0:T(8,128)(2,1)S(1)}, u32[]{:S(2)}, u32[]{:S(2)}) collective-permute-start(bf16[128,1024]{1,0:T(8,128)(2,1)} %bitcast.5), channel_id=1, source_target_pairs={{0,1},{1,0},{2,3},{3,2},{4,5},{5,4},{6,7},{7,6},{8,9},{9,8},{10,11... | collective-permute-start | bytes 786440 | tf_op jit(solution)/shard_map/ppermute | solution.py:297
  3.0 0.7 %copy-start = (f32[1,4096]{1,0:T(1,128)S(1)}, f32[1,4096]{1,0:T(1,128)}, u32[]{:S(2)}) copy-start(f32[1,4096]{1,0:T(1,128)} %refs_1_.9) | copy-start | bytes 49156
  3.7 0.9 %copy-start.2 = (bf16[1,128,1024]{2,1,0:T(8,128)(2,1)S(1)}, bf16[1,128,1024]{2,1,0:T(8,128)(2,1)}, u32[]{:S(2)}) copy-start(bf16[1,128,1024]{2,1,0:T(8,128)(2,1)} %param.6) | copy-start | bytes 786436
  4.6 4.8 %copy-start.1 = (f32[1,4096]{1,0:T(1,128)S(1)}, f32[1,4096]{1,0:T(1,128)}, u32[]{:S(2)}) copy-start(f32[1,4096]{1,0:T(1,128)} %refs_1_.9) | copy-start | bytes 49156
  9.5 1.5 %collective-permute-start.1 = (bf16[128,1024]{1,0:T(8,128)(2,1)S(1)}, bf16[128,1024]{1,0:T(8,128)(2,1)S(1)}, u32[]{:S(2)}, u32[]{:S(2)}) collective-permute-start(bf16[128,1024]{1,0:T(8,128)(2,1)S(1)} %collective-permute-done.refs_1_), channel_id=1, source_target_pairs={{0,1},{1,0},{2,3},{3,2},{4,5},{5,4},{6,7},{7,6},{8,9},{9,8},{10,11... | collective-permute-start | bytes 786440 | tf_op jit(solution)/shard_map/ppermute | solution.py:297
  10.4 5.8 %copy-start.3 = (bf16[1,128,1024]{2,1,0:T(8,128)(2,1)S(1)}, bf16[1,128,1024]{2,1,0:T(8,128)(2,1)}, u32[]{:S(2)}) copy-start(bf16[1,128,1024]{2,1,0:T(8,128)(2,1)} %param.6) | copy-start | bytes 786436
  10.4 5.8 %copy-start.4 = (bf16[128,1024]{1,0:T(8,128)(2,1)S(1)}, bf16[128,1024]{1,0:T(8,128)(2,1)}, u32[]{:S(2)}) copy-start(bf16[128,1024]{1,0:T(8,128)(2,1)} %refs_4_.1) | copy-start | bytes 786436
  10.4 5.8 %copy-start.5 = (s32[9]{0:T(128)S(1)}, s32[9]{0:T(128)}, u32[]{:S(2)}) copy-start(s32[9]{0:T(128)} %doc_ref.3) | copy-start | bytes 112
  11.5 3.7 %collective-permute-start.3 = (bf16[64,128]{1,0:T(8,128)(2,1)S(1)}, bf16[64,128]{1,0:T(8,128)(2,1)S(1)}, u32[]{:S(2)}, u32[]{:S(2)}) collective-permute-start(bf16[64,128]{1,0:T(8,128)(2,1)S(1)} %get-tuple-element.50), channel_id=1, source_target_pairs={{0,1},{1,2},{2,3},{3,0},{4,5},{5,6},{6,7},{7,4},{8,9},{9,10},{10,1... | collective-permute-start | bytes 49160 | tf_op jit(solution)/shard_map/ppermute | solution.py:300
  11.7 3.7 %collective-permute-start.4 = (bf16[64,128]{1,0:T(8,128)(2,1)S(1)}, bf16[64,128]{1,0:T(8,128)(2,1)S(1)}, u32[]{:S(2)}, u32[]{:S(2)}) collective-permute-start(bf16[64,128]{1,0:T(8,128)(2,1)S(1)} %get-tuple-element.51), channel_id=1, source_target_pairs={{0,2},{1,3},{2,0},{3,1},{4,6},{5,7},{6,4},{7,5},{8,10},{9,11},{10,... | collective-permute-start | bytes 49160 | tf_op jit(solution)/shard_map/ppermute | solution.py:300
  13.4 2.8 %collective-permute-start.5 = (bf16[64,128]{1,0:T(8,128)(2,1)S(1)}, bf16[64,128]{1,0:T(8,128)(2,1)S(1)}, u32[]{:S(2)}, u32[]{:S(2)}) collective-permute-start(bf16[64,128]{1,0:T(8,128)(2,1)S(1)} %get-tuple-element.52), channel_id=1, source_target_pairs={{0,3},{1,0},{2,1},{3,2},{4,7},{5,4},{6,5},{7,6},{8,11},{9,8},{10,9... | collective-permute-start | bytes 49160 | tf_op jit(solution)/shard_map/ppermute | solution.py:300
  18.2 11.9 %collective-permute-start.8 = (bf16[128,1024]{1,0:T(8,128)(2,1)S(1)}, bf16[128,1024]{1,0:T(8,128)(2,1)S(1)}, u32[]{:S(2)}, u32[]{:S(2)}) collective-permute-start(bf16[128,1024]{1,0:T(8,128)(2,1)S(1)} %get-tuple-element.53), channel_id=1, source_target_pairs={{0,4},{1,5},{2,6},{3,7},{4,8},{5,9},{6,10},{7,11},{8,12},{9,13},{1... | collective-permute-start | bytes 786440 | tf_op jit(solution)/shard_map/ppermute | solution.py:297
  19.8 16.1 %collective-permute-start.6 = (bf16[128,1024]{1,0:T(8,128)(2,1)S(1)}, bf16[128,1024]{1,0:T(8,128)(2,1)S(1)}, u32[]{:S(2)}, u32[]{:S(2)}) collective-permute-start(bf16[128,1024]{1,0:T(8,128)(2,1)S(1)} %get-tuple-element.53), channel_id=1, source_target_pairs={{0,6},{1,7},{2,4},{3,5},{4,10},{5,11},{6,8},{7,9},{8,14},{9,15},{1... | collective-permute-start | bytes 786440 | tf_op jit(solution)/shard_map/ppermute | solution.py:297
  30.1 6.4 %collective-permute-start.9 = (bf16[128,1024]{1,0:T(8,128)(2,1)S(1)}, bf16[128,1024]{1,0:T(8,128)(2,1)S(1)}, u32[]{:S(2)}, u32[]{:S(2)}) collective-permute-start(bf16[128,1024]{1,0:T(8,128)(2,1)S(1)} %collective-permute-done.8.refs_0_.x_ref), channel_id=1, source_target_pairs={{0,1},{1,0},{2,3},{3,2},{4,5},{5,4},{6,7},{7,6},{8,9},{9,8},{10,11... | collective-permute-start | bytes 786440 | tf_op jit(solution)/shard_map/ppermute | solution.py:297
  35.9 1.6 %collective-permute-start.7 = (bf16[128,1024]{1,0:T(8,128)(2,1)S(1)}, bf16[128,1024]{1,0:T(8,128)(2,1)S(1)}, u32[]{:S(2)}, u32[]{:S(2)}) collective-permute-start(bf16[128,1024]{1,0:T(8,128)(2,1)S(1)} %collective-permute-done.6.refs_0_), channel_id=1, source_target_pairs={{0,1},{1,0},{2,3},{3,2},{4,5},{5,4},{6,7},{7,6},{8,9},{9,8},{10,11... | collective-permute-start | bytes 786440 | tf_op jit(solution)/shard_map/ppermute | solution.py:297
  37.9 3.2 %collective-permute-start.10 = (bf16[64,128]{1,0:T(8,128)(2,1)S(1)}, bf16[64,128]{1,0:T(8,128)(2,1)S(1)}, u32[]{:S(2)}, u32[]{:S(2)}) collective-permute-start(bf16[64,128]{1,0:T(8,128)(2,1)S(1)} %get-tuple-element.62), channel_id=1, source_target_pairs={{0,1},{1,2},{2,3},{3,0},{4,5},{5,6},{6,7},{7,4},{8,9},{9,10},{10,1... | collective-permute-start | bytes 49160 | tf_op jit(solution)/shard_map/ppermute | solution.py:300
  38.4 3.7 %collective-permute-start.11 = (bf16[64,128]{1,0:T(8,128)(2,1)S(1)}, bf16[64,128]{1,0:T(8,128)(2,1)S(1)}, u32[]{:S(2)}, u32[]{:S(2)}) collective-permute-start(bf16[64,128]{1,0:T(8,128)(2,1)S(1)} %get-tuple-element.63), channel_id=1, source_target_pairs={{0,2},{1,3},{2,0},{3,1},{4,6},{5,7},{6,4},{7,5},{8,10},{9,11},{10,... | collective-permute-start | bytes 49160 | tf_op jit(solution)/shard_map/ppermute | solution.py:300
  39.4 2.7 %collective-permute-start.12 = (bf16[64,128]{1,0:T(8,128)(2,1)S(1)}, bf16[64,128]{1,0:T(8,128)(2,1)S(1)}, u32[]{:S(2)}, u32[]{:S(2)}) collective-permute-start(bf16[64,128]{1,0:T(8,128)(2,1)S(1)} %get-tuple-element.64), channel_id=1, source_target_pairs={{0,3},{1,0},{2,1},{3,2},{4,7},{5,4},{6,5},{7,6},{8,11},{9,8},{10,9... | collective-permute-start | bytes 49160 | tf_op jit(solution)/shard_map/ppermute | solution.py:300

commit v2 on v1

--- a/solution.py
+++ b/solution.py
@@ -105,9 +105,9 @@
         gain_ref, wq_ref, wkv_ref, accq_out, acckv_out, ssq_out = rest
     else:
         gain_ref, wq_ref, wkv_ref, accq_ref, acckv_ref, ssq_ref, accq_out, acckv_out, ssq_out = rest
-    width = xs[0].shape[1]
     me = lax.axis_index("head")
     for i, x_ref in enumerate(xs):
+        width = x_ref.shape[1]
         block = places[i](me)
         normed, ssq = gained(x_ref[...], gain_ref, block)
         rows = rows_of(block, width)
@@ -146,16 +146,16 @@
     xs, rest = refs[:count], refs[count:]
     gain_ref, wkv_ref, acckv_ref, ssq_ref = rest[:4]
     scale_ref, pieces, turned = rest[4], rest[5:-1], rest[-1]
-    width = xs[0].shape[1]
     n = lax.axis_size("head")
     me = lax.axis_index("head")
     total, ssq = acckv_ref[...], ssq_ref[...]
     for i, x_ref in enumerate(xs):
         block = places[i](me)
+        width = x_ref.shape[1]
         normed, more = gained(x_ref[...], gain_ref, block)
         ssq = ssq + more
         total = total + jnp.dot(normed, wkv_ref[rows_of(block, width), :], preferred_element_type=f32)
-    scale = lax.rsqrt(jnp.sum(ssq, axis=1, keepdims=True) / (n * width) + epsilon)
+    scale = lax.rsqrt(jnp.sum(ssq, axis=1, keepdims=True) / gain_ref.shape[1] + epsilon)
     scale_ref[...] = jnp.broadcast_to(scale, scale_ref.shape)
     kv = (total * scale).astype(bf16)
     columns = kv.shape[1]
@@ -165,14 +165,10 @@
     group, which, feature = row // (2 * features), (row // features) % 2, row % features
     choose = jnp.where(col == (feature * KVH + group) * 2 + which, 1.0, 0.0).astype(bf16)
     turned[...] = lax.dot_general(choose, kv, (((1,), (1,)), ((), ())), preferred_element_type=f32)
-    for k in range(n):
-        group_there = group_of(lax.rem(me + k, n), n)
-        rows = pl.ds(pl.multiple_of(group_there * 2 * features, 2 * features), 2 * features)
-        pieces[k][...] = turned[rows, :].astype(bf16)
-
-
-def group_of(head_index, n):
-    return head_index * KVH // n
+    size = 2 * features
+    for flip in range(n):
+        group_there = lax.bitwise_xor(me, jnp.int32(flip)) * KVH // n
+        pieces[flip][...] = turned[pl.ds(pl.multiple_of(group_there * size, size), size), :].astype(bf16)
 
 
 def last_kv(xs, places, gain, wkv, acckv, ssq, n):
@@ -218,65 +214,95 @@
     )(*operands)
 
 
-def attend_kernel(n, sections, turn, doc_ref, q_ref, x_ref, *refs):
-    pieces, rest = refs[:n], refs[n:]
+def openings_kernel(sections, doc_ref, first_ref, second_ref):
+    tokens = first_ref.shape[0]
+    for turn, out_ref in enumerate((first_ref, second_ref)):
+        start = (sections - 1 + turn - lax.axis_index("section")) * tokens
+        here = start + lax.broadcasted_iota(jnp.int32, out_ref.shape, 0)
+        opened = jnp.zeros(out_ref.shape, jnp.int32)
+        end = jnp.int32(0)
+        for d in range(doc_ref.shape[0]):
+            end = end + doc_ref[d]
+            opened = jnp.where(end <= here, end, opened)
+        out_ref[...] = opened
+
+
+def openings(doc_lengths, tokens, sections):
+    return pl.pallas_call(
+        functools.partial(openings_kernel, sections),
+        out_shape=(VMEM((tokens, HD), jnp.int32),) * 2,
+        in_specs=[smem],
+        out_specs=(vmem,) * 2,
+        compiler_params=params,
+        name="openings",
+    )(doc_lengths)
+
+
+def attend_kernel(n, sections, turn, heads, x_count, extra_count, gathered, *refs):
+    opened_ref, q_ref = refs[:2]
+    x_refs, rest = refs[2 : 2 + x_count], refs[2 + x_count :]
+    extras, outs = rest[:extra_count], rest[extra_count:]
+    if gathered:
+        *outs, gather = outs
+    out_ref = outs[0]
     tokens = q_ref.shape[0]
-    me = lax.axis_index("head")
     section = lax.axis_index("section")
-    first_start = (sections - 1 - section) * tokens
-    features = pieces[0].shape[0] // 2
-    if turn == 1:
-        fresh_ref, out_ref, keys_ref, values_ref, gather = rest
-        start, base = first_start, first_start
+    base = (sections - 1 - section) * tokens
+    start = base + (turn - 1) * tokens
+    if gathered:
+        features = extras[0].shape[0] // 2
+        for flip in range(n):
+            source = lax.bitwise_xor(lax.axis_index("head"), jnp.int32(flip))
+            piece = extras[flip][...].astype(f32)
+            rows = pl.ds(pl.multiple_of(source * features, features), features)
+            gather[0, rows, :] = piece[:features]
+            gather[1, rows, :] = piece[features:]
+        keys, values = gather[0].astype(bf16), gather[1].astype(bf16)
+        extras = extras[n:]
+        if turn == 1:
+            outs[1][...], outs[2][...] = keys, values
     else:
-        old_keys, old_values, out_ref, gather = rest
-        start, base = first_start + tokens, first_start
-    for k in range(n):
-        source = lax.rem(me + n - k, n)
-        piece = pieces[k][...].astype(f32)
-        rows = pl.ds(pl.multiple_of(source * features, features), features)
-        gather[0, rows, :] = piece[:features]
-        gather[1, rows, :] = piece[features:]
-    keys, values = gather[0].astype(bf16), gather[1].astype(bf16)
-    if turn == 1:
-        keys_ref[...], values_ref[...] = keys, values
+        keys, values, *extras = extras[0][...], extras[1][...], *extras[2:]
+    if turn == 2:
+        keys = jnp.concatenate([extras[0][...], keys], axis=1)
+        values = jnp.concatenate([extras[1][...], values], axis=1)
     else:
-        keys = jnp.concatenate([old_keys[...], keys], axis=1)
-        values = jnp.concatenate([old_values[...], values], axis=1)
-    here = start + lax.broadcasted_iota(jnp.int32, (tokens, 1), 0)
-    there = base + lax.broadcasted_iota(jnp.int32, (1, keys.shape[1]), 1)
-    opened = jnp.zeros((tokens, 1), jnp.int32)
-    end = jnp.int32(0)
-    for d in range(doc_ref.shape[0]):
-        end = end + doc_ref[d]
-        opened = jnp.where(end <= here, end, opened)
-    allowed = (there >= opened) & (there <= here)
-    for h in range(q_ref.shape[1] // HD):
-        columns = slice(h * HD, (h + 1) * HD)
-        scores = jnp.dot(q_ref[:, columns], keys, preferred_element_type=f32) * (1.0 / math.sqrt(HD))
-        scores = jnp.where(allowed, scores, masked_score)
-        expon = jnp.exp(scores - jnp.max(scores, axis=1, keepdims=True))
-        weights = (expon * (1.0 / jnp.sum(expon, axis=1, keepdims=True))).astype(bf16)
-        mixed = lax.dot_general(weights, values, (((1,), (1,)), ((), ())), preferred_element_type=f32)
-        out = (x_ref[:, columns].astype(f32) + mixed.astype(bf16).astype(f32)).astype(bf16)
+        fresh_ref = extras[0]
+    here = start + lax.broadcasted_iota(jnp.int32, (tokens, keys.shape[1]), 0)
+    there = base + lax.broadcasted_iota(jnp.int32, (tokens, keys.shape[1]), 1)
+    allowed = (there >= opened_ref[:, 0:1]) & (there <= here)
+    count = heads[1] - heads[0]
+    stacked = jnp.concatenate([q_ref[:, h * HD : (h + 1) * HD] for h in range(*heads)], axis=0)
+    scores = jnp.dot(stacked, keys, preferred_element_type=f32) * (1.0 / math.sqrt(HD))
+    scores = jnp.where(allowed[None], scores.reshape(count, tokens, -1), masked_score)
+    expon = jnp.exp(scores - jnp.max(scores, axis=2, keepdims=True))
+    weights = (expon * (1.0 / jnp.sum(expon, axis=2, keepdims=True))).astype(bf16)
+    mixed = lax.dot_general(
+        weights.reshape(count * tokens, -1), values, (((1,), (1,)), ((), ())), preferred_element_type=f32
+    ).astype(bf16)
+    for i in range(count):
+        column = (heads[0] + i) * HD
+        x_width = x_refs[0].shape[1]
+        x_ref, inside = x_refs[column // x_width], column % x_width
+        out = x_ref[:, inside : inside + HD].astype(f32) + mixed[i * tokens : (i + 1) * tokens].astype(f32)
         if turn == 1:
-            out = jnp.where(section == sections - 1, fresh_ref[:, columns].astype(f32), out.astype(f32)).astype(bf16)
-        out_ref[:, columns] = out
-
-
-def attend(doc_lengths, q, x, pieces, turn, extra, sections):
-    n = len(pieces)
+            out = out.astype(bf16).astype(f32)
+            out = jnp.where(section == sections - 1, fresh_ref[:, column : column + HD].astype(f32), out)
+        out_ref[:, i * HD : (i + 1) * HD] = out.astype(bf16)
+
+
+def attend(opened, q, xs, extra, turn, heads, gathered, n, sections):
     tokens = q.shape[0]
-    out = (jax.ShapeDtypeStruct(q.shape, bf16),)
-    if turn == 1:
+    out = (jax.ShapeDtypeStruct((tokens, (heads[1] - heads[0]) * HD), bf16),)
+    if turn == 1 and gathered:
         out = out + (VMEM((HD, tokens), bf16),) * 2
-    operands = [doc_lengths, q, x, *pieces, *extra]
-    return pl.pallas_call(
-        functools.partial(attend_kernel, n, sections, turn),
+    operands = [opened, q, *xs, *extra]
+    return pl.pallas_call(
+        functools.partial(attend_kernel, n, sections, turn, heads, len(xs), len(extra), gathered),
         out_shape=out,
-        in_specs=[smem] + [vmem] * (len(operands) - 1),
+        in_specs=[vmem] * len(operands),
         out_specs=(vmem,) * len(out),
-        scratch_shapes=[VMEM((2, HD, tokens), f32)],
+        scratch_shapes=[VMEM((2, HD, tokens), f32)] if gathered else [],
         cost_estimate=cost(8 * tokens * tokens * q.shape[1], 2 * q.size),
         compiler_params=params,
         name="attend",
@@ -289,6 +315,9 @@
     own = entering[0]
     w_q, w_kv = w_query[0], w_key_value[0]
     gain = norm_gain
+    tokens, width = own.shape
+    heads = w_q.shape[1] // HD
+    half = heads // 2
 
     def moved(array, by, flip):
         pairs = [
@@ -296,51 +325,70 @@
         ]
         return lax.ppermute(array, ("section", "head"), pairs)
 
-    def turned(array, by):
-        return lax.ppermute(array, "head", [(h, (h + by) % n) for h in range(n)])
-
-    def finish(xs, places, wq, wkv, state, x, turn, extra):
-        accq, acckv, ssq = state
+    def exchanged(xs, places, wkv, state):
+        _, acckv, ssq = state
         scale, *pieces = last_kv(xs, places, gain, wkv, acckv, ssq, n)
-        arrived = [pieces[0]] + [turned(pieces[k], k) for k in range(1, n)]
-        q = last_q(xs, places, gain, wq, accq, scale)
-        return attend(doc_lengths, q, x, arrived, turn, extra, sections)
-
-    paired = n == 4
-    xor = [functools.partial(lambda flip, me: lax.bitwise_xor(me, jnp.int32(flip)), flip) for flip in range(4)]
-    others = [functools.partial(lambda k, me: lax.rem(me + k, jnp.int32(n)), k) for k in range(n)]
+        crossing = {flip: moved(pieces[flip], 0, flip) for flip in range(n - 1, 0, -1)}
+        return scale, [pieces[0]] + [crossing[flip] for flip in range(1, n)]
 
     def rest_of(array):
         every = lax.all_gather(array, "head", axis=0)
         me = lax.axis_index("head")
         return [lax.dynamic_index_in_dim(every, (me + k) % n, 0, False) for k in range(1, n)]
 
+    paired = n == 4
+    others = [functools.partial(lambda k, me: lax.rem(me + k, jnp.int32(n)), k) for k in range(n)]
+
+    def place(flip, parts=1, part=0):
+        return lambda me: lax.bitwise_xor(me, jnp.int32(flip)) * parts + part
+
     if paired:
         over = moved(own, 0, 2)
         beside = moved(own, 0, 1)
     *state, wq, wkv = first_block(own, gain, w_q, w_kv)
+    opened = openings(doc_lengths, tokens, sections)
     if paired:
-        over, *state = lax.optimization_barrier((over, *state))
+        over, opened, *state = lax.optimization_barrier((over, opened, *state))
         passed = moved(over, 0, 1)
-        state = more_blocks([beside, over], [xor[1], xor[2]], gain, wq, wkv, state)
-        last, places = [passed], [xor[3]]
+        state = more_blocks([beside, over], [place(1), place(2)], gain, wq, wkv, state)
+        last, places = [passed], [place(3)]
     else:
         last, places = rest_of(own), others[1:]
-    sent, keys, values = finish(last, places, wq, wkv, state, own, 1, [fresh_slice])
+    scale, received = exchanged(last, places, wkv, state)
+    q = last_q(last, places, gain, wq, state[0], scale)
+    first_heads = (0, half) if paired else (0, heads)
+    sent, keys, values = attend(
+        opened[0], q, [own], [*received, fresh_slice], 1, first_heads, True, n, sections
+    )
 
     if paired:
-        mine = moved(sent, 1, 0)
-        over = moved(sent, 1, 2)
-        beside = moved(mine, 0, 1)
-        passed = moved(over, 0, 1)
-        state = more_blocks([mine], [xor[0]], gain, wq, wkv, None)
-        state = more_blocks([over, beside], [xor[2], xor[1]], gain, wq, wkv, state)
-        last, places = [passed], [xor[3]]
+        mine_a = moved(sent, 1, 0)
+        (sent,) = attend(
+            opened[0], q, [own], [keys, values, fresh_slice], 1, (half, heads), False, n, sections
+        )
+        over_b = moved(sent, 1, 2)
+        mine_b = moved(sent, 1, 0)
+        mine_a, _ = lax.optimization_barrier((mine_a, sent))
+        over_a = moved(mine_a, 0, 2)
+        beside_a = moved(mine_a, 0, 1)
+        state = more_blocks([mine_a], [place(0, 2, 0)], gain, wq, wkv, None)
+        mine_b, over_b, *state = lax.optimization_barrier((mine_b, over_b, *state))
+        beside_b = moved(mine_b, 0, 1)
+        passed_b = moved(over_b, 0, 1)
+        passed_a = moved(over_a, 0, 1)
+        early = [beside_a, over_a, mine_b, over_b]
+        places = [place(1, 2, 0), place(2, 2, 0), place(0, 2, 1), place(2, 2, 1)]
+        state = more_blocks(early, places, gain, wq, wkv, state)
+        last, places = [passed_a, beside_b, passed_b], [place(3, 2, 0), place(1, 2, 1), place(3, 2, 1)]
+        mine = [mine_a, mine_b]
     else:
-        mine = moved(sent, 1, 0)
-        state = more_blocks([mine], [others[0]], gain, wq, wkv, None)
-        last, places = rest_of(mine), others[1:]
-    return finish(last, places, wq, wkv, state, mine, 2, [keys, values])[0][None]
+        mine = [moved(sent, 1, 0)]
+        state = more_blocks(mine, others[:1], gain, wq, wkv, None)
+        last, places = rest_of(mine[0]), others[1:]
+    scale, received = exchanged(last, places, wkv, state)
+    q = last_q(last, places, gain, wq, state[0], scale)
+    out = attend(opened[1], q, mine, [*received, keys, values], 2, (0, heads), True, n, sections)
+    return out[0][None]
 
 
 def solution(mesh):

time: 44.9 us -> 40.2 us (0.90)
  waiting for transfers between devices: 17.6 us -> 10.7 us
  starting transfers between devices: 12.4 us -> 15.3 us
  Pallas kernels: 12.5 us -> 11.4 us
  local copies, waits for them, and re-layouts: 1.69 us -> 2.33 us
    ppermute x7 -> x17, starting transfers between devices: 6.6 us -> 15.3 us  [moved(): return lax.ppermute(array, ('section', 'head'), pairs)]
    ppermute x6 -> x0, starting transfers between devices: 5.79 us -> none  [turned(): return lax.ppermute(array, 'head', [(h, (h + by) % n) for h in range(n)])]
    ppermute x7 -> x17, waiting for transfers between devices: 15.4 us -> 10.7 us  [moved(): return lax.ppermute(array, ('section', 'head'), pairs)]
    ppermute x6 -> x0, waiting for transfers between devices: 2.16 us -> none  [turned(): return lax.ppermute(array, 'head', [(h, (h + by) % n) for h in range(n)])]
    pallas_call x2 -> x4, Pallas kernels: 4.12 us -> 3.18 us  [the longest x3 2.55 us: attend(): pl.pallas_call(functools.partial(attend_kernel, n, sections, turn, heads,...]
    unnamed x12, local copies, waits for them, and re-layouts: 1.69 us -> 2.33 us
  transfers between devices with their start and end apart: 13 -> 17, of which waited for: 8 -> 10; matrix products, arithmetic and copies ran while one was open for 0% -> 0% of each run, Pallas kernels for 17% -> 21%
where the time goes in v2:
time: 40.2 us; the launch traced here: 39.9 us
  starting transfers between devices  15.3 us (38%)
  Pallas kernels  11.4 us (28%)
  waiting for transfers between devices  10.7 us (27%)
  local copies, waits for them, and re-layouts  2.33 us (6%)
    ppermute x17, starting transfers between devices, moved(): return lax.ppermute(array, ('section', 'head'), pairs)  15.3 us
    ppermute x17, waiting for transfers between devices, moved(): return lax.ppermute(array, ('section', 'head'), pairs)  10.7 us
    pallas_call x1, Pallas kernels, first_block(): pl.pallas_call(first_block_kernel, out_shape=(VMEM((tokens, wq.shape[1]),...  4.17 us
    pallas_call x3, Pallas kernels, attend(): pl.pallas_call(functools.partial(attend_kernel, n, sections, turn, heads,...  2.55 us
    unnamed x12, local copies, waits for them, and re-layouts  2.33 us
    pallas_call x3, Pallas kernels, more_blocks(): pl.pallas_call(functools.partial(blocks_kernel, len(xs), state is None, p...  2.1 us
    pallas_call x2, Pallas kernels, last_q(): pl.pallas_call(functools.partial(last_q_kernel, len(xs), places), out_sha...  1.04 us
    pallas_call x2, Pallas kernels, last_kv(): pl.pallas_call(functools.partial(last_kv_kernel, len(xs), places), out_sh...  0.95 us
  transfers between devices with their start and end apart: 17, of which 10 were waited for; matrix products, arithmetic and copies ran while one was open for 0% of the time, Pallas kernels for 21%

profile of v2, /device:TPU:0, one launch (start us, length us, event | category | flops | bytes accessed | tf_op | source)
XLA Modules:
  0.0 39.9 jit_solution(5889377554980090662)
XLA Ops:
  0.0 3.0 %collective-permute-start = (bf16[128,1024]{1,0:T(8,128)(2,1)}, bf16[128,1024]{1,0:T(8,128)(2,1)S(1)}, u32[]{:S(2)}, u32[]{:S(2)}) collective-permute-start(bf16[128,1024]{1,0:T(8,128)(2,1)} %bitcast.4), channel_id=1, source_target_pairs={{0,2},{1,3},{2,0},{3,1},{4,6},{5,7},{6,4},{7,5},{8,10},{9,11},{10,... | collective-permute-start | bytes 786440 | tf_op jit(solution)/shard_map/ppermute | solution.py:326
  3.0 0.0 collective-permute-start.2
  3.0 0.0 copy-start.5
  3.0 0.7 %copy-done.5 = s32[9]{0:T(128)S(1)} copy-done((s32[9]{0:T(128)S(1)}, s32[9]{0:T(128)}, u32[]{:S(2)}) %copy-start.5) | copy-done | bytes 60
  3.6 0.6 %openings.1 = (s32[128,128]{1,0:T(8,128)S(1)}, s32[128,128]{1,0:T(8,128)S(1)}) custom-call(s32[9]{0:T(128)S(1)} %copy-done.5), custom_call_target="tpu_custom_call" | custom-call | tf_op jit(solution)/shard_map/openings/pallas_call | solution.py:231
  4.3 0.0 copy-start
  4.3 0.9 %copy-done = bf16[1,128,1024]{2,1,0:T(8,128)(2,1)S(1)} copy-done((bf16[1,128,1024]{2,1,0:T(8,128)(2,1)S(1)}, bf16[1,128,1024]{2,1,0:T(8,128)(2,1)}, u32[]{:S(2)}) %copy-start) | copy-done | bytes 262168
  5.2 0.0 copy-start.2
  5.2 0.7 %copy-done.2 = f32[1,4096]{1,0:T(1,128)S(1)} copy-done((f32[1,4096]{1,0:T(1,128)S(1)}, f32[1,4096]{1,0:T(1,128)}, u32[]{:S(2)}) %copy-start.2) | copy-done | bytes 16408
  5.9 0.0 copy-start.3
  5.9 4.2 %load_and_first_block.1 = (f32[128,1024]{1,0:T(8,128)S(1)}, f32[128,256]{1,0:T(8,128)S(1)}, f32[128,128]{1,0:T(8,128)S(1)}, bf16[4096,1024]{1,0:T(8,128)(2,1)S(1)}, bf16[4096,256]{1,0:T(8,128)(2,1)S(1)}) custom-call(bf16[128,1024]{1,0:T(8,128)(2,1)S(1)} %bitcast.6, f32[1,4096]{1,0:T(1,128)S(1)} %copy-done.2, bf16[4096,1024]{1,0:T(8,128)(2,1)} %bitcast.9, ...), custom_call_target="tpu_custom_call" | custom-call | flops 335544320 | bytes 10485760 | tf_op jit(solution)/shard_map/load_and_first_block/pallas_call | solution.py:84
  10.1 0.0 collective-permute-done.refs_1_
  10.1 0.6 %collective-permute-start.1 = (bf16[128,1024]{1,0:T(8,128)(2,1)S(1)}, bf16[128,1024]{1,0:T(8,128)(2,1)S(1)}, u32[]{:S(2)}, u32[]{:S(2)}) collective-permute-start(bf16[128,1024]{1,0:T(8,128)(2,1)S(1)} %collective-permute-done.refs_1_), channel_id=1, source_target_pairs={{0,1},{1,0},{2,3},{3,2},{4,5},{5,4},{6,7},{7,6},{8,9},{9,8},{10,11... | collective-permute-start | bytes 786440 | tf_op jit(solution)/shard_map/ppermute | solution.py:326
  10.7 0.0 collective-permute-done.2.refs_0_
  10.7 0.0 copy-done.3
  10.7 0.9 %more_blocks.3 = (f32[128,1024]{1,0:T(8,128)S(1)}, f32[128,256]{1,0:T(8,128)S(1)}, f32[128,128]{1,0:T(8,128)S(1)}) custom-call(bf16[128,1024]{1,0:T(8,128)(2,1)S(1)} %collective-permute-done.2.refs_0_, bf16[128,1024]{1,0:T(8,128)(2,1)S(1)} %collective-permute-done.refs_1_, f32[1,4096]{1,0:T(1,128)S(1)} %copy-done.3, ...), custom_call_target="tpu_custom_call" | custom-call | flops 671088640 | bytes 524288 | tf_op jit(solution)/shard_map/more_blocks/pallas_call | solution.py:132
  11.6 0.0 copy-start.1
  11.6 0.0 copy-start.4
  11.6 0.2 collective-permute-done.1.refs_0_
  11.9 0.5 %last_block_key_value.2 = (f32[128,128]{1,0:T(8,128)S(1)}, bf16[64,128]{1,0:T(8,128)(2,1)S(1)}, bf16[64,128]{1,0:T(8,128)(2,1)S(1)}, bf16[64,128]{1,0:T(8,128)(2,1)S(1)}, bf16[64,128]{1,0:T(8,128)(2,1)S(1)}) custom-call(bf16[128,1024]{1,0:T(8,128)(2,1)S(1)} %collective-permute-done.1.refs_0_, f32[1,4096]{1,0:T(1,128)S(1)} %copy-done.3, ...), custom_call_target="tpu_custom_call" | custom-call | flops 67108864 | bytes 262144 | tf_op jit(solution)/shard_map/last_block_key_value/pallas_call | solution.py:178
  12.3 0.4 %collective-permute-start.3 = (bf16[64,128]{1,0:T(8,128)(2,1)S(1)}, bf16[64,128]{1,0:T(8,128)(2,1)S(1)}, u32[]{:S(2)}, u32[]{:S(2)}) collective-permute-start(bf16[64,128]{1,0:T(8,128)(2,1)S(1)} %get-tuple-element.64), channel_id=1, source_target_pairs={{0,1},{1,0},{2,3},{3,2},{4,5},{5,4},{6,7},{7,6},{8,9},{9,8},{10,11... | collective-permute-start | bytes 49160 | tf_op jit(solution)/shard_map/ppermute | solution.py:326
  12.8 0.7 %collective-permute-start.4 = (bf16[64,128]{1,0:T(8,128)(2,1)S(1)}, bf16[64,128]{1,0:T(8,128)(2,1)S(1)}, u32[]{:S(2)}, u32[]{:S(2)}) collective-permute-start(bf16[64,128]{1,0:T(8,128)(2,1)S(1)} %get-tuple-element.65), channel_id=1, source_target_pairs={{0,2},{1,3},{2,0},{3,1},{4,6},{5,7},{6,4},{7,5},{8,10},{9,11},{10,... | collective-permute-start | bytes 49160 | tf_op jit(solution)/shard_map/ppermute | solution.py:326
  13.4 0.8 %collective-permute-start.5 = (bf16[64,128]{1,0:T(8,128)(2,1)S(1)}, bf16[64,128]{1,0:T(8,128)(2,1)S(1)}, u32[]{:S(2)}, u32[]{:S(2)}) collective-permute-start(bf16[64,128]{1,0:T(8,128)(2,1)S(1)} %get-tuple-element.66), channel_id=1, source_target_pairs={{0,3},{1,2},{2,1},{3,0},{4,7},{5,6},{6,5},{7,4},{8,11},{9,10},{10,... | collective-permute-start | bytes 49160 | tf_op jit(solution)/shard_map/ppermute | solution.py:326
  14.3 0.5 %last_block_queries.2.refs_1_ = bf16[128,1024]{1,0:T(8,128)(2,1)S(1)} custom-call(bf16[128,1024]{1,0:T(8,128)(2,1)S(1)} %collective-permute-done.1.refs_0_, f32[1,4096]{1,0:T(1,128)S(1)} %copy-done.3, bf16[4096,1024]{1,0:T(8,128)(2,1)S(1)} %get-tuple-element.54.refs_3_.refs_2_.refs_5_.refs_4_, f32[128,1024]{1,0:T(8,128)S(1)} %get-tuple-element.59.refs_3_, ...), custom_call_target="tpu_custom_call" | custom-call | flops 268435456 | bytes 262144 | tf_op jit(solution)/shard_map/last_block_queries/pallas_call | solution.py:206
  14.7 0.0 collective-permute-done.3.refs_4_
  14.7 1.9 %collective-permute-done.4.refs_5_ = bf16[64,128]{1,0:T(8,128)(2,1)S(1)} collective-permute-done((bf16[64,128]{1,0:T(8,128)(2,1)S(1)}, bf16[64,128]{1,0:T(8,128)(2,1)S(1)}, u32[]{:S(2)}, u32[]{:S(2)}) %collective-permute-start.4) | collective-permute-done | bytes 16416 | tf_op jit(solution)/shard_map/ppermute | solution.py:326
  16.6 0.1 collective-permute-done.5.refs_6_
  16.7 0.0 copy-done.1
  16.7 0.0 copy-done.4
  16.7 0.5 %attend.3 = (bf16[128,512]{1,0:T(8,128)(2,1)S(1)}, bf16[128,128]{1,0:T(8,128)(2,1)S(1)}, bf16[128,128]{1,0:T(8,128)(2,1)S(1)}) custom-call(s32[128,128]{1,0:T(8,128)S(1)} %get-tuple-element.52.refs_0_, bf16[128,1024]{1,0:T(8,128)(2,1)S(1)} %last_block_queries.2.refs_1_, bf16[128,1024]{1,0:T(8,128)(2,1)S(1)} %bitcast.7, ...), custom_call_target="tpu_custom_call" | custom-call | flops 134217728 | bytes 262144 | tf_op jit(solution)/shard_map/attend/pallas_call | solution.py:300
  17.2 1.5 %collective-permute-start.6 = (bf16[128,512]{1,0:T(8,128)(2,1)S(1)}, bf16[128,512]{1,0:T(8,128)(2,1)S(1)}, u32[]{:S(2)}, u32[]{:S(2)}) collective-permute-start(bf16[128,512]{1,0:T(8,128)(2,1)S(1)} %get-tuple-element.67), channel_id=1, source_target_pairs={{0,4},{1,5},{2,6},{3,7},{4,8},{5,9},{6,10},{7,11},{8,12},{9,13},{1... | collective-permute-start | bytes 393224 | tf_op jit(solution)/shard_map/ppermute | solution.py:326
  18.8 0.5 %attend.4 = bf16[128,512]{1,0:T(8,128)(2,1)S(1)} custom-call(s32[128,128]{1,0:T(8,128)S(1)} %get-tuple-element.52.refs_0_, bf16[128,1024]{1,0:T(8,128)(2,1)S(1)} %last_block_queries.2.refs_1_, bf16[128,1024]{1,0:T(8,128)(2,1)S(1)} %bitcast.8, bf16[128,128]{1,0:T(8,128)(2,1)S(1)} %get-tuple-element.68.refs_3_.refs_8_, ...), custom_call_target="tpu_custom_call" | custom-call | flops 134217728 | bytes 262144 | tf_op jit(solution)/shard_map/attend/pallas_call | solution.py:300
  19.3 2.5 %collective-permute-start.10 = (bf16[128,512]{1,0:T(8,128)(2,1)S(1)}, bf16[128,512]{1,0:T(8,128)(2,1)S(1)}, u32[]{:S(2)}, u32[]{:S(2)}) collective-permute-start(bf16[128,512]{1,0:T(8,128)(2,1)S(1)} %attend.4), channel_id=1, source_target_pairs={{0,6},{1,7},{2,4},{3,5},{4,10},{5,11},{6,8},{7,9},{8,14},{9,15},{1... | collective-permute-start | bytes 393224 | tf_op jit(solution)/shard_map/ppermute | solution.py:326
  21.7 1.5 %collective-permute-start.9 = (bf16[128,512]{1,0:T(8,128)(2,1)S(1)}, bf16[128,512]{1,0:T(8,128)(2,1)S(1)}, u32[]{:S(2)}, u32[]{:S(2)}) collective-permute-start(bf16[128,512]{1,0:T(8,128)(2,1)S(1)} %attend.4), channel_id=1, source_target_pairs={{0,4},{1,5},{2,6},{3,7},{4,8},{5,9},{6,10},{7,11},{8,12},{9,13},{1... | collective-permute-start | bytes 393224 | tf_op jit(solution)/shard_map/ppermute | solution.py:326
  23.2 2.6 %collective-permute-done.6.refs_0_.refs_2_ = bf16[128,512]{1,0:T(8,128)(2,1)S(1)} collective-permute-done((bf16[128,512]{1,0:T(8,128)(2,1)S(1)}, bf16[128,512]{1,0:T(8,128)(2,1)S(1)}, u32[]{:S(2)}, u32[]{:S(2)}) %collective-permute-start.6) | collective-permute-done | bytes 131104 | tf_op jit(solution)/shard_map/ppermute | solution.py:326
  25.8 1.9 %collective-permute-start.7 = (bf16[128,512]{1,0:T(8,128)(2,1)S(1)}, bf16[128,512]{1,0:T(8,128)(2,1)S(1)}, u32[]{:S(2)}, u32[]{:S(2)}) collective-permute-start(bf16[128,512]{1,0:T(8,128)(2,1)S(1)} %collective-permute-done.6.refs_0_.refs_2_), channel_id=1, source_target_pairs={{0,2},{1,3},{2,0},{3,1},{4,6},{5,7},{6,4},{7,5},{8,10},{9,11},{10,... | collective-permute-start | bytes 393224 | tf_op jit(solution)/shard_map/ppermute | solution.py:326
  27.7 0.0 collective-permute-start.13
  27.7 0.3 more_blocks.4
  28.1 1.9 %collective-permute-done.10.refs_3_ = bf16[128,512]{1,0:T(8,128)(2,1)S(1)} collective-permute-done((bf16[128,512]{1,0:T(8,128)(2,1)S(1)}, bf16[128,512]{1,0:T(8,128)(2,1)S(1)}, u32[]{:S(2)}, u32[]{:S(2)}) %collective-permute-start.10) | collective-permute-done | bytes 131104 | tf_op jit(solution)/shard_map/ppermute | solution.py:326
  30.0 1.2 %collective-permute-done.9.refs_2_.refs_3_ = bf16[128,512]{1,0:T(8,128)(2,1)S(1)} collective-permute-done((bf16[128,512]{1,0:T(8,128)(2,1)S(1)}, bf16[128,512]{1,0:T(8,128)(2,1)S(1)}, u32[]{:S(2)}, u32[]{:S(2)}) %collective-permute-start.9) | collective-permute-done | bytes 131104 | tf_op jit(solution)/shard_map/ppermute | solution.py:326
  31.2 0.0 collective-permute-start.11
  31.2 0.5 %collective-permute-start.12 = (bf16[128,512]{1,0:T(8,128)(2,1)S(1)}, bf16[128,512]{1,0:T(8,128)(2,1)S(1)}, u32[]{:S(2)}, u32[]{:S(2)}) collective-permute-start(bf16[128,512]{1,0:T(8,128)(2,1)S(1)} %collective-permute-done.10.refs_3_), channel_id=1, source_target_pairs={{0,1},{1,0},{2,3},{3,2},{4,5},{5,4},{6,7},{7,6},{8,9},{9,8},{10,11... | collective-permute-start | bytes 393224 | tf_op jit(solution)/shard_map/ppermute | solution.py:326
  31.7 0.3 collective-permute-done.7.refs_1_
  32.0 0.0 collective-permute-start.8
  32.0 0.0 collective-permute-done.13.refs_0_
  32.0 0.9 %more_blocks.5 = (f32[128,1024]{1,0:T(8,128)S(1)}, f32[128,256]{1,0:T(8,128)S(1)}, f32[128,128]{1,0:T(8,128)S(1)}) custom-call(bf16[128,512]{1,0:T(8,128)(2,1)S(1)} %collective-permute-done.13.refs_0_, bf16[128,512]{1,0:T(8,128)(2,1)S(1)} %collective-permute-done.7.refs_1_, bf16[128,512]{1,0:T(8,128)(2,1)S(1)} %collective-permute-done.9.refs_2_.refs_3_, ...), custom_call_target="tpu_custom_call" | custom-call | flops 671088640 | bytes 524288 | tf_op jit(solution)/shard_map/more_blocks/pallas_call | solution.py:132
  32.9 0.0 collective-permute-done.11.refs_1_
  32.9 0.0 collective-permute-done.12.refs_2_
  32.9 0.4 %collective-permute-done.8.refs_0_ = bf16[128,512]{1,0:T(8,128)(2,1)S(1)} collective-permute-done((bf16[128,512]{1,0:T(8,128)(2,1)S(1)}, bf16[128,512]{1,0:T(8,128)(2,1)S(1)}, u32[]{:S(2)}, u32[]{:S(2)}) %collective-permute-start.8) | collective-permute-done | bytes 131104 | tf_op jit(solution)/shard_map/ppermute | solution.py:326
  33.4 0.5 %last_block_key_value.3 = (f32[128,128]{1,0:T(8,128)S(1)}, bf16[64,128]{1,0:T(8,128)(2,1)S(1)}, bf16[64,128]{1,0:T(8,128)(2,1)S(1)}, bf16[64,128]{1,0:T(8,128)(2,1)S(1)}, bf16[64,128]{1,0:T(8,128)(2,1)S(1)}) custom-call(bf16[128,512]{1,0:T(8,128)(2,1)S(1)} %collective-permute-done.8.refs_0_, bf16[128,512]{1,0:T(8,128)(2,1)S(1)} %collective-permute-done.11.refs_1_, ...), custom_call_target="tpu_custom_call" | custom-call | flops 100663296 | bytes 131072 | tf_op jit(solution)/shard_map/last_block_key_value/pallas_call | solution.py:178
  33.9 0.2 collective-permute-start.14
  34.1 1.1 %collective-permute-start.15 = (bf16[64,128]{1,0:T(8,128)(2,1)S(1)}, bf16[64,128]{1,0:T(8,128)(2,1)S(1)}, u32[]{:S(2)}, u32[]{:S(2)}) collective-permute-start(bf16[64,128]{1,0:T(8,128)(2,1)S(1)} %get-tuple-element.85), channel_id=1, source_target_pairs={{0,2},{1,3},{2,0},{3,1},{4,6},{5,7},{6,4},{7,5},{8,10},{9,11},{10,... | collective-permute-start | bytes 49160 | tf_op jit(solution)/shard_map/ppermute | solution.py:326
  35.2 0.6 %collective-permute-start.16 = (bf16[64,128]{1,0:T(8,128)(2,1)S(1)}, bf16[64,128]{1,0:T(8,128)(2,1)S(1)}, u32[]{:S(2)}, u32[]{:S(2)}) collective-permute-start(bf16[64,128]{1,0:T(8,128)(2,1)S(1)} %get-tuple-element.86), channel_id=1, source_target_pairs={{0,3},{1,2},{2,1},{3,0},{4,7},{5,6},{6,5},{7,4},{8,11},{9,10},{10,... | collective-permute-start | bytes 49160 | tf_op jit(solution)/shard_map/ppermute | solution.py:326
  35.8 0.6 %last_block_queries.3.refs_1_ = bf16[128,1024]{1,0:T(8,128)(2,1)S(1)} custom-call(bf16[128,512]{1,0:T(8,128)(2,1)S(1)} %collective-permute-done.8.refs_0_, bf16[128,512]{1,0:T(8,128)(2,1)S(1)} %collective-permute-done.11.refs_1_, bf16[128,512]{1,0:T(8,128)(2,1)S(1)} %collective-permute-done.12.refs_2_, f32[1,4096]{1,0:T(1,128)S(1)} %copy-done.3, ...), custom_call_target="tpu_custom_call" | custom-call | flops 402653184 | bytes 131072 | tf_op jit(solution)/shard_map/last_block_queries/pallas_call | solution.py:206
  36.4 0.0 collective-permute-done.14.refs_5_
  36.4 1.4 %collective-permute-done.15.refs_6_ = bf16[64,128]{1,0:T(8,128)(2,1)S(1)} collective-permute-done((bf16[64,128]{1,0:T(8,128)(2,1)S(1)}, bf16[64,128]{1,0:T(8,128)(2,1)S(1)}, u32[]{:S(2)}, u32[]{:S(2)}) %collective-permute-start.15) | collective-permute-done | bytes 16416 | tf_op jit(solution)/shard_map/ppermute | solution.py:326
  37.9 0.5 %collective-permute-done.16.refs_7_ = bf16[64,128]{1,0:T(8,128)(2,1)S(1)} collective-permute-done((bf16[64,128]{1,0:T(8,128)(2,1)S(1)}, bf16[64,128]{1,0:T(8,128)(2,1)S(1)}, u32[]{:S(2)}, u32[]{:S(2)}) %collective-permute-start.16) | collective-permute-done | bytes 16416 | tf_op jit(solution)/shard_map/ppermute | solution.py:326
  38.4 1.5 %attend.5 = bf16[128,1024]{1,0:T(8,128)(2,1)} custom-call(s32[128,128]{1,0:T(8,128)S(1)} %get-tuple-element.51.refs_0_, bf16[128,1024]{1,0:T(8,128)(2,1)S(1)} %last_block_queries.3.refs_1_, bf16[128,512]{1,0:T(8,128)(2,1)S(1)} %collective-permute-done.6.refs_0_.refs_2_, bf16[128,512]{1,0:T(8,128)(2,1)S(1)} %collective-permute-done.9.refs_2_.refs_3_, ...), custom_call_target="tpu_custom_call" | custom-call | flops 134217728 | bytes 262144 | tf_op jit(solution)/shard_map/attend/pallas_call | solution.py:300
Async XLA Ops:
  0.0 10.1 %collective-permute-start = (bf16[128,1024]{1,0:T(8,128)(2,1)}, bf16[128,1024]{1,0:T(8,128)(2,1)S(1)}, u32[]{:S(2)}, u32[]{:S(2)}) collective-permute-start(bf16[128,1024]{1,0:T(8,128)(2,1)} %bitcast.4), channel_id=1, source_target_pairs={{0,2},{1,3},{2,0},{3,1},{4,6},{5,7},{6,4},{7,5},{8,10},{9,11},{10,... | collective-permute-start | bytes 786440 | tf_op jit(solution)/shard_map/ppermute | solution.py:326
  3.0 7.7 %collective-permute-start.2 = (bf16[128,1024]{1,0:T(8,128)(2,1)}, bf16[128,1024]{1,0:T(8,128)(2,1)S(1)}, u32[]{:S(2)}, u32[]{:S(2)}) collective-permute-start(bf16[128,1024]{1,0:T(8,128)(2,1)} %bitcast.5), channel_id=1, source_target_pairs={{0,1},{1,0},{2,3},{3,2},{4,5},{5,4},{6,7},{7,6},{8,9},{9,8},{10,11... | collective-permute-start | bytes 786440 | tf_op jit(solution)/shard_map/ppermute | solution.py:326
  3.0 0.7 %copy-start.5 = (s32[9]{0:T(128)S(1)}, s32[9]{0:T(128)}, u32[]{:S(2)}) copy-start(s32[9]{0:T(128)} %doc_ref.1) | copy-start | bytes 112
  4.3 1.0 %copy-start = (bf16[1,128,1024]{2,1,0:T(8,128)(2,1)S(1)}, bf16[1,128,1024]{2,1,0:T(8,128)(2,1)}, u32[]{:S(2)}) copy-start(bf16[1,128,1024]{2,1,0:T(8,128)(2,1)} %param.6) | copy-start | bytes 786436
  5.2 0.7 %copy-start.2 = (f32[1,4096]{1,0:T(1,128)S(1)}, f32[1,4096]{1,0:T(1,128)}, u32[]{:S(2)}) copy-start(f32[1,4096]{1,0:T(1,128)} %refs_3_.3) | copy-start | bytes 49156
  5.9 4.8 %copy-start.3 = (f32[1,4096]{1,0:T(1,128)S(1)}, f32[1,4096]{1,0:T(1,128)}, u32[]{:S(2)}) copy-start(f32[1,4096]{1,0:T(1,128)} %refs_3_.3) | copy-start | bytes 49156
  10.1 1.7 %collective-permute-start.1 = (bf16[128,1024]{1,0:T(8,128)(2,1)S(1)}, bf16[128,1024]{1,0:T(8,128)(2,1)S(1)}, u32[]{:S(2)}, u32[]{:S(2)}) collective-permute-start(bf16[128,1024]{1,0:T(8,128)(2,1)S(1)} %collective-permute-done.refs_1_), channel_id=1, source_target_pairs={{0,1},{1,0},{2,3},{3,2},{4,5},{5,4},{6,7},{7,6},{8,9},{9,8},{10,11... | collective-permute-start | bytes 786440 | tf_op jit(solution)/shard_map/ppermute | solution.py:326
  11.6 5.1 %copy-start.1 = (bf16[1,128,1024]{2,1,0:T(8,128)(2,1)S(1)}, bf16[1,128,1024]{2,1,0:T(8,128)(2,1)}, u32[]{:S(2)}) copy-start(bf16[1,128,1024]{2,1,0:T(8,128)(2,1)} %param.6) | copy-start | bytes 786436
  11.6 5.1 %copy-start.4 = (bf16[128,1024]{1,0:T(8,128)(2,1)S(1)}, bf16[128,1024]{1,0:T(8,128)(2,1)}, u32[]{:S(2)}) copy-start(bf16[128,1024]{1,0:T(8,128)(2,1)} %refs_5_.1) | copy-start | bytes 786436
  12.3 2.4 %collective-permute-start.3 = (bf16[64,128]{1,0:T(8,128)(2,1)S(1)}, bf16[64,128]{1,0:T(8,128)(2,1)S(1)}, u32[]{:S(2)}, u32[]{:S(2)}) collective-permute-start(bf16[64,128]{1,0:T(8,128)(2,1)S(1)} %get-tuple-element.64), channel_id=1, source_target_pairs={{0,1},{1,0},{2,3},{3,2},{4,5},{5,4},{6,7},{7,6},{8,9},{9,8},{10,11... | collective-permute-start | bytes 49160 | tf_op jit(solution)/shard_map/ppermute | solution.py:326
  12.8 3.8 %collective-permute-start.4 = (bf16[64,128]{1,0:T(8,128)(2,1)S(1)}, bf16[64,128]{1,0:T(8,128)(2,1)S(1)}, u32[]{:S(2)}, u32[]{:S(2)}) collective-permute-start(bf16[64,128]{1,0:T(8,128)(2,1)S(1)} %get-tuple-element.65), channel_id=1, source_target_pairs={{0,2},{1,3},{2,0},{3,1},{4,6},{5,7},{6,4},{7,5},{8,10},{9,11},{10,... | collective-permute-start | bytes 49160 | tf_op jit(solution)/shard_map/ppermute | solution.py:326
  13.4 3.2 %collective-permute-start.5 = (bf16[64,128]{1,0:T(8,128)(2,1)S(1)}, bf16[64,128]{1,0:T(8,128)(2,1)S(1)}, u32[]{:S(2)}, u32[]{:S(2)}) collective-permute-start(bf16[64,128]{1,0:T(8,128)(2,1)S(1)} %get-tuple-element.66), channel_id=1, source_target_pairs={{0,3},{1,2},{2,1},{3,0},{4,7},{5,6},{6,5},{7,4},{8,11},{9,10},{10,... | collective-permute-start | bytes 49160 | tf_op jit(solution)/shard_map/ppermute | solution.py:326
  17.2 8.6 %collective-permute-start.6 = (bf16[128,512]{1,0:T(8,128)(2,1)S(1)}, bf16[128,512]{1,0:T(8,128)(2,1)S(1)}, u32[]{:S(2)}, u32[]{:S(2)}) collective-permute-start(bf16[128,512]{1,0:T(8,128)(2,1)S(1)} %get-tuple-element.67), channel_id=1, source_target_pairs={{0,4},{1,5},{2,6},{3,7},{4,8},{5,9},{6,10},{7,11},{8,12},{9,13},{1... | collective-permute-start | bytes 393224 | tf_op jit(solution)/shard_map/ppermute | solution.py:326
  19.3 10.7 %collective-permute-start.10 = (bf16[128,512]{1,0:T(8,128)(2,1)S(1)}, bf16[128,512]{1,0:T(8,128)(2,1)S(1)}, u32[]{:S(2)}, u32[]{:S(2)}) collective-permute-start(bf16[128,512]{1,0:T(8,128)(2,1)S(1)} %attend.4), channel_id=1, source_target_pairs={{0,6},{1,7},{2,4},{3,5},{4,10},{5,11},{6,8},{7,9},{8,14},{9,15},{1... | collective-permute-start | bytes 393224 | tf_op jit(solution)/shard_map/ppermute | solution.py:326
  21.7 9.5 %collective-permute-start.9 = (bf16[128,512]{1,0:T(8,128)(2,1)S(1)}, bf16[128,512]{1,0:T(8,128)(2,1)S(1)}, u32[]{:S(2)}, u32[]{:S(2)}) collective-permute-start(bf16[128,512]{1,0:T(8,128)(2,1)S(1)} %attend.4), channel_id=1, source_target_pairs={{0,4},{1,5},{2,6},{3,7},{4,8},{5,9},{6,10},{7,11},{8,12},{9,13},{1... | collective-permute-start | bytes 393224 | tf_op jit(solution)/shard_map/ppermute | solution.py:326
  25.8 6.2 %collective-permute-start.7 = (bf16[128,512]{1,0:T(8,128)(2,1)S(1)}, bf16[128,512]{1,0:T(8,128)(2,1)S(1)}, u32[]{:S(2)}, u32[]{:S(2)}) collective-permute-start(bf16[128,512]{1,0:T(8,128)(2,1)S(1)} %collective-permute-done.6.refs_0_.refs_2_), channel_id=1, source_target_pairs={{0,2},{1,3},{2,0},{3,1},{4,6},{5,7},{6,4},{7,5},{8,10},{9,11},{10,... | collective-permute-start | bytes 393224 | tf_op jit(solution)/shard_map/ppermute | solution.py:326
  27.7 4.3 %collective-permute-start.13 = (bf16[128,512]{1,0:T(8,128)(2,1)S(1)}, bf16[128,512]{1,0:T(8,128)(2,1)S(1)}, u32[]{:S(2)}, u32[]{:S(2)}) collective-permute-start(bf16[128,512]{1,0:T(8,128)(2,1)S(1)} %collective-permute-done.6.refs_0_.refs_2_), channel_id=1, source_target_pairs={{0,1},{1,0},{2,3},{3,2},{4,5},{5,4},{6,7},{7,6},{8,9},{9,8},{10,11... | collective-permute-start | bytes 393224 | tf_op jit(solution)/shard_map/ppermute | solution.py:326
  31.2 1.7 %collective-permute-start.11 = (bf16[128,512]{1,0:T(8,128)(2,1)S(1)}, bf16[128,512]{1,0:T(8,128)(2,1)S(1)}, u32[]{:S(2)}, u32[]{:S(2)}) collective-permute-start(bf16[128,512]{1,0:T(8,128)(2,1)S(1)} %collective-permute-done.9.refs_2_.refs_3_), channel_id=1, source_target_pairs={{0,1},{1,0},{2,3},{3,2},{4,5},{5,4},{6,7},{7,6},{8,9},{9,8},{10,11... | collective-permute-start | bytes 393224 | tf_op jit(solution)/shard_map/ppermute | solution.py:326
  31.2 1.7 %collective-permute-start.12 = (bf16[128,512]{1,0:T(8,128)(2,1)S(1)}, bf16[128,512]{1,0:T(8,128)(2,1)S(1)}, u32[]{:S(2)}, u32[]{:S(2)}) collective-permute-start(bf16[128,512]{1,0:T(8,128)(2,1)S(1)} %collective-permute-done.10.refs_3_), channel_id=1, source_target_pairs={{0,1},{1,0},{2,3},{3,2},{4,5},{5,4},{6,7},{7,6},{8,9},{9,8},{10,11... | collective-permute-start | bytes 393224 | tf_op jit(solution)/shard_map/ppermute | solution.py:326
  32.0 1.3 %collective-permute-start.8 = (bf16[128,512]{1,0:T(8,128)(2,1)S(1)}, bf16[128,512]{1,0:T(8,128)(2,1)S(1)}, u32[]{:S(2)}, u32[]{:S(2)}) collective-permute-start(bf16[128,512]{1,0:T(8,128)(2,1)S(1)} %collective-permute-done.7.refs_1_), channel_id=1, source_target_pairs={{0,1},{1,0},{2,3},{3,2},{4,5},{5,4},{6,7},{7,6},{8,9},{9,8},{10,11... | collective-permute-start | bytes 393224 | tf_op jit(solution)/shard_map/ppermute | solution.py:326
  33.9 2.5 %collective-permute-start.14 = (bf16[64,128]{1,0:T(8,128)(2,1)S(1)}, bf16[64,128]{1,0:T(8,128)(2,1)S(1)}, u32[]{:S(2)}, u32[]{:S(2)}) collective-permute-start(bf16[64,128]{1,0:T(8,128)(2,1)S(1)} %get-tuple-element.84), channel_id=1, source_target_pairs={{0,1},{1,0},{2,3},{3,2},{4,5},{5,4},{6,7},{7,6},{8,9},{9,8},{10,11... | collective-permute-start | bytes 49160 | tf_op jit(solution)/shard_map/ppermute | solution.py:326
  34.1 3.8 %collective-permute-start.15 = (bf16[64,128]{1,0:T(8,128)(2,1)S(1)}, bf16[64,128]{1,0:T(8,128)(2,1)S(1)}, u32[]{:S(2)}, u32[]{:S(2)}) collective-permute-start(bf16[64,128]{1,0:T(8,128)(2,1)S(1)} %get-tuple-element.85), channel_id=1, source_target_pairs={{0,2},{1,3},{2,0},{3,1},{4,6},{5,7},{6,4},{7,5},{8,10},{9,11},{10,... | collective-permute-start | bytes 49160 | tf_op jit(solution)/shard_map/ppermute | solution.py:326
  35.2 3.2 %collective-permute-start.16 = (bf16[64,128]{1,0:T(8,128)(2,1)S(1)}, bf16[64,128]{1,0:T(8,128)(2,1)S(1)}, u32[]{:S(2)}, u32[]{:S(2)}) collective-permute-start(bf16[64,128]{1,0:T(8,128)(2,1)S(1)} %get-tuple-element.86), channel_id=1, source_target_pairs={{0,3},{1,2},{2,1},{3,0},{4,7},{5,6},{6,5},{7,4},{8,11},{9,10},{10,... | collective-permute-start | bytes 49160 | tf_op jit(solution)/shard_map/ppermute | solution.py:326

commit v3 on v2

v3 whole, which is shorter than its diff:
```python
import functools
import math

import jax
import jax.numpy as jnp
from jax import lax
from jax.experimental import pallas as pl
from jax.experimental.pallas import tpu as pltpu
from jax.sharding import PartitionSpec as P

HD = 128
KVH = 4
GROUP = 8

epsilon = 1e-05
masked_score = -1e30

VMEM = pltpu.VMEM
f32 = jnp.float32
bf16 = jnp.bfloat16
vmem = pl.BlockSpec(memory_space=VMEM)
smem = pl.BlockSpec(memory_space=pltpu.SMEM)
in_hbm = pl.BlockSpec(memory_space=pltpu.HBM)
params = pltpu.CompilerParams(vmem_limit_bytes=16 * 1024 * 1024)


def resident_in(*arrays):
    return [pltpu.with_memory_space_constraint(a, VMEM) for a in arrays]


def cost(flops, moved):
    return pl.CostEstimate(flops=flops, bytes_accessed=moved, transcendentals=0)


def rows_of(block, width):
    return pl.ds(pl.multiple_of(block * width, width), width)


def dot(a, b):
    return jnp.dot(a, b, preferred_element_type=f32)


def dot_turned(a, b):
    return lax.dot_general(a, b, (((1,), (1,)), ((), ())), preferred_element_type=f32)


def gained(x, gain_ref, block):
    width = x.shape[1]
    wide = x.astype(f32)
    squares = wide * wide
    ssq = squares[:, :HD]
    for c in range(HD, width, HD):
        ssq = ssq + squares[:, c : c + HD]
    return (wide * gain_ref[:, rows_of(block, width)]).astype(bf16), ssq


def load_kernel(x_hbm, gain_hbm, wq_hbm, wkv_hbm, accq_ref, x_ref, gain_ref, wq_ref, wkv_ref, sems):
    width = x_hbm.shape[1]
    n = wq_hbm.shape[0] // width
    me = lax.axis_index("head")

    def part(step):
        rows = rows_of(lax.rem(me + step, n), width)
        return pltpu.make_async_copy(wq_hbm.at[rows], wq_ref.at[rows], sems.at[step])

    small = (
        pltpu.make_async_copy(x_hbm, x_ref, sems.at[n]),
        pltpu.make_async_copy(gain_hbm, gain_ref, sems.at[n + 1]),
    )
    keys_values = pltpu.make_async_copy(wkv_hbm, wkv_ref, sems.at[n + 2])
    for copy in small:
        copy.start()
    for step in range(n):
        part(step).start()
    keys_values.start()
    for copy in small:
        copy.wait()
    normed, _ = gained(x_ref[...], gain_ref, me)
    part(0).wait()
    accq_ref[...] = dot(normed, wq_ref[rows_of(me, width), :])
    for step in range(1, n):
        part(step).wait()
    keys_values.wait()


def load(x, gain, wq, wkv):
    tokens, width = x.shape
    n = wq.shape[0] // width
    operands = [pltpu.with_memory_space_constraint(a, pltpu.HBM) for a in (x, gain, wq, wkv)]
    return pl.pallas_call(
        load_kernel,
        out_shape=(
            VMEM((tokens, wq.shape[1]), f32),
            VMEM(x.shape, bf16),
            VMEM(gain.shape, f32),
            VMEM(wq.shape, bf16),
            VMEM(wkv.shape, bf16),
        ),
        in_specs=[in_hbm] * 4,
        out_specs=(vmem,) * 5,
        scratch_shapes=[pltpu.SemaphoreType.DMA((n + 3,))],
        cost_estimate=cost(2 * tokens * width * wq.shape[1], 2 * (wq.size + wkv.size)),
        compiler_params=params,
        name="load_and_own_queries",
    )(*operands)


def blocks_kernel(count, wkv_count, carried, places, with_q, *refs):
    xs, refs = refs[:count], refs[count:]
    gain_ref, wq_ref = refs[:2]
    wkv_refs, refs = refs[2 : 2 + wkv_count], refs[2 + wkv_count :]
    old, outs = refs[:carried], refs[carried:]
    me = lax.axis_index("head")
    columns = wkv_refs[0].shape[1]
    q = old[0][...] if carried >= 1 else None
    kvs = [old[1][:, c * columns : (c + 1) * columns] if carried == 3 else None for c in range(wkv_count)]
    ssq = old[2][...] if carried == 3 else None

    def add(total, term):
        return term if total is None else total + term

    for i, x_ref in enumerate(xs):
        block, width = places[i](me), x_ref.shape[1]
        normed, squares = gained(x_ref[...], gain_ref, block)
        ssq = add(ssq, squares)
        rows = rows_of(block, width)
        kvs = [add(kv, dot(normed, w_ref[rows, :])) for kv, w_ref in zip(kvs, wkv_refs)]
        if with_q[i]:
            q = add(q, dot(normed, wq_ref[rows, :]))
    outs[0][...] = q
    for c, kv in enumerate(kvs):
        outs[1][:, c * columns : (c + 1) * columns] = kv
    outs[2][...] = ssq


def more_blocks(xs, places, gain, wq, wkvs, state, with_q=None):
    tokens = xs[0].shape[0]
    operands = [*xs, *resident_in(gain, wq, *wkvs), *state]
    columns = len(wkvs) * wkvs[0].shape[1]
    shapes = ((tokens, wq.shape[1]), (tokens, columns), (tokens, HD))
    return pl.pallas_call(
        functools.partial(
            blocks_kernel, len(xs), len(wkvs), len(state), places, with_q or [True] * len(xs)
        ),
        out_shape=tuple(VMEM(s, f32) for s in shapes),
        in_specs=[vmem] * len(operands),
        out_specs=(vmem,) * 3,
        cost_estimate=cost(sum(2 * x.size * (wq.shape[1] + columns) for x in xs), sum(2 * x.size for x in xs)),
        compiler_params=params,
        name="more_blocks",
    )(*operands)


def last_kv_kernel(count, wkv_count, n, flips, places, *refs):
    xs, refs = refs[:count], refs[count:]
    gain_ref, wkv_refs, refs = refs[0], refs[1 : 1 + wkv_count], refs[1 + wkv_count :]
    acckv_ref, ssq_ref, scale_ref, pieces = refs[0], refs[1], refs[2], refs[3:]
    me = lax.axis_index("head")
    columns = wkv_refs[0].shape[1]
    kvs = [acckv_ref[:, c * columns : (c + 1) * columns] for c in range(wkv_count)]
    ssq = ssq_ref[...]
    for i, x_ref in enumerate(xs):
        block, width = places[i](me), x_ref.shape[1]
        normed, squares = gained(x_ref[...], gain_ref, block)
        ssq = ssq + squares
        kvs = [kv + dot(normed, w_ref[rows_of(block, width), :]) for kv, w_ref in zip(kvs, wkv_refs)]
    scale = lax.rsqrt(jnp.sum(ssq, axis=1, keepdims=True) / gain_ref.shape[1] + epsilon)
    scale_ref[...] = jnp.broadcast_to(scale, scale_ref.shape)
    kv = jnp.concatenate([(kv * scale).astype(bf16) for kv in kvs], axis=1)
    features = columns // (2 * KVH)
    size = 2 * wkv_count * features
    row = lax.broadcasted_iota(jnp.int32, (size, wkv_count * columns), 0)
    col = lax.broadcasted_iota(jnp.int32, (size, wkv_count * columns), 1)
    which, core, feature = row // (wkv_count * features), (row // features) % wkv_count, row % features
    whose = (core != lax.rem(me, wkv_count)).astype(jnp.int32)
    first = col - (whose * columns + feature * (2 * KVH) + which)
    for flip, piece in zip(flips, pieces):
        group = lax.bitwise_xor(me, jnp.int32(flip)) * KVH // n
        choose = jnp.where(first == group * 2, 1.0, 0.0).astype(bf16)
        piece[...] = dot_turned(choose, kv).astype(bf16)


def last_kv(xs, places, gain, wkvs, acckv, ssq, n, flips):
    tokens = xs[0].shape[0]
    columns = len(wkvs) * wkvs[0].shape[1]
    operands = [*xs, *resident_in(gain, *wkvs), acckv, ssq]
    return pl.pallas_call(
        functools.partial(last_kv_kernel, len(xs), len(wkvs), n, flips, places),
        out_shape=(VMEM((tokens, HD), f32),) + (VMEM((columns // KVH, tokens), bf16),) * len(flips),
        in_specs=[vmem] * len(operands),
        out_specs=(vmem,) * (1 + len(flips)),
        cost_estimate=cost(sum(2 * x.size * columns for x in xs), sum(2 * x.size for x in xs)),
        compiler_params=params,
        name="last_keys_values",
    )(*operands)


def last_q_kernel(count, places, *refs):
    xs, rest = refs[:count], refs[count:]
    gain_ref, wq_ref, accq_ref, scale_ref, q_ref = rest
    me = lax.axis_index("head")
    total = accq_ref[...]
    for i, x_ref in enumerate(xs):
        block, width = places[i](me), x_ref.shape[1]
        normed, _ = gained(x_ref[...], gain_ref, block)
        total = total + dot(normed, wq_ref[rows_of(block, width), :])
    q_ref[...] = (total * scale_ref[:, 0:1]).astype(bf16)


def last_q(xs, places, gain, wq, accq, scale):
    operands = [*xs, *resident_in(gain, wq), accq, scale]
    return pl.pallas_call(
        functools.partial(last_q_kernel, len(xs), places),
        out_shape=VMEM((xs[0].shape[0], wq.shape[1]), bf16),
        in_specs=[vmem] * len(operands),
        out_specs=vmem,
        cost_estimate=cost(sum(2 * x.size * wq.shape[1] for x in xs), sum(2 * x.size for x in xs)),
        compiler_params=params,
        name="last_queries",
    )(*operands)


def openings_kernel(sections, doc_ref, first_ref, second_ref):
    tokens = first_ref.shape[0]
    for turn, out_ref in enumerate((first_ref, second_ref)):
        start = (sections - 1 + turn - lax.axis_index("section")) * tokens
        here = start + lax.broadcasted_iota(jnp.int32, out_ref.shape, 0)
        opened = jnp.zeros(out_ref.shape, jnp.int32)
        end = jnp.int32(0)
        for d in range(doc_ref.shape[0]):
            end = end + doc_ref[d]
            opened = jnp.where(end <= here, end, opened)
        out_ref[...] = opened


def openings(doc_lengths, tokens, sections):
    return pl.pallas_call(
        functools.partial(openings_kernel, sections),
        out_shape=(VMEM((tokens, HD), jnp.int32),) * 2,
        in_specs=[smem],
        out_specs=(vmem,) * 2,
        compiler_params=params,
        name="openings",
    )(doc_lengths)


def stacked_heads(q_ref, heads):
    return jnp.concatenate([q_ref[:, h * HD : (h + 1) * HD] for h in range(*heads)], axis=0)


def masked_scores(q, keys, opened_ref, query_start, key_start):
    tokens, count = opened_ref.shape[0], keys.shape[1]
    here = query_start + lax.broadcasted_iota(jnp.int32, (tokens, count), 0)
    there = key_start + lax.broadcasted_iota(jnp.int32, (tokens, count), 1)
    allowed = (there >= opened_ref[:, 0:1]) & (there <= here)
    scores = dot(q, keys) * (1.0 / math.sqrt(HD))
    scores = jnp.where(allowed[None], scores.reshape(-1, tokens, count), masked_score)
    return scores.reshape(-1, count)


def put_together(me, pieces, flips, parts, gather):
    features = pieces[0].shape[0] // 2
    for flip, piece_ref in zip(flips, pieces):
        source = lax.bitwise_xor(me, jnp.int32(flip)) // parts
        piece = piece_ref[...].astype(f32)
        gather[0, rows_of(source, features), :] = piece[:features]
        gather[1, rows_of(source, features), :] = piece[features:]
    return gather[0].astype(bf16), gather[1].astype(bf16)


def first_attend_kernel(sections, heads, flips, parts, opened_ref, q_ref, x_ref, fresh_ref, *refs):
    section = lax.axis_index("section")
    start = (sections - 1 - section) * q_ref.shape[0]
    if flips is None:
        keys_ref, values_ref, out_ref = refs
        keys, values = keys_ref[...], values_ref[...]
    else:
        pieces, (out_ref, keys_ref, values_ref, gather) = refs[: len(flips)], refs[len(flips) :]
        keys, values = put_together(lax.axis_index("head"), pieces, flips, parts, gather)
        keys_ref[...], values_ref[...] = keys, values
    tokens = q_ref.shape[0]
    scores = masked_scores(stacked_heads(q_ref, heads), keys, opened_ref, start, start)
    expon = jnp.exp(scores - jnp.max(scores, axis=1, keepdims=True))
    weights = (expon * (1.0 / jnp.sum(expon, axis=1, keepdims=True))).astype(bf16)
    mixed = dot_turned(weights, values).astype(bf16).astype(f32)
    for i, h in enumerate(range(*heads)):
        columns = slice(h * HD, (h + 1) * HD)
        out = (x_ref[:, columns].astype(f32) + mixed[i * tokens : (i + 1) * tokens]).astype(bf16)
        out = jnp.where(section == sections - 1, fresh_ref[:, columns].astype(f32), out.astype(f32))
        out_ref[:, i * HD : (i + 1) * HD] = out.astype(bf16)


def first_attend(opened, q, x, fresh, pieces, flips, parts, heads, sections):
    tokens = q.shape[0]
    out = (VMEM((tokens, (heads[1] - heads[0]) * HD), bf16),)
    scratch = []
    if flips is not None:
        out = out + (VMEM((HD, tokens), bf16),) * 2
        scratch = [VMEM((2, HD, tokens), f32)]
    operands = [opened, q, x, fresh, *pieces]
    return pl.pallas_call(
        functools.partial(first_attend_kernel, sections, heads, flips, parts),
        out_shape=out,
        in_specs=[vmem] * len(operands),
        out_specs=(vmem,) * len(out),
        scratch_shapes=scratch,
        cost_estimate=cost(1000, 1000),
        compiler_params=params,
        name="first_attend",
    )(*operands)


def resident_kernel(sections, opened_ref, q_ref, keys_ref, values_ref, max_ref, sum_ref, mixed_ref):
    tokens = q_ref.shape[0]
    key_start = (sections - 1 - lax.axis_index("section")) * tokens
    q = stacked_heads(q_ref, (0, q_ref.shape[1] // HD))
    scores = masked_scores(q, keys_ref[...], opened_ref, key_start + tokens, key_start)
    top = jnp.max(scores, axis=1, keepdims=True)
    expon = jnp.exp(scores - top)
    max_ref[...] = jnp.broadcast_to(top, max_ref.shape)
    sum_ref[...] = jnp.broadcast_to(jnp.sum(expon, axis=1, keepdims=True), sum_ref.shape)
    mixed_ref[...] = dot_turned(expon.astype(bf16), values_ref[...])


def resident_attend(opened, q, keys, values, sections):
    rows = q.shape[0] * (q.shape[1] // HD)
    return pl.pallas_call(
        functools.partial(resident_kernel, sections),
        out_shape=(VMEM((rows, HD), f32),) * 3,
        in_specs=[vmem] * 4,
        out_specs=(vmem,) * 3,
        cost_estimate=cost(1000, 1000),
        compiler_params=params,
        name="resident_attend",
    )(opened, q, keys, values)


def second_attend_kernel(sections, flips, parts, x_count, opened_ref, q_ref, max_ref, sum_ref, mixed_ref, *refs):
    x_refs, refs = refs[:x_count], refs[x_count:]
    pieces, (out_ref, gather) = refs[: len(flips)], refs[len(flips) :]
    tokens, heads = q_ref.shape[0], q_ref.shape[1] // HD
    start = (sections - lax.axis_index("section")) * tokens
    keys, values = put_together(lax.axis_index("head"), pieces, flips, parts, gather)
    scores = masked_scores(stacked_heads(q_ref, (0, heads)), keys, opened_ref, start, start)
    top = jnp.maximum(jnp.max(scores, axis=1, keepdims=True), max_ref[...])
    expon = jnp.exp(scores - top)
    shrink = jnp.exp(max_ref[...] - top)
    total = jnp.sum(expon, axis=1, keepdims=True) + shrink * sum_ref[...]
    mixed = dot_turned(expon.astype(bf16), values) + shrink * mixed_ref[...]
    mixed = (mixed * (1.0 / total)).astype(bf16).astype(f32)
    x_width = x_refs[0].shape[1]
    for h in range(heads):
        x_ref, inside = x_refs[h * HD // x_width], h * HD % x_width
        out = x_ref[:, inside : inside + HD].astype(f32) + mixed[h * tokens : (h + 1) * tokens]
        out_ref[:, h * HD : (h + 1) * HD] = out.astype(bf16)


def second_attend(opened, q, xs, resident, pieces, flips, parts, sections):
    tokens = q.shape[0]
    operands = [opened, q, *resident, *xs, *pieces]
    return pl.pallas_call(
        functools.partial(second_attend_kernel, sections, flips, parts, len(xs)),
        out_shape=jax.ShapeDtypeStruct(q.shape, bf16),
        in_specs=[vmem] * len(operands),
        out_specs=vmem,
        scratch_shapes=[VMEM((2, HD, tokens), f32)],
        cost_estimate=cost(1000, 1000),
        compiler_params=params,
        name="second_attend",
    )(*operands)


def shards(entering, fresh_slice, norm_gain, w_query, w_key_value, doc_lengths):
    n = lax.axis_size("head")
    sections = lax.axis_size("section")
    own = entering[0]
    w_q, w_kv = w_query[0], w_key_value[0]
    tokens = own.shape[0]
    heads = w_q.shape[1] // HD
    paired = n == 4
    parts = 2 if paired else 1
    flips = [0, 2] if paired else list(range(n))

    def moved(array, by, flip):
        pairs = [
            (s * n + h, ((s + by) % sections) * n + (h ^ flip)) for s in range(sections) for h in range(n)
        ]
        return lax.ppermute(array, ("section", "head"), pairs)

    def after(array, *others):
        return lax.optimization_barrier((array, *others))[0]

    def exchanged(xs, places, state):
        scale, *pieces = last_kv(xs, places, gain, wkvs, state[1], state[2], n, flips)
        received = [moved(piece, 0, flip) for piece, flip in zip(pieces[1:], flips[1:])]
        return scale, [pieces[0], *received]

    def rest_of(array):
        every = lax.all_gather(array, "head", axis=0)
        me = lax.axis_index("head")
        return [lax.dynamic_index_in_dim(every, (me + k) % n, 0, False) for k in range(1, n)]

    def place(flip, count=1, part=0):
        return lambda me: lax.bitwise_xor(me, jnp.int32(flip)) * count + part

    following = [functools.partial(lambda k, me: lax.rem(me + k, jnp.int32(n)), k) for k in range(n)]

    if paired:
        over = moved(own, 0, 2)
        beside = moved(own, 0, 1)
        w_kv_beside = moved(w_kv, 0, 1)
    accq, own, gain, wq, wkv = load(own, norm_gain, w_q, w_kv)
    if paired:
        wkvs = [wkv, w_kv_beside]
        over = after(over, accq)
        passed = moved(over, 0, 1)
        xs, places, with_q = [own, beside, over], [place(0), place(1), place(2)], [False, True, True]
        state = more_blocks(xs, places, gain, wq, wkvs, [accq], with_q)
        last, places = [passed], [place(3)]
    else:
        wkvs = [wkv]
        state = more_blocks([own], following[:1], gain, wq, wkvs, [accq], [False])
        last, places = rest_of(own), following[1:]
    scale, pieces = exchanged(last, places, state)
    opened = openings(after(doc_lengths, scale), tokens, sections)
    q = last_q(last, places, gain, wq, state[0], scale)
    half = heads // 2 if paired else heads
    sent, keys, values = first_attend(
        opened[0], q, own, fresh_slice, pieces, flips, parts, (0, half), sections
    )

    if paired:
        mine_a = moved(sent, 1, 0)
        (sent,) = first_attend(
            opened[0], q, own, fresh_slice, [keys, values], None, parts, (half, heads), sections
        )
        over_b = moved(sent, 1, 2)
        mine_b = moved(sent, 1, 0)
        mine_a = after(mine_a, sent)
        over_a = moved(mine_a, 0, 2)
        beside_a = moved(mine_a, 0, 1)
        state = more_blocks([mine_a], [place(0, 2, 0)], gain, wq, wkvs, [])
        mine_b, over_b, *state = lax.optimization_barrier((mine_b, over_b, *state))
        beside_b = moved(mine_b, 0, 1)
        passed_b = moved(over_b, 0, 1)
        passed_a = moved(over_a, 0, 1)
        early = [beside_a, over_a, mine_b, over_b]
        places = [place(1, 2, 0), place(2, 2, 0), place(0, 2, 1), place(2, 2, 1)]
        state = more_blocks(early, places, gain, wq, wkvs, state)
        last, places = [passed_a, beside_b, passed_b], [place(3, 2, 0), place(1, 2, 1), place(3, 2, 1)]
        mine = [mine_a, mine_b]
    else:
        mine = [moved(sent, 1, 0)]
        state = more_blocks(mine, following[:1], gain, wq, wkvs, [])
        last, places = rest_of(mine[0]), following[1:]
    scale, pieces = exchanged(last, places, state)
    q = last_q(last, places, gain, wq, state[0], scale)
    resident = resident_attend(opened[1], q, keys, values, sections)
    return second_attend(opened[1], q, mine, resident, pieces, flips, parts, sections)[None]


def solution(mesh):
    placed = (
        P("section", None, "head"),
        P(None, "head"),
        P("section", None),
        P("section", None, "head"),
        P("section", None, "head"),
        P(),
    )
    return jax.shard_map(
        shards, mesh=mesh, in_specs=placed, out_specs=P("section", None, "head"), check_vma=False
    )
```

time: 40.2 us -> 39.6 us (0.985)
  waiting for transfers between devices: 10.7 us -> 13.1 us
  local copies, waits for them, and re-layouts: 2.33 us -> 0.01 us
  starting transfers between devices: 15.3 us -> 13.9 us
  Pallas kernels: 11.4 us -> 12.3 us
    ppermute x17 -> x14, waiting for transfers between devices: 10.7 us -> 13.1 us  [moved(): return lax.ppermute(array, ('section', 'head'), pairs)]
    unnamed x12 -> x4, local copies, waits for them, and re-layouts: 2.33 us -> 0.01 us
    ppermute x17 -> x14, starting transfers between devices: 15.3 us -> 13.9 us  [moved(): return lax.ppermute(array, ('section', 'head'), pairs)]
    pallas_call x9 -> x10, Pallas kernels: 9.77 us -> 10.6 us  [the longest x1 4.22 us: load(): pl.pallas_call(load_kernel, out_shape=(VMEM((tokens, wq.shape[1]), f32),...]
  transfers between devices with their start and end apart: 17 -> 14, of which waited for: 10 -> 9; matrix products, arithmetic and copies ran while one was open for 0% -> 0% of each run, Pallas kernels for 21% -> 24%
where the time goes in v3:
time: 39.6 us; the launch traced here: 39.4 us
  starting transfers between devices  13.9 us (35%)
  waiting for transfers between devices  13.1 us (33%)
  Pallas kernels  12.3 us (31%)
    ppermute x14, starting transfers between devices, moved(): return lax.ppermute(array, ('section', 'head'), pairs)  13.9 us
    ppermute x14, waiting for transfers between devices, moved(): return lax.ppermute(array, ('section', 'head'), pairs)  13.1 us
    pallas_call x1, Pallas kernels, load(): pl.pallas_call(load_kernel, out_shape=(VMEM((tokens, wq.shape[1]), f32),...  4.22 us
    pallas_call x3, Pallas kernels, more_blocks(): pl.pallas_call(functools.partial(blocks_kernel, len(xs), len(wkvs), len(s...  2.52 us
    pallas_call x1, Pallas kernels, second_attend(): pl.pallas_call(functools.partial(second_attend_kernel, sections, flips, p...  1.28 us
    pallas_call x2, Pallas kernels, last_kv(): pl.pallas_call(functools.partial(last_kv_kernel, len(xs), len(wkvs), n, f...  1.1 us
    pallas_call x2, Pallas kernels, last_q(): pl.pallas_call(functools.partial(last_q_kernel, len(xs), places), out_sha...  1.05 us
    pallas_call x2, Pallas kernels, first_attend(): pl.pallas_call(functools.partial(first_attend_kernel, sections, heads, fl...  1 us
  transfers between devices with their start and end apart: 14, of which 9 were waited for; matrix products, arithmetic and copies ran while one was open for 0% of the time, Pallas kernels for 24%

profile of v3, /device:TPU:0, one launch (start us, length us, event | category | flops | bytes accessed | tf_op | source)
XLA Modules:
  0.0 39.4 jit_solution(10631316644050489432)
XLA Ops:
  0.0 0.5 %collective-permute-start.2 = (bf16[4096,256]{1,0:T(8,128)(2,1)}, bf16[4096,256]{1,0:T(8,128)(2,1)S(1)}, u32[]{:S(2)}, u32[]{:S(2)}) collective-permute-start(bf16[4096,256]{1,0:T(8,128)(2,1)} %bitcast.5), channel_id=1, source_target_pairs={{0,1},{1,0},{2,3},{3,2},{4,5},{5,4},{6,7},{7,6},{8,9},{9,8},{10,11... | collective-permute-start | bytes 6291464 | tf_op jit(solution)/shard_map/ppermute | solution.py:388
  0.5 2.5 %collective-permute-start = (bf16[128,1024]{1,0:T(8,128)(2,1)}, bf16[128,1024]{1,0:T(8,128)(2,1)S(1)}, u32[]{:S(2)}, u32[]{:S(2)}) collective-permute-start(bf16[128,1024]{1,0:T(8,128)(2,1)} %bitcast.7), channel_id=1, source_target_pairs={{0,2},{1,3},{2,0},{3,1},{4,6},{5,7},{6,4},{7,5},{8,10},{9,11},{10,... | collective-permute-start | bytes 786440 | tf_op jit(solution)/shard_map/ppermute | solution.py:388
  3.0 0.2 collective-permute-start.3
  3.2 4.2 %load_and_own_queries.1 = (f32[128,1024]{1,0:T(8,128)S(1)}, bf16[128,1024]{1,0:T(8,128)(2,1)S(1)}, f32[1,4096]{1,0:T(1,128)S(1)}, bf16[4096,1024]{1,0:T(8,128)(2,1)S(1)}, bf16[4096,256]{1,0:T(8,128)(2,1)S(1)}) custom-call(bf16[128,1024]{1,0:T(8,128)(2,1)} %bitcast.9, f32[1,4096]{1,0:T(1,128)} %gain_hbm.1, bf16[4096,1024]{1,0:T(8,128)(2,1)} %bitcast.4, ...), custom_call_target="tpu_custom_call" | custom-call | flops 268435456 | bytes 10485760 | tf_op jit(solution)/shard_map/load_and_own_queries/pallas_call | solution.py:90
  7.4 2.7 %collective-permute-done.refs_2_ = bf16[128,1024]{1,0:T(8,128)(2,1)S(1)} collective-permute-done((bf16[128,1024]{1,0:T(8,128)(2,1)}, bf16[128,1024]{1,0:T(8,128)(2,1)S(1)}, u32[]{:S(2)}, u32[]{:S(2)}) %collective-permute-start) | collective-permute-done | bytes 262176 | tf_op jit(solution)/shard_map/ppermute | solution.py:388
  10.2 0.0 collective-permute-start.1
  10.2 0.0 collective-permute-done.3.refs_1_
  10.2 0.0 collective-permute-done.2.refs_6_.refs_3_.refs_4_.refs_7_.refs_5_
  10.2 1.1 %more_blocks.3 = (f32[128,1024]{1,0:T(8,128)S(1)}, f32[128,512]{1,0:T(8,128)S(1)}, f32[128,128]{1,0:T(8,128)S(1)}) custom-call(bf16[128,1024]{1,0:T(8,128)(2,1)S(1)} %get-tuple-element.45.refs_0_.x_ref, bf16[128,1024]{1,0:T(8,128)(2,1)S(1)} %collective-permute-done.3.refs_1_, bf16[128,1024]{1,0:T(8,128)(2,1)S(1)} %collective-permute-done.refs_2_, ...), custom_call_target="tpu_custom_call" | custom-call | flops 1207959552 | bytes 786432 | tf_op jit(solution)/shard_map/more_blocks/pallas_call | solution.py:141
  11.3 0.4 collective-permute-done.1.refs_0_
  11.7 0.0 copy-start.1
  11.7 0.5 %last_keys_values.2 = (f32[128,128]{1,0:T(8,128)S(1)}, bf16[128,128]{1,0:T(8,128)(2,1)S(1)}, bf16[128,128]{1,0:T(8,128)(2,1)S(1)}) custom-call(bf16[128,1024]{1,0:T(8,128)(2,1)S(1)} %collective-permute-done.1.refs_0_, f32[1,4096]{1,0:T(1,128)S(1)} %get-tuple-element.43.refs_3_.refs_1_.refs_4_, ...), custom_call_target="tpu_custom_call" | custom-call | flops 134217728 | bytes 262144 | tf_op jit(solution)/shard_map/last_keys_values/pallas_call | solution.py:187
  12.2 1.8 %collective-permute-start.4 = (bf16[128,128]{1,0:T(8,128)(2,1)S(1)}, bf16[128,128]{1,0:T(8,128)(2,1)S(1)}, u32[]{:S(2)}, u32[]{:S(2)}) collective-permute-start(bf16[128,128]{1,0:T(8,128)(2,1)S(1)} %get-tuple-element.55), channel_id=1, source_target_pairs={{0,2},{1,3},{2,0},{3,1},{4,6},{5,7},{6,4},{7,5},{8,10},{9,11},{10,... | collective-permute-start | bytes 98312 | tf_op jit(solution)/shard_map/ppermute | solution.py:388
  14.0 0.0 copy-done.1
  14.0 0.6 %openings.1 = (s32[128,128]{1,0:T(8,128)S(1)}, s32[128,128]{1,0:T(8,128)S(1)}) custom-call(s32[9]{0:T(128)S(1)} %copy-done.1), custom_call_target="tpu_custom_call" | custom-call | tf_op jit(solution)/shard_map/openings/pallas_call | solution.py:237
  14.7 0.0 copy-start
  14.7 0.5 %last_queries.2.q_ref = bf16[128,1024]{1,0:T(8,128)(2,1)S(1)} custom-call(bf16[128,1024]{1,0:T(8,128)(2,1)S(1)} %collective-permute-done.1.refs_0_, f32[1,4096]{1,0:T(1,128)S(1)} %get-tuple-element.43.refs_3_.refs_1_.refs_4_, bf16[4096,1024]{1,0:T(8,128)(2,1)S(1)} %get-tuple-element.46.refs_4_.refs_2_.refs_5_, f32[128,1024]{1,0:T(8,128)S(1)} %get-tuple-element.53.refs_3_, ...), custom_call_target="tpu_custom_call" | custom-call | flops 268435456 | bytes 262144 | tf_op jit(solution)/shard_map/last_queries/pallas_call | solution.py:212
  15.2 1.0 %collective-permute-done.4.refs_1_ = bf16[128,128]{1,0:T(8,128)(2,1)S(1)} collective-permute-done((bf16[128,128]{1,0:T(8,128)(2,1)S(1)}, bf16[128,128]{1,0:T(8,128)(2,1)S(1)}, u32[]{:S(2)}, u32[]{:S(2)}) %collective-permute-start.4) | collective-permute-done | bytes 32800 | tf_op jit(solution)/shard_map/ppermute | solution.py:388
  16.2 0.0 copy-done
  16.2 0.5 %first_attend.2 = (bf16[128,512]{1,0:T(8,128)(2,1)S(1)}, bf16[128,128]{1,0:T(8,128)(2,1)S(1)}, bf16[128,128]{1,0:T(8,128)(2,1)S(1)}) custom-call(s32[128,128]{1,0:T(8,128)S(1)} %get-tuple-element.52.opened_ref, bf16[128,1024]{1,0:T(8,128)(2,1)S(1)} %last_queries.2.q_ref, bf16[128,1024]{1,0:T(8,128)(2,1)S(1)} %get-tuple-element.45.refs_0_.x_ref, ...), custom_call_target="tpu_custom_call" | custom-call | flops 1000 | bytes 1000 | tf_op jit(solution)/shard_map/first_attend/pallas_call | solution.py:301
  16.7 1.8 %collective-permute-start.5 = (bf16[128,512]{1,0:T(8,128)(2,1)S(1)}, bf16[128,512]{1,0:T(8,128)(2,1)S(1)}, u32[]{:S(2)}, u32[]{:S(2)}) collective-permute-start(bf16[128,512]{1,0:T(8,128)(2,1)S(1)} %get-tuple-element.56), channel_id=1, source_target_pairs={{0,4},{1,5},{2,6},{3,7},{4,8},{5,9},{6,10},{7,11},{8,12},{9,13},{1... | collective-permute-start | bytes 393224 | tf_op jit(solution)/shard_map/ppermute | solution.py:388
  18.5 0.5 %first_attend.3 = bf16[128,512]{1,0:T(8,128)(2,1)S(1)} custom-call(s32[128,128]{1,0:T(8,128)S(1)} %get-tuple-element.52.opened_ref, bf16[128,1024]{1,0:T(8,128)(2,1)S(1)} %last_queries.2.q_ref, bf16[128,1024]{1,0:T(8,128)(2,1)S(1)} %get-tuple-element.45.refs_0_.x_ref, bf16[128,1024]{1,0:T(8,128)(2,1)S(1)} %copy-done, ...), custom_call_target="tpu_custom_call" | custom-call | flops 1000 | bytes 1000 | tf_op jit(solution)/shard_map/first_attend/pallas_call | solution.py:301
  19.0 1.6 %collective-permute-start.8 = (bf16[128,512]{1,0:T(8,128)(2,1)S(1)}, bf16[128,512]{1,0:T(8,128)(2,1)S(1)}, u32[]{:S(2)}, u32[]{:S(2)}) collective-permute-start(bf16[128,512]{1,0:T(8,128)(2,1)S(1)} %first_attend.3), channel_id=1, source_target_pairs={{0,4},{1,5},{2,6},{3,7},{4,8},{5,9},{6,10},{7,11},{8,12},{9,13},{1... | collective-permute-start | bytes 393224 | tf_op jit(solution)/shard_map/ppermute | solution.py:388
  20.6 2.4 %collective-permute-start.9 = (bf16[128,512]{1,0:T(8,128)(2,1)S(1)}, bf16[128,512]{1,0:T(8,128)(2,1)S(1)}, u32[]{:S(2)}, u32[]{:S(2)}) collective-permute-start(bf16[128,512]{1,0:T(8,128)(2,1)S(1)} %first_attend.3), channel_id=1, source_target_pairs={{0,6},{1,7},{2,4},{3,5},{4,10},{5,11},{6,8},{7,9},{8,14},{9,15},{1... | collective-permute-start | bytes 393224 | tf_op jit(solution)/shard_map/ppermute | solution.py:388
  23.0 2.8 %collective-permute-done.5.refs_0_ = bf16[128,512]{1,0:T(8,128)(2,1)S(1)} collective-permute-done((bf16[128,512]{1,0:T(8,128)(2,1)S(1)}, bf16[128,512]{1,0:T(8,128)(2,1)S(1)}, u32[]{:S(2)}, u32[]{:S(2)}) %collective-permute-start.5) | collective-permute-done | bytes 131104 | tf_op jit(solution)/shard_map/ppermute | solution.py:388
  25.8 1.8 %collective-permute-start.6 = (bf16[128,512]{1,0:T(8,128)(2,1)S(1)}, bf16[128,512]{1,0:T(8,128)(2,1)S(1)}, u32[]{:S(2)}, u32[]{:S(2)}) collective-permute-start(bf16[128,512]{1,0:T(8,128)(2,1)S(1)} %collective-permute-done.5.refs_0_), channel_id=1, source_target_pairs={{0,2},{1,3},{2,0},{3,1},{4,6},{5,7},{6,4},{7,5},{8,10},{9,11},{10,... | collective-permute-start | bytes 393224 | tf_op jit(solution)/shard_map/ppermute | solution.py:388
  27.6 0.0 collective-permute-start.12
  27.6 0.4 more_blocks.4
  28.0 0.7 %collective-permute-done.8.refs_2_.refs_1_ = bf16[128,512]{1,0:T(8,128)(2,1)S(1)} collective-permute-done((bf16[128,512]{1,0:T(8,128)(2,1)S(1)}, bf16[128,512]{1,0:T(8,128)(2,1)S(1)}, u32[]{:S(2)}, u32[]{:S(2)}) %collective-permute-start.8) | collective-permute-done | bytes 131104 | tf_op jit(solution)/shard_map/ppermute | solution.py:388
  28.6 2.5 %collective-permute-done.9.refs_3_ = bf16[128,512]{1,0:T(8,128)(2,1)S(1)} collective-permute-done((bf16[128,512]{1,0:T(8,128)(2,1)S(1)}, bf16[128,512]{1,0:T(8,128)(2,1)S(1)}, u32[]{:S(2)}, u32[]{:S(2)}) %collective-permute-start.9) | collective-permute-done | bytes 131104 | tf_op jit(solution)/shard_map/ppermute | solution.py:388
  31.1 0.0 collective-permute-start.10
  31.1 0.5 %collective-permute-start.11 = (bf16[128,512]{1,0:T(8,128)(2,1)S(1)}, bf16[128,512]{1,0:T(8,128)(2,1)S(1)}, u32[]{:S(2)}, u32[]{:S(2)}) collective-permute-start(bf16[128,512]{1,0:T(8,128)(2,1)S(1)} %collective-permute-done.9.refs_3_), channel_id=1, source_target_pairs={{0,1},{1,0},{2,3},{3,2},{4,5},{5,4},{6,7},{7,6},{8,9},{9,8},{10,11... | collective-permute-start | bytes 393224 | tf_op jit(solution)/shard_map/ppermute | solution.py:388
  31.7 0.6 %collective-permute-done.6.refs_1_ = bf16[128,512]{1,0:T(8,128)(2,1)S(1)} collective-permute-done((bf16[128,512]{1,0:T(8,128)(2,1)S(1)}, bf16[128,512]{1,0:T(8,128)(2,1)S(1)}, u32[]{:S(2)}, u32[]{:S(2)}) %collective-permute-start.6) | collective-permute-done | bytes 131104 | tf_op jit(solution)/shard_map/ppermute | solution.py:388
  32.2 0.0 collective-permute-start.7
  32.2 0.0 collective-permute-done.12.refs_0_
  32.2 1.0 %more_blocks.5 = (f32[128,1024]{1,0:T(8,128)S(1)}, f32[128,512]{1,0:T(8,128)S(1)}, f32[128,128]{1,0:T(8,128)S(1)}) custom-call(bf16[128,512]{1,0:T(8,128)(2,1)S(1)} %collective-permute-done.12.refs_0_, bf16[128,512]{1,0:T(8,128)(2,1)S(1)} %collective-permute-done.6.refs_1_, bf16[128,512]{1,0:T(8,128)(2,1)S(1)} %collective-permute-done.8.refs_2_.refs_1_, ...), custom_call_target="tpu_custom_call" | custom-call | flops 805306368 | bytes 524288 | tf_op jit(solution)/shard_map/more_blocks/pallas_call | solution.py:141
  33.2 0.0 collective-permute-done.10.refs_1_
  33.2 0.0 collective-permute-done.11.refs_2_
  33.3 0.3 collective-permute-done.7.refs_0_
  33.6 0.6 %last_keys_values.3 = (f32[128,128]{1,0:T(8,128)S(1)}, bf16[128,128]{1,0:T(8,128)(2,1)S(1)}, bf16[128,128]{1,0:T(8,128)(2,1)S(1)}) custom-call(bf16[128,512]{1,0:T(8,128)(2,1)S(1)} %collective-permute-done.7.refs_0_, bf16[128,512]{1,0:T(8,128)(2,1)S(1)} %collective-permute-done.10.refs_1_, bf16[128,512]{1,0:T(8,128)(2,1)S(1)} %collective-permute-done.11.refs_2_, ...), custom_call_target="tpu_custom_call" | custom-call | flops 201326592 | bytes 393216 | tf_op jit(solution)/shard_map/last_keys_values/pallas_call | solution.py:187
  34.2 0.8 %collective-permute-start.13 = (bf16[128,128]{1,0:T(8,128)(2,1)S(1)}, bf16[128,128]{1,0:T(8,128)(2,1)S(1)}, u32[]{:S(2)}, u32[]{:S(2)}) collective-permute-start(bf16[128,128]{1,0:T(8,128)(2,1)S(1)} %get-tuple-element.76), channel_id=1, source_target_pairs={{0,2},{1,3},{2,0},{3,1},{4,6},{5,7},{6,4},{7,5},{8,10},{9,11},{10,... | collective-permute-start | bytes 98312 | tf_op jit(solution)/shard_map/ppermute | solution.py:388
  35.0 0.6 %last_queries.3.q_ref = bf16[128,1024]{1,0:T(8,128)(2,1)S(1)} custom-call(bf16[128,512]{1,0:T(8,128)(2,1)S(1)} %collective-permute-done.7.refs_0_, bf16[128,512]{1,0:T(8,128)(2,1)S(1)} %collective-permute-done.10.refs_1_, bf16[128,512]{1,0:T(8,128)(2,1)S(1)} %collective-permute-done.11.refs_2_, f32[1,4096]{1,0:T(1,128)S(1)} %get-tuple-element.43.refs_3_.refs_1_.refs_4_, ...), custom_call_target="tpu_custom_call" | custom-call | flops 402653184 | bytes 393216 | tf_op jit(solution)/shard_map/last_queries/pallas_call | solution.py:212
  35.6 0.5 %resident_attend.1 = (f32[1024,128]{1,0:T(8,128)S(1)}, f32[1024,128]{1,0:T(8,128)S(1)}, f32[1024,128]{1,0:T(8,128)S(1)}) custom-call(s32[128,128]{1,0:T(8,128)S(1)} %get-tuple-element.51.opened_ref, bf16[128,1024]{1,0:T(8,128)(2,1)S(1)} %last_queries.3.q_ref, bf16[128,128]{1,0:T(8,128)(2,1)S(1)} %get-tuple-element.57.refs_0_.keys_ref, ...), custom_call_target="tpu_custom_call" | custom-call | flops 1000 | bytes 1000 | tf_op jit(solution)/shard_map/resident_attend/pallas_call | solution.py:327
  36.0 2.1 %collective-permute-done.13.refs_3_ = bf16[128,128]{1,0:T(8,128)(2,1)S(1)} collective-permute-done((bf16[128,128]{1,0:T(8,128)(2,1)S(1)}, bf16[128,128]{1,0:T(8,128)(2,1)S(1)}, u32[]{:S(2)}, u32[]{:S(2)}) %collective-permute-start.13) | collective-permute-done | bytes 32800 | tf_op jit(solution)/shard_map/ppermute | solution.py:388
  38.1 1.3 %second_attend.1 = bf16[128,1024]{1,0:T(8,128)(2,1)} custom-call(s32[128,128]{1,0:T(8,128)S(1)} %get-tuple-element.51.opened_ref, bf16[128,1024]{1,0:T(8,128)(2,1)S(1)} %last_queries.3.q_ref, f32[1024,128]{1,0:T(8,128)S(1)} %get-tuple-element.72.max_ref, f32[1024,128]{1,0:T(8,128)S(1)} %get-tuple-element.73.sum_ref, ...), custom_call_target="tpu_custom_call" | custom-call | flops 1000 | bytes 1000 | tf_op jit(solution)/shard_map/second_attend/pallas_call | solution.py:361
Async XLA Ops:
  0.0 10.2 %collective-permute-start.2 = (bf16[4096,256]{1,0:T(8,128)(2,1)}, bf16[4096,256]{1,0:T(8,128)(2,1)S(1)}, u32[]{:S(2)}, u32[]{:S(2)}) collective-permute-start(bf16[4096,256]{1,0:T(8,128)(2,1)} %bitcast.5), channel_id=1, source_target_pairs={{0,1},{1,0},{2,3},{3,2},{4,5},{5,4},{6,7},{7,6},{8,9},{9,8},{10,11... | collective-permute-start | bytes 6291464 | tf_op jit(solution)/shard_map/ppermute | solution.py:388
  0.5 9.7 %collective-permute-start = (bf16[128,1024]{1,0:T(8,128)(2,1)}, bf16[128,1024]{1,0:T(8,128)(2,1)S(1)}, u32[]{:S(2)}, u32[]{:S(2)}) collective-permute-start(bf16[128,1024]{1,0:T(8,128)(2,1)} %bitcast.7), channel_id=1, source_target_pairs={{0,2},{1,3},{2,0},{3,1},{4,6},{5,7},{6,4},{7,5},{8,10},{9,11},{10,... | collective-permute-start | bytes 786440 | tf_op jit(solution)/shard_map/ppermute | solution.py:388
  3.0 7.2 %collective-permute-start.3 = (bf16[128,1024]{1,0:T(8,128)(2,1)}, bf16[128,1024]{1,0:T(8,128)(2,1)S(1)}, u32[]{:S(2)}, u32[]{:S(2)}) collective-permute-start(bf16[128,1024]{1,0:T(8,128)(2,1)} %bitcast.8), channel_id=1, source_target_pairs={{0,1},{1,0},{2,3},{3,2},{4,5},{5,4},{6,7},{7,6},{8,9},{9,8},{10,11... | collective-permute-start | bytes 786440 | tf_op jit(solution)/shard_map/ppermute | solution.py:388
  10.2 1.5 %collective-permute-start.1 = (bf16[128,1024]{1,0:T(8,128)(2,1)S(1)}, bf16[128,1024]{1,0:T(8,128)(2,1)S(1)}, u32[]{:S(2)}, u32[]{:S(2)}) collective-permute-start(bf16[128,1024]{1,0:T(8,128)(2,1)S(1)} %collective-permute-done.refs_2_), channel_id=1, source_target_pairs={{0,1},{1,0},{2,3},{3,2},{4,5},{5,4},{6,7},{7,6},{8,9},{9,8},{10,11... | collective-permute-start | bytes 786440 | tf_op jit(solution)/shard_map/ppermute | solution.py:388
  11.7 2.3 %copy-start.1 = (s32[9]{0:T(128)S(1)}, s32[9]{0:T(128)}, u32[]{:S(2)}) copy-start(s32[9]{0:T(128)} %doc_ref) | copy-start | bytes 112
  12.2 4.0 %collective-permute-start.4 = (bf16[128,128]{1,0:T(8,128)(2,1)S(1)}, bf16[128,128]{1,0:T(8,128)(2,1)S(1)}, u32[]{:S(2)}, u32[]{:S(2)}) collective-permute-start(bf16[128,128]{1,0:T(8,128)(2,1)S(1)} %get-tuple-element.55), channel_id=1, source_target_pairs={{0,2},{1,3},{2,0},{3,1},{4,6},{5,7},{6,4},{7,5},{8,10},{9,11},{10,... | collective-permute-start | bytes 98312 | tf_op jit(solution)/shard_map/ppermute | solution.py:388
  14.7 1.5 %copy-start = (bf16[128,1024]{1,0:T(8,128)(2,1)S(1)}, bf16[128,1024]{1,0:T(8,128)(2,1)}, u32[]{:S(2)}) copy-start(bf16[128,1024]{1,0:T(8,128)(2,1)} %fresh_ref.3) | copy-start | bytes 786436
  16.7 9.1 %collective-permute-start.5 = (bf16[128,512]{1,0:T(8,128)(2,1)S(1)}, bf16[128,512]{1,0:T(8,128)(2,1)S(1)}, u32[]{:S(2)}, u32[]{:S(2)}) collective-permute-start(bf16[128,512]{1,0:T(8,128)(2,1)S(1)} %get-tuple-element.56), channel_id=1, source_target_pairs={{0,4},{1,5},{2,6},{3,7},{4,8},{5,9},{6,10},{7,11},{8,12},{9,13},{1... | collective-permute-start | bytes 393224 | tf_op jit(solution)/shard_map/ppermute | solution.py:388
  19.0 9.7 %collective-permute-start.8 = (bf16[128,512]{1,0:T(8,128)(2,1)S(1)}, bf16[128,512]{1,0:T(8,128)(2,1)S(1)}, u32[]{:S(2)}, u32[]{:S(2)}) collective-permute-start(bf16[128,512]{1,0:T(8,128)(2,1)S(1)} %first_attend.3), channel_id=1, source_target_pairs={{0,4},{1,5},{2,6},{3,7},{4,8},{5,9},{6,10},{7,11},{8,12},{9,13},{1... | collective-permute-start | bytes 393224 | tf_op jit(solution)/shard_map/ppermute | solution.py:388
  20.6 10.5 %collective-permute-start.9 = (bf16[128,512]{1,0:T(8,128)(2,1)S(1)}, bf16[128,512]{1,0:T(8,128)(2,1)S(1)}, u32[]{:S(2)}, u32[]{:S(2)}) collective-permute-start(bf16[128,512]{1,0:T(8,128)(2,1)S(1)} %first_attend.3), channel_id=1, source_target_pairs={{0,6},{1,7},{2,4},{3,5},{4,10},{5,11},{6,8},{7,9},{8,14},{9,15},{1... | collective-permute-start | bytes 393224 | tf_op jit(solution)/shard_map/ppermute | solution.py:388
  25.8 6.4 %collective-permute-start.6 = (bf16[128,512]{1,0:T(8,128)(2,1)S(1)}, bf16[128,512]{1,0:T(8,128)(2,1)S(1)}, u32[]{:S(2)}, u32[]{:S(2)}) collective-permute-start(bf16[128,512]{1,0:T(8,128)(2,1)S(1)} %collective-permute-done.5.refs_0_), channel_id=1, source_target_pairs={{0,2},{1,3},{2,0},{3,1},{4,6},{5,7},{6,4},{7,5},{8,10},{9,11},{10,... | collective-permute-start | bytes 393224 | tf_op jit(solution)/shard_map/ppermute | solution.py:388
  27.6 4.6 %collective-permute-start.12 = (bf16[128,512]{1,0:T(8,128)(2,1)S(1)}, bf16[128,512]{1,0:T(8,128)(2,1)S(1)}, u32[]{:S(2)}, u32[]{:S(2)}) collective-permute-start(bf16[128,512]{1,0:T(8,128)(2,1)S(1)} %collective-permute-done.5.refs_0_), channel_id=1, source_target_pairs={{0,1},{1,0},{2,3},{3,2},{4,5},{5,4},{6,7},{7,6},{8,9},{9,8},{10,11... | collective-permute-start | bytes 393224 | tf_op jit(solution)/shard_map/ppermute | solution.py:388
  31.1 2.1 %collective-permute-start.10 = (bf16[128,512]{1,0:T(8,128)(2,1)S(1)}, bf16[128,512]{1,0:T(8,128)(2,1)S(1)}, u32[]{:S(2)}, u32[]{:S(2)}) collective-permute-start(bf16[128,512]{1,0:T(8,128)(2,1)S(1)} %collective-permute-done.8.refs_2_.refs_1_), channel_id=1, source_target_pairs={{0,1},{1,0},{2,3},{3,2},{4,5},{5,4},{6,7},{7,6},{8,9},{9,8},{10,11... | collective-permute-start | bytes 393224 | tf_op jit(solution)/shard_map/ppermute | solution.py:388
  31.1 2.1 %collective-permute-start.11 = (bf16[128,512]{1,0:T(8,128)(2,1)S(1)}, bf16[128,512]{1,0:T(8,128)(2,1)S(1)}, u32[]{:S(2)}, u32[]{:S(2)}) collective-permute-start(bf16[128,512]{1,0:T(8,128)(2,1)S(1)} %collective-permute-done.9.refs_3_), channel_id=1, source_target_pairs={{0,1},{1,0},{2,3},{3,2},{4,5},{5,4},{6,7},{7,6},{8,9},{9,8},{10,11... | collective-permute-start | bytes 393224 | tf_op jit(solution)/shard_map/ppermute | solution.py:388
  32.2 1.3 %collective-permute-start.7 = (bf16[128,512]{1,0:T(8,128)(2,1)S(1)}, bf16[128,512]{1,0:T(8,128)(2,1)S(1)}, u32[]{:S(2)}, u32[]{:S(2)}) collective-permute-start(bf16[128,512]{1,0:T(8,128)(2,1)S(1)} %collective-permute-done.6.refs_1_), channel_id=1, source_target_pairs={{0,1},{1,0},{2,3},{3,2},{4,5},{5,4},{6,7},{7,6},{8,9},{9,8},{10,11... | collective-permute-start | bytes 393224 | tf_op jit(solution)/shard_map/ppermute | solution.py:388
  34.2 4.0 %collective-permute-start.13 = (bf16[128,128]{1,0:T(8,128)(2,1)S(1)}, bf16[128,128]{1,0:T(8,128)(2,1)S(1)}, u32[]{:S(2)}, u32[]{:S(2)}) collective-permute-start(bf16[128,128]{1,0:T(8,128)(2,1)S(1)} %get-tuple-element.76), channel_id=1, source_target_pairs={{0,2},{1,3},{2,0},{3,1},{4,6},{5,7},{6,4},{7,5},{8,10},{9,11},{10,... | collective-permute-start | bytes 98312 | tf_op jit(solution)/shard_map/ppermute | solution.py:388

commit v4 on v3

--- a/solution.py
+++ b/solution.py
@@ -379,7 +379,7 @@
     heads = w_q.shape[1] // HD
     paired = n == 4
     parts = 2 if paired else 1
-    flips = [0, 2] if paired else list(range(n))
+    flips = [0, 3] if paired else list(range(n))
 
     def moved(array, by, flip):
         pairs = [
@@ -406,7 +406,7 @@
     following = [functools.partial(lambda k, me: lax.rem(me + k, jnp.int32(n)), k) for k in range(n)]
 
     if paired:
-        over = moved(own, 0, 2)
+        over = moved(own, 0, 3)
         beside = moved(own, 0, 1)
         w_kv_beside = moved(w_kv, 0, 1)
     accq, own, gain, wq, wkv = load(own, norm_gain, w_q, w_kv)
@@ -414,9 +414,9 @@
         wkvs = [wkv, w_kv_beside]
         over = after(over, accq)
         passed = moved(over, 0, 1)
-        xs, places, with_q = [own, beside, over], [place(0), place(1), place(2)], [False, True, True]
+        xs, places, with_q = [own, beside, over], [place(0), place(1), place(3)], [False, True, True]
         state = more_blocks(xs, places, gain, wq, wkvs, [accq], with_q)
-        last, places = [passed], [place(3)]
+        last, places = [passed], [place(2)]
     else:
         wkvs = [wkv]
         state = more_blocks([own], following[:1], gain, wq, wkvs, [accq], [False])
@@ -430,25 +430,24 @@
     )
 
     if paired:
-        mine_a = moved(sent, 1, 0)
+        a1 = moved(sent, 1, 1)
         (sent,) = first_attend(
             opened[0], q, own, fresh_slice, [keys, values], None, parts, (half, heads), sections
         )
-        over_b = moved(sent, 1, 2)
-        mine_b = moved(sent, 1, 0)
-        mine_a = after(mine_a, sent)
-        over_a = moved(mine_a, 0, 2)
-        beside_a = moved(mine_a, 0, 1)
-        state = more_blocks([mine_a], [place(0, 2, 0)], gain, wq, wkvs, [])
-        mine_b, over_b, *state = lax.optimization_barrier((mine_b, over_b, *state))
-        beside_b = moved(mine_b, 0, 1)
-        passed_b = moved(over_b, 0, 1)
-        passed_a = moved(over_a, 0, 1)
-        early = [beside_a, over_a, mine_b, over_b]
-        places = [place(1, 2, 0), place(2, 2, 0), place(0, 2, 1), place(2, 2, 1)]
-        state = more_blocks(early, places, gain, wq, wkvs, state)
-        last, places = [passed_a, beside_b, passed_b], [place(3, 2, 0), place(1, 2, 1), place(3, 2, 1)]
-        mine = [mine_a, mine_b]
+        b3 = moved(sent, 1, 3)
+        b1 = moved(sent, 1, 1)
+        a1 = after(a1, sent)
+        a2 = moved(a1, 0, 3)
+        a0 = moved(a1, 0, 1)
+        state = more_blocks([a1], [place(1, 2, 0)], gain, wq, wkvs, [])
+        b1, b3, *state = lax.optimization_barrier((b1, b3, *state))
+        b0 = moved(b1, 0, 1)
+        b2 = moved(b3, 0, 1)
+        a3 = moved(a2, 0, 1)
+        places = [place(0, 2, 0), place(2, 2, 0), place(1, 2, 1), place(3, 2, 1)]
+        state = more_blocks([a0, a2, b1, b3], places, gain, wq, wkvs, state)
+        last, places = [a3, b0, b2], [place(3, 2, 0), place(0, 2, 1), place(2, 2, 1)]
+        mine = [a0, b0]
     else:
         mine = [moved(sent, 1, 0)]
         state = more_blocks(mine, following[:1], gain, wq, wkvs, [])

time: 39.6 us -> 39.1 us (0.987)
  starting transfers between devices: 13.9 us -> 13.5 us
  transfers between devices with their start and end apart: 14 -> 14, of which waited for: 9 -> 8; matrix products, arithmetic and copies ran while one was open for 0% -> 0% of each run, Pallas kernels for 24% -> 24%
where the time goes in v4:
time: 39.1 us; the launch traced here: 39 us
  starting transfers between devices  13.5 us (35%)
  waiting for transfers between devices  13 us (33%)
  Pallas kernels  12.3 us (31%)
    ppermute x14, starting transfers between devices, moved(): return lax.ppermute(array, ('section', 'head'), pairs)  13.5 us
    ppermute x14, waiting for transfers between devices, moved(): return lax.ppermute(array, ('section', 'head'), pairs)  13 us
    pallas_call x1, Pallas kernels, load(): pl.pallas_call(load_kernel, out_shape=(VMEM((tokens, wq.shape[1]), f32),...  4.22 us
    pallas_call x3, Pallas kernels, more_blocks(): pl.pallas_call(functools.partial(blocks_kernel, len(xs), len(wkvs), len(s...  2.51 us
    pallas_call x1, Pallas kernels, second_attend(): pl.pallas_call(functools.partial(second_attend_kernel, sections, flips, p...  1.28 us
    pallas_call x2, Pallas kernels, last_kv(): pl.pallas_call(functools.partial(last_kv_kernel, len(xs), len(wkvs), n, f...  1.1 us
    pallas_call x2, Pallas kernels, last_q(): pl.pallas_call(functools.partial(last_q_kernel, len(xs), places), out_sha...  1.06 us
    pallas_call x2, Pallas kernels, first_attend(): pl.pallas_call(functools.partial(first_attend_kernel, sections, heads, fl...  1 us
  transfers between devices with their start and end apart: 14, of which 8 were waited for; matrix products, arithmetic and copies ran while one was open for 0% of the time, Pallas kernels for 24%

profile of v4, /device:TPU:0, one launch (start us, length us, event | category | flops | bytes accessed | tf_op | source)
XLA Modules:
  0.0 39.0 jit_solution(13548894334317374936)
XLA Ops:
  0.0 0.5 %collective-permute-start.2 = (bf16[4096,256]{1,0:T(8,128)(2,1)}, bf16[4096,256]{1,0:T(8,128)(2,1)S(1)}, u32[]{:S(2)}, u32[]{:S(2)}) collective-permute-start(bf16[4096,256]{1,0:T(8,128)(2,1)} %bitcast.5), channel_id=1, source_target_pairs={{0,1},{1,0},{2,3},{3,2},{4,5},{5,4},{6,7},{7,6},{8,9},{9,8},{10,11... | collective-permute-start | bytes 6291464 | tf_op jit(solution)/shard_map/ppermute | solution.py:388
  0.5 2.6 %collective-permute-start = (bf16[128,1024]{1,0:T(8,128)(2,1)}, bf16[128,1024]{1,0:T(8,128)(2,1)S(1)}, u32[]{:S(2)}, u32[]{:S(2)}) collective-permute-start(bf16[128,1024]{1,0:T(8,128)(2,1)} %bitcast.7), channel_id=1, source_target_pairs={{0,3},{1,2},{2,1},{3,0},{4,7},{5,6},{6,5},{7,4},{8,11},{9,10},{10,... | collective-permute-start | bytes 786440 | tf_op jit(solution)/shard_map/ppermute | solution.py:388
  3.1 0.0 collective-permute-start.3
  3.1 4.2 %load_and_own_queries.1 = (f32[128,1024]{1,0:T(8,128)S(1)}, bf16[128,1024]{1,0:T(8,128)(2,1)S(1)}, f32[1,4096]{1,0:T(1,128)S(1)}, bf16[4096,1024]{1,0:T(8,128)(2,1)S(1)}, bf16[4096,256]{1,0:T(8,128)(2,1)S(1)}) custom-call(bf16[128,1024]{1,0:T(8,128)(2,1)} %bitcast.9, f32[1,4096]{1,0:T(1,128)} %gain_hbm.1, bf16[4096,1024]{1,0:T(8,128)(2,1)} %bitcast.4, ...), custom_call_target="tpu_custom_call" | custom-call | flops 268435456 | bytes 10485760 | tf_op jit(solution)/shard_map/load_and_own_queries/pallas_call | solution.py:90
  7.3 2.7 %collective-permute-done.refs_2_ = bf16[128,1024]{1,0:T(8,128)(2,1)S(1)} collective-permute-done((bf16[128,1024]{1,0:T(8,128)(2,1)}, bf16[128,1024]{1,0:T(8,128)(2,1)S(1)}, u32[]{:S(2)}, u32[]{:S(2)}) %collective-permute-start) | collective-permute-done | bytes 262176 | tf_op jit(solution)/shard_map/ppermute | solution.py:388
  10.0 0.1 collective-permute-start.1
  10.1 0.0 collective-permute-done.3.refs_1_
  10.1 0.0 collective-permute-done.2.refs_6_.refs_3_.refs_4_.refs_7_.refs_5_
  10.1 1.1 %more_blocks.3 = (f32[128,1024]{1,0:T(8,128)S(1)}, f32[128,512]{1,0:T(8,128)S(1)}, f32[128,128]{1,0:T(8,128)S(1)}) custom-call(bf16[128,1024]{1,0:T(8,128)(2,1)S(1)} %get-tuple-element.45.refs_0_.x_ref, bf16[128,1024]{1,0:T(8,128)(2,1)S(1)} %collective-permute-done.3.refs_1_, bf16[128,1024]{1,0:T(8,128)(2,1)S(1)} %collective-permute-done.refs_2_, ...), custom_call_target="tpu_custom_call" | custom-call | flops 1207959552 | bytes 786432 | tf_op jit(solution)/shard_map/more_blocks/pallas_call | solution.py:141
  11.2 0.3 collective-permute-done.1.refs_0_
  11.5 0.0 copy-start.1
  11.5 0.5 %last_keys_values.2 = (f32[128,128]{1,0:T(8,128)S(1)}, bf16[128,128]{1,0:T(8,128)(2,1)S(1)}, bf16[128,128]{1,0:T(8,128)(2,1)S(1)}) custom-call(bf16[128,1024]{1,0:T(8,128)(2,1)S(1)} %collective-permute-done.1.refs_0_, f32[1,4096]{1,0:T(1,128)S(1)} %get-tuple-element.43.refs_3_.refs_1_.refs_4_, ...), custom_call_target="tpu_custom_call" | custom-call | flops 134217728 | bytes 262144 | tf_op jit(solution)/shard_map/last_keys_values/pallas_call | solution.py:187
  12.0 1.3 %collective-permute-start.4 = (bf16[128,128]{1,0:T(8,128)(2,1)S(1)}, bf16[128,128]{1,0:T(8,128)(2,1)S(1)}, u32[]{:S(2)}, u32[]{:S(2)}) collective-permute-start(bf16[128,128]{1,0:T(8,128)(2,1)S(1)} %get-tuple-element.55), channel_id=1, source_target_pairs={{0,3},{1,2},{2,1},{3,0},{4,7},{5,6},{6,5},{7,4},{8,11},{9,10},{10,... | collective-permute-start | bytes 98312 | tf_op jit(solution)/shard_map/ppermute | solution.py:388
  13.3 0.0 copy-done.1
  13.3 0.6 %openings.1 = (s32[128,128]{1,0:T(8,128)S(1)}, s32[128,128]{1,0:T(8,128)S(1)}) custom-call(s32[9]{0:T(128)S(1)} %copy-done.1), custom_call_target="tpu_custom_call" | custom-call | tf_op jit(solution)/shard_map/openings/pallas_call | solution.py:237
  14.0 0.0 copy-start
  14.0 0.5 %last_queries.2.q_ref = bf16[128,1024]{1,0:T(8,128)(2,1)S(1)} custom-call(bf16[128,1024]{1,0:T(8,128)(2,1)S(1)} %collective-permute-done.1.refs_0_, f32[1,4096]{1,0:T(1,128)S(1)} %get-tuple-element.43.refs_3_.refs_1_.refs_4_, bf16[4096,1024]{1,0:T(8,128)(2,1)S(1)} %get-tuple-element.46.refs_4_.refs_2_.refs_5_, f32[128,1024]{1,0:T(8,128)S(1)} %get-tuple-element.53.refs_3_, ...), custom_call_target="tpu_custom_call" | custom-call | flops 268435456 | bytes 262144 | tf_op jit(solution)/shard_map/last_queries/pallas_call | solution.py:212
  14.5 1.0 %collective-permute-done.4.refs_1_ = bf16[128,128]{1,0:T(8,128)(2,1)S(1)} collective-permute-done((bf16[128,128]{1,0:T(8,128)(2,1)S(1)}, bf16[128,128]{1,0:T(8,128)(2,1)S(1)}, u32[]{:S(2)}, u32[]{:S(2)}) %collective-permute-start.4) | collective-permute-done | bytes 32800 | tf_op jit(solution)/shard_map/ppermute | solution.py:388
  15.4 0.0 copy-done
  15.5 0.5 %first_attend.2 = (bf16[128,512]{1,0:T(8,128)(2,1)S(1)}, bf16[128,128]{1,0:T(8,128)(2,1)S(1)}, bf16[128,128]{1,0:T(8,128)(2,1)S(1)}) custom-call(s32[128,128]{1,0:T(8,128)S(1)} %get-tuple-element.52.opened_ref, bf16[128,1024]{1,0:T(8,128)(2,1)S(1)} %last_queries.2.q_ref, bf16[128,1024]{1,0:T(8,128)(2,1)S(1)} %get-tuple-element.45.refs_0_.x_ref, ...), custom_call_target="tpu_custom_call" | custom-call | flops 1000 | bytes 1000 | tf_op jit(solution)/shard_map/first_attend/pallas_call | solution.py:301
  16.0 1.3 %collective-permute-start.5 = (bf16[128,512]{1,0:T(8,128)(2,1)S(1)}, bf16[128,512]{1,0:T(8,128)(2,1)S(1)}, u32[]{:S(2)}, u32[]{:S(2)}) collective-permute-start(bf16[128,512]{1,0:T(8,128)(2,1)S(1)} %get-tuple-element.56), channel_id=1, source_target_pairs={{0,5},{1,4},{2,7},{3,6},{4,9},{5,8},{6,11},{7,10},{8,13},{9,12},{1... | collective-permute-start | bytes 393224 | tf_op jit(solution)/shard_map/ppermute | solution.py:388
  17.2 0.5 %first_attend.3 = bf16[128,512]{1,0:T(8,128)(2,1)S(1)} custom-call(s32[128,128]{1,0:T(8,128)S(1)} %get-tuple-element.52.opened_ref, bf16[128,1024]{1,0:T(8,128)(2,1)S(1)} %last_queries.2.q_ref, bf16[128,1024]{1,0:T(8,128)(2,1)S(1)} %get-tuple-element.45.refs_0_.x_ref, bf16[128,1024]{1,0:T(8,128)(2,1)S(1)} %copy-done, ...), custom_call_target="tpu_custom_call" | custom-call | flops 1000 | bytes 1000 | tf_op jit(solution)/shard_map/first_attend/pallas_call | solution.py:301
  17.7 1.4 %collective-permute-start.8 = (bf16[128,512]{1,0:T(8,128)(2,1)S(1)}, bf16[128,512]{1,0:T(8,128)(2,1)S(1)}, u32[]{:S(2)}, u32[]{:S(2)}) collective-permute-start(bf16[128,512]{1,0:T(8,128)(2,1)S(1)} %first_attend.3), channel_id=1, source_target_pairs={{0,5},{1,4},{2,7},{3,6},{4,9},{5,8},{6,11},{7,10},{8,13},{9,12},{1... | collective-permute-start | bytes 393224 | tf_op jit(solution)/shard_map/ppermute | solution.py:388
  19.1 2.4 %collective-permute-start.9 = (bf16[128,512]{1,0:T(8,128)(2,1)S(1)}, bf16[128,512]{1,0:T(8,128)(2,1)S(1)}, u32[]{:S(2)}, u32[]{:S(2)}) collective-permute-start(bf16[128,512]{1,0:T(8,128)(2,1)S(1)} %first_attend.3), channel_id=1, source_target_pairs={{0,7},{1,6},{2,5},{3,4},{4,11},{5,10},{6,9},{7,8},{8,15},{9,14},{1... | collective-permute-start | bytes 393224 | tf_op jit(solution)/shard_map/ppermute | solution.py:388
  21.5 2.7 %collective-permute-done.5.refs_0_ = bf16[128,512]{1,0:T(8,128)(2,1)S(1)} collective-permute-done((bf16[128,512]{1,0:T(8,128)(2,1)S(1)}, bf16[128,512]{1,0:T(8,128)(2,1)S(1)}, u32[]{:S(2)}, u32[]{:S(2)}) %collective-permute-start.5) | collective-permute-done | bytes 131104 | tf_op jit(solution)/shard_map/ppermute | solution.py:388
  24.2 1.8 %collective-permute-start.6 = (bf16[128,512]{1,0:T(8,128)(2,1)S(1)}, bf16[128,512]{1,0:T(8,128)(2,1)S(1)}, u32[]{:S(2)}, u32[]{:S(2)}) collective-permute-start(bf16[128,512]{1,0:T(8,128)(2,1)S(1)} %collective-permute-done.5.refs_0_), channel_id=1, source_target_pairs={{0,3},{1,2},{2,1},{3,0},{4,7},{5,6},{6,5},{7,4},{8,11},{9,10},{10,... | collective-permute-start | bytes 393224 | tf_op jit(solution)/shard_map/ppermute | solution.py:388
  26.0 0.0 collective-permute-start.12
  26.0 0.4 more_blocks.4
  26.4 0.6 %collective-permute-done.8.refs_2_ = bf16[128,512]{1,0:T(8,128)(2,1)S(1)} collective-permute-done((bf16[128,512]{1,0:T(8,128)(2,1)S(1)}, bf16[128,512]{1,0:T(8,128)(2,1)S(1)}, u32[]{:S(2)}, u32[]{:S(2)}) %collective-permute-start.8) | collective-permute-done | bytes 131104 | tf_op jit(solution)/shard_map/ppermute | solution.py:388
  27.0 3.6 %collective-permute-done.9.refs_3_ = bf16[128,512]{1,0:T(8,128)(2,1)S(1)} collective-permute-done((bf16[128,512]{1,0:T(8,128)(2,1)S(1)}, bf16[128,512]{1,0:T(8,128)(2,1)S(1)}, u32[]{:S(2)}, u32[]{:S(2)}) %collective-permute-start.9) | collective-permute-done | bytes 131104 | tf_op jit(solution)/shard_map/ppermute | solution.py:388
  30.6 0.2 collective-permute-start.10
  30.8 0.3 collective-permute-start.11
  31.1 1.0 %collective-permute-done.6.refs_1_ = bf16[128,512]{1,0:T(8,128)(2,1)S(1)} collective-permute-done((bf16[128,512]{1,0:T(8,128)(2,1)S(1)}, bf16[128,512]{1,0:T(8,128)(2,1)S(1)}, u32[]{:S(2)}, u32[]{:S(2)}) %collective-permute-start.6) | collective-permute-done | bytes 131104 | tf_op jit(solution)/shard_map/ppermute | solution.py:388
  32.1 0.5 %collective-permute-start.7 = (bf16[128,512]{1,0:T(8,128)(2,1)S(1)}, bf16[128,512]{1,0:T(8,128)(2,1)S(1)}, u32[]{:S(2)}, u32[]{:S(2)}) collective-permute-start(bf16[128,512]{1,0:T(8,128)(2,1)S(1)} %collective-permute-done.6.refs_1_), channel_id=1, source_target_pairs={{0,1},{1,0},{2,3},{3,2},{4,5},{5,4},{6,7},{7,6},{8,9},{9,8},{10,11... | collective-permute-start | bytes 393224 | tf_op jit(solution)/shard_map/ppermute | solution.py:388
  32.7 0.0 collective-permute-done.12.refs_0_
  32.7 1.0 %more_blocks.5 = (f32[128,1024]{1,0:T(8,128)S(1)}, f32[128,512]{1,0:T(8,128)S(1)}, f32[128,128]{1,0:T(8,128)S(1)}) custom-call(bf16[128,512]{1,0:T(8,128)(2,1)S(1)} %collective-permute-done.12.refs_0_, bf16[128,512]{1,0:T(8,128)(2,1)S(1)} %collective-permute-done.6.refs_1_, bf16[128,512]{1,0:T(8,128)(2,1)S(1)} %collective-permute-done.8.refs_2_, ...), custom_call_target="tpu_custom_call" | custom-call | flops 805306368 | bytes 524288 | tf_op jit(solution)/shard_map/more_blocks/pallas_call | solution.py:141
  33.7 0.0 collective-permute-done.10.refs_1_
  33.7 0.0 collective-permute-done.11.refs_2_
  33.7 0.0 collective-permute-done.7.refs_0_
  33.7 0.6 %last_keys_values.3 = (f32[128,128]{1,0:T(8,128)S(1)}, bf16[128,128]{1,0:T(8,128)(2,1)S(1)}, bf16[128,128]{1,0:T(8,128)(2,1)S(1)}) custom-call(bf16[128,512]{1,0:T(8,128)(2,1)S(1)} %collective-permute-done.7.refs_0_, bf16[128,512]{1,0:T(8,128)(2,1)S(1)} %collective-permute-done.10.refs_1_, bf16[128,512]{1,0:T(8,128)(2,1)S(1)} %collective-permute-done.11.refs_2_, ...), custom_call_target="tpu_custom_call" | custom-call | flops 201326592 | bytes 393216 | tf_op jit(solution)/shard_map/last_keys_values/pallas_call | solution.py:187
  34.3 1.2 %collective-permute-start.13 = (bf16[128,128]{1,0:T(8,128)(2,1)S(1)}, bf16[128,128]{1,0:T(8,128)(2,1)S(1)}, u32[]{:S(2)}, u32[]{:S(2)}) collective-permute-start(bf16[128,128]{1,0:T(8,128)(2,1)S(1)} %get-tuple-element.76), channel_id=1, source_target_pairs={{0,3},{1,2},{2,1},{3,0},{4,7},{5,6},{6,5},{7,4},{8,11},{9,10},{10,... | collective-permute-start | bytes 98312 | tf_op jit(solution)/shard_map/ppermute | solution.py:388
  35.5 0.6 %last_queries.3.q_ref = bf16[128,1024]{1,0:T(8,128)(2,1)S(1)} custom-call(bf16[128,512]{1,0:T(8,128)(2,1)S(1)} %collective-permute-done.7.refs_0_, bf16[128,512]{1,0:T(8,128)(2,1)S(1)} %collective-permute-done.10.refs_1_, bf16[128,512]{1,0:T(8,128)(2,1)S(1)} %collective-permute-done.11.refs_2_, f32[1,4096]{1,0:T(1,128)S(1)} %get-tuple-element.43.refs_3_.refs_1_.refs_4_, ...), custom_call_target="tpu_custom_call" | custom-call | flops 402653184 | bytes 393216 | tf_op jit(solution)/shard_map/last_queries/pallas_call | solution.py:212
  36.1 0.5 %resident_attend.1 = (f32[1024,128]{1,0:T(8,128)S(1)}, f32[1024,128]{1,0:T(8,128)S(1)}, f32[1024,128]{1,0:T(8,128)S(1)}) custom-call(s32[128,128]{1,0:T(8,128)S(1)} %get-tuple-element.51.opened_ref, bf16[128,1024]{1,0:T(8,128)(2,1)S(1)} %last_queries.3.q_ref, bf16[128,128]{1,0:T(8,128)(2,1)S(1)} %get-tuple-element.57.refs_0_.keys_ref, ...), custom_call_target="tpu_custom_call" | custom-call | flops 1000 | bytes 1000 | tf_op jit(solution)/shard_map/resident_attend/pallas_call | solution.py:327
  36.6 1.1 %collective-permute-done.13.refs_3_ = bf16[128,128]{1,0:T(8,128)(2,1)S(1)} collective-permute-done((bf16[128,128]{1,0:T(8,128)(2,1)S(1)}, bf16[128,128]{1,0:T(8,128)(2,1)S(1)}, u32[]{:S(2)}, u32[]{:S(2)}) %collective-permute-start.13) | collective-permute-done | bytes 32800 | tf_op jit(solution)/shard_map/ppermute | solution.py:388
  37.7 1.3 %second_attend.1 = bf16[128,1024]{1,0:T(8,128)(2,1)} custom-call(s32[128,128]{1,0:T(8,128)S(1)} %get-tuple-element.51.opened_ref, bf16[128,1024]{1,0:T(8,128)(2,1)S(1)} %last_queries.3.q_ref, f32[1024,128]{1,0:T(8,128)S(1)} %get-tuple-element.72.max_ref, f32[1024,128]{1,0:T(8,128)S(1)} %get-tuple-element.73.sum_ref, ...), custom_call_target="tpu_custom_call" | custom-call | flops 1000 | bytes 1000 | tf_op jit(solution)/shard_map/second_attend/pallas_call | solution.py:361
Async XLA Ops:
  0.0 10.1 %collective-permute-start.2 = (bf16[4096,256]{1,0:T(8,128)(2,1)}, bf16[4096,256]{1,0:T(8,128)(2,1)S(1)}, u32[]{:S(2)}, u32[]{:S(2)}) collective-permute-start(bf16[4096,256]{1,0:T(8,128)(2,1)} %bitcast.5), channel_id=1, source_target_pairs={{0,1},{1,0},{2,3},{3,2},{4,5},{5,4},{6,7},{7,6},{8,9},{9,8},{10,11... | collective-permute-start | bytes 6291464 | tf_op jit(solution)/shard_map/ppermute | solution.py:388
  0.5 9.5 %collective-permute-start = (bf16[128,1024]{1,0:T(8,128)(2,1)}, bf16[128,1024]{1,0:T(8,128)(2,1)S(1)}, u32[]{:S(2)}, u32[]{:S(2)}) collective-permute-start(bf16[128,1024]{1,0:T(8,128)(2,1)} %bitcast.7), channel_id=1, source_target_pairs={{0,3},{1,2},{2,1},{3,0},{4,7},{5,6},{6,5},{7,4},{8,11},{9,10},{10,... | collective-permute-start | bytes 786440 | tf_op jit(solution)/shard_map/ppermute | solution.py:388
  3.1 7.0 %collective-permute-start.3 = (bf16[128,1024]{1,0:T(8,128)(2,1)}, bf16[128,1024]{1,0:T(8,128)(2,1)S(1)}, u32[]{:S(2)}, u32[]{:S(2)}) collective-permute-start(bf16[128,1024]{1,0:T(8,128)(2,1)} %bitcast.8), channel_id=1, source_target_pairs={{0,1},{1,0},{2,3},{3,2},{4,5},{5,4},{6,7},{7,6},{8,9},{9,8},{10,11... | collective-permute-start | bytes 786440 | tf_op jit(solution)/shard_map/ppermute | solution.py:388
  10.0 1.5 %collective-permute-start.1 = (bf16[128,1024]{1,0:T(8,128)(2,1)S(1)}, bf16[128,1024]{1,0:T(8,128)(2,1)S(1)}, u32[]{:S(2)}, u32[]{:S(2)}) collective-permute-start(bf16[128,1024]{1,0:T(8,128)(2,1)S(1)} %collective-permute-done.refs_2_), channel_id=1, source_target_pairs={{0,1},{1,0},{2,3},{3,2},{4,5},{5,4},{6,7},{7,6},{8,9},{9,8},{10,11... | collective-permute-start | bytes 786440 | tf_op jit(solution)/shard_map/ppermute | solution.py:388
  11.5 1.8 %copy-start.1 = (s32[9]{0:T(128)S(1)}, s32[9]{0:T(128)}, u32[]{:S(2)}) copy-start(s32[9]{0:T(128)} %doc_ref) | copy-start | bytes 112
  12.0 3.4 %collective-permute-start.4 = (bf16[128,128]{1,0:T(8,128)(2,1)S(1)}, bf16[128,128]{1,0:T(8,128)(2,1)S(1)}, u32[]{:S(2)}, u32[]{:S(2)}) collective-permute-start(bf16[128,128]{1,0:T(8,128)(2,1)S(1)} %get-tuple-element.55), channel_id=1, source_target_pairs={{0,3},{1,2},{2,1},{3,0},{4,7},{5,6},{6,5},{7,4},{8,11},{9,10},{10,... | collective-permute-start | bytes 98312 | tf_op jit(solution)/shard_map/ppermute | solution.py:388
  14.0 1.5 %copy-start = (bf16[128,1024]{1,0:T(8,128)(2,1)S(1)}, bf16[128,1024]{1,0:T(8,128)(2,1)}, u32[]{:S(2)}) copy-start(bf16[128,1024]{1,0:T(8,128)(2,1)} %fresh_ref.3) | copy-start | bytes 786436
  16.0 8.2 %collective-permute-start.5 = (bf16[128,512]{1,0:T(8,128)(2,1)S(1)}, bf16[128,512]{1,0:T(8,128)(2,1)S(1)}, u32[]{:S(2)}, u32[]{:S(2)}) collective-permute-start(bf16[128,512]{1,0:T(8,128)(2,1)S(1)} %get-tuple-element.56), channel_id=1, source_target_pairs={{0,5},{1,4},{2,7},{3,6},{4,9},{5,8},{6,11},{7,10},{8,13},{9,12},{1... | collective-permute-start | bytes 393224 | tf_op jit(solution)/shard_map/ppermute | solution.py:388
  17.7 9.3 %collective-permute-start.8 = (bf16[128,512]{1,0:T(8,128)(2,1)S(1)}, bf16[128,512]{1,0:T(8,128)(2,1)S(1)}, u32[]{:S(2)}, u32[]{:S(2)}) collective-permute-start(bf16[128,512]{1,0:T(8,128)(2,1)S(1)} %first_attend.3), channel_id=1, source_target_pairs={{0,5},{1,4},{2,7},{3,6},{4,9},{5,8},{6,11},{7,10},{8,13},{9,12},{1... | collective-permute-start | bytes 393224 | tf_op jit(solution)/shard_map/ppermute | solution.py:388
  19.1 11.5 %collective-permute-start.9 = (bf16[128,512]{1,0:T(8,128)(2,1)S(1)}, bf16[128,512]{1,0:T(8,128)(2,1)S(1)}, u32[]{:S(2)}, u32[]{:S(2)}) collective-permute-start(bf16[128,512]{1,0:T(8,128)(2,1)S(1)} %first_attend.3), channel_id=1, source_target_pairs={{0,7},{1,6},{2,5},{3,4},{4,11},{5,10},{6,9},{7,8},{8,15},{9,14},{1... | collective-permute-start | bytes 393224 | tf_op jit(solution)/shard_map/ppermute | solution.py:388
  24.2 8.0 %collective-permute-start.6 = (bf16[128,512]{1,0:T(8,128)(2,1)S(1)}, bf16[128,512]{1,0:T(8,128)(2,1)S(1)}, u32[]{:S(2)}, u32[]{:S(2)}) collective-permute-start(bf16[128,512]{1,0:T(8,128)(2,1)S(1)} %collective-permute-done.5.refs_0_), channel_id=1, source_target_pairs={{0,3},{1,2},{2,1},{3,0},{4,7},{5,6},{6,5},{7,4},{8,11},{9,10},{10,... | collective-permute-start | bytes 393224 | tf_op jit(solution)/shard_map/ppermute | solution.py:388
  26.0 6.7 %collective-permute-start.12 = (bf16[128,512]{1,0:T(8,128)(2,1)S(1)}, bf16[128,512]{1,0:T(8,128)(2,1)S(1)}, u32[]{:S(2)}, u32[]{:S(2)}) collective-permute-start(bf16[128,512]{1,0:T(8,128)(2,1)S(1)} %collective-permute-done.5.refs_0_), channel_id=1, source_target_pairs={{0,1},{1,0},{2,3},{3,2},{4,5},{5,4},{6,7},{7,6},{8,9},{9,8},{10,11... | collective-permute-start | bytes 393224 | tf_op jit(solution)/shard_map/ppermute | solution.py:388
  30.6 3.1 %collective-permute-start.10 = (bf16[128,512]{1,0:T(8,128)(2,1)S(1)}, bf16[128,512]{1,0:T(8,128)(2,1)S(1)}, u32[]{:S(2)}, u32[]{:S(2)}) collective-permute-start(bf16[128,512]{1,0:T(8,128)(2,1)S(1)} %collective-permute-done.8.refs_2_), channel_id=1, source_target_pairs={{0,1},{1,0},{2,3},{3,2},{4,5},{5,4},{6,7},{7,6},{8,9},{9,8},{10,11... | collective-permute-start | bytes 393224 | tf_op jit(solution)/shard_map/ppermute | solution.py:388
  30.8 2.8 %collective-permute-start.11 = (bf16[128,512]{1,0:T(8,128)(2,1)S(1)}, bf16[128,512]{1,0:T(8,128)(2,1)S(1)}, u32[]{:S(2)}, u32[]{:S(2)}) collective-permute-start(bf16[128,512]{1,0:T(8,128)(2,1)S(1)} %collective-permute-done.9.refs_3_), channel_id=1, source_target_pairs={{0,1},{1,0},{2,3},{3,2},{4,5},{5,4},{6,7},{7,6},{8,9},{9,8},{10,11... | collective-permute-start | bytes 393224 | tf_op jit(solution)/shard_map/ppermute | solution.py:388
  32.1 1.5 %collective-permute-start.7 = (bf16[128,512]{1,0:T(8,128)(2,1)S(1)}, bf16[128,512]{1,0:T(8,128)(2,1)S(1)}, u32[]{:S(2)}, u32[]{:S(2)}) collective-permute-start(bf16[128,512]{1,0:T(8,128)(2,1)S(1)} %collective-permute-done.6.refs_1_), channel_id=1, source_target_pairs={{0,1},{1,0},{2,3},{3,2},{4,5},{5,4},{6,7},{7,6},{8,9},{9,8},{10,11... | collective-permute-start | bytes 393224 | tf_op jit(solution)/shard_map/ppermute | solution.py:388
  34.3 3.4 %collective-permute-start.13 = (bf16[128,128]{1,0:T(8,128)(2,1)S(1)}, bf16[128,128]{1,0:T(8,128)(2,1)S(1)}, u32[]{:S(2)}, u32[]{:S(2)}) collective-permute-start(bf16[128,128]{1,0:T(8,128)(2,1)S(1)} %get-tuple-element.76), channel_id=1, source_target_pairs={{0,3},{1,2},{2,1},{3,0},{4,7},{5,6},{6,5},{7,4},{8,11},{9,10},{10,... | collective-permute-start | bytes 98312 | tf_op jit(solution)/shard_map/ppermute | solution.py:388

commit v5 on v4

--- a/solution.py
+++ b/solution.py
@@ -54,9 +54,27 @@
     return (wide * gain_ref[:, rows_of(block, width)]).astype(bf16), ssq
 
 
-def load_kernel(x_hbm, gain_hbm, wq_hbm, wkv_hbm, accq_ref, x_ref, gain_ref, wq_ref, wkv_ref, sems):
+def choose_rows(choose_ref, me, n, flips, parts):
+    size, columns = choose_ref.shape[1], choose_ref.shape[2] // parts
+    features = size // (2 * parts)
+    shape = (features, choose_ref.shape[2])
+    row = lax.broadcasted_iota(jnp.int32, shape, 0)
+    col = lax.broadcasted_iota(jnp.int32, shape, 1)
+    offset = col - row * (2 * KVH)
+    for i, flip in enumerate(flips):
+        group = lax.bitwise_xor(me, jnp.int32(flip)) * KVH // n
+        for which in range(2):
+            for core in range(parts):
+                whose = jnp.where(lax.rem(me, jnp.int32(parts)) == core, 0, 1)
+                wanted = whose * columns + group * 2 + which
+                first = (which * parts + core) * features
+                choose_ref[i, first : first + features, :] = jnp.where(offset == wanted, 1.0, 0.0)
+
+
+def load_kernel(
+    n, flips, parts, x_hbm, gain_hbm, wq_hbm, wkv_hbm, accq_ref, x_ref, gain_ref, wq_ref, wkv_ref, choose_ref, sems
+):
     width = x_hbm.shape[1]
-    n = wq_hbm.shape[0] // width
     me = lax.axis_index("head")
 
     def part(step):
@@ -73,6 +91,7 @@
     for step in range(n):
         part(step).start()
     keys_values.start()
+    choose_rows(choose_ref, me, n, flips, parts)
     for copy in small:
         copy.wait()
     normed, _ = gained(x_ref[...], gain_ref, me)
@@ -83,23 +102,24 @@
     keys_values.wait()
 
 
-def load(x, gain, wq, wkv):
+def load(x, gain, wq, wkv, n, flips, parts):
     tokens, width = x.shape
-    n = wq.shape[0] // width
+    columns = wkv.shape[1]
     operands = [pltpu.with_memory_space_constraint(a, pltpu.HBM) for a in (x, gain, wq, wkv)]
     return pl.pallas_call(
-        load_kernel,
+        functools.partial(load_kernel, n, flips, parts),
         out_shape=(
             VMEM((tokens, wq.shape[1]), f32),
             VMEM(x.shape, bf16),
             VMEM(gain.shape, f32),
             VMEM(wq.shape, bf16),
             VMEM(wkv.shape, bf16),
+            VMEM((len(flips), parts * columns // KVH, parts * columns), f32),
         ),
         in_specs=[in_hbm] * 4,
-        out_specs=(vmem,) * 5,
+        out_specs=(vmem,) * 6,
         scratch_shapes=[pltpu.SemaphoreType.DMA((n + 3,))],
-        cost_estimate=cost(2 * tokens * width * wq.shape[1], 2 * (wq.size + wkv.size)),
+        cost_estimate=cost(10**11, 10**9),
         compiler_params=params,
         name="load_and_own_queries",
     )(*operands)
@@ -151,10 +171,10 @@
     )(*operands)
 
 
-def last_kv_kernel(count, wkv_count, n, flips, places, *refs):
+def last_kv_kernel(count, wkv_count, places, *refs):
     xs, refs = refs[:count], refs[count:]
     gain_ref, wkv_refs, refs = refs[0], refs[1 : 1 + wkv_count], refs[1 + wkv_count :]
-    acckv_ref, ssq_ref, scale_ref, pieces = refs[0], refs[1], refs[2], refs[3:]
+    choose_ref, acckv_ref, ssq_ref, scale_ref, *pieces = refs
     me = lax.axis_index("head")
     columns = wkv_refs[0].shape[1]
     kvs = [acckv_ref[:, c * columns : (c + 1) * columns] for c in range(wkv_count)]
@@ -167,28 +187,20 @@
     scale = lax.rsqrt(jnp.sum(ssq, axis=1, keepdims=True) / gain_ref.shape[1] + epsilon)
     scale_ref[...] = jnp.broadcast_to(scale, scale_ref.shape)
     kv = jnp.concatenate([(kv * scale).astype(bf16) for kv in kvs], axis=1)
-    features = columns // (2 * KVH)
-    size = 2 * wkv_count * features
-    row = lax.broadcasted_iota(jnp.int32, (size, wkv_count * columns), 0)
-    col = lax.broadcasted_iota(jnp.int32, (size, wkv_count * columns), 1)
-    which, core, feature = row // (wkv_count * features), (row // features) % wkv_count, row % features
-    whose = (core != lax.rem(me, wkv_count)).astype(jnp.int32)
-    first = col - (whose * columns + feature * (2 * KVH) + which)
-    for flip, piece in zip(flips, pieces):
-        group = lax.bitwise_xor(me, jnp.int32(flip)) * KVH // n
-        choose = jnp.where(first == group * 2, 1.0, 0.0).astype(bf16)
-        piece[...] = dot_turned(choose, kv).astype(bf16)
-
-
-def last_kv(xs, places, gain, wkvs, acckv, ssq, n, flips):
+    for i, piece in enumerate(pieces):
+        piece[...] = dot_turned(choose_ref[i].astype(bf16), kv).astype(bf16)
+
+
+def last_kv(xs, places, gain, wkvs, choose, acckv, ssq):
     tokens = xs[0].shape[0]
     columns = len(wkvs) * wkvs[0].shape[1]
-    operands = [*xs, *resident_in(gain, *wkvs), acckv, ssq]
-    return pl.pallas_call(
-        functools.partial(last_kv_kernel, len(xs), len(wkvs), n, flips, places),
-        out_shape=(VMEM((tokens, HD), f32),) + (VMEM((columns // KVH, tokens), bf16),) * len(flips),
+    operands = [*xs, *resident_in(gain, *wkvs, choose), acckv, ssq]
+    count = choose.shape[0]
+    return pl.pallas_call(
+        functools.partial(last_kv_kernel, len(xs), len(wkvs), places),
+        out_shape=(VMEM((tokens, HD), f32),) + (VMEM((columns // KVH, tokens), bf16),) * count,
         in_specs=[vmem] * len(operands),
-        out_specs=(vmem,) * (1 + len(flips)),
+        out_specs=(vmem,) * (1 + count),
         cost_estimate=cost(sum(2 * x.size * columns for x in xs), sum(2 * x.size for x in xs)),
         compiler_params=params,
         name="last_keys_values",
@@ -391,7 +403,7 @@
         return lax.optimization_barrier((array, *others))[0]
 
     def exchanged(xs, places, state):
-        scale, *pieces = last_kv(xs, places, gain, wkvs, state[1], state[2], n, flips)
+        scale, *pieces = last_kv(xs, places, gain, wkvs, choose, state[1], state[2])
         received = [moved(piece, 0, flip) for piece, flip in zip(pieces[1:], flips[1:])]
         return scale, [pieces[0], *received]
 
@@ -409,7 +421,7 @@
         over = moved(own, 0, 3)
         beside = moved(own, 0, 1)
         w_kv_beside = moved(w_kv, 0, 1)
-    accq, own, gain, wq, wkv = load(own, norm_gain, w_q, w_kv)
+    accq, own, gain, wq, wkv, choose = load(own, norm_gain, w_q, w_kv, n, flips, parts)
     if paired:
         wkvs = [wkv, w_kv_beside]
         over = after(over, accq)
@@ -434,19 +446,19 @@
         (sent,) = first_attend(
             opened[0], q, own, fresh_slice, [keys, values], None, parts, (half, heads), sections
         )
+        b1 = moved(sent, 1, 1)
         b3 = moved(sent, 1, 3)
-        b1 = moved(sent, 1, 1)
         a1 = after(a1, sent)
         a2 = moved(a1, 0, 3)
         a0 = moved(a1, 0, 1)
         state = more_blocks([a1], [place(1, 2, 0)], gain, wq, wkvs, [])
-        b1, b3, *state = lax.optimization_barrier((b1, b3, *state))
+        b3, b1, *state = lax.optimization_barrier((b3, b1, *state))
+        b2 = moved(b3, 0, 1)
         b0 = moved(b1, 0, 1)
-        b2 = moved(b3, 0, 1)
         a3 = moved(a2, 0, 1)
-        places = [place(0, 2, 0), place(2, 2, 0), place(1, 2, 1), place(3, 2, 1)]
-        state = more_blocks([a0, a2, b1, b3], places, gain, wq, wkvs, state)
-        last, places = [a3, b0, b2], [place(3, 2, 0), place(0, 2, 1), place(2, 2, 1)]
+        places = [place(0, 2, 0), place(2, 2, 0), *(place(flip, 2, 1) for flip in (3, 1, 2))]
+        state = more_blocks([a0, a2, b3, b1, b2], places, gain, wq, wkvs, state)
+        last, places = [a3, b0], [place(3, 2, 0), place(0, 2, 1)]
         mine = [a0, b0]
     else:
         mine = [moved(sent, 1, 0)]

time: 39.1 us -> 38.1 us (0.974)
  waiting for transfers between devices: 13 us -> 9.95 us
  starting transfers between devices: 13.5 us -> 15.6 us
    ppermute x14, waiting for transfers between devices: 13 us -> 9.95 us  [moved(): return lax.ppermute(array, ('section', 'head'), pairs)]
    ppermute x14, starting transfers between devices: 13.5 us -> 15.6 us  [moved(): return lax.ppermute(array, ('section', 'head'), pairs)]
  transfers between devices with their start and end apart: 14 -> 14, of which waited for: 8 -> 9; matrix products, arithmetic and copies ran while one was open for 0% -> 0% of each run, Pallas kernels for 24% -> 25%
where the time goes in v5:
time: 38.1 us; the launch traced here: 38 us
  starting transfers between devices  15.6 us (41%)
  Pallas kernels  12.3 us (32%)
  waiting for transfers between devices  9.95 us (26%)
    ppermute x14, starting transfers between devices, moved(): return lax.ppermute(array, ('section', 'head'), pairs)  15.6 us
    ppermute x14, waiting for transfers between devices, moved(): return lax.ppermute(array, ('section', 'head'), pairs)  9.95 us
    pallas_call x1, Pallas kernels, load(): pl.pallas_call(functools.partial(load_kernel, n, flips, parts), out_shape...  4.23 us
    pallas_call x3, Pallas kernels, more_blocks(): pl.pallas_call(functools.partial(blocks_kernel, len(xs), len(wkvs), len(s...  2.71 us
    pallas_call x1, Pallas kernels, second_attend(): pl.pallas_call(functools.partial(second_attend_kernel, sections, flips, p...  1.28 us
    pallas_call x2, Pallas kernels, last_kv(): pl.pallas_call(functools.partial(last_kv_kernel, len(xs), len(wkvs), plac...  1.04 us
    pallas_call x2, Pallas kernels, first_attend(): pl.pallas_call(functools.partial(first_attend_kernel, sections, heads, fl...  1 us
    pallas_call x2, Pallas kernels, last_q(): pl.pallas_call(functools.partial(last_q_kernel, len(xs), places), out_sha...  0.92 us
  transfers between devices with their start and end apart: 14, of which 9 were waited for; matrix products, arithmetic and copies ran while one was open for 0% of the time, Pallas kernels for 25%

profile of v5, /device:TPU:0, one launch (start us, length us, event | category | flops | bytes accessed | tf_op | source)
XLA Modules:
  0.0 38.0 jit_solution(14284937896132092707)
XLA Ops:
  0.0 2.4 %collective-permute-start = (bf16[128,1024]{1,0:T(8,128)(2,1)}, bf16[128,1024]{1,0:T(8,128)(2,1)S(1)}, u32[]{:S(2)}, u32[]{:S(2)}) collective-permute-start(bf16[128,1024]{1,0:T(8,128)(2,1)} %bitcast.7), channel_id=1, source_target_pairs={{0,3},{1,2},{2,1},{3,0},{4,7},{5,6},{6,5},{7,4},{8,11},{9,10},{10,... | collective-permute-start | bytes 786440 | tf_op jit(solution)/shard_map/ppermute | solution.py:400
  2.4 0.7 %collective-permute-start.3 = (bf16[128,1024]{1,0:T(8,128)(2,1)}, bf16[128,1024]{1,0:T(8,128)(2,1)S(1)}, u32[]{:S(2)}, u32[]{:S(2)}) collective-permute-start(bf16[128,1024]{1,0:T(8,128)(2,1)} %bitcast.8), channel_id=1, source_target_pairs={{0,1},{1,0},{2,3},{3,2},{4,5},{5,4},{6,7},{7,6},{8,9},{9,8},{10,11... | collective-permute-start | bytes 786440 | tf_op jit(solution)/shard_map/ppermute | solution.py:400
  3.1 0.0 collective-permute-start.2
  3.1 4.2 %load_and_own_queries.1 = (f32[128,1024]{1,0:T(8,128)S(1)}, bf16[128,1024]{1,0:T(8,128)(2,1)S(1)}, f32[1,4096]{1,0:T(1,128)S(1)}, bf16[4096,1024]{1,0:T(8,128)(2...) custom-call(bf16[128,1024]{1,0:T(8,128)(2,1)} %bitcast.9, f32[1,4096]{1,0:T(1,128)} %gain_hbm.1, ...), custom_call_target="tpu_custom_call" | custom-call | flops 99999997952 | bytes 1000000000 | tf_op jit(solution)/shard_map/load_and_own_queries/pallas_call | solution.py:109
  7.3 2.1 %collective-permute-done.refs_2_ = bf16[128,1024]{1,0:T(8,128)(2,1)S(1)} collective-permute-done((bf16[128,1024]{1,0:T(8,128)(2,1)}, bf16[128,1024]{1,0:T(8,128)(2,1)S(1)}, u32[]{:S(2)}, u32[]{:S(2)}) %collective-permute-start) | collective-permute-done | bytes 262176 | tf_op jit(solution)/shard_map/ppermute | solution.py:400
  9.4 0.1 collective-permute-start.1
  9.5 0.0 collective-permute-done.3.refs_1_
  9.5 0.0 collective-permute-done.2.refs_6_.refs_3_.refs_4_.refs_8_
  9.5 1.1 %more_blocks.3 = (f32[128,1024]{1,0:T(8,128)S(1)}, f32[128,512]{1,0:T(8,128)S(1)}, f32[128,128]{1,0:T(8,128)S(1)}) custom-call(bf16[128,1024]{1,0:T(8,128)(2,1)S(1)} %get-tuple-element.47.refs_0_.x_ref, bf16[128,1024]{1,0:T(8,128)(2,1)S(1)} %collective-permute-done.3.refs_1_, bf16[128,1024]{1,0:T(8,128)(2,1)S(1)} %collective-permute-done.refs_2_, ...), custom_call_target="tpu_custom_call" | custom-call | flops 1207959552 | bytes 786432 | tf_op jit(solution)/shard_map/more_blocks/pallas_call | solution.py:161
  10.7 0.3 collective-permute-done.1.refs_0_
  10.9 0.0 copy-start.1
  10.9 0.5 %last_keys_values.2 = (f32[128,128]{1,0:T(8,128)S(1)}, bf16[128,128]{1,0:T(8,128)(2,1)S(1)}, bf16[128,128]{1,0:T(8,128)(2,1)S(1)}) custom-call(bf16[128,1024]{1,0:T(8,128)(2,1)S(1)} %collective-permute-done.1.refs_0_, f32[1,4096]{1,0:T(1,128)S(1)} %get-tuple-element.44.refs_3_.refs_1_.refs_5_.refs_2_, ...), custom_call_target="tpu_custom_call" | custom-call | flops 134217728 | bytes 262144 | tf_op jit(solution)/shard_map/last_keys_values/pallas_call | solution.py:199
  11.5 2.2 %collective-permute-start.4 = (bf16[128,128]{1,0:T(8,128)(2,1)S(1)}, bf16[128,128]{1,0:T(8,128)(2,1)S(1)}, u32[]{:S(2)}, u32[]{:S(2)}) collective-permute-start(bf16[128,128]{1,0:T(8,128)(2,1)S(1)} %get-tuple-element.57), channel_id=1, source_target_pairs={{0,3},{1,2},{2,1},{3,0},{4,7},{5,6},{6,5},{7,4},{8,11},{9,10},{10,... | collective-permute-start | bytes 98312 | tf_op jit(solution)/shard_map/ppermute | solution.py:400
  13.7 0.0 copy-done.1
  13.7 0.6 %openings.1 = (s32[128,128]{1,0:T(8,128)S(1)}, s32[128,128]{1,0:T(8,128)S(1)}) custom-call(s32[9]{0:T(128)S(1)} %copy-done.1), custom_call_target="tpu_custom_call" | custom-call | tf_op jit(solution)/shard_map/openings/pallas_call | solution.py:249
  14.3 0.0 copy-start
  14.3 0.5 %last_queries.2.q_ref = bf16[128,1024]{1,0:T(8,128)(2,1)S(1)} custom-call(bf16[128,1024]{1,0:T(8,128)(2,1)S(1)} %collective-permute-done.1.refs_0_, f32[1,4096]{1,0:T(1,128)S(1)} %get-tuple-element.44.refs_3_.refs_1_.refs_5_.refs_2_, bf16[4096,1024]{1,0:T(8,128)(2,1)S(1)} %get-tuple-element.48.refs_4_.refs_2_.refs_6_.refs_3_, ...), custom_call_target="tpu_custom_call" | custom-call | flops 268435456 | bytes 262144 | tf_op jit(solution)/shard_map/last_queries/pallas_call | solution.py:224
  14.8 0.5 %collective-permute-done.4.refs_1_ = bf16[128,128]{1,0:T(8,128)(2,1)S(1)} collective-permute-done((bf16[128,128]{1,0:T(8,128)(2,1)S(1)}, bf16[128,128]{1,0:T(8,128)(2,1)S(1)}, u32[]{:S(2)}, u32[]{:S(2)}) %collective-permute-start.4) | collective-permute-done | bytes 32800 | tf_op jit(solution)/shard_map/ppermute | solution.py:400
  15.3 0.0 copy-done
  15.3 0.5 %first_attend.2 = (bf16[128,512]{1,0:T(8,128)(2,1)S(1)}, bf16[128,128]{1,0:T(8,128)(2,1)S(1)}, bf16[128,128]{1,0:T(8,128)(2,1)S(1)}) custom-call(s32[128,128]{1,0:T(8,128)S(1)} %get-tuple-element.54.opened_ref, bf16[128,1024]{1,0:T(8,128)(2,1)S(1)} %last_queries.2.q_ref, bf16[128,1024]{1,0:T(8,128)(2,1)S(1)} %get-tuple-element.47.refs_0_.x_ref, ...), custom_call_target="tpu_custom_call" | custom-call | flops 1000 | bytes 1000 | tf_op jit(solution)/shard_map/first_attend/pallas_call | solution.py:313
  15.8 1.7 %collective-permute-start.5 = (bf16[128,512]{1,0:T(8,128)(2,1)S(1)}, bf16[128,512]{1,0:T(8,128)(2,1)S(1)}, u32[]{:S(2)}, u32[]{:S(2)}) collective-permute-start(bf16[128,512]{1,0:T(8,128)(2,1)S(1)} %get-tuple-element.58), channel_id=1, source_target_pairs={{0,5},{1,4},{2,7},{3,6},{4,9},{5,8},{6,11},{7,10},{8,13},{9,12},{1... | collective-permute-start | bytes 393224 | tf_op jit(solution)/shard_map/ppermute | solution.py:400
  17.5 0.5 %first_attend.3 = bf16[128,512]{1,0:T(8,128)(2,1)S(1)} custom-call(s32[128,128]{1,0:T(8,128)S(1)} %get-tuple-element.54.opened_ref, bf16[128,1024]{1,0:T(8,128)(2,1)S(1)} %last_queries.2.q_ref, bf16[128,1024]{1,0:T(8,128)(2,1)S(1)} %get-tuple-element.47.refs_0_.x_ref, bf16[128,1024]{1,0:T(8,128)(2,1)S(1)} %copy-done, ...), custom_call_target="tpu_custom_call" | custom-call | flops 1000 | bytes 1000 | tf_op jit(solution)/shard_map/first_attend/pallas_call | solution.py:313
  18.0 2.6 %collective-permute-start.8 = (bf16[128,512]{1,0:T(8,128)(2,1)S(1)}, bf16[128,512]{1,0:T(8,128)(2,1)S(1)}, u32[]{:S(2)}, u32[]{:S(2)}) collective-permute-start(bf16[128,512]{1,0:T(8,128)(2,1)S(1)} %first_attend.3), channel_id=1, source_target_pairs={{0,7},{1,6},{2,5},{3,4},{4,11},{5,10},{6,9},{7,8},{8,15},{9,14},{1... | collective-permute-start | bytes 393224 | tf_op jit(solution)/shard_map/ppermute | solution.py:400
  20.6 1.3 %collective-permute-start.9 = (bf16[128,512]{1,0:T(8,128)(2,1)S(1)}, bf16[128,512]{1,0:T(8,128)(2,1)S(1)}, u32[]{:S(2)}, u32[]{:S(2)}) collective-permute-start(bf16[128,512]{1,0:T(8,128)(2,1)S(1)} %first_attend.3), channel_id=1, source_target_pairs={{0,5},{1,4},{2,7},{3,6},{4,9},{5,8},{6,11},{7,10},{8,13},{9,12},{1... | collective-permute-start | bytes 393224 | tf_op jit(solution)/shard_map/ppermute | solution.py:400
  21.8 2.3 %collective-permute-done.5.refs_0_ = bf16[128,512]{1,0:T(8,128)(2,1)S(1)} collective-permute-done((bf16[128,512]{1,0:T(8,128)(2,1)S(1)}, bf16[128,512]{1,0:T(8,128)(2,1)S(1)}, u32[]{:S(2)}, u32[]{:S(2)}) %collective-permute-start.5) | collective-permute-done | bytes 131104 | tf_op jit(solution)/shard_map/ppermute | solution.py:400
  24.1 2.2 %collective-permute-start.6 = (bf16[128,512]{1,0:T(8,128)(2,1)S(1)}, bf16[128,512]{1,0:T(8,128)(2,1)S(1)}, u32[]{:S(2)}, u32[]{:S(2)}) collective-permute-start(bf16[128,512]{1,0:T(8,128)(2,1)S(1)} %collective-permute-done.5.refs_0_), channel_id=1, source_target_pairs={{0,3},{1,2},{2,1},{3,0},{4,7},{5,6},{6,5},{7,4},{8,11},{9,10},{10,... | collective-permute-start | bytes 393224 | tf_op jit(solution)/shard_map/ppermute | solution.py:400
  26.3 0.4 more_blocks.4
  26.7 1.6 %collective-permute-done.8.refs_2_ = bf16[128,512]{1,0:T(8,128)(2,1)S(1)} collective-permute-done((bf16[128,512]{1,0:T(8,128)(2,1)S(1)}, bf16[128,512]{1,0:T(8,128)(2,1)S(1)}, u32[]{:S(2)}, u32[]{:S(2)}) %collective-permute-start.8) | collective-permute-done | bytes 131104 | tf_op jit(solution)/shard_map/ppermute | solution.py:400
  28.3 1.6 %collective-permute-done.9.refs_3_ = bf16[128,512]{1,0:T(8,128)(2,1)S(1)} collective-permute-done((bf16[128,512]{1,0:T(8,128)(2,1)S(1)}, bf16[128,512]{1,0:T(8,128)(2,1)S(1)}, u32[]{:S(2)}, u32[]{:S(2)}) %collective-permute-start.9) | collective-permute-done | bytes 131104 | tf_op jit(solution)/shard_map/ppermute | solution.py:400
  29.9 0.3 collective-permute-start.12
  30.2 0.2 collective-permute-start.11
  30.4 0.3 collective-permute-start.10
  30.7 0.6 %collective-permute-done.6.refs_1_ = bf16[128,512]{1,0:T(8,128)(2,1)S(1)} collective-permute-done((bf16[128,512]{1,0:T(8,128)(2,1)S(1)}, bf16[128,512]{1,0:T(8,128)(2,1)S(1)}, u32[]{:S(2)}, u32[]{:S(2)}) %collective-permute-start.6) | collective-permute-done | bytes 131104 | tf_op jit(solution)/shard_map/ppermute | solution.py:400
  31.4 0.1 collective-permute-start.7
  31.5 0.0 collective-permute-done.12.refs_4_
  31.5 0.1 collective-permute-done.11.refs_0_
  31.6 1.2 %more_blocks.5 = (f32[128,1024]{1,0:T(8,128)S(1)}, f32[128,512]{1,0:T(8,128)S(1)}, f32[128,128]{1,0:T(8,128)S(1)}) custom-call(bf16[128,512]{1,0:T(8,128)(2,1)S(1)} %collective-permute-done.11.refs_0_, bf16[128,512]{1,0:T(8,128)(2,1)S(1)} %collective-permute-done.6.refs_1_, bf16[128,512]{1,0:T(8,128)(2,1)S(1)} %collective-permute-done.8.refs_2_, ...), custom_call_target="tpu_custom_call" | custom-call | flops 1006632960 | bytes 655360 | tf_op jit(solution)/shard_map/more_blocks/pallas_call | solution.py:161
  32.8 0.0 collective-permute-done.10.refs_1_
  32.8 0.0 collective-permute-done.7.refs_0_
  32.8 0.5 %last_keys_values.3 = (f32[128,128]{1,0:T(8,128)S(1)}, bf16[128,128]{1,0:T(8,128)(2,1)S(1)}, bf16[128,128]{1,0:T(8,128)(2,1)S(1)}) custom-call(bf16[128,512]{1,0:T(8,128)(2,1)S(1)} %collective-permute-done.7.refs_0_, bf16[128,512]{1,0:T(8,128)(2,1)S(1)} %collective-permute-done.10.refs_1_, f32[1,4096]{1,0:T(1,128)S(1)} %get-tuple-element.44.refs_3_.refs_1_.refs_5_.refs_2_, ...), custom_call_target="tpu_custom_call" | custom-call | flops 134217728 | bytes 262144 | tf_op jit(solution)/shard_map/last_keys_values/pallas_call | solution.py:199
  33.3 1.6 %collective-permute-start.13 = (bf16[128,128]{1,0:T(8,128)(2,1)S(1)}, bf16[128,128]{1,0:T(8,128)(2,1)S(1)}, u32[]{:S(2)}, u32[]{:S(2)}) collective-permute-start(bf16[128,128]{1,0:T(8,128)(2,1)S(1)} %get-tuple-element.78), channel_id=1, source_target_pairs={{0,3},{1,2},{2,1},{3,0},{4,7},{5,6},{6,5},{7,4},{8,11},{9,10},{10,... | collective-permute-start | bytes 98312 | tf_op jit(solution)/shard_map/ppermute | solution.py:400
  34.9 0.4 %last_queries.3.q_ref = bf16[128,1024]{1,0:T(8,128)(2,1)S(1)} custom-call(bf16[128,512]{1,0:T(8,128)(2,1)S(1)} %collective-permute-done.7.refs_0_, bf16[128,512]{1,0:T(8,128)(2,1)S(1)} %collective-permute-done.10.refs_1_, f32[1,4096]{1,0:T(1,128)S(1)} %get-tuple-element.44.refs_3_.refs_1_.refs_5_.refs_2_, ...), custom_call_target="tpu_custom_call" | custom-call | flops 268435456 | bytes 262144 | tf_op jit(solution)/shard_map/last_queries/pallas_call | solution.py:224
  35.4 0.5 %resident_attend.1 = (f32[1024,128]{1,0:T(8,128)S(1)}, f32[1024,128]{1,0:T(8,128)S(1)}, f32[1024,128]{1,0:T(8,128)S(1)}) custom-call(s32[128,128]{1,0:T(8,128)S(1)} %get-tuple-element.53.opened_ref, bf16[128,1024]{1,0:T(8,128)(2,1)S(1)} %last_queries.3.q_ref, bf16[128,128]{1,0:T(8,128)(2,1)S(1)} %get-tuple-element.59.refs_0_.keys_ref, ...), custom_call_target="tpu_custom_call" | custom-call | flops 1000 | bytes 1000 | tf_op jit(solution)/shard_map/resident_attend/pallas_call | solution.py:339
  35.9 0.9 %collective-permute-done.13.refs_3_ = bf16[128,128]{1,0:T(8,128)(2,1)S(1)} collective-permute-done((bf16[128,128]{1,0:T(8,128)(2,1)S(1)}, bf16[128,128]{1,0:T(8,128)(2,1)S(1)}, u32[]{:S(2)}, u32[]{:S(2)}) %collective-permute-start.13) | collective-permute-done | bytes 32800 | tf_op jit(solution)/shard_map/ppermute | solution.py:400
  36.7 1.3 %second_attend.1 = bf16[128,1024]{1,0:T(8,128)(2,1)} custom-call(s32[128,128]{1,0:T(8,128)S(1)} %get-tuple-element.53.opened_ref, bf16[128,1024]{1,0:T(8,128)(2,1)S(1)} %last_queries.3.q_ref, f32[1024,128]{1,0:T(8,128)S(1)} %get-tuple-element.74.max_ref, f32[1024,128]{1,0:T(8,128)S(1)} %get-tuple-element.75.sum_ref, ...), custom_call_target="tpu_custom_call" | custom-call | flops 1000 | bytes 1000 | tf_op jit(solution)/shard_map/second_attend/pallas_call | solution.py:373
Async XLA Ops:
  0.0 9.4 %collective-permute-start = (bf16[128,1024]{1,0:T(8,128)(2,1)}, bf16[128,1024]{1,0:T(8,128)(2,1)S(1)}, u32[]{:S(2)}, u32[]{:S(2)}) collective-permute-start(bf16[128,1024]{1,0:T(8,128)(2,1)} %bitcast.7), channel_id=1, source_target_pairs={{0,3},{1,2},{2,1},{3,0},{4,7},{5,6},{6,5},{7,4},{8,11},{9,10},{10,... | collective-permute-start | bytes 786440 | tf_op jit(solution)/shard_map/ppermute | solution.py:400
  2.4 7.1 %collective-permute-start.3 = (bf16[128,1024]{1,0:T(8,128)(2,1)}, bf16[128,1024]{1,0:T(8,128)(2,1)S(1)}, u32[]{:S(2)}, u32[]{:S(2)}) collective-permute-start(bf16[128,1024]{1,0:T(8,128)(2,1)} %bitcast.8), channel_id=1, source_target_pairs={{0,1},{1,0},{2,3},{3,2},{4,5},{5,4},{6,7},{7,6},{8,9},{9,8},{10,11... | collective-permute-start | bytes 786440 | tf_op jit(solution)/shard_map/ppermute | solution.py:400
  3.1 6.4 %collective-permute-start.2 = (bf16[4096,256]{1,0:T(8,128)(2,1)}, bf16[4096,256]{1,0:T(8,128)(2,1)S(1)}, u32[]{:S(2)}, u32[]{:S(2)}) collective-permute-start(bf16[4096,256]{1,0:T(8,128)(2,1)} %bitcast.5), channel_id=1, source_target_pairs={{0,1},{1,0},{2,3},{3,2},{4,5},{5,4},{6,7},{7,6},{8,9},{9,8},{10,11... | collective-permute-start | bytes 6291464 | tf_op jit(solution)/shard_map/ppermute | solution.py:400
  9.4 1.5 %collective-permute-start.1 = (bf16[128,1024]{1,0:T(8,128)(2,1)S(1)}, bf16[128,1024]{1,0:T(8,128)(2,1)S(1)}, u32[]{:S(2)}, u32[]{:S(2)}) collective-permute-start(bf16[128,1024]{1,0:T(8,128)(2,1)S(1)} %collective-permute-done.refs_2_), channel_id=1, source_target_pairs={{0,1},{1,0},{2,3},{3,2},{4,5},{5,4},{6,7},{7,6},{8,9},{9,8},{10,11... | collective-permute-start | bytes 786440 | tf_op jit(solution)/shard_map/ppermute | solution.py:400
  10.9 2.7 %copy-start.1 = (s32[9]{0:T(128)S(1)}, s32[9]{0:T(128)}, u32[]{:S(2)}) copy-start(s32[9]{0:T(128)} %doc_ref) | copy-start | bytes 112
  11.5 3.8 %collective-permute-start.4 = (bf16[128,128]{1,0:T(8,128)(2,1)S(1)}, bf16[128,128]{1,0:T(8,128)(2,1)S(1)}, u32[]{:S(2)}, u32[]{:S(2)}) collective-permute-start(bf16[128,128]{1,0:T(8,128)(2,1)S(1)} %get-tuple-element.57), channel_id=1, source_target_pairs={{0,3},{1,2},{2,1},{3,0},{4,7},{5,6},{6,5},{7,4},{8,11},{9,10},{10,... | collective-permute-start | bytes 98312 | tf_op jit(solution)/shard_map/ppermute | solution.py:400
  14.3 1.0 %copy-start = (bf16[128,1024]{1,0:T(8,128)(2,1)S(1)}, bf16[128,1024]{1,0:T(8,128)(2,1)}, u32[]{:S(2)}) copy-start(bf16[128,1024]{1,0:T(8,128)(2,1)} %fresh_ref.3) | copy-start | bytes 786436
  15.8 8.4 %collective-permute-start.5 = (bf16[128,512]{1,0:T(8,128)(2,1)S(1)}, bf16[128,512]{1,0:T(8,128)(2,1)S(1)}, u32[]{:S(2)}, u32[]{:S(2)}) collective-permute-start(bf16[128,512]{1,0:T(8,128)(2,1)S(1)} %get-tuple-element.58), channel_id=1, source_target_pairs={{0,5},{1,4},{2,7},{3,6},{4,9},{5,8},{6,11},{7,10},{8,13},{9,12},{1... | collective-permute-start | bytes 393224 | tf_op jit(solution)/shard_map/ppermute | solution.py:400
  18.0 10.3 %collective-permute-start.8 = (bf16[128,512]{1,0:T(8,128)(2,1)S(1)}, bf16[128,512]{1,0:T(8,128)(2,1)S(1)}, u32[]{:S(2)}, u32[]{:S(2)}) collective-permute-start(bf16[128,512]{1,0:T(8,128)(2,1)S(1)} %first_attend.3), channel_id=1, source_target_pairs={{0,7},{1,6},{2,5},{3,4},{4,11},{5,10},{6,9},{7,8},{8,15},{9,14},{1... | collective-permute-start | bytes 393224 | tf_op jit(solution)/shard_map/ppermute | solution.py:400
  20.6 9.4 %collective-permute-start.9 = (bf16[128,512]{1,0:T(8,128)(2,1)S(1)}, bf16[128,512]{1,0:T(8,128)(2,1)S(1)}, u32[]{:S(2)}, u32[]{:S(2)}) collective-permute-start(bf16[128,512]{1,0:T(8,128)(2,1)S(1)} %first_attend.3), channel_id=1, source_target_pairs={{0,5},{1,4},{2,7},{3,6},{4,9},{5,8},{6,11},{7,10},{8,13},{9,12},{1... | collective-permute-start | bytes 393224 | tf_op jit(solution)/shard_map/ppermute | solution.py:400
  24.1 7.2 %collective-permute-start.6 = (bf16[128,512]{1,0:T(8,128)(2,1)S(1)}, bf16[128,512]{1,0:T(8,128)(2,1)S(1)}, u32[]{:S(2)}, u32[]{:S(2)}) collective-permute-start(bf16[128,512]{1,0:T(8,128)(2,1)S(1)} %collective-permute-done.5.refs_0_), channel_id=1, source_target_pairs={{0,3},{1,2},{2,1},{3,0},{4,7},{5,6},{6,5},{7,4},{8,11},{9,10},{10,... | collective-permute-start | bytes 393224 | tf_op jit(solution)/shard_map/ppermute | solution.py:400
  29.9 1.5 %collective-permute-start.12 = (bf16[128,512]{1,0:T(8,128)(2,1)S(1)}, bf16[128,512]{1,0:T(8,128)(2,1)S(1)}, u32[]{:S(2)}, u32[]{:S(2)}) collective-permute-start(bf16[128,512]{1,0:T(8,128)(2,1)S(1)} %collective-permute-done.8.refs_2_), channel_id=1, source_target_pairs={{0,1},{1,0},{2,3},{3,2},{4,5},{5,4},{6,7},{7,6},{8,9},{9,8},{10,11... | collective-permute-start | bytes 393224 | tf_op jit(solution)/shard_map/ppermute | solution.py:400
  30.2 1.3 %collective-permute-start.11 = (bf16[128,512]{1,0:T(8,128)(2,1)S(1)}, bf16[128,512]{1,0:T(8,128)(2,1)S(1)}, u32[]{:S(2)}, u32[]{:S(2)}) collective-permute-start(bf16[128,512]{1,0:T(8,128)(2,1)S(1)} %collective-permute-done.5.refs_0_), channel_id=1, source_target_pairs={{0,1},{1,0},{2,3},{3,2},{4,5},{5,4},{6,7},{7,6},{8,9},{9,8},{10,11... | collective-permute-start | bytes 393224 | tf_op jit(solution)/shard_map/ppermute | solution.py:400
  30.4 2.3 %collective-permute-start.10 = (bf16[128,512]{1,0:T(8,128)(2,1)S(1)}, bf16[128,512]{1,0:T(8,128)(2,1)S(1)}, u32[]{:S(2)}, u32[]{:S(2)}) collective-permute-start(bf16[128,512]{1,0:T(8,128)(2,1)S(1)} %collective-permute-done.9.refs_3_), channel_id=1, source_target_pairs={{0,1},{1,0},{2,3},{3,2},{4,5},{5,4},{6,7},{7,6},{8,9},{9,8},{10,11... | collective-permute-start | bytes 393224 | tf_op jit(solution)/shard_map/ppermute | solution.py:400
  31.4 1.4 %collective-permute-start.7 = (bf16[128,512]{1,0:T(8,128)(2,1)S(1)}, bf16[128,512]{1,0:T(8,128)(2,1)S(1)}, u32[]{:S(2)}, u32[]{:S(2)}) collective-permute-start(bf16[128,512]{1,0:T(8,128)(2,1)S(1)} %collective-permute-done.6.refs_1_), channel_id=1, source_target_pairs={{0,1},{1,0},{2,3},{3,2},{4,5},{5,4},{6,7},{7,6},{8,9},{9,8},{10,11... | collective-permute-start | bytes 393224 | tf_op jit(solution)/shard_map/ppermute | solution.py:400
  33.3 3.4 %collective-permute-start.13 = (bf16[128,128]{1,0:T(8,128)(2,1)S(1)}, bf16[128,128]{1,0:T(8,128)(2,1)S(1)}, u32[]{:S(2)}, u32[]{:S(2)}) collective-permute-start(bf16[128,128]{1,0:T(8,128)(2,1)S(1)} %get-tuple-element.78), channel_id=1, source_target_pairs={{0,3},{1,2},{2,1},{3,0},{4,7},{5,6},{6,5},{7,4},{8,11},{9,10},{10,... | collective-permute-start | bytes 98312 | tf_op jit(solution)/shard_map/ppermute | solution.py:400

commit v6 on v5

--- a/solution.py
+++ b/solution.py
@@ -13,6 +13,7 @@
 GROUP = 8
 
 epsilon = 1e-05
+score_scale = math.log2(math.e) / math.sqrt(HD)
 masked_score = -1e30
 
 VMEM = pltpu.VMEM
@@ -36,6 +37,10 @@
     return pl.ds(pl.multiple_of(block * width, width), width)
 
 
+def from_start(start, width):
+    return pl.ds(pl.multiple_of(start, HD), width)
+
+
 def dot(a, b):
     return jnp.dot(a, b, preferred_element_type=f32)
 
@@ -44,14 +49,14 @@
     return lax.dot_general(a, b, (((1,), (1,)), ((), ())), preferred_element_type=f32)
 
 
-def gained(x, gain_ref, block):
+def gained(x, gain_ref, start):
     width = x.shape[1]
     wide = x.astype(f32)
     squares = wide * wide
     ssq = squares[:, :HD]
     for c in range(HD, width, HD):
         ssq = ssq + squares[:, c : c + HD]
-    return (wide * gain_ref[:, rows_of(block, width)]).astype(bf16), ssq
+    return (wide * gain_ref[:, from_start(start, width)]).astype(bf16), ssq
 
 
 def choose_rows(choose_ref, me, n, flips, parts):
@@ -94,7 +99,7 @@
     choose_rows(choose_ref, me, n, flips, parts)
     for copy in small:
         copy.wait()
-    normed, _ = gained(x_ref[...], gain_ref, me)
+    normed, _ = gained(x_ref[...], gain_ref, me * width)
     part(0).wait()
     accq_ref[...] = dot(normed, wq_ref[rows_of(me, width), :])
     for step in range(1, n):
@@ -140,10 +145,10 @@
         return term if total is None else total + term
 
     for i, x_ref in enumerate(xs):
-        block, width = places[i](me), x_ref.shape[1]
-        normed, squares = gained(x_ref[...], gain_ref, block)
+        start, width = places[i](me), x_ref.shape[1]
+        normed, squares = gained(x_ref[...], gain_ref, start)
         ssq = add(ssq, squares)
-        rows = rows_of(block, width)
+        rows = from_start(start, width)
         kvs = [add(kv, dot(normed, w_ref[rows, :])) for kv, w_ref in zip(kvs, wkv_refs)]
         if with_q[i]:
             q = add(q, dot(normed, wq_ref[rows, :]))
@@ -180,10 +185,10 @@
     kvs = [acckv_ref[:, c * columns : (c + 1) * columns] for c in range(wkv_count)]
     ssq = ssq_ref[...]
     for i, x_ref in enumerate(xs):
-        block, width = places[i](me), x_ref.shape[1]
-        normed, squares = gained(x_ref[...], gain_ref, block)
+        start, width = places[i](me), x_ref.shape[1]
+        normed, squares = gained(x_ref[...], gain_ref, start)
         ssq = ssq + squares
-        kvs = [kv + dot(normed, w_ref[rows_of(block, width), :]) for kv, w_ref in zip(kvs, wkv_refs)]
+        kvs = [kv + dot(normed, w_ref[from_start(start, width), :]) for kv, w_ref in zip(kvs, wkv_refs)]
     scale = lax.rsqrt(jnp.sum(ssq, axis=1, keepdims=True) / gain_ref.shape[1] + epsilon)
     scale_ref[...] = jnp.broadcast_to(scale, scale_ref.shape)
     kv = jnp.concatenate([(kv * scale).astype(bf16) for kv in kvs], axis=1)
@@ -213,9 +218,9 @@
     me = lax.axis_index("head")
     total = accq_ref[...]
     for i, x_ref in enumerate(xs):
-        block, width = places[i](me), x_ref.shape[1]
-        normed, _ = gained(x_ref[...], gain_ref, block)
-        total = total + dot(normed, wq_ref[rows_of(block, width), :])
+        start, width = places[i](me), x_ref.shape[1]
+        normed, _ = gained(x_ref[...], gain_ref, start)
+        total = total + dot(normed, wq_ref[from_start(start, width), :])
     q_ref[...] = (total * scale_ref[:, 0:1]).astype(bf16)
 
 
@@ -265,9 +270,14 @@
     here = query_start + lax.broadcasted_iota(jnp.int32, (tokens, count), 0)
     there = key_start + lax.broadcasted_iota(jnp.int32, (tokens, count), 1)
     allowed = (there >= opened_ref[:, 0:1]) & (there <= here)
-    scores = dot(q, keys) * (1.0 / math.sqrt(HD))
-    scores = jnp.where(allowed[None], scores.reshape(-1, tokens, count), masked_score)
+    scores = jnp.where(allowed[None], dot(q, keys).reshape(-1, tokens, count), masked_score)
     return scores.reshape(-1, count)
+
+
+def mixed_and_sums(expon, values):
+    both = jnp.concatenate([values, jnp.ones(values.shape, bf16)], axis=0)
+    both = dot_turned(expon.astype(bf16), both)
+    return both[:, :HD], both[:, HD:]
 
 
 def put_together(me, pieces, flips, parts, gather):
@@ -292,9 +302,9 @@
         keys_ref[...], values_ref[...] = keys, values
     tokens = q_ref.shape[0]
     scores = masked_scores(stacked_heads(q_ref, heads), keys, opened_ref, start, start)
-    expon = jnp.exp(scores - jnp.max(scores, axis=1, keepdims=True))
-    weights = (expon * (1.0 / jnp.sum(expon, axis=1, keepdims=True))).astype(bf16)
-    mixed = dot_turned(weights, values).astype(bf16).astype(f32)
+    expon = jnp.exp2((scores - jnp.max(scores, axis=1, keepdims=True)) * score_scale)
+    mixed, total = mixed_and_sums(expon, values)
+    mixed = (mixed * (1.0 / total)).astype(bf16).astype(f32)
     for i, h in enumerate(range(*heads)):
         columns = slice(h * HD, (h + 1) * HD)
         out = (x_ref[:, columns].astype(f32) + mixed[i * tokens : (i + 1) * tokens]).astype(bf16)
@@ -328,10 +338,9 @@
     q = stacked_heads(q_ref, (0, q_ref.shape[1] // HD))
     scores = masked_scores(q, keys_ref[...], opened_ref, key_start + tokens, key_start)
     top = jnp.max(scores, axis=1, keepdims=True)
-    expon = jnp.exp(scores - top)
+    expon = jnp.exp2((scores - top) * score_scale)
     max_ref[...] = jnp.broadcast_to(top, max_ref.shape)
-    sum_ref[...] = jnp.broadcast_to(jnp.sum(expon, axis=1, keepdims=True), sum_ref.shape)
-    mixed_ref[...] = dot_turned(expon.astype(bf16), values_ref[...])
+    mixed_ref[...], sum_ref[...] = mixed_and_sums(expon, values_ref[...])
 
 
 def resident_attend(opened, q, keys, values, sections):
@@ -355,14 +364,14 @@
     keys, values = put_together(lax.axis_index("head"), pieces, flips, parts, gather)
     scores = masked_scores(stacked_heads(q_ref, (0, heads)), keys, opened_ref, start, start)
     top = jnp.maximum(jnp.max(scores, axis=1, keepdims=True), max_ref[...])
-    expon = jnp.exp(scores - top)
-    shrink = jnp.exp(max_ref[...] - top)
-    total = jnp.sum(expon, axis=1, keepdims=True) + shrink * sum_ref[...]
-    mixed = dot_turned(expon.astype(bf16), values) + shrink * mixed_ref[...]
+    expon = jnp.exp2((scores - top) * score_scale)
+    shrink = jnp.exp2((max_ref[...] - top) * score_scale)
+    mixed, total = mixed_and_sums(expon, values)
+    total = total + shrink * sum_ref[...]
+    mixed = mixed + shrink * mixed_ref[...]
     mixed = (mixed * (1.0 / total)).astype(bf16).astype(f32)
-    x_width = x_refs[0].shape[1]
-    for h in range(heads):
-        x_ref, inside = x_refs[h * HD // x_width], h * HD % x_width
+    where = [(x_ref, inside) for x_ref in x_refs for inside in range(0, x_ref.shape[1], HD)]
+    for h, (x_ref, inside) in enumerate(where):
         out = x_ref[:, inside : inside + HD].astype(f32) + mixed[h * tokens : (h + 1) * tokens]
         out_ref[:, h * HD : (h + 1) * HD] = out.astype(bf16)
 
@@ -387,7 +396,7 @@
     sections = lax.axis_size("section")
     own = entering[0]
     w_q, w_kv = w_query[0], w_key_value[0]
-    tokens = own.shape[0]
+    tokens, width = own.shape
     heads = w_q.shape[1] // HD
     paired = n == 4
     parts = 2 if paired else 1
@@ -412,10 +421,10 @@
         me = lax.axis_index("head")
         return [lax.dynamic_index_in_dim(every, (me + k) % n, 0, False) for k in range(1, n)]
 
-    def place(flip, count=1, part=0):
-        return lambda me: lax.bitwise_xor(me, jnp.int32(flip)) * count + part
-
-    following = [functools.partial(lambda k, me: lax.rem(me + k, jnp.int32(n)), k) for k in range(n)]
+    def place(flip, offset=0):
+        return lambda me: lax.bitwise_xor(me, jnp.int32(flip)) * width + offset
+
+    following = [functools.partial(lambda k, me: lax.rem(me + k, jnp.int32(n)) * width, k) for k in range(n)]
 
     if paired:
         over = moved(own, 0, 3)
@@ -436,29 +445,30 @@
     scale, pieces = exchanged(last, places, state)
     opened = openings(after(doc_lengths, scale), tokens, sections)
     q = last_q(last, places, gain, wq, state[0], scale)
-    half = heads // 2 if paired else heads
+    part = heads // 2 if paired else heads
+    split = part * HD
     sent, keys, values = first_attend(
-        opened[0], q, own, fresh_slice, pieces, flips, parts, (0, half), sections
+        opened[0], q, own, fresh_slice, pieces, flips, parts, (0, part), sections
     )
 
     if paired:
         a1 = moved(sent, 1, 1)
         (sent,) = first_attend(
-            opened[0], q, own, fresh_slice, [keys, values], None, parts, (half, heads), sections
+            opened[0], q, own, fresh_slice, [keys, values], None, parts, (part, heads), sections
         )
         b1 = moved(sent, 1, 1)
         b3 = moved(sent, 1, 3)
         a1 = after(a1, sent)
         a2 = moved(a1, 0, 3)
         a0 = moved(a1, 0, 1)
-        state = more_blocks([a1], [place(1, 2, 0)], gain, wq, wkvs, [])
+        state = more_blocks([a1], [place(1)], gain, wq, wkvs, [])
         b3, b1, *state = lax.optimization_barrier((b3, b1, *state))
         b2 = moved(b3, 0, 1)
         b0 = moved(b1, 0, 1)
         a3 = moved(a2, 0, 1)
-        places = [place(0, 2, 0), place(2, 2, 0), *(place(flip, 2, 1) for flip in (3, 1, 2))]
+        places = [place(0), place(2), *(place(flip, split) for flip in (3, 1, 2))]
         state = more_blocks([a0, a2, b3, b1, b2], places, gain, wq, wkvs, state)
-        last, places = [a3, b0], [place(3, 2, 0), place(0, 2, 1)]
+        last, places = [a3, b0], [place(3), place(0, split)]
         mine = [a0, b0]
     else:
         mine = [moved(sent, 1, 0)]

time: 38.1 us -> 38.1 us (level)
  transfers between devices with their start and end apart: 14 -> 14, of which waited for: 9 -> 8; matrix products, arithmetic and copies ran while one was open for 0% -> 0% of each run, Pallas kernels for 25% -> 25%
where the time goes in v6:
time: 38.1 us; the launch traced here: 38 us
  starting transfers between devices  15.6 us (41%)
  Pallas kernels  12.4 us (33%)
  waiting for transfers between devices  9.83 us (26%)
    ppermute x14, starting transfers between devices, moved(): return lax.ppermute(array, ('section', 'head'), pairs)  15.6 us
    ppermute x14, waiting for transfers between devices, moved(): return lax.ppermute(array, ('section', 'head'), pairs)  9.83 us
    pallas_call x1, Pallas kernels, load(): pl.pallas_call(functools.partial(load_kernel, n, flips, parts), out_shape...  4.23 us
    pallas_call x3, Pallas kernels, more_blocks(): pl.pallas_call(functools.partial(blocks_kernel, len(xs), len(wkvs), len(s...  2.72 us
    pallas_call x1, Pallas kernels, second_attend(): pl.pallas_call(functools.partial(second_attend_kernel, sections, flips, p...  1.32 us
    pallas_call x2, Pallas kernels, last_kv(): pl.pallas_call(functools.partial(last_kv_kernel, len(xs), len(wkvs), plac...  1.04 us
    pallas_call x2, Pallas kernels, first_attend(): pl.pallas_call(functools.partial(first_attend_kernel, sections, heads, fl...  0.96 us
    pallas_call x2, Pallas kernels, last_q(): pl.pallas_call(functools.partial(last_q_kernel, len(xs), places), out_sha...  0.92 us
  transfers between devices with their start and end apart: 14, of which 8 were waited for; matrix products, arithmetic and copies ran while one was open for 0% of the time, Pallas kernels for 25%

profile of v6, /device:TPU:0, one launch (start us, length us, event | category | flops | bytes accessed | tf_op | source)
XLA Modules:
  0.0 38.0 jit_solution(16260228025122961441)
XLA Ops:
  0.0 2.4 %collective-permute-start = (bf16[128,1024]{1,0:T(8,128)(2,1)}, bf16[128,1024]{1,0:T(8,128)(2,1)S(1)}, u32[]{:S(2)}, u32[]{:S(2)}) collective-permute-start(bf16[128,1024]{1,0:T(8,128)(2,1)} %bitcast.7), channel_id=1, source_target_pairs={{0,3},{1,2},{2,1},{3,0},{4,7},{5,6},{6,5},{7,4},{8,11},{9,10},{10,... | collective-permute-start | bytes 786440 | tf_op jit(solution)/shard_map/ppermute | solution.py:409
  2.4 0.7 %collective-permute-start.3 = (bf16[128,1024]{1,0:T(8,128)(2,1)}, bf16[128,1024]{1,0:T(8,128)(2,1)S(1)}, u32[]{:S(2)}, u32[]{:S(2)}) collective-permute-start(bf16[128,1024]{1,0:T(8,128)(2,1)} %bitcast.8), channel_id=1, source_target_pairs={{0,1},{1,0},{2,3},{3,2},{4,5},{5,4},{6,7},{7,6},{8,9},{9,8},{10,11... | collective-permute-start | bytes 786440 | tf_op jit(solution)/shard_map/ppermute | solution.py:409
  3.1 0.0 collective-permute-start.2
  3.1 4.2 %load_and_own_queries.1 = (f32[128,1024]{1,0:T(8,128)S(1)}, bf16[128,1024]{1,0:T(8,128)(2,1)S(1)}, f32[1,4096]{1,0:T(1,128)S(1)}, bf16[4096,1024]{1,0:T(8,128)(2...) custom-call(bf16[128,1024]{1,0:T(8,128)(2,1)} %bitcast.9, f32[1,4096]{1,0:T(1,128)} %gain_hbm.1, ...), custom_call_target="tpu_custom_call" | custom-call | flops 99999997952 | bytes 1000000000 | tf_op jit(solution)/shard_map/load_and_own_queries/pallas_call | solution.py:114
  7.3 2.1 %collective-permute-done.refs_2_ = bf16[128,1024]{1,0:T(8,128)(2,1)S(1)} collective-permute-done((bf16[128,1024]{1,0:T(8,128)(2,1)}, bf16[128,1024]{1,0:T(8,128)(2,1)S(1)}, u32[]{:S(2)}, u32[]{:S(2)}) %collective-permute-start) | collective-permute-done | bytes 262176 | tf_op jit(solution)/shard_map/ppermute | solution.py:409
  9.4 0.1 collective-permute-start.1
  9.5 0.0 collective-permute-done.3.refs_1_
  9.5 0.0 collective-permute-done.2.refs_6_.refs_3_.refs_4_.refs_8_
  9.5 1.1 %more_blocks.3 = (f32[128,1024]{1,0:T(8,128)S(1)}, f32[128,512]{1,0:T(8,128)S(1)}, f32[128,128]{1,0:T(8,128)S(1)}) custom-call(bf16[128,1024]{1,0:T(8,128)(2,1)S(1)} %get-tuple-element.47.refs_0_.x_ref, bf16[128,1024]{1,0:T(8,128)(2,1)S(1)} %collective-permute-done.3.refs_1_, bf16[128,1024]{1,0:T(8,128)(2,1)S(1)} %collective-permute-done.refs_2_, ...), custom_call_target="tpu_custom_call" | custom-call | flops 1207959552 | bytes 786432 | tf_op jit(solution)/shard_map/more_blocks/pallas_call | solution.py:166
  10.7 0.3 collective-permute-done.1.refs_0_
  10.9 0.0 copy-start.1
  10.9 0.5 %last_keys_values.2 = (f32[128,128]{1,0:T(8,128)S(1)}, bf16[128,128]{1,0:T(8,128)(2,1)S(1)}, bf16[128,128]{1,0:T(8,128)(2,1)S(1)}) custom-call(bf16[128,1024]{1,0:T(8,128)(2,1)S(1)} %collective-permute-done.1.refs_0_, f32[1,4096]{1,0:T(1,128)S(1)} %get-tuple-element.44.refs_3_.refs_1_.refs_5_.refs_2_, ...), custom_call_target="tpu_custom_call" | custom-call | flops 134217728 | bytes 262144 | tf_op jit(solution)/shard_map/last_keys_values/pallas_call | solution.py:204
  11.5 2.2 %collective-permute-start.4 = (bf16[128,128]{1,0:T(8,128)(2,1)S(1)}, bf16[128,128]{1,0:T(8,128)(2,1)S(1)}, u32[]{:S(2)}, u32[]{:S(2)}) collective-permute-start(bf16[128,128]{1,0:T(8,128)(2,1)S(1)} %get-tuple-element.57), channel_id=1, source_target_pairs={{0,3},{1,2},{2,1},{3,0},{4,7},{5,6},{6,5},{7,4},{8,11},{9,10},{10,... | collective-permute-start | bytes 98312 | tf_op jit(solution)/shard_map/ppermute | solution.py:409
  13.7 0.0 copy-done.1
  13.7 0.6 %openings.1 = (s32[128,128]{1,0:T(8,128)S(1)}, s32[128,128]{1,0:T(8,128)S(1)}) custom-call(s32[9]{0:T(128)S(1)} %copy-done.1), custom_call_target="tpu_custom_call" | custom-call | tf_op jit(solution)/shard_map/openings/pallas_call | solution.py:254
  14.3 0.0 copy-start
  14.3 0.5 %last_queries.2.q_ref = bf16[128,1024]{1,0:T(8,128)(2,1)S(1)} custom-call(bf16[128,1024]{1,0:T(8,128)(2,1)S(1)} %collective-permute-done.1.refs_0_, f32[1,4096]{1,0:T(1,128)S(1)} %get-tuple-element.44.refs_3_.refs_1_.refs_5_.refs_2_, bf16[4096,1024]{1,0:T(8,128)(2,1)S(1)} %get-tuple-element.48.refs_4_.refs_2_.refs_6_.refs_3_, ...), custom_call_target="tpu_custom_call" | custom-call | flops 268435456 | bytes 262144 | tf_op jit(solution)/shard_map/last_queries/pallas_call | solution.py:229
  14.8 0.5 %collective-permute-done.4.refs_1_ = bf16[128,128]{1,0:T(8,128)(2,1)S(1)} collective-permute-done((bf16[128,128]{1,0:T(8,128)(2,1)S(1)}, bf16[128,128]{1,0:T(8,128)(2,1)S(1)}, u32[]{:S(2)}, u32[]{:S(2)}) %collective-permute-start.4) | collective-permute-done | bytes 32800 | tf_op jit(solution)/shard_map/ppermute | solution.py:409
  15.3 0.0 copy-done
  15.3 0.5 %first_attend.2 = (bf16[128,512]{1,0:T(8,128)(2,1)S(1)}, bf16[128,128]{1,0:T(8,128)(2,1)S(1)}, bf16[128,128]{1,0:T(8,128)(2,1)S(1)}) custom-call(s32[128,128]{1,0:T(8,128)S(1)} %get-tuple-element.54.opened_ref, bf16[128,1024]{1,0:T(8,128)(2,1)S(1)} %last_queries.2.q_ref, bf16[128,1024]{1,0:T(8,128)(2,1)S(1)} %get-tuple-element.47.refs_0_.x_ref, ...), custom_call_target="tpu_custom_call" | custom-call | flops 1000 | bytes 1000 | tf_op jit(solution)/shard_map/first_attend/pallas_call | solution.py:323
  15.8 1.7 %collective-permute-start.5 = (bf16[128,512]{1,0:T(8,128)(2,1)S(1)}, bf16[128,512]{1,0:T(8,128)(2,1)S(1)}, u32[]{:S(2)}, u32[]{:S(2)}) collective-permute-start(bf16[128,512]{1,0:T(8,128)(2,1)S(1)} %get-tuple-element.58), channel_id=1, source_target_pairs={{0,5},{1,4},{2,7},{3,6},{4,9},{5,8},{6,11},{7,10},{8,13},{9,12},{1... | collective-permute-start | bytes 393224 | tf_op jit(solution)/shard_map/ppermute | solution.py:409
  17.5 0.5 %first_attend.3 = bf16[128,512]{1,0:T(8,128)(2,1)S(1)} custom-call(s32[128,128]{1,0:T(8,128)S(1)} %get-tuple-element.54.opened_ref, bf16[128,1024]{1,0:T(8,128)(2,1)S(1)} %last_queries.2.q_ref, bf16[128,1024]{1,0:T(8,128)(2,1)S(1)} %get-tuple-element.47.refs_0_.x_ref, bf16[128,1024]{1,0:T(8,128)(2,1)S(1)} %copy-done, ...), custom_call_target="tpu_custom_call" | custom-call | flops 1000 | bytes 1000 | tf_op jit(solution)/shard_map/first_attend/pallas_call | solution.py:323
  18.0 2.6 %collective-permute-start.8 = (bf16[128,512]{1,0:T(8,128)(2,1)S(1)}, bf16[128,512]{1,0:T(8,128)(2,1)S(1)}, u32[]{:S(2)}, u32[]{:S(2)}) collective-permute-start(bf16[128,512]{1,0:T(8,128)(2,1)S(1)} %first_attend.3), channel_id=1, source_target_pairs={{0,7},{1,6},{2,5},{3,4},{4,11},{5,10},{6,9},{7,8},{8,15},{9,14},{1... | collective-permute-start | bytes 393224 | tf_op jit(solution)/shard_map/ppermute | solution.py:409
  20.5 1.3 %collective-permute-start.9 = (bf16[128,512]{1,0:T(8,128)(2,1)S(1)}, bf16[128,512]{1,0:T(8,128)(2,1)S(1)}, u32[]{:S(2)}, u32[]{:S(2)}) collective-permute-start(bf16[128,512]{1,0:T(8,128)(2,1)S(1)} %first_attend.3), channel_id=1, source_target_pairs={{0,5},{1,4},{2,7},{3,6},{4,9},{5,8},{6,11},{7,10},{8,13},{9,12},{1... | collective-permute-start | bytes 393224 | tf_op jit(solution)/shard_map/ppermute | solution.py:409
  21.8 2.3 %collective-permute-done.5.refs_0_ = bf16[128,512]{1,0:T(8,128)(2,1)S(1)} collective-permute-done((bf16[128,512]{1,0:T(8,128)(2,1)S(1)}, bf16[128,512]{1,0:T(8,128)(2,1)S(1)}, u32[]{:S(2)}, u32[]{:S(2)}) %collective-permute-start.5) | collective-permute-done | bytes 131104 | tf_op jit(solution)/shard_map/ppermute | solution.py:409
  24.1 2.2 %collective-permute-start.6 = (bf16[128,512]{1,0:T(8,128)(2,1)S(1)}, bf16[128,512]{1,0:T(8,128)(2,1)S(1)}, u32[]{:S(2)}, u32[]{:S(2)}) collective-permute-start(bf16[128,512]{1,0:T(8,128)(2,1)S(1)} %collective-permute-done.5.refs_0_), channel_id=1, source_target_pairs={{0,3},{1,2},{2,1},{3,0},{4,7},{5,6},{6,5},{7,4},{8,11},{9,10},{10,... | collective-permute-start | bytes 393224 | tf_op jit(solution)/shard_map/ppermute | solution.py:409
  26.3 0.4 more_blocks.4
  26.7 1.6 %collective-permute-done.8.refs_2_ = bf16[128,512]{1,0:T(8,128)(2,1)S(1)} collective-permute-done((bf16[128,512]{1,0:T(8,128)(2,1)S(1)}, bf16[128,512]{1,0:T(8,128)(2,1)S(1)}, u32[]{:S(2)}, u32[]{:S(2)}) %collective-permute-start.8) | collective-permute-done | bytes 131104 | tf_op jit(solution)/shard_map/ppermute | solution.py:409
  28.3 1.6 %collective-permute-done.9.refs_3_ = bf16[128,512]{1,0:T(8,128)(2,1)S(1)} collective-permute-done((bf16[128,512]{1,0:T(8,128)(2,1)S(1)}, bf16[128,512]{1,0:T(8,128)(2,1)S(1)}, u32[]{:S(2)}, u32[]{:S(2)}) %collective-permute-start.9) | collective-permute-done | bytes 131104 | tf_op jit(solution)/shard_map/ppermute | solution.py:409
  29.9 0.3 collective-permute-start.12
  30.1 0.2 collective-permute-start.11
  30.4 0.3 collective-permute-start.10
  30.7 0.7 %collective-permute-done.6.refs_1_ = bf16[128,512]{1,0:T(8,128)(2,1)S(1)} collective-permute-done((bf16[128,512]{1,0:T(8,128)(2,1)S(1)}, bf16[128,512]{1,0:T(8,128)(2,1)S(1)}, u32[]{:S(2)}, u32[]{:S(2)}) %collective-permute-start.6) | collective-permute-done | bytes 131104 | tf_op jit(solution)/shard_map/ppermute | solution.py:409
  31.3 0.1 collective-permute-start.7
  31.4 0.0 collective-permute-done.12.refs_4_
  31.5 0.0 collective-permute-done.11.refs_0_
  31.5 1.2 %more_blocks.5 = (f32[128,1024]{1,0:T(8,128)S(1)}, f32[128,512]{1,0:T(8,128)S(1)}, f32[128,128]{1,0:T(8,128)S(1)}) custom-call(bf16[128,512]{1,0:T(8,128)(2,1)S(1)} %collective-permute-done.11.refs_0_, bf16[128,512]{1,0:T(8,128)(2,1)S(1)} %collective-permute-done.6.refs_1_, bf16[128,512]{1,0:T(8,128)(2,1)S(1)} %collective-permute-done.8.refs_2_, ...), custom_call_target="tpu_custom_call" | custom-call | flops 1006632960 | bytes 655360 | tf_op jit(solution)/shard_map/more_blocks/pallas_call | solution.py:166
  32.7 0.0 collective-permute-done.10.refs_1_
  32.7 0.0 collective-permute-done.7.refs_0_
  32.7 0.5 %last_keys_values.3 = (f32[128,128]{1,0:T(8,128)S(1)}, bf16[128,128]{1,0:T(8,128)(2,1)S(1)}, bf16[128,128]{1,0:T(8,128)(2,1)S(1)}) custom-call(bf16[128,512]{1,0:T(8,128)(2,1)S(1)} %collective-permute-done.7.refs_0_, bf16[128,512]{1,0:T(8,128)(2,1)S(1)} %collective-permute-done.10.refs_1_, f32[1,4096]{1,0:T(1,128)S(1)} %get-tuple-element.44.refs_3_.refs_1_.refs_5_.refs_2_, ...), custom_call_target="tpu_custom_call" | custom-call | flops 134217728 | bytes 262144 | tf_op jit(solution)/shard_map/last_keys_values/pallas_call | solution.py:204
  33.2 1.6 %collective-permute-start.13 = (bf16[128,128]{1,0:T(8,128)(2,1)S(1)}, bf16[128,128]{1,0:T(8,128)(2,1)S(1)}, u32[]{:S(2)}, u32[]{:S(2)}) collective-permute-start(bf16[128,128]{1,0:T(8,128)(2,1)S(1)} %get-tuple-element.78), channel_id=1, source_target_pairs={{0,3},{1,2},{2,1},{3,0},{4,7},{5,6},{6,5},{7,4},{8,11},{9,10},{10,... | collective-permute-start | bytes 98312 | tf_op jit(solution)/shard_map/ppermute | solution.py:409
  34.9 0.4 %last_queries.3.q_ref = bf16[128,1024]{1,0:T(8,128)(2,1)S(1)} custom-call(bf16[128,512]{1,0:T(8,128)(2,1)S(1)} %collective-permute-done.7.refs_0_, bf16[128,512]{1,0:T(8,128)(2,1)S(1)} %collective-permute-done.10.refs_1_, f32[1,4096]{1,0:T(1,128)S(1)} %get-tuple-element.44.refs_3_.refs_1_.refs_5_.refs_2_, ...), custom_call_target="tpu_custom_call" | custom-call | flops 268435456 | bytes 262144 | tf_op jit(solution)/shard_map/last_queries/pallas_call | solution.py:229
  35.3 0.6 %resident_attend.1 = (f32[1024,128]{1,0:T(8,128)S(1)}, f32[1024,128]{1,0:T(8,128)S(1)}, f32[1024,128]{1,0:T(8,128)S(1)}) custom-call(s32[128,128]{1,0:T(8,128)S(1)} %get-tuple-element.53.opened_ref, bf16[128,1024]{1,0:T(8,128)(2,1)S(1)} %last_queries.3.q_ref, bf16[128,128]{1,0:T(8,128)(2,1)S(1)} %get-tuple-element.59.refs_0_.keys_ref, ...), custom_call_target="tpu_custom_call" | custom-call | flops 1000 | bytes 1000 | tf_op jit(solution)/shard_map/resident_attend/pallas_call | solution.py:348
  35.9 0.8 %collective-permute-done.13.refs_3_ = bf16[128,128]{1,0:T(8,128)(2,1)S(1)} collective-permute-done((bf16[128,128]{1,0:T(8,128)(2,1)S(1)}, bf16[128,128]{1,0:T(8,128)(2,1)S(1)}, u32[]{:S(2)}, u32[]{:S(2)}) %collective-permute-start.13) | collective-permute-done | bytes 32800 | tf_op jit(solution)/shard_map/ppermute | solution.py:409
  36.7 1.3 %second_attend.1 = bf16[128,1024]{1,0:T(8,128)(2,1)} custom-call(s32[128,128]{1,0:T(8,128)S(1)} %get-tuple-element.53.opened_ref, bf16[128,1024]{1,0:T(8,128)(2,1)S(1)} %last_queries.3.q_ref, f32[1024,128]{1,0:T(8,128)S(1)} %get-tuple-element.74.max_ref, f32[1024,128]{1,0:T(8,128)S(1)} %get-tuple-element.75.sum_ref, ...), custom_call_target="tpu_custom_call" | custom-call | flops 1000 | bytes 1000 | tf_op jit(solution)/shard_map/second_attend/pallas_call | solution.py:382
Async XLA Ops:
  0.0 9.4 %collective-permute-start = (bf16[128,1024]{1,0:T(8,128)(2,1)}, bf16[128,1024]{1,0:T(8,128)(2,1)S(1)}, u32[]{:S(2)}, u32[]{:S(2)}) collective-permute-start(bf16[128,1024]{1,0:T(8,128)(2,1)} %bitcast.7), channel_id=1, source_target_pairs={{0,3},{1,2},{2,1},{3,0},{4,7},{5,6},{6,5},{7,4},{8,11},{9,10},{10,... | collective-permute-start | bytes 786440 | tf_op jit(solution)/shard_map/ppermute | solution.py:409
  2.4 7.1 %collective-permute-start.3 = (bf16[128,1024]{1,0:T(8,128)(2,1)}, bf16[128,1024]{1,0:T(8,128)(2,1)S(1)}, u32[]{:S(2)}, u32[]{:S(2)}) collective-permute-start(bf16[128,1024]{1,0:T(8,128)(2,1)} %bitcast.8), channel_id=1, source_target_pairs={{0,1},{1,0},{2,3},{3,2},{4,5},{5,4},{6,7},{7,6},{8,9},{9,8},{10,11... | collective-permute-start | bytes 786440 | tf_op jit(solution)/shard_map/ppermute | solution.py:409
  3.1 6.4 %collective-permute-start.2 = (bf16[4096,256]{1,0:T(8,128)(2,1)}, bf16[4096,256]{1,0:T(8,128)(2,1)S(1)}, u32[]{:S(2)}, u32[]{:S(2)}) collective-permute-start(bf16[4096,256]{1,0:T(8,128)(2,1)} %bitcast.5), channel_id=1, source_target_pairs={{0,1},{1,0},{2,3},{3,2},{4,5},{5,4},{6,7},{7,6},{8,9},{9,8},{10,11... | collective-permute-start | bytes 6291464 | tf_op jit(solution)/shard_map/ppermute | solution.py:409
  9.4 1.5 %collective-permute-start.1 = (bf16[128,1024]{1,0:T(8,128)(2,1)S(1)}, bf16[128,1024]{1,0:T(8,128)(2,1)S(1)}, u32[]{:S(2)}, u32[]{:S(2)}) collective-permute-start(bf16[128,1024]{1,0:T(8,128)(2,1)S(1)} %collective-permute-done.refs_2_), channel_id=1, source_target_pairs={{0,1},{1,0},{2,3},{3,2},{4,5},{5,4},{6,7},{7,6},{8,9},{9,8},{10,11... | collective-permute-start | bytes 786440 | tf_op jit(solution)/shard_map/ppermute | solution.py:409
  10.9 2.7 %copy-start.1 = (s32[9]{0:T(128)S(1)}, s32[9]{0:T(128)}, u32[]{:S(2)}) copy-start(s32[9]{0:T(128)} %doc_ref) | copy-start | bytes 112
  11.5 3.8 %collective-permute-start.4 = (bf16[128,128]{1,0:T(8,128)(2,1)S(1)}, bf16[128,128]{1,0:T(8,128)(2,1)S(1)}, u32[]{:S(2)}, u32[]{:S(2)}) collective-permute-start(bf16[128,128]{1,0:T(8,128)(2,1)S(1)} %get-tuple-element.57), channel_id=1, source_target_pairs={{0,3},{1,2},{2,1},{3,0},{4,7},{5,6},{6,5},{7,4},{8,11},{9,10},{10,... | collective-permute-start | bytes 98312 | tf_op jit(solution)/shard_map/ppermute | solution.py:409
  14.3 1.0 %copy-start = (bf16[128,1024]{1,0:T(8,128)(2,1)S(1)}, bf16[128,1024]{1,0:T(8,128)(2,1)}, u32[]{:S(2)}) copy-start(bf16[128,1024]{1,0:T(8,128)(2,1)} %fresh_ref.3) | copy-start | bytes 786436
  15.8 8.4 %collective-permute-start.5 = (bf16[128,512]{1,0:T(8,128)(2,1)S(1)}, bf16[128,512]{1,0:T(8,128)(2,1)S(1)}, u32[]{:S(2)}, u32[]{:S(2)}) collective-permute-start(bf16[128,512]{1,0:T(8,128)(2,1)S(1)} %get-tuple-element.58), channel_id=1, source_target_pairs={{0,5},{1,4},{2,7},{3,6},{4,9},{5,8},{6,11},{7,10},{8,13},{9,12},{1... | collective-permute-start | bytes 393224 | tf_op jit(solution)/shard_map/ppermute | solution.py:409
  18.0 10.3 %collective-permute-start.8 = (bf16[128,512]{1,0:T(8,128)(2,1)S(1)}, bf16[128,512]{1,0:T(8,128)(2,1)S(1)}, u32[]{:S(2)}, u32[]{:S(2)}) collective-permute-start(bf16[128,512]{1,0:T(8,128)(2,1)S(1)} %first_attend.3), channel_id=1, source_target_pairs={{0,7},{1,6},{2,5},{3,4},{4,11},{5,10},{6,9},{7,8},{8,15},{9,14},{1... | collective-permute-start | bytes 393224 | tf_op jit(solution)/shard_map/ppermute | solution.py:409
  20.5 9.3 %collective-permute-start.9 = (bf16[128,512]{1,0:T(8,128)(2,1)S(1)}, bf16[128,512]{1,0:T(8,128)(2,1)S(1)}, u32[]{:S(2)}, u32[]{:S(2)}) collective-permute-start(bf16[128,512]{1,0:T(8,128)(2,1)S(1)} %first_attend.3), channel_id=1, source_target_pairs={{0,5},{1,4},{2,7},{3,6},{4,9},{5,8},{6,11},{7,10},{8,13},{9,12},{1... | collective-permute-start | bytes 393224 | tf_op jit(solution)/shard_map/ppermute | solution.py:409
  24.1 7.2 %collective-permute-start.6 = (bf16[128,512]{1,0:T(8,128)(2,1)S(1)}, bf16[128,512]{1,0:T(8,128)(2,1)S(1)}, u32[]{:S(2)}, u32[]{:S(2)}) collective-permute-start(bf16[128,512]{1,0:T(8,128)(2,1)S(1)} %collective-permute-done.5.refs_0_), channel_id=1, source_target_pairs={{0,3},{1,2},{2,1},{3,0},{4,7},{5,6},{6,5},{7,4},{8,11},{9,10},{10,... | collective-permute-start | bytes 393224 | tf_op jit(solution)/shard_map/ppermute | solution.py:409
  29.9 1.6 %collective-permute-start.12 = (bf16[128,512]{1,0:T(8,128)(2,1)S(1)}, bf16[128,512]{1,0:T(8,128)(2,1)S(1)}, u32[]{:S(2)}, u32[]{:S(2)}) collective-permute-start(bf16[128,512]{1,0:T(8,128)(2,1)S(1)} %collective-permute-done.8.refs_2_), channel_id=1, source_target_pairs={{0,1},{1,0},{2,3},{3,2},{4,5},{5,4},{6,7},{7,6},{8,9},{9,8},{10,11... | collective-permute-start | bytes 393224 | tf_op jit(solution)/shard_map/ppermute | solution.py:409
  30.1 1.3 %collective-permute-start.11 = (bf16[128,512]{1,0:T(8,128)(2,1)S(1)}, bf16[128,512]{1,0:T(8,128)(2,1)S(1)}, u32[]{:S(2)}, u32[]{:S(2)}) collective-permute-start(bf16[128,512]{1,0:T(8,128)(2,1)S(1)} %collective-permute-done.5.refs_0_), channel_id=1, source_target_pairs={{0,1},{1,0},{2,3},{3,2},{4,5},{5,4},{6,7},{7,6},{8,9},{9,8},{10,11... | collective-permute-start | bytes 393224 | tf_op jit(solution)/shard_map/ppermute | solution.py:409
  30.4 2.3 %collective-permute-start.10 = (bf16[128,512]{1,0:T(8,128)(2,1)S(1)}, bf16[128,512]{1,0:T(8,128)(2,1)S(1)}, u32[]{:S(2)}, u32[]{:S(2)}) collective-permute-start(bf16[128,512]{1,0:T(8,128)(2,1)S(1)} %collective-permute-done.9.refs_3_), channel_id=1, source_target_pairs={{0,1},{1,0},{2,3},{3,2},{4,5},{5,4},{6,7},{7,6},{8,9},{9,8},{10,11... | collective-permute-start | bytes 393224 | tf_op jit(solution)/shard_map/ppermute | solution.py:409
  31.3 1.4 %collective-permute-start.7 = (bf16[128,512]{1,0:T(8,128)(2,1)S(1)}, bf16[128,512]{1,0:T(8,128)(2,1)S(1)}, u32[]{:S(2)}, u32[]{:S(2)}) collective-permute-start(bf16[128,512]{1,0:T(8,128)(2,1)S(1)} %collective-permute-done.6.refs_1_), channel_id=1, source_target_pairs={{0,1},{1,0},{2,3},{3,2},{4,5},{5,4},{6,7},{7,6},{8,9},{9,8},{10,11... | collective-permute-start | bytes 393224 | tf_op jit(solution)/shard_map/ppermute | solution.py:409
  33.2 3.4 %collective-permute-start.13 = (bf16[128,128]{1,0:T(8,128)(2,1)S(1)}, bf16[128,128]{1,0:T(8,128)(2,1)S(1)}, u32[]{:S(2)}, u32[]{:S(2)}) collective-permute-start(bf16[128,128]{1,0:T(8,128)(2,1)S(1)} %get-tuple-element.78), channel_id=1, source_target_pairs={{0,3},{1,2},{2,1},{3,0},{4,7},{5,6},{6,5},{7,4},{8,11},{9,10},{10,... | collective-permute-start | bytes 98312 | tf_op jit(solution)/shard_map/ppermute | solution.py:409

commit v7 on v6

--- a/solution.py
+++ b/solution.py
@@ -49,9 +49,22 @@
     return lax.dot_general(a, b, (((1,), (1,)), ((), ())), preferred_element_type=f32)
 
 
-def gained(x, gain_ref, start):
-    width = x.shape[1]
-    wide = x.astype(f32)
+def picked(x_ref, fresh_ref, offset, first):
+    wide = x_ref[...].astype(f32)
+    if fresh_ref is None:
+        return wide
+    return jnp.where(first, fresh_ref[:, offset : offset + wide.shape[1]].astype(f32), wide)
+
+
+def blocks_of(refs, count, offsets):
+    xs, rest = refs[:count], refs[count:]
+    if offsets is None:
+        return [(x, None, 0) for x in xs], rest
+    return list(zip(xs, rest[:count], offsets)), rest[count:]
+
+
+def gained(wide, gain_ref, start):
+    width = wide.shape[1]
     squares = wide * wide
     ssq = squares[:, :HD]
     for c in range(HD, width, HD):
@@ -99,7 +112,7 @@
     choose_rows(choose_ref, me, n, flips, parts)
     for copy in small:
         copy.wait()
-    normed, _ = gained(x_ref[...], gain_ref, me * width)
+    normed, _ = gained(x_ref[...].astype(f32), gain_ref, me * width)
     part(0).wait()
     accq_ref[...] = dot(normed, wq_ref[rows_of(me, width), :])
     for step in range(1, n):
@@ -130,8 +143,9 @@
     )(*operands)
 
 
-def blocks_kernel(count, wkv_count, carried, places, with_q, *refs):
-    xs, refs = refs[:count], refs[count:]
+def blocks_kernel(count, wkv_count, carried, places, offsets, with_q, *refs):
+    blocks, refs = blocks_of(refs, count, offsets)
+    first = lax.axis_index("section") == 0
     gain_ref, wq_ref = refs[:2]
     wkv_refs, refs = refs[2 : 2 + wkv_count], refs[2 + wkv_count :]
     old, outs = refs[:carried], refs[carried:]
@@ -144,9 +158,9 @@
     def add(total, term):
         return term if total is None else total + term
 
-    for i, x_ref in enumerate(xs):
-        start, width = places[i](me), x_ref.shape[1]
-        normed, squares = gained(x_ref[...], gain_ref, start)
+    for i, block in enumerate(blocks):
+        start, width = places[i](me), block[0].shape[1]
+        normed, squares = gained(picked(*block, first), gain_ref, start)
         ssq = add(ssq, squares)
         rows = from_start(start, width)
         kvs = [add(kv, dot(normed, w_ref[rows, :])) for kv, w_ref in zip(kvs, wkv_refs)]
@@ -158,14 +172,14 @@
     outs[2][...] = ssq
 
 
-def more_blocks(xs, places, gain, wq, wkvs, state, with_q=None):
+def more_blocks(xs, places, gain, wq, wkvs, state, with_q=None, fresh=(), offsets=None):
     tokens = xs[0].shape[0]
-    operands = [*xs, *resident_in(gain, wq, *wkvs), *state]
+    operands = [*xs, *fresh, *resident_in(gain, wq, *wkvs), *state]
     columns = len(wkvs) * wkvs[0].shape[1]
     shapes = ((tokens, wq.shape[1]), (tokens, columns), (tokens, HD))
     return pl.pallas_call(
         functools.partial(
-            blocks_kernel, len(xs), len(wkvs), len(state), places, with_q or [True] * len(xs)
+            blocks_kernel, len(xs), len(wkvs), len(state), places, offsets, with_q or [True] * len(xs)
         ),
         out_shape=tuple(VMEM(s, f32) for s in shapes),
         in_specs=[vmem] * len(operands),
@@ -176,17 +190,18 @@
     )(*operands)
 
 
-def last_kv_kernel(count, wkv_count, places, *refs):
-    xs, refs = refs[:count], refs[count:]
+def last_kv_kernel(count, wkv_count, places, offsets, *refs):
+    blocks, refs = blocks_of(refs, count, offsets)
+    first = lax.axis_index("section") == 0
     gain_ref, wkv_refs, refs = refs[0], refs[1 : 1 + wkv_count], refs[1 + wkv_count :]
     choose_ref, acckv_ref, ssq_ref, scale_ref, *pieces = refs
     me = lax.axis_index("head")
     columns = wkv_refs[0].shape[1]
     kvs = [acckv_ref[:, c * columns : (c + 1) * columns] for c in range(wkv_count)]
     ssq = ssq_ref[...]
-    for i, x_ref in enumerate(xs):
-        start, width = places[i](me), x_ref.shape[1]
-        normed, squares = gained(x_ref[...], gain_ref, start)
+    for i, block in enumerate(blocks):
+        start, width = places[i](me), block[0].shape[1]
+        normed, squares = gained(picked(*block, first), gain_ref, start)
         ssq = ssq + squares
         kvs = [kv + dot(normed, w_ref[from_start(start, width), :]) for kv, w_ref in zip(kvs, wkv_refs)]
     scale = lax.rsqrt(jnp.sum(ssq, axis=1, keepdims=True) / gain_ref.shape[1] + epsilon)
@@ -196,13 +211,13 @@
         piece[...] = dot_turned(choose_ref[i].astype(bf16), kv).astype(bf16)
 
 
-def last_kv(xs, places, gain, wkvs, choose, acckv, ssq):
+def last_kv(xs, places, gain, wkvs, choose, acckv, ssq, fresh=(), offsets=None):
     tokens = xs[0].shape[0]
     columns = len(wkvs) * wkvs[0].shape[1]
-    operands = [*xs, *resident_in(gain, *wkvs, choose), acckv, ssq]
+    operands = [*xs, *fresh, *resident_in(gain, *wkvs, choose), acckv, ssq]
     count = choose.shape[0]
     return pl.pallas_call(
-        functools.partial(last_kv_kernel, len(xs), len(wkvs), places),
+        functools.partial(last_kv_kernel, len(xs), len(wkvs), places, offsets),
         out_shape=(VMEM((tokens, HD), f32),) + (VMEM((columns // KVH, tokens), bf16),) * count,
         in_specs=[vmem] * len(operands),
         out_specs=(vmem,) * (1 + count),
@@ -212,22 +227,23 @@
     )(*operands)
 
 
-def last_q_kernel(count, places, *refs):
-    xs, rest = refs[:count], refs[count:]
+def last_q_kernel(count, places, offsets, *refs):
+    blocks, rest = blocks_of(refs, count, offsets)
+    first = lax.axis_index("section") == 0
     gain_ref, wq_ref, accq_ref, scale_ref, q_ref = rest
     me = lax.axis_index("head")
     total = accq_ref[...]
-    for i, x_ref in enumerate(xs):
-        start, width = places[i](me), x_ref.shape[1]
-        normed, _ = gained(x_ref[...], gain_ref, start)
+    for i, block in enumerate(blocks):
+        start, width = places[i](me), block[0].shape[1]
+        normed, _ = gained(picked(*block, first), gain_ref, start)
         total = total + dot(normed, wq_ref[from_start(start, width), :])
     q_ref[...] = (total * scale_ref[:, 0:1]).astype(bf16)
 
 
-def last_q(xs, places, gain, wq, accq, scale):
-    operands = [*xs, *resident_in(gain, wq), accq, scale]
-    return pl.pallas_call(
-        functools.partial(last_q_kernel, len(xs), places),
+def last_q(xs, places, gain, wq, accq, scale, fresh=(), offsets=None):
+    operands = [*xs, *fresh, *resident_in(gain, wq), accq, scale]
+    return pl.pallas_call(
+        functools.partial(last_q_kernel, len(xs), places, offsets),
         out_shape=VMEM((xs[0].shape[0], wq.shape[1]), bf16),
         in_specs=[vmem] * len(operands),
         out_specs=vmem,
@@ -290,9 +306,8 @@
     return gather[0].astype(bf16), gather[1].astype(bf16)
 
 
-def first_attend_kernel(sections, heads, flips, parts, opened_ref, q_ref, x_ref, fresh_ref, *refs):
-    section = lax.axis_index("section")
-    start = (sections - 1 - section) * q_ref.shape[0]
+def first_attend_kernel(sections, heads, flips, parts, opened_ref, q_ref, x_ref, *refs):
+    start = (sections - 1 - lax.axis_index("section")) * q_ref.shape[0]
     if flips is None:
         keys_ref, values_ref, out_ref = refs
         keys, values = keys_ref[...], values_ref[...]
@@ -307,26 +322,25 @@
     mixed = (mixed * (1.0 / total)).astype(bf16).astype(f32)
     for i, h in enumerate(range(*heads)):
         columns = slice(h * HD, (h + 1) * HD)
-        out = (x_ref[:, columns].astype(f32) + mixed[i * tokens : (i + 1) * tokens]).astype(bf16)
-        out = jnp.where(section == sections - 1, fresh_ref[:, columns].astype(f32), out.astype(f32))
+        out = x_ref[:, columns].astype(f32) + mixed[i * tokens : (i + 1) * tokens]
         out_ref[:, i * HD : (i + 1) * HD] = out.astype(bf16)
 
 
-def first_attend(opened, q, x, fresh, pieces, flips, parts, heads, sections):
+def first_attend(opened, q, x, pieces, flips, parts, heads, sections):
     tokens = q.shape[0]
     out = (VMEM((tokens, (heads[1] - heads[0]) * HD), bf16),)
     scratch = []
     if flips is not None:
         out = out + (VMEM((HD, tokens), bf16),) * 2
         scratch = [VMEM((2, HD, tokens), f32)]
-    operands = [opened, q, x, fresh, *pieces]
+    operands = [opened, q, x, *pieces]
     return pl.pallas_call(
         functools.partial(first_attend_kernel, sections, heads, flips, parts),
         out_shape=out,
         in_specs=[vmem] * len(operands),
         out_specs=(vmem,) * len(out),
         scratch_shapes=scratch,
-        cost_estimate=cost(1000, 1000),
+        cost_estimate=cost(10**10, 1000),
         compiler_params=params,
         name="first_attend",
     )(*operands)
@@ -350,14 +364,18 @@
         out_shape=(VMEM((rows, HD), f32),) * 3,
         in_specs=[vmem] * 4,
         out_specs=(vmem,) * 3,
-        cost_estimate=cost(1000, 1000),
+        cost_estimate=cost(10**10, 1000),
         compiler_params=params,
         name="resident_attend",
     )(opened, q, keys, values)
 
 
-def second_attend_kernel(sections, flips, parts, x_count, opened_ref, q_ref, max_ref, sum_ref, mixed_ref, *refs):
+def second_attend_kernel(
+    sections, flips, parts, x_count, with_fresh, opened_ref, q_ref, max_ref, sum_ref, mixed_ref, *refs
+):
     x_refs, refs = refs[:x_count], refs[x_count:]
+    fresh_ref, refs = (refs[0], refs[1:]) if with_fresh else (None, refs)
+    first = lax.axis_index("section") == 0
     pieces, (out_ref, gather) = refs[: len(flips)], refs[len(flips) :]
     tokens, heads = q_ref.shape[0], q_ref.shape[1] // HD
     start = (sections - lax.axis_index("section")) * tokens
@@ -372,20 +390,21 @@
     mixed = (mixed * (1.0 / total)).astype(bf16).astype(f32)
     where = [(x_ref, inside) for x_ref in x_refs for inside in range(0, x_ref.shape[1], HD)]
     for h, (x_ref, inside) in enumerate(where):
-        out = x_ref[:, inside : inside + HD].astype(f32) + mixed[h * tokens : (h + 1) * tokens]
+        x = picked(x_ref.at[:, inside : inside + HD], fresh_ref, h * HD, first)
+        out = x + mixed[h * tokens : (h + 1) * tokens]
         out_ref[:, h * HD : (h + 1) * HD] = out.astype(bf16)
 
 
-def second_attend(opened, q, xs, resident, pieces, flips, parts, sections):
+def second_attend(opened, q, xs, fresh, resident, pieces, flips, parts, sections):
     tokens = q.shape[0]
-    operands = [opened, q, *resident, *xs, *pieces]
-    return pl.pallas_call(
-        functools.partial(second_attend_kernel, sections, flips, parts, len(xs)),
+    operands = [opened, q, *resident, *xs, *fresh, *pieces]
+    return pl.pallas_call(
+        functools.partial(second_attend_kernel, sections, flips, parts, len(xs), len(fresh) == 1),
         out_shape=jax.ShapeDtypeStruct(q.shape, bf16),
         in_specs=[vmem] * len(operands),
         out_specs=vmem,
         scratch_shapes=[VMEM((2, HD, tokens), f32)],
-        cost_estimate=cost(1000, 1000),
+        cost_estimate=cost(10**10, 1000),
         compiler_params=params,
         name="second_attend",
     )(*operands)
@@ -402,17 +421,19 @@
     parts = 2 if paired else 1
     flips = [0, 3] if paired else list(range(n))
 
-    def moved(array, by, flip):
+    def moved(array, by, flip, among=None):
         pairs = [
-            (s * n + h, ((s + by) % sections) * n + (h ^ flip)) for s in range(sections) for h in range(n)
+            (s * n + h, (s + by) * n + (h ^ flip))
+            for s in among or range(sections - by)
+            for h in range(n)
         ]
         return lax.ppermute(array, ("section", "head"), pairs)
 
     def after(array, *others):
         return lax.optimization_barrier((array, *others))[0]
 
-    def exchanged(xs, places, state):
-        scale, *pieces = last_kv(xs, places, gain, wkvs, choose, state[1], state[2])
+    def exchanged(xs, places, state, *fresh):
+        scale, *pieces = last_kv(xs, places, gain, wkvs, choose, state[1], state[2], *fresh)
         received = [moved(piece, 0, flip) for piece, flip in zip(pieces[1:], flips[1:])]
         return scale, [pieces[0], *received]
 
@@ -431,9 +452,10 @@
         beside = moved(own, 0, 1)
         w_kv_beside = moved(w_kv, 0, 1)
     accq, own, gain, wq, wkv, choose = load(own, norm_gain, w_q, w_kv, n, flips, parts)
+    opened = openings(after(doc_lengths, accq), tokens, sections)
     if paired:
         wkvs = [wkv, w_kv_beside]
-        over = after(over, accq)
+        over, *opened = lax.optimization_barrier((over, *opened))
         passed = moved(over, 0, 1)
         xs, places, with_q = [own, beside, over], [place(0), place(1), place(3)], [False, True, True]
         state = more_blocks(xs, places, gain, wq, wkvs, [accq], with_q)
@@ -443,41 +465,48 @@
         state = more_blocks([own], following[:1], gain, wq, wkvs, [accq], [False])
         last, places = rest_of(own), following[1:]
     scale, pieces = exchanged(last, places, state)
-    opened = openings(after(doc_lengths, scale), tokens, sections)
     q = last_q(last, places, gain, wq, state[0], scale)
     part = heads // 2 if paired else heads
     split = part * HD
-    sent, keys, values = first_attend(
-        opened[0], q, own, fresh_slice, pieces, flips, parts, (0, part), sections
-    )
+    sent, keys, values = first_attend(opened[0], q, own, pieces, flips, parts, (0, part), sections)
 
     if paired:
+        rest, start = range(1, sections), range(1)
+        f0 = fresh_slice
+        f3 = moved(after(f0, scale), 0, 3, start)
         a1 = moved(sent, 1, 1)
         (sent,) = first_attend(
-            opened[0], q, own, fresh_slice, [keys, values], None, parts, (part, heads), sections
+            opened[0], q, own, [keys, values], None, parts, (part, heads), sections
         )
+        f1 = moved(after(f0, scale), 0, 1, start)
         b1 = moved(sent, 1, 1)
         b3 = moved(sent, 1, 3)
         a1 = after(a1, sent)
-        a2 = moved(a1, 0, 3)
-        a0 = moved(a1, 0, 1)
-        state = more_blocks([a1], [place(1)], gain, wq, wkvs, [])
+        a2 = moved(a1, 0, 3, rest)
+        a0 = moved(a1, 0, 1, rest)
+        state = more_blocks([a1], [place(1)], gain, wq, wkvs, [], None, [f1], [0])
+        f3 = after(f3, sent)
+        f2 = moved(f3, 0, 1, start)
         b3, b1, *state = lax.optimization_barrier((b3, b1, *state))
-        b2 = moved(b3, 0, 1)
-        b0 = moved(b1, 0, 1)
-        a3 = moved(a2, 0, 1)
+        b2 = moved(b3, 0, 1, rest)
+        b0 = moved(b1, 0, 1, rest)
+        a3 = moved(a2, 0, 1, rest)
         places = [place(0), place(2), *(place(flip, split) for flip in (3, 1, 2))]
-        state = more_blocks([a0, a2, b3, b1, b2], places, gain, wq, wkvs, state)
+        state = more_blocks(
+            [a0, a2, b3, b1, b2], places, gain, wq, wkvs, state, None,
+            [f0, f2, f3, f1, f2], [0, 0, split, split, split],
+        )
         last, places = [a3, b0], [place(3), place(0, split)]
-        mine = [a0, b0]
+        mine, fresh, own_fresh = [a0, b0], ([f3, f0], [0, split]), [f0]
     else:
-        mine = [moved(sent, 1, 0)]
+        mine = [jnp.where(lax.axis_index("section") == 0, fresh_slice, moved(sent, 1, 0))]
         state = more_blocks(mine, following[:1], gain, wq, wkvs, [])
         last, places = rest_of(mine[0]), following[1:]
-    scale, pieces = exchanged(last, places, state)
-    q = last_q(last, places, gain, wq, state[0], scale)
+        fresh, own_fresh = (), []
+    scale, pieces = exchanged(last, places, state, *fresh)
+    q = last_q(last, places, gain, wq, state[0], scale, *fresh)
     resident = resident_attend(opened[1], q, keys, values, sections)
-    return second_attend(opened[1], q, mine, resident, pieces, flips, parts, sections)[None]
+    return second_attend(opened[1], q, mine, own_fresh, resident, pieces, flips, parts, sections)[None]
 
 
 def solution(mesh):

time: 38.1 us -> 45.4 us (1.19)
  the two profiles are of different devices: /device:TPU:0 before, /device:TPU:15 now
where the time goes in v7:
time: 45.4 us; the launch traced here: 45.1 us
  starting transfers between devices  26.4 us (58%)
  Pallas kernels  12.4 us (27%)
  waiting for transfers between devices  5.94 us (13%)
    ppermute x17, starting transfers between devices, moved(): return lax.ppermute(array, ('section', 'head'), pairs)  26.4 us
    ppermute x17, waiting for transfers between devices, moved(): return lax.ppermute(array, ('section', 'head'), pairs)  5.94 us
    pallas_call x1, Pallas kernels, load(): pl.pallas_call(functools.partial(load_kernel, n, flips, parts), out_shape...  4.24 us
    pallas_call x3, Pallas kernels, more_blocks(): pl.pallas_call(functools.partial(blocks_kernel, len(xs), len(wkvs), len(s...  2.75 us
    pallas_call x1, Pallas kernels, second_attend(): pl.pallas_call(functools.partial(second_attend_kernel, sections, flips, p...  1.34 us
    pallas_call x2, Pallas kernels, last_kv(): pl.pallas_call(functools.partial(last_kv_kernel, len(xs), len(wkvs), plac...  1.02 us
    pallas_call x2, Pallas kernels, first_attend(): pl.pallas_call(functools.partial(first_attend_kernel, sections, heads, fl...  0.96 us
    pallas_call x2, Pallas kernels, last_q(): pl.pallas_call(functools.partial(last_q_kernel, len(xs), places, offsets)...  0.92 us
  transfers between devices with their start and end apart: 17, of which 3 were waited for; matrix products, arithmetic and copies ran while one was open for 0% of the time, Pallas kernels for 22%

profile of v7, /device:TPU:15, one launch (start us, length us, event | category | flops | bytes accessed | tf_op | source)
XLA Modules:
  0.0 45.1 jit_solution(3032183041313582147)
XLA Ops:
  0.0 0.8 %collective-permute-start = (bf16[128,1024]{1,0:T(8,128)(2,1)}, bf16[128,1024]{1,0:T(8,128)(2,1)S(1)}, u32[]{:S(2)}, u32[]{:S(2)}) collective-permute-start(bf16[128,1024]{1,0:T(8,128)(2,1)} %bitcast.7), channel_id=1, source_target_pairs={{0,3},{1,2},{2,1},{3,0},{4,7},{5,6},{6,5},{7,4},{8,11},{9,10},{10,... | collective-permute-start | bytes 786440 | tf_op jit(solution)/shard_map/ppermute | solution.py:430
  0.8 0.0 collective-permute-start.2
  0.8 0.5 %collective-permute-start.3 = (bf16[4096,256]{1,0:T(8,128)(2,1)}, bf16[4096,256]{1,0:T(8,128)(2,1)S(1)}, u32[]{:S(2)}, u32[]{:S(2)}) collective-permute-start(bf16[4096,256]{1,0:T(8,128)(2,1)} %bitcast.5), channel_id=1, source_target_pairs={{0,1},{1,0},{2,3},{3,2},{4,5},{5,4},{6,7},{7,6},{8,9},{9,8},{10,11... | collective-permute-start | bytes 6291464 | tf_op jit(solution)/shard_map/ppermute | solution.py:430
  1.3 0.0 copy-start.1
  1.3 4.2 %load_and_own_queries.1 = (f32[128,1024]{1,0:T(8,128)S(1)}, bf16[128,1024]{1,0:T(8,128)(2,1)S(1)}, f32[1,4096]{1,0:T(1,128)S(1)}, bf16[4096,1024]{1,0:T(8,128)(2...) custom-call(bf16[128,1024]{1,0:T(8,128)(2,1)} %bitcast.9, f32[1,4096]{1,0:T(1,128)} %gain_hbm.1, ...), custom_call_target="tpu_custom_call" | custom-call | flops 99999997952 | bytes 1000000000 | tf_op jit(solution)/shard_map/load_and_own_queries/pallas_call | solution.py:127
  5.5 0.0 copy-done.1
  5.6 0.6 %openings.1 = (s32[128,128]{1,0:T(8,128)S(1)}, s32[128,128]{1,0:T(8,128)S(1)}) custom-call(s32[9]{0:T(128)S(1)} %copy-done.1), custom_call_target="tpu_custom_call" | custom-call | tf_op jit(solution)/shard_map/openings/pallas_call | solution.py:270
  6.2 2.9 %collective-permute-done.refs_2_ = bf16[128,1024]{1,0:T(8,128)(2,1)S(1)} collective-permute-done((bf16[128,1024]{1,0:T(8,128)(2,1)}, bf16[128,1024]{1,0:T(8,128)(2,1)S(1)}, u32[]{:S(2)}, u32[]{:S(2)}) %collective-permute-start) | collective-permute-done | bytes 262176 | tf_op jit(solution)/shard_map/ppermute | solution.py:430
  9.1 0.4 collective-permute-start.1
  9.5 0.0 collective-permute-done.2.refs_1_
  9.5 0.0 collective-permute-done.3.refs_6_.refs_3_.refs_5_.refs_13_
  9.5 1.1 %more_blocks.3 = (f32[128,1024]{1,0:T(8,128)S(1)}, f32[128,512]{1,0:T(8,128)S(1)}, f32[128,128]{1,0:T(8,128)S(1)}) custom-call(bf16[128,1024]{1,0:T(8,128)(2,1)S(1)} %get-tuple-element.55.refs_0_.x_ref, bf16[128,1024]{1,0:T(8,128)(2,1)S(1)} %collective-permute-done.2.refs_1_, bf16[128,1024]{1,0:T(8,128)(2,1)S(1)} %collective-permute-done.refs_2_, ...), custom_call_target="tpu_custom_call" | custom-call | flops 1207959552 | bytes 786432 | tf_op jit(solution)/shard_map/more_blocks/pallas_call | solution.py:180
  10.6 0.0 collective-permute-done.1.refs_0_
  10.7 0.0 copy-start
  10.7 0.5 %last_keys_values.2 = (f32[128,128]{1,0:T(8,128)S(1)}, bf16[128,128]{1,0:T(8,128)(2,1)S(1)}, bf16[128,128]{1,0:T(8,128)(2,1)S(1)}) custom-call(bf16[128,1024]{1,0:T(8,128)(2,1)S(1)} %collective-permute-done.1.refs_0_, f32[1,4096]{1,0:T(1,128)S(1)} %get-tuple-element.53.refs_3_.refs_1_.refs_2_.refs_10_.refs_4_, ...), custom_call_target="tpu_custom_call" | custom-call | flops 134217728 | bytes 262144 | tf_op jit(solution)/shard_map/last_keys_values/pallas_call | solution.py:219
  11.2 0.5 %collective-permute-start.4 = (bf16[128,128]{1,0:T(8,128)(2,1)S(1)}, bf16[128,128]{1,0:T(8,128)(2,1)S(1)}, u32[]{:S(2)}, u32[]{:S(2)}) collective-permute-start(bf16[128,128]{1,0:T(8,128)(2,1)S(1)} %get-tuple-element.63), channel_id=1, source_target_pairs={{0,3},{1,2},{2,1},{3,0},{4,7},{5,6},{6,5},{7,4},{8,11},{9,10},{10,... | collective-permute-start | bytes 98312 | tf_op jit(solution)/shard_map/ppermute | solution.py:430
  11.7 0.0 copy-done
  11.7 0.7 %collective-permute-start.12 = (bf16[128,1024]{1,0:T(8,128)(2,1)S(1)}, bf16[128,1024]{1,0:T(8,128)(2,1)S(1)}, u32[]{:S(2)}, u32[]{:S(2)}) collective-permute-start(bf16[128,1024]{1,0:T(8,128)(2,1)S(1)} %copy-done), channel_id=1, source_target_pairs={{0,3},{1,2},{2,1},{3,0}} | collective-permute-start | bytes 786440 | tf_op jit(solution)/shard_map/ppermute | solution.py:430
  12.3 0.7 %collective-permute-start.10 = (bf16[128,1024]{1,0:T(8,128)(2,1)S(1)}, bf16[128,1024]{1,0:T(8,128)(2,1)S(1)}, u32[]{:S(2)}, u32[]{:S(2)}) collective-permute-start(bf16[128,1024]{1,0:T(8,128)(2,1)S(1)} %copy-done), channel_id=1, source_target_pairs={{0,1},{1,0},{2,3},{3,2}} | collective-permute-start | bytes 786440 | tf_op jit(solution)/shard_map/ppermute | solution.py:430
  13.0 0.5 %last_queries.2.q_ref = bf16[128,1024]{1,0:T(8,128)(2,1)S(1)} custom-call(bf16[128,1024]{1,0:T(8,128)(2,1)S(1)} %collective-permute-done.1.refs_0_, f32[1,4096]{1,0:T(1,128)S(1)} %get-tuple-element.53.refs_3_.refs_1_.refs_2_.refs_10_.refs_4_, bf16[4096,1024]{1,0:T(8,128)(2,1)S(1)} %get-tuple-element.54.refs_4_.refs_2_.refs_3_.refs_11_.refs_5_, ...), custom_call_target="tpu_custom_call" | custom-call | flops 268435456 | bytes 262144 | tf_op jit(solution)/shard_map/last_queries/pallas_call | solution.py:245
  13.5 1.1 %collective-permute-done.4.refs_1_ = bf16[128,128]{1,0:T(8,128)(2,1)S(1)} collective-permute-done((bf16[128,128]{1,0:T(8,128)(2,1)S(1)}, bf16[128,128]{1,0:T(8,128)(2,1)S(1)}, u32[]{:S(2)}, u32[]{:S(2)}) %collective-permute-start.4) | collective-permute-done | bytes 32800 | tf_op jit(solution)/shard_map/ppermute | solution.py:430
  14.6 0.5 %first_attend.2 = (bf16[128,512]{1,0:T(8,128)(2,1)S(1)}, bf16[128,128]{1,0:T(8,128)(2,1)S(1)}, bf16[128,128]{1,0:T(8,128)(2,1)S(1)}) custom-call(s32[128,128]{1,0:T(8,128)S(1)} %get-tuple-element.51.opened_ref, bf16[128,1024]{1,0:T(8,128)(2,1)S(1)} %last_queries.2.q_ref, bf16[128,1024]{1,0:T(8,128)(2,1)S(1)} %get-tuple-element.55.refs_0_.x_ref, ...), custom_call_target="tpu_custom_call" | custom-call | flops 10000000000 | bytes 1000 | tf_op jit(solution)/shard_map/first_attend/pallas_call | solution.py:337
  15.1 3.4 %collective-permute-start.5 = (bf16[128,512]{1,0:T(8,128)(2,1)S(1)}, bf16[128,512]{1,0:T(8,128)(2,1)S(1)}, u32[]{:S(2)}, u32[]{:S(2)}) collective-permute-start(bf16[128,512]{1,0:T(8,128)(2,1)S(1)} %get-tuple-element.64), channel_id=1, source_target_pairs={{0,5},{1,4},{2,7},{3,6},{4,9},{5,8},{6,11},{7,10},{8,13},{9,12},{1... | collective-permute-start | bytes 393224 | tf_op jit(solution)/shard_map/ppermute | solution.py:430
  18.5 0.5 %first_attend.3 = bf16[128,512]{1,0:T(8,128)(2,1)S(1)} custom-call(s32[128,128]{1,0:T(8,128)S(1)} %get-tuple-element.51.opened_ref, bf16[128,1024]{1,0:T(8,128)(2,1)S(1)} %last_queries.2.q_ref, bf16[128,1024]{1,0:T(8,128)(2,1)S(1)} %get-tuple-element.55.refs_0_.x_ref, bf16[128,128]{1,0:T(8,128)(2,1)S(1)} %get-tuple-element.65.refs_0_.keys_ref, ...), custom_call_target="tpu_custom_call" | custom-call | flops 10000000000 | bytes 1000 | tf_op jit(solution)/shard_map/first_attend/pallas_call | solution.py:337
  19.0 3.1 %collective-permute-start.8 = (bf16[128,512]{1,0:T(8,128)(2,1)S(1)}, bf16[128,512]{1,0:T(8,128)(2,1)S(1)}, u32[]{:S(2)}, u32[]{:S(2)}) collective-permute-start(bf16[128,512]{1,0:T(8,128)(2,1)S(1)} %first_attend.3), channel_id=1, source_target_pairs={{0,7},{1,6},{2,5},{3,4},{4,11},{5,10},{6,9},{7,8},{8,15},{9,14},{1... | collective-permute-start | bytes 393224 | tf_op jit(solution)/shard_map/ppermute | solution.py:430
  22.1 3.4 %collective-permute-start.9 = (bf16[128,512]{1,0:T(8,128)(2,1)S(1)}, bf16[128,512]{1,0:T(8,128)(2,1)S(1)}, u32[]{:S(2)}, u32[]{:S(2)}) collective-permute-start(bf16[128,512]{1,0:T(8,128)(2,1)S(1)} %first_attend.3), channel_id=1, source_target_pairs={{0,5},{1,4},{2,7},{3,6},{4,9},{5,8},{6,11},{7,10},{8,13},{9,12},{1... | collective-permute-start | bytes 393224 | tf_op jit(solution)/shard_map/ppermute | solution.py:430
  25.5 0.0 collective-permute-done.12.refs_7_.refs_2_
  25.5 0.7 %collective-permute-start.15 = (bf16[128,1024]{1,0:T(8,128)(2,1)S(1)}, bf16[128,1024]{1,0:T(8,128)(2,1)S(1)}, u32[]{:S(2)}, u32[]{:S(2)}) collective-permute-start(bf16[128,1024]{1,0:T(8,128)(2,1)S(1)} %collective-permute-done.12.refs_7_.refs_2_), channel_id=1, source_target_pairs={{0,1},{1,0},{2,3},{3,2}} | collective-permute-start | bytes 786440 | tf_op jit(solution)/shard_map/ppermute | solution.py:430
  26.2 0.0 collective-permute-done.5.refs_0_
  26.2 3.3 %collective-permute-start.6 = (bf16[128,512]{1,0:T(8,128)(2,1)S(1)}, bf16[128,512]{1,0:T(8,128)(2,1)S(1)}, u32[]{:S(2)}, u32[]{:S(2)}) collective-permute-start(bf16[128,512]{1,0:T(8,128)(2,1)S(1)} %collective-permute-done.5.refs_0_), channel_id=1, source_target_pairs={{4,7},{5,6},{6,5},{7,4},{8,11},{9,10},{10,9},{11,8},{12,15},{13,14... | collective-permute-start | bytes 393224 | tf_op jit(solution)/shard_map/ppermute | solution.py:430
  29.4 0.0 collective-permute-done.10.refs_1_.refs_8_
  29.5 2.3 %collective-permute-start.13 = (bf16[128,512]{1,0:T(8,128)(2,1)S(1)}, bf16[128,512]{1,0:T(8,128)(2,1)S(1)}, u32[]{:S(2)}, u32[]{:S(2)}) collective-permute-start(bf16[128,512]{1,0:T(8,128)(2,1)S(1)} %collective-permute-done.5.refs_0_), channel_id=1, source_target_pairs={{4,5},{5,4},{6,7},{7,6},{8,9},{9,8},{10,11},{11,10},{12,13},{13,12... | collective-permute-start | bytes 393224 | tf_op jit(solution)/shard_map/ppermute | solution.py:430
  31.7 0.4 more_blocks.4
  32.1 0.0 collective-permute-done.8.refs_2_
  32.1 0.0 collective-permute-done.9.refs_3_
  32.1 2.1 %collective-permute-start.14 = (bf16[128,512]{1,0:T(8,128)(2,1)S(1)}, bf16[128,512]{1,0:T(8,128)(2,1)S(1)}, u32[]{:S(2)}, u32[]{:S(2)}) collective-permute-start(bf16[128,512]{1,0:T(8,128)(2,1)S(1)} %collective-permute-done.8.refs_2_), channel_id=1, source_target_pairs={{4,5},{5,4},{6,7},{7,6},{8,9},{9,8},{10,11},{11,10},{12,13},{13,12... | collective-permute-start | bytes 393224 | tf_op jit(solution)/shard_map/ppermute | solution.py:430
  34.2 2.2 %collective-permute-start.11 = (bf16[128,512]{1,0:T(8,128)(2,1)S(1)}, bf16[128,512]{1,0:T(8,128)(2,1)S(1)}, u32[]{:S(2)}, u32[]{:S(2)}) collective-permute-start(bf16[128,512]{1,0:T(8,128)(2,1)S(1)} %collective-permute-done.9.refs_3_), channel_id=1, source_target_pairs={{4,5},{5,4},{6,7},{7,6},{8,9},{9,8},{10,11},{11,10},{12,13},{13,12... | collective-permute-start | bytes 393224 | tf_op jit(solution)/shard_map/ppermute | solution.py:430
  36.5 0.0 collective-permute-done.6.refs_1_
  36.5 2.1 %collective-permute-start.7 = (bf16[128,512]{1,0:T(8,128)(2,1)S(1)}, bf16[128,512]{1,0:T(8,128)(2,1)S(1)}, u32[]{:S(2)}, u32[]{:S(2)}) collective-permute-start(bf16[128,512]{1,0:T(8,128)(2,1)S(1)} %collective-permute-done.6.refs_1_), channel_id=1, source_target_pairs={{4,5},{5,4},{6,7},{7,6},{8,9},{9,8},{10,11},{11,10},{12,13},{13,12... | collective-permute-start | bytes 393224 | tf_op jit(solution)/shard_map/ppermute | solution.py:430
  38.6 0.0 collective-permute-done.13.refs_0_
  38.6 0.0 collective-permute-done.14.refs_4_
  38.6 0.0 collective-permute-done.15.refs_6_.refs_9_
  38.6 1.2 %more_blocks.5 = (f32[128,1024]{1,0:T(8,128)S(1)}, f32[128,512]{1,0:T(8,128)S(1)}, f32[128,128]{1,0:T(8,128)S(1)}) custom-call(bf16[128,512]{1,0:T(8,128)(2,1)S(1)} %collective-permute-done.13.refs_0_, bf16[128,512]{1,0:T(8,128)(2,1)S(1)} %collective-permute-done.6.refs_1_, bf16[128,512]{1,0:T(8,128)(2,1)S(1)} %collective-permute-done.8.refs_2_, ...), custom_call_target="tpu_custom_call" | custom-call | flops 1006632960 | bytes 655360 | tf_op jit(solution)/shard_map/more_blocks/pallas_call | solution.py:180
  39.8 0.0 collective-permute-done.11.refs_1_
  39.8 0.0 collective-permute-done.7.refs_0_
  39.8 0.5 %last_keys_values.3 = (f32[128,128]{1,0:T(8,128)S(1)}, bf16[128,128]{1,0:T(8,128)(2,1)S(1)}, bf16[128,128]{1,0:T(8,128)(2,1)S(1)}) custom-call(bf16[128,512]{1,0:T(8,128)(2,1)S(1)} %collective-permute-done.7.refs_0_, bf16[128,512]{1,0:T(8,128)(2,1)S(1)} %collective-permute-done.11.refs_1_, bf16[128,1024]{1,0:T(8,128)(2,1)S(1)} %collective-permute-done.12.refs_7_.refs_2_, ...), custom_call_target="tpu_custom_call" | custom-call | flops 134217728 | bytes 262144 | tf_op jit(solution)/shard_map/last_keys_values/pallas_call | solution.py:219
  40.4 0.5 %collective-permute-start.16 = (bf16[128,128]{1,0:T(8,128)(2,1)S(1)}, bf16[128,128]{1,0:T(8,128)(2,1)S(1)}, u32[]{:S(2)}, u32[]{:S(2)}) collective-permute-start(bf16[128,128]{1,0:T(8,128)(2,1)S(1)} %get-tuple-element.86), channel_id=1, source_target_pairs={{0,3},{1,2},{2,1},{3,0},{4,7},{5,6},{6,5},{7,4},{8,11},{9,10},{10,... | collective-permute-start | bytes 98312 | tf_op jit(solution)/shard_map/ppermute | solution.py:430
  40.8 0.5 %last_queries.3.q_ref = bf16[128,1024]{1,0:T(8,128)(2,1)S(1)} custom-call(bf16[128,512]{1,0:T(8,128)(2,1)S(1)} %collective-permute-done.7.refs_0_, bf16[128,512]{1,0:T(8,128)(2,1)S(1)} %collective-permute-done.11.refs_1_, bf16[128,1024]{1,0:T(8,128)(2,1)S(1)} %collective-permute-done.12.refs_7_.refs_2_, bf16[128,1024]{1,0:T(8,128)(2,1)S(1)} %copy-done, ...), custom_call_target="tpu_custom_call" | custom-call | flops 268435456 | bytes 262144 | tf_op jit(solution)/shard_map/last_queries/pallas_call | solution.py:245
  41.3 0.6 %resident_attend.1 = (f32[1024,128]{1,0:T(8,128)S(1)}, f32[1024,128]{1,0:T(8,128)S(1)}, f32[1024,128]{1,0:T(8,128)S(1)}) custom-call(s32[128,128]{1,0:T(8,128)S(1)} %get-tuple-element.50.opened_ref, bf16[128,1024]{1,0:T(8,128)(2,1)S(1)} %last_queries.3.q_ref, bf16[128,128]{1,0:T(8,128)(2,1)S(1)} %get-tuple-element.65.refs_0_.keys_ref, ...), custom_call_target="tpu_custom_call" | custom-call | flops 10000000000 | bytes 1000 | tf_op jit(solution)/shard_map/resident_attend/pallas_call | solution.py:362
  41.9 1.9 %collective-permute-done.16.refs_4_ = bf16[128,128]{1,0:T(8,128)(2,1)S(1)} collective-permute-done((bf16[128,128]{1,0:T(8,128)(2,1)S(1)}, bf16[128,128]{1,0:T(8,128)(2,1)S(1)}, u32[]{:S(2)}, u32[]{:S(2)}) %collective-permute-start.16) | collective-permute-done | bytes 32800 | tf_op jit(solution)/shard_map/ppermute | solution.py:430
  43.8 1.3 %second_attend.1 = bf16[128,1024]{1,0:T(8,128)(2,1)} custom-call(s32[128,128]{1,0:T(8,128)S(1)} %get-tuple-element.50.opened_ref, bf16[128,1024]{1,0:T(8,128)(2,1)S(1)} %last_queries.3.q_ref, f32[1024,128]{1,0:T(8,128)S(1)} %get-tuple-element.82.max_ref, f32[1024,128]{1,0:T(8,128)S(1)} %get-tuple-element.83.sum_ref, ...), custom_call_target="tpu_custom_call" | custom-call | flops 10000000000 | bytes 1000 | tf_op jit(solution)/shard_map/second_attend/pallas_call | solution.py:401
Async XLA Ops:
  0.0 9.1 %collective-permute-start = (bf16[128,1024]{1,0:T(8,128)(2,1)}, bf16[128,1024]{1,0:T(8,128)(2,1)S(1)}, u32[]{:S(2)}, u32[]{:S(2)}) collective-permute-start(bf16[128,1024]{1,0:T(8,128)(2,1)} %bitcast.7), channel_id=1, source_target_pairs={{0,3},{1,2},{2,1},{3,0},{4,7},{5,6},{6,5},{7,4},{8,11},{9,10},{10,... | collective-permute-start | bytes 786440 | tf_op jit(solution)/shard_map/ppermute | solution.py:430
  0.8 8.7 %collective-permute-start.2 = (bf16[128,1024]{1,0:T(8,128)(2,1)}, bf16[128,1024]{1,0:T(8,128)(2,1)S(1)}, u32[]{:S(2)}, u32[]{:S(2)}) collective-permute-start(bf16[128,1024]{1,0:T(8,128)(2,1)} %bitcast.8), channel_id=1, source_target_pairs={{0,1},{1,0},{2,3},{3,2},{4,5},{5,4},{6,7},{7,6},{8,9},{9,8},{10,11... | collective-permute-start | bytes 786440 | tf_op jit(solution)/shard_map/ppermute | solution.py:430
  0.8 8.7 %collective-permute-start.3 = (bf16[4096,256]{1,0:T(8,128)(2,1)}, bf16[4096,256]{1,0:T(8,128)(2,1)S(1)}, u32[]{:S(2)}, u32[]{:S(2)}) collective-permute-start(bf16[4096,256]{1,0:T(8,128)(2,1)} %bitcast.5), channel_id=1, source_target_pairs={{0,1},{1,0},{2,3},{3,2},{4,5},{5,4},{6,7},{7,6},{8,9},{9,8},{10,11... | collective-permute-start | bytes 6291464 | tf_op jit(solution)/shard_map/ppermute | solution.py:430
  1.3 4.3 %copy-start.1 = (s32[9]{0:T(128)S(1)}, s32[9]{0:T(128)}, u32[]{:S(2)}) copy-start(s32[9]{0:T(128)} %doc_ref) | copy-start | bytes 112
  9.1 1.6 %collective-permute-start.1 = (bf16[128,1024]{1,0:T(8,128)(2,1)S(1)}, bf16[128,1024]{1,0:T(8,128)(2,1)S(1)}, u32[]{:S(2)}, u32[]{:S(2)}) collective-permute-start(bf16[128,1024]{1,0:T(8,128)(2,1)S(1)} %collective-permute-done.refs_2_), channel_id=1, source_target_pairs={{0,1},{1,0},{2,3},{3,2},{4,5},{5,4},{6,7},{7,6},{8,9},{9,8},{10,11... | collective-permute-start | bytes 786440 | tf_op jit(solution)/shard_map/ppermute | solution.py:430
  10.7 1.0 %copy-start = (bf16[128,1024]{1,0:T(8,128)(2,1)S(1)}, bf16[128,1024]{1,0:T(8,128)(2,1)}, u32[]{:S(2)}) copy-start(bf16[128,1024]{1,0:T(8,128)(2,1)} %refs_2_.1) | copy-start | bytes 786436
  11.2 3.4 %collective-permute-start.4 = (bf16[128,128]{1,0:T(8,128)(2,1)S(1)}, bf16[128,128]{1,0:T(8,128)(2,1)S(1)}, u32[]{:S(2)}, u32[]{:S(2)}) collective-permute-start(bf16[128,128]{1,0:T(8,128)(2,1)S(1)} %get-tuple-element.63), channel_id=1, source_target_pairs={{0,3},{1,2},{2,1},{3,0},{4,7},{5,6},{6,5},{7,4},{8,11},{9,10},{10,... | collective-permute-start | bytes 98312 | tf_op jit(solution)/shard_map/ppermute | solution.py:430
  11.7 13.8 %collective-permute-start.12 = (bf16[128,1024]{1,0:T(8,128)(2,1)S(1)}, bf16[128,1024]{1,0:T(8,128)(2,1)S(1)}, u32[]{:S(2)}, u32[]{:S(2)}) collective-permute-start(bf16[128,1024]{1,0:T(8,128)(2,1)S(1)} %copy-done), channel_id=1, source_target_pairs={{0,3},{1,2},{2,1},{3,0}} | collective-permute-start | bytes 786440 | tf_op jit(solution)/shard_map/ppermute | solution.py:430
  12.3 17.1 %collective-permute-start.10 = (bf16[128,1024]{1,0:T(8,128)(2,1)S(1)}, bf16[128,1024]{1,0:T(8,128)(2,1)S(1)}, u32[]{:S(2)}, u32[]{:S(2)}) collective-permute-start(bf16[128,1024]{1,0:T(8,128)(2,1)S(1)} %copy-done), channel_id=1, source_target_pairs={{0,1},{1,0},{2,3},{3,2}} | collective-permute-start | bytes 786440 | tf_op jit(solution)/shard_map/ppermute | solution.py:430
  15.1 11.1 %collective-permute-start.5 = (bf16[128,512]{1,0:T(8,128)(2,1)S(1)}, bf16[128,512]{1,0:T(8,128)(2,1)S(1)}, u32[]{:S(2)}, u32[]{:S(2)}) collective-permute-start(bf16[128,512]{1,0:T(8,128)(2,1)S(1)} %get-tuple-element.64), channel_id=1, source_target_pairs={{0,5},{1,4},{2,7},{3,6},{4,9},{5,8},{6,11},{7,10},{8,13},{9,12},{1... | collective-permute-start | bytes 393224 | tf_op jit(solution)/shard_map/ppermute | solution.py:430
  19.0 13.1 %collective-permute-start.8 = (bf16[128,512]{1,0:T(8,128)(2,1)S(1)}, bf16[128,512]{1,0:T(8,128)(2,1)S(1)}, u32[]{:S(2)}, u32[]{:S(2)}) collective-permute-start(bf16[128,512]{1,0:T(8,128)(2,1)S(1)} %first_attend.3), channel_id=1, source_target_pairs={{0,7},{1,6},{2,5},{3,4},{4,11},{5,10},{6,9},{7,8},{8,15},{9,14},{1... | collective-permute-start | bytes 393224 | tf_op jit(solution)/shard_map/ppermute | solution.py:430
  22.1 10.1 %collective-permute-start.9 = (bf16[128,512]{1,0:T(8,128)(2,1)S(1)}, bf16[128,512]{1,0:T(8,128)(2,1)S(1)}, u32[]{:S(2)}, u32[]{:S(2)}) collective-permute-start(bf16[128,512]{1,0:T(8,128)(2,1)S(1)} %first_attend.3), channel_id=1, source_target_pairs={{0,5},{1,4},{2,7},{3,6},{4,9},{5,8},{6,11},{7,10},{8,13},{9,12},{1... | collective-permute-start | bytes 393224 | tf_op jit(solution)/shard_map/ppermute | solution.py:430
  25.5 13.1 %collective-permute-start.15 = (bf16[128,1024]{1,0:T(8,128)(2,1)S(1)}, bf16[128,1024]{1,0:T(8,128)(2,1)S(1)}, u32[]{:S(2)}, u32[]{:S(2)}) collective-permute-start(bf16[128,1024]{1,0:T(8,128)(2,1)S(1)} %collective-permute-done.12.refs_7_.refs_2_), channel_id=1, source_target_pairs={{0,1},{1,0},{2,3},{3,2}} | collective-permute-start | bytes 786440 | tf_op jit(solution)/shard_map/ppermute | solution.py:430
  26.2 10.3 %collective-permute-start.6 = (bf16[128,512]{1,0:T(8,128)(2,1)S(1)}, bf16[128,512]{1,0:T(8,128)(2,1)S(1)}, u32[]{:S(2)}, u32[]{:S(2)}) collective-permute-start(bf16[128,512]{1,0:T(8,128)(2,1)S(1)} %collective-permute-done.5.refs_0_), channel_id=1, source_target_pairs={{4,7},{5,6},{6,5},{7,4},{8,11},{9,10},{10,9},{11,8},{12,15},{13,14... | collective-permute-start | bytes 393224 | tf_op jit(solution)/shard_map/ppermute | solution.py:430
  29.5 9.1 %collective-permute-start.13 = (bf16[128,512]{1,0:T(8,128)(2,1)S(1)}, bf16[128,512]{1,0:T(8,128)(2,1)S(1)}, u32[]{:S(2)}, u32[]{:S(2)}) collective-permute-start(bf16[128,512]{1,0:T(8,128)(2,1)S(1)} %collective-permute-done.5.refs_0_), channel_id=1, source_target_pairs={{4,5},{5,4},{6,7},{7,6},{8,9},{9,8},{10,11},{11,10},{12,13},{13,12... | collective-permute-start | bytes 393224 | tf_op jit(solution)/shard_map/ppermute | solution.py:430
  32.1 6.5 %collective-permute-start.14 = (bf16[128,512]{1,0:T(8,128)(2,1)S(1)}, bf16[128,512]{1,0:T(8,128)(2,1)S(1)}, u32[]{:S(2)}, u32[]{:S(2)}) collective-permute-start(bf16[128,512]{1,0:T(8,128)(2,1)S(1)} %collective-permute-done.8.refs_2_), channel_id=1, source_target_pairs={{4,5},{5,4},{6,7},{7,6},{8,9},{9,8},{10,11},{11,10},{12,13},{13,12... | collective-permute-start | bytes 393224 | tf_op jit(solution)/shard_map/ppermute | solution.py:430
  34.2 5.6 %collective-permute-start.11 = (bf16[128,512]{1,0:T(8,128)(2,1)S(1)}, bf16[128,512]{1,0:T(8,128)(2,1)S(1)}, u32[]{:S(2)}, u32[]{:S(2)}) collective-permute-start(bf16[128,512]{1,0:T(8,128)(2,1)S(1)} %collective-permute-done.9.refs_3_), channel_id=1, source_target_pairs={{4,5},{5,4},{6,7},{7,6},{8,9},{9,8},{10,11},{11,10},{12,13},{13,12... | collective-permute-start | bytes 393224 | tf_op jit(solution)/shard_map/ppermute | solution.py:430
  36.5 3.4 %collective-permute-start.7 = (bf16[128,512]{1,0:T(8,128)(2,1)S(1)}, bf16[128,512]{1,0:T(8,128)(2,1)S(1)}, u32[]{:S(2)}, u32[]{:S(2)}) collective-permute-start(bf16[128,512]{1,0:T(8,128)(2,1)S(1)} %collective-permute-done.6.refs_1_), channel_id=1, source_target_pairs={{4,5},{5,4},{6,7},{7,6},{8,9},{9,8},{10,11},{11,10},{12,13},{13,12... | collective-permute-start | bytes 393224 | tf_op jit(solution)/shard_map/ppermute | solution.py:430
  40.4 3.4 %collective-permute-start.16 = (bf16[128,128]{1,0:T(8,128)(2,1)S(1)}, bf16[128,128]{1,0:T(8,128)(2,1)S(1)}, u32[]{:S(2)}, u32[]{:S(2)}) collective-permute-start(bf16[128,128]{1,0:T(8,128)(2,1)S(1)} %get-tuple-element.86), channel_id=1, source_target_pairs={{0,3},{1,2},{2,1},{3,0},{4,7},{5,6},{6,5},{7,4},{8,11},{9,10},{10,... | collective-permute-start | bytes 98312 | tf_op jit(solution)/shard_map/ppermute | solution.py:430

commit v8 on v6

--- a/solution.py
+++ b/solution.py
@@ -214,23 +214,37 @@
 
 def last_q_kernel(count, places, *refs):
     xs, rest = refs[:count], refs[count:]
-    gain_ref, wq_ref, accq_ref, scale_ref, q_ref = rest
+    gain_ref, wq_ref, accq_ref, scale_ref, *rest = rest
     me = lax.axis_index("head")
     total = accq_ref[...]
     for i, x_ref in enumerate(xs):
         start, width = places[i](me), x_ref.shape[1]
         normed, _ = gained(x_ref[...], gain_ref, start)
         total = total + dot(normed, wq_ref[from_start(start, width), :])
-    q_ref[...] = (total * scale_ref[:, 0:1]).astype(bf16)
-
-
-def last_q(xs, places, gain, wq, accq, scale):
-    operands = [*xs, *resident_in(gain, wq), accq, scale]
+    q = (total * scale_ref[:, 0:1]).astype(bf16)
+    if len(rest) == 1:
+        rest[0][...] = q
+        return
+    piece_ref, fresh_ref, q_ref, bundle_ref = rest
+    q_ref[...] = q
+    late = bundle_ref.shape[1] - HD
+    last = lax.axis_index("section") == lax.axis_size("section") - 1
+    sent = jnp.where(last, fresh_ref[:, -late:].astype(f32), q[:, -late:].astype(f32))
+    bundle_ref[:, :late] = sent.astype(bf16)
+    bundle_ref[:, late:] = piece_ref[...]
+
+
+def last_q(xs, places, gain, wq, accq, scale, bundled=(), late=0):
+    operands = [*xs, *resident_in(gain, wq), accq, scale, *bundled]
+    tokens = xs[0].shape[0]
+    out = [VMEM((tokens, wq.shape[1]), bf16)]
+    if bundled:
+        out.append(VMEM((tokens, late + HD), bf16))
     return pl.pallas_call(
         functools.partial(last_q_kernel, len(xs), places),
-        out_shape=VMEM((xs[0].shape[0], wq.shape[1]), bf16),
+        out_shape=tuple(out),
         in_specs=[vmem] * len(operands),
-        out_specs=vmem,
+        out_specs=(vmem,) * len(out),
         cost_estimate=cost(sum(2 * x.size * wq.shape[1] for x in xs), sum(2 * x.size for x in xs)),
         compiler_params=params,
         name="last_queries",
@@ -288,6 +302,39 @@
         gather[0, rows_of(source, features), :] = piece[:features]
         gather[1, rows_of(source, features), :] = piece[features:]
     return gather[0].astype(bf16), gather[1].astype(bf16)
+
+
+def peer_attend_kernel(sections, flips, parts, opened_ref, bundle_ref, x_ref, piece_ref, out_ref, gather):
+    section = lax.axis_index("section")
+    tokens, width = out_ref.shape
+    start = (sections - 1 - section) * tokens
+    pieces = [piece_ref, bundle_ref.at[:, width:]]
+    keys, values = put_together(lax.axis_index("head"), pieces, flips, parts, gather)
+    q = stacked_heads(bundle_ref, (0, width // HD))
+    scores = masked_scores(q, keys, opened_ref, start, start)
+    expon = jnp.exp2((scores - jnp.max(scores, axis=1, keepdims=True)) * score_scale)
+    mixed, total = mixed_and_sums(expon, values)
+    mixed = (mixed * (1.0 / total)).astype(bf16).astype(f32)
+    for h in range(width // HD):
+        columns = slice(h * HD, (h + 1) * HD)
+        x = x_ref[:, x_ref.shape[1] - width + h * HD : x_ref.shape[1] - width + (h + 1) * HD].astype(f32)
+        out = (x + mixed[h * tokens : (h + 1) * tokens]).astype(bf16).astype(f32)
+        out = jnp.where(section == sections - 1, bundle_ref[:, columns].astype(f32), out)
+        out_ref[:, columns] = out.astype(bf16)
+
+
+def peer_attend(opened, bundle, x, piece, flips, parts, sections):
+    tokens, width = x.shape[0], bundle.shape[1] - HD
+    return pl.pallas_call(
+        functools.partial(peer_attend_kernel, sections, flips, parts),
+        out_shape=VMEM((tokens, width), bf16),
+        in_specs=[vmem] * 4,
+        out_specs=vmem,
+        scratch_shapes=[VMEM((2, HD, tokens), f32)],
+        cost_estimate=cost(1000, 1000),
+        compiler_params=params,
+        name="peer_attend",
+    )(opened, bundle, x, piece)
 
 
 def first_attend_kernel(sections, heads, flips, parts, opened_ref, q_ref, x_ref, fresh_ref, *refs):
@@ -326,7 +373,7 @@
         in_specs=[vmem] * len(operands),
         out_specs=(vmem,) * len(out),
         scratch_shapes=scratch,
-        cost_estimate=cost(1000, 1000),
+        cost_estimate=cost(10**10, 1000),
         compiler_params=params,
         name="first_attend",
     )(*operands)
@@ -414,7 +461,7 @@
     def exchanged(xs, places, state):
         scale, *pieces = last_kv(xs, places, gain, wkvs, choose, state[1], state[2])
         received = [moved(piece, 0, flip) for piece, flip in zip(pieces[1:], flips[1:])]
-        return scale, [pieces[0], *received]
+        return scale, [pieces[0], *received], pieces
 
     def rest_of(array):
         every = lax.all_gather(array, "head", axis=0)
@@ -431,9 +478,10 @@
         beside = moved(own, 0, 1)
         w_kv_beside = moved(w_kv, 0, 1)
     accq, own, gain, wq, wkv, choose = load(own, norm_gain, w_q, w_kv, n, flips, parts)
+    opened = openings(after(doc_lengths, accq), tokens, sections)
     if paired:
         wkvs = [wkv, w_kv_beside]
-        over = after(over, accq)
+        over, *opened = lax.optimization_barrier((over, *opened))
         passed = moved(over, 0, 1)
         xs, places, with_q = [own, beside, over], [place(0), place(1), place(3)], [False, True, True]
         state = more_blocks(xs, places, gain, wq, wkvs, [accq], with_q)
@@ -442,11 +490,14 @@
         wkvs = [wkv]
         state = more_blocks([own], following[:1], gain, wq, wkvs, [accq], [False])
         last, places = rest_of(own), following[1:]
-    scale, pieces = exchanged(last, places, state)
-    opened = openings(after(doc_lengths, scale), tokens, sections)
-    q = last_q(last, places, gain, wq, state[0], scale)
+    scale, pieces, made = exchanged(last, places, state)
     part = heads // 2 if paired else heads
     split = part * HD
+    if paired:
+        q, bundle = last_q(last, places, gain, wq, state[0], scale, [made[0], fresh_slice], width - split)
+        bundle = moved(bundle, 0, 3)
+    else:
+        (q,) = last_q(last, places, gain, wq, state[0], scale)
     sent, keys, values = first_attend(
         opened[0], q, own, fresh_slice, pieces, flips, parts, (0, part), sections
     )
@@ -457,25 +508,27 @@
             opened[0], q, own, fresh_slice, [keys, values], None, parts, (part, heads), sections
         )
         b1 = moved(sent, 1, 1)
-        b3 = moved(sent, 1, 3)
-        a1 = after(a1, sent)
+        bundle = after(bundle, sent)
+        peers = peer_attend(opened[0], bundle, over, made[1], flips, parts, sections)
+        b2 = moved(peers, 1, 1)
+        a1 = after(a1, peers)
         a2 = moved(a1, 0, 3)
         a0 = moved(a1, 0, 1)
         state = more_blocks([a1], [place(1)], gain, wq, wkvs, [])
-        b3, b1, *state = lax.optimization_barrier((b3, b1, *state))
-        b2 = moved(b3, 0, 1)
+        b2, b1, *state = lax.optimization_barrier((b2, b1, *state))
+        b3 = moved(b2, 0, 1)
         b0 = moved(b1, 0, 1)
         a3 = moved(a2, 0, 1)
-        places = [place(0), place(2), *(place(flip, split) for flip in (3, 1, 2))]
-        state = more_blocks([a0, a2, b3, b1, b2], places, gain, wq, wkvs, state)
+        places = [place(0), place(2), *(place(flip, split) for flip in (2, 1, 3))]
+        state = more_blocks([a0, a2, b2, b1, b3], places, gain, wq, wkvs, state)
         last, places = [a3, b0], [place(3), place(0, split)]
         mine = [a0, b0]
     else:
         mine = [moved(sent, 1, 0)]
         state = more_blocks(mine, following[:1], gain, wq, wkvs, [])
         last, places = rest_of(mine[0]), following[1:]
-    scale, pieces = exchanged(last, places, state)
-    q = last_q(last, places, gain, wq, state[0], scale)
+    scale, pieces, _ = exchanged(last, places, state)
+    (q,) = last_q(last, places, gain, wq, state[0], scale)
     resident = resident_attend(opened[1], q, keys, values, sections)
     return second_attend(opened[1], q, mine, resident, pieces, flips, parts, sections)[None]
 

time: 38.1 us -> 37.7 us (0.990)
  waiting for transfers between devices: 9.83 us -> 9.11 us
  Pallas kernels: 12.4 us -> 12.9 us
    ppermute x14 -> x15, waiting for transfers between devices: 9.83 us -> 9.11 us  [moved(): return lax.ppermute(array, ('section', 'head'), pairs)]
    pallas_call x0 -> x1, Pallas kernels: none -> 0.49 us  [peer_attend(): pl.pallas_call(functools.partial(peer_attend_kernel, sections, flips, par...]
    ppermute x14 -> x15, starting transfers between devices: 15.6 us -> 15.4 us  [moved(): return lax.ppermute(array, ('section', 'head'), pairs)]
  transfers between devices with their start and end apart: 14 -> 15, of which waited for: 8 -> 9; matrix products, arithmetic and copies ran while one was open for 0% -> 0% of each run, Pallas kernels for 25% -> 28%
where the time goes in v8:
time: 37.7 us; the launch traced here: 37.6 us
  starting transfers between devices  15.4 us (41%)
  Pallas kernels  12.9 us (34%)
  waiting for transfers between devices  9.11 us (24%)
    ppermute x15, starting transfers between devices, moved(): return lax.ppermute(array, ('section', 'head'), pairs)  15.4 us
    ppermute x15, waiting for transfers between devices, moved(): return lax.ppermute(array, ('section', 'head'), pairs)  9.11 us
    pallas_call x1, Pallas kernels, load(): pl.pallas_call(functools.partial(load_kernel, n, flips, parts), out_shape...  4.24 us
    pallas_call x3, Pallas kernels, more_blocks(): pl.pallas_call(functools.partial(blocks_kernel, len(xs), len(wkvs), len(s...  2.72 us
    pallas_call x1, Pallas kernels, second_attend(): pl.pallas_call(functools.partial(second_attend_kernel, sections, flips, p...  1.32 us
    pallas_call x2, Pallas kernels, last_kv(): pl.pallas_call(functools.partial(last_kv_kernel, len(xs), len(wkvs), plac...  1.04 us
    pallas_call x2, Pallas kernels, first_attend(): pl.pallas_call(functools.partial(first_attend_kernel, sections, heads, fl...  0.96 us
    pallas_call x2, Pallas kernels, last_q(): pl.pallas_call(functools.partial(last_q_kernel, len(xs), places), out_sha...  0.92 us
  transfers between devices with their start and end apart: 15, of which 9 were waited for; matrix products, arithmetic and copies ran while one was open for 0% of the time, Pallas kernels for 28%

profile of v8, /device:TPU:0, one launch (start us, length us, event | category | flops | bytes accessed | tf_op | source)
XLA Modules:
  0.0 37.6 jit_solution(11994705499123592715)
XLA Ops:
  0.0 2.4 %collective-permute-start = (bf16[128,1024]{1,0:T(8,128)(2,1)}, bf16[128,1024]{1,0:T(8,128)(2,1)S(1)}, u32[]{:S(2)}, u32[]{:S(2)}) collective-permute-start(bf16[128,1024]{1,0:T(8,128)(2,1)} %bitcast.7), channel_id=1, source_target_pairs={{0,3},{1,2},{2,1},{3,0},{4,7},{5,6},{6,5},{7,4},{8,11},{9,10},{10,... | collective-permute-start | bytes 786440 | tf_op jit(solution)/shard_map/ppermute | solution.py:456
  2.4 0.7 %collective-permute-start.2 = (bf16[128,1024]{1,0:T(8,128)(2,1)}, bf16[128,1024]{1,0:T(8,128)(2,1)S(1)}, u32[]{:S(2)}, u32[]{:S(2)}) collective-permute-start(bf16[128,1024]{1,0:T(8,128)(2,1)} %bitcast.8), channel_id=1, source_target_pairs={{0,1},{1,0},{2,3},{3,2},{4,5},{5,4},{6,7},{7,6},{8,9},{9,8},{10,11... | collective-permute-start | bytes 786440 | tf_op jit(solution)/shard_map/ppermute | solution.py:456
  3.1 0.0 collective-permute-start.3
  3.1 0.0 copy-start.1
  3.1 4.2 %load_and_own_queries.1 = (f32[128,1024]{1,0:T(8,128)S(1)}, bf16[128,1024]{1,0:T(8,128)(2,1)S(1)}, f32[1,4096]{1,0:T(1,128)S(1)}, bf16[4096,1024]{1,0:T(8,128)(2...) custom-call(bf16[128,1024]{1,0:T(8,128)(2,1)} %bitcast.9, f32[1,4096]{1,0:T(1,128)} %gain_hbm.1, ...), custom_call_target="tpu_custom_call" | custom-call | flops 99999997952 | bytes 1000000000 | tf_op jit(solution)/shard_map/load_and_own_queries/pallas_call | solution.py:114
  7.3 0.0 copy-done.1
  7.3 0.6 %openings.1 = (s32[128,128]{1,0:T(8,128)S(1)}, s32[128,128]{1,0:T(8,128)S(1)}) custom-call(s32[9]{0:T(128)S(1)} %copy-done.1), custom_call_target="tpu_custom_call" | custom-call | tf_op jit(solution)/shard_map/openings/pallas_call | solution.py:268
  8.0 1.4 %collective-permute-done.refs_2_.x_ref = bf16[128,1024]{1,0:T(8,128)(2,1)S(1)} collective-permute-done((bf16[128,1024]{1,0:T(8,128)(2,1)}, bf16[128,1024]{1,0:T(8,128)(2,1)S(1)}, u32[]{:S(2)}, u32[]{:S(2)}) %collective-permute-start) | collective-permute-done | bytes 262176 | tf_op jit(solution)/shard_map/ppermute | solution.py:456
  9.4 0.1 collective-permute-start.1
  9.5 0.0 collective-permute-done.2.refs_1_
  9.5 0.0 collective-permute-done.3.refs_6_.refs_3_.refs_4_.refs_8_
  9.5 1.1 %more_blocks.3 = (f32[128,1024]{1,0:T(8,128)S(1)}, f32[128,512]{1,0:T(8,128)S(1)}, f32[128,128]{1,0:T(8,128)S(1)}) custom-call(bf16[128,1024]{1,0:T(8,128)(2,1)S(1)} %get-tuple-element.56.refs_0_.x_ref, bf16[128,1024]{1,0:T(8,128)(2,1)S(1)} %collective-permute-done.2.refs_1_, bf16[128,1024]{1,0:T(8,128)(2,1)S(1)} %collective-permute-done.refs_2_.x_ref, ...), custom_call_target="tpu_custom_call" | custom-call | flops 1207959552 | bytes 786432 | tf_op jit(solution)/shard_map/more_blocks/pallas_call | solution.py:166
  10.7 0.3 collective-permute-done.1.refs_0_
  10.9 0.0 copy-start
  10.9 0.5 %last_keys_values.2 = (f32[128,128]{1,0:T(8,128)S(1)}, bf16[128,128]{1,0:T(8,128)(2,1)S(1)}, bf16[128,128]{1,0:T(8,128)(2,1)S(1)}) custom-call(bf16[128,1024]{1,0:T(8,128)(2,1)S(1)} %collective-permute-done.1.refs_0_, f32[1,4096]{1,0:T(1,128)S(1)} %get-tuple-element.54.refs_3_.refs_1_.refs_5_.refs_2_, ...), custom_call_target="tpu_custom_call" | custom-call | flops 134217728 | bytes 262144 | tf_op jit(solution)/shard_map/last_keys_values/pallas_call | solution.py:204
  11.5 2.2 %collective-permute-start.4 = (bf16[128,128]{1,0:T(8,128)(2,1)S(1)}, bf16[128,128]{1,0:T(8,128)(2,1)S(1)}, u32[]{:S(2)}, u32[]{:S(2)}) collective-permute-start(bf16[128,128]{1,0:T(8,128)(2,1)S(1)} %get-tuple-element.65.piece_ref), channel_id=1, source_target_pairs={{0,3},{1,2},{2,1},{3,0},{4,7},{5,6},{6,5},{7,4},{8,11},{9,10},{10,... | collective-permute-start | bytes 98312 | tf_op jit(solution)/shard_map/ppermute | solution.py:456
  13.7 0.0 copy-done
  13.7 0.5 %last_queries.2 = (bf16[128,1024]{1,0:T(8,128)(2,1)S(1)}, bf16[128,640]{1,0:T(8,128)(2,1)S(1)}) custom-call(bf16[128,1024]{1,0:T(8,128)(2,1)S(1)} %collective-permute-done.1.refs_0_, f32[1,4096]{1,0:T(1,128)S(1)} %get-tuple-element.54.refs_3_.refs_1_.refs_5_.refs_2_, bf16[4096,1024]{1,0:T(8,128)(2,1)S(1)} %get-tuple-element.55.refs_4_.refs_2_.refs_6_.refs_3_, ...), custom_call_target="tpu_custom_call" | custom-call | flops 268435456 | bytes 262144 | tf_op jit(solution)/shard_map/last_queries/pallas_call | solution.py:243
  14.1 0.4 %collective-permute-start.6 = (bf16[128,640]{1,0:T(8,128)(2,1)S(1)}, bf16[128,640]{1,0:T(8,128)(2,1)S(1)}, u32[]{:S(2)}, u32[]{:S(2)}) collective-permute-start(bf16[128,640]{1,0:T(8,128)(2,1)S(1)} %get-tuple-element.67), channel_id=1, source_target_pairs={{0,3},{1,2},{2,1},{3,0},{4,7},{5,6},{6,5},{7,4},{8,11},{9,10},{10,... | collective-permute-start | bytes 491528 | tf_op jit(solution)/shard_map/ppermute | solution.py:456
  14.6 0.7 %collective-permute-done.4.refs_1_ = bf16[128,128]{1,0:T(8,128)(2,1)S(1)} collective-permute-done((bf16[128,128]{1,0:T(8,128)(2,1)S(1)}, bf16[128,128]{1,0:T(8,128)(2,1)S(1)}, u32[]{:S(2)}, u32[]{:S(2)}) %collective-permute-start.4) | collective-permute-done | bytes 32800 | tf_op jit(solution)/shard_map/ppermute | solution.py:456
  15.3 0.5 %first_attend.2 = (bf16[128,512]{1,0:T(8,128)(2,1)S(1)}, bf16[128,128]{1,0:T(8,128)(2,1)S(1)}, bf16[128,128]{1,0:T(8,128)(2,1)S(1)}) custom-call(s32[128,128]{1,0:T(8,128)S(1)} %get-tuple-element.52.opened_ref, bf16[128,1024]{1,0:T(8,128)(2,1)S(1)} %get-tuple-element.64.q_ref, bf16[128,1024]{1,0:T(8,128)(2,1)S(1)} %get-tuple-element.56.refs_0_.x_ref, ...), custom_call_target="tpu_custom_call" | custom-call | flops 10000000000 | bytes 1000 | tf_op jit(solution)/shard_map/first_attend/pallas_call | solution.py:370
  15.8 1.7 %collective-permute-start.5 = (bf16[128,512]{1,0:T(8,128)(2,1)S(1)}, bf16[128,512]{1,0:T(8,128)(2,1)S(1)}, u32[]{:S(2)}, u32[]{:S(2)}) collective-permute-start(bf16[128,512]{1,0:T(8,128)(2,1)S(1)} %get-tuple-element.66), channel_id=1, source_target_pairs={{0,5},{1,4},{2,7},{3,6},{4,9},{5,8},{6,11},{7,10},{8,13},{9,12},{1... | collective-permute-start | bytes 393224 | tf_op jit(solution)/shard_map/ppermute | solution.py:456
  17.5 0.5 %first_attend.3 = bf16[128,512]{1,0:T(8,128)(2,1)S(1)} custom-call(s32[128,128]{1,0:T(8,128)S(1)} %get-tuple-element.52.opened_ref, bf16[128,1024]{1,0:T(8,128)(2,1)S(1)} %get-tuple-element.64.q_ref, bf16[128,1024]{1,0:T(8,128)(2,1)S(1)} %get-tuple-element.56.refs_0_.x_ref, bf16[128,1024]{1,0:T(8,128)(2,1)S(1)} %copy-done, ...), custom_call_target="tpu_custom_call" | custom-call | flops 10000000000 | bytes 1000 | tf_op jit(solution)/shard_map/first_attend/pallas_call | solution.py:370
  17.9 1.6 %collective-permute-start.10 = (bf16[128,512]{1,0:T(8,128)(2,1)S(1)}, bf16[128,512]{1,0:T(8,128)(2,1)S(1)}, u32[]{:S(2)}, u32[]{:S(2)}) collective-permute-start(bf16[128,512]{1,0:T(8,128)(2,1)S(1)} %first_attend.3), channel_id=1, source_target_pairs={{0,5},{1,4},{2,7},{3,6},{4,9},{5,8},{6,11},{7,10},{8,13},{9,12},{1... | collective-permute-start | bytes 393224 | tf_op jit(solution)/shard_map/ppermute | solution.py:456
  19.5 0.7 %collective-permute-done.6.bundle_ref = bf16[128,640]{1,0:T(8,128)(2,1)S(1)} collective-permute-done((bf16[128,640]{1,0:T(8,128)(2,1)S(1)}, bf16[128,640]{1,0:T(8,128)(2,1)S(1)}, u32[]{:S(2)}, u32[]{:S(2)}) %collective-permute-start.6) | collective-permute-done | bytes 163872 | tf_op jit(solution)/shard_map/ppermute | solution.py:456
  20.2 0.5 %peer_attend.1 = bf16[128,512]{1,0:T(8,128)(2,1)S(1)} custom-call(s32[128,128]{1,0:T(8,128)S(1)} %get-tuple-element.52.opened_ref, bf16[128,640]{1,0:T(8,128)(2,1)S(1)} %collective-permute-done.6.bundle_ref, bf16[128,1024]{1,0:T(8,128)(2,1)S(1)} %collective-permute-done.refs_2_.x_ref, bf16[128,128]{1,0:T(8,128)(2,1)S(1)} %get-tuple-element.65.piece_ref), custom_call_target="tpu_custom_call" | custom-call | flops 1000 | bytes 1000 | tf_op jit(solution)/shard_map/peer_attend/pallas_call | solution.py:328
  20.7 1.7 %collective-permute-start.9 = (bf16[128,512]{1,0:T(8,128)(2,1)S(1)}, bf16[128,512]{1,0:T(8,128)(2,1)S(1)}, u32[]{:S(2)}, u32[]{:S(2)}) collective-permute-start(bf16[128,512]{1,0:T(8,128)(2,1)S(1)} %peer_attend.1), channel_id=1, source_target_pairs={{0,5},{1,4},{2,7},{3,6},{4,9},{5,8},{6,11},{7,10},{8,13},{9,12},{1... | collective-permute-start | bytes 393224 | tf_op jit(solution)/shard_map/ppermute | solution.py:456
  22.5 1.6 %collective-permute-done.5.refs_0_ = bf16[128,512]{1,0:T(8,128)(2,1)S(1)} collective-permute-done((bf16[128,512]{1,0:T(8,128)(2,1)S(1)}, bf16[128,512]{1,0:T(8,128)(2,1)S(1)}, u32[]{:S(2)}, u32[]{:S(2)}) %collective-permute-start.5) | collective-permute-done | bytes 131104 | tf_op jit(solution)/shard_map/ppermute | solution.py:456
  24.1 2.2 %collective-permute-start.7 = (bf16[128,512]{1,0:T(8,128)(2,1)S(1)}, bf16[128,512]{1,0:T(8,128)(2,1)S(1)}, u32[]{:S(2)}, u32[]{:S(2)}) collective-permute-start(bf16[128,512]{1,0:T(8,128)(2,1)S(1)} %collective-permute-done.5.refs_0_), channel_id=1, source_target_pairs={{0,3},{1,2},{2,1},{3,0},{4,7},{5,6},{6,5},{7,4},{8,11},{9,10},{10,... | collective-permute-start | bytes 393224 | tf_op jit(solution)/shard_map/ppermute | solution.py:456
  26.3 0.0 collective-permute-start.12
  26.3 0.4 more_blocks.4
  26.7 0.2 collective-permute-done.10.refs_3_
  26.9 2.8 %collective-permute-done.9.refs_2_ = bf16[128,512]{1,0:T(8,128)(2,1)S(1)} collective-permute-done((bf16[128,512]{1,0:T(8,128)(2,1)S(1)}, bf16[128,512]{1,0:T(8,128)(2,1)S(1)}, u32[]{:S(2)}, u32[]{:S(2)}) %collective-permute-start.9) | collective-permute-done | bytes 131104 | tf_op jit(solution)/shard_map/ppermute | solution.py:456
  29.7 0.3 collective-permute-start.13
  30.0 0.2 collective-permute-start.11
  30.3 0.0 collective-permute-done.7.refs_1_
  30.3 0.3 collective-permute-start.8
  30.5 0.0 collective-permute-done.12.refs_0_
  30.5 0.6 %collective-permute-done.13.refs_4_ = bf16[128,512]{1,0:T(8,128)(2,1)S(1)} collective-permute-done((bf16[128,512]{1,0:T(8,128)(2,1)S(1)}, bf16[128,512]{1,0:T(8,128)(2,1)S(1)}, u32[]{:S(2)}, u32[]{:S(2)}) %collective-permute-start.13) | collective-permute-done | bytes 131104 | tf_op jit(solution)/shard_map/ppermute | solution.py:456
  31.1 1.2 %more_blocks.5 = (f32[128,1024]{1,0:T(8,128)S(1)}, f32[128,512]{1,0:T(8,128)S(1)}, f32[128,128]{1,0:T(8,128)S(1)}) custom-call(bf16[128,512]{1,0:T(8,128)(2,1)S(1)} %collective-permute-done.12.refs_0_, bf16[128,512]{1,0:T(8,128)(2,1)S(1)} %collective-permute-done.7.refs_1_, bf16[128,512]{1,0:T(8,128)(2,1)S(1)} %collective-permute-done.9.refs_2_, ...), custom_call_target="tpu_custom_call" | custom-call | flops 1006632960 | bytes 655360 | tf_op jit(solution)/shard_map/more_blocks/pallas_call | solution.py:166
  32.3 0.0 collective-permute-done.11.refs_1_
  32.3 0.0 collective-permute-done.8.refs_0_
  32.3 0.5 %last_keys_values.3 = (f32[128,128]{1,0:T(8,128)S(1)}, bf16[128,128]{1,0:T(8,128)(2,1)S(1)}, bf16[128,128]{1,0:T(8,128)(2,1)S(1)}) custom-call(bf16[128,512]{1,0:T(8,128)(2,1)S(1)} %collective-permute-done.8.refs_0_, bf16[128,512]{1,0:T(8,128)(2,1)S(1)} %collective-permute-done.11.refs_1_, f32[1,4096]{1,0:T(1,128)S(1)} %get-tuple-element.54.refs_3_.refs_1_.refs_5_.refs_2_, ...), custom_call_target="tpu_custom_call" | custom-call | flops 134217728 | bytes 262144 | tf_op jit(solution)/shard_map/last_keys_values/pallas_call | solution.py:204
  32.8 1.7 %collective-permute-start.14 = (bf16[128,128]{1,0:T(8,128)(2,1)S(1)}, bf16[128,128]{1,0:T(8,128)(2,1)S(1)}, u32[]{:S(2)}, u32[]{:S(2)}) collective-permute-start(bf16[128,128]{1,0:T(8,128)(2,1)S(1)} %get-tuple-element.88), channel_id=1, source_target_pairs={{0,3},{1,2},{2,1},{3,0},{4,7},{5,6},{6,5},{7,4},{8,11},{9,10},{10,... | collective-permute-start | bytes 98312 | tf_op jit(solution)/shard_map/ppermute | solution.py:456
  34.5 0.4 %last_queries.3.q_ref = bf16[128,1024]{1,0:T(8,128)(2,1)S(1)} custom-call(bf16[128,512]{1,0:T(8,128)(2,1)S(1)} %collective-permute-done.8.refs_0_, bf16[128,512]{1,0:T(8,128)(2,1)S(1)} %collective-permute-done.11.refs_1_, f32[1,4096]{1,0:T(1,128)S(1)} %get-tuple-element.54.refs_3_.refs_1_.refs_5_.refs_2_, ...), custom_call_target="tpu_custom_call" | custom-call | flops 268435456 | bytes 262144 | tf_op jit(solution)/shard_map/last_queries/pallas_call | solution.py:243
  35.0 0.6 %resident_attend.1 = (f32[1024,128]{1,0:T(8,128)S(1)}, f32[1024,128]{1,0:T(8,128)S(1)}, f32[1024,128]{1,0:T(8,128)S(1)}) custom-call(s32[128,128]{1,0:T(8,128)S(1)} %get-tuple-element.51.opened_ref, bf16[128,1024]{1,0:T(8,128)(2,1)S(1)} %last_queries.3.q_ref, bf16[128,128]{1,0:T(8,128)(2,1)S(1)} %get-tuple-element.68.refs_0_.keys_ref, ...), custom_call_target="tpu_custom_call" | custom-call | flops 1000 | bytes 1000 | tf_op jit(solution)/shard_map/resident_attend/pallas_call | solution.py:395
  35.5 0.7 %collective-permute-done.14.refs_3_ = bf16[128,128]{1,0:T(8,128)(2,1)S(1)} collective-permute-done((bf16[128,128]{1,0:T(8,128)(2,1)S(1)}, bf16[128,128]{1,0:T(8,128)(2,1)S(1)}, u32[]{:S(2)}, u32[]{:S(2)}) %collective-permute-start.14) | collective-permute-done | bytes 32800 | tf_op jit(solution)/shard_map/ppermute | solution.py:456
  36.2 1.3 %second_attend.1 = bf16[128,1024]{1,0:T(8,128)(2,1)} custom-call(s32[128,128]{1,0:T(8,128)S(1)} %get-tuple-element.51.opened_ref, bf16[128,1024]{1,0:T(8,128)(2,1)S(1)} %last_queries.3.q_ref, f32[1024,128]{1,0:T(8,128)S(1)} %get-tuple-element.84.max_ref, f32[1024,128]{1,0:T(8,128)S(1)} %get-tuple-element.85.sum_ref, ...), custom_call_target="tpu_custom_call" | custom-call | flops 1000 | bytes 1000 | tf_op jit(solution)/shard_map/second_attend/pallas_call | solution.py:429
Async XLA Ops:
  0.0 9.4 %collective-permute-start = (bf16[128,1024]{1,0:T(8,128)(2,1)}, bf16[128,1024]{1,0:T(8,128)(2,1)S(1)}, u32[]{:S(2)}, u32[]{:S(2)}) collective-permute-start(bf16[128,1024]{1,0:T(8,128)(2,1)} %bitcast.7), channel_id=1, source_target_pairs={{0,3},{1,2},{2,1},{3,0},{4,7},{5,6},{6,5},{7,4},{8,11},{9,10},{10,... | collective-permute-start | bytes 786440 | tf_op jit(solution)/shard_map/ppermute | solution.py:456
  2.4 7.1 %collective-permute-start.2 = (bf16[128,1024]{1,0:T(8,128)(2,1)}, bf16[128,1024]{1,0:T(8,128)(2,1)S(1)}, u32[]{:S(2)}, u32[]{:S(2)}) collective-permute-start(bf16[128,1024]{1,0:T(8,128)(2,1)} %bitcast.8), channel_id=1, source_target_pairs={{0,1},{1,0},{2,3},{3,2},{4,5},{5,4},{6,7},{7,6},{8,9},{9,8},{10,11... | collective-permute-start | bytes 786440 | tf_op jit(solution)/shard_map/ppermute | solution.py:456
  3.1 6.4 %collective-permute-start.3 = (bf16[4096,256]{1,0:T(8,128)(2,1)}, bf16[4096,256]{1,0:T(8,128)(2,1)S(1)}, u32[]{:S(2)}, u32[]{:S(2)}) collective-permute-start(bf16[4096,256]{1,0:T(8,128)(2,1)} %bitcast.5), channel_id=1, source_target_pairs={{0,1},{1,0},{2,3},{3,2},{4,5},{5,4},{6,7},{7,6},{8,9},{9,8},{10,11... | collective-permute-start | bytes 6291464 | tf_op jit(solution)/shard_map/ppermute | solution.py:456
  3.1 4.3 %copy-start.1 = (s32[9]{0:T(128)S(1)}, s32[9]{0:T(128)}, u32[]{:S(2)}) copy-start(s32[9]{0:T(128)} %doc_ref) | copy-start | bytes 112
  9.4 1.5 %collective-permute-start.1 = (bf16[128,1024]{1,0:T(8,128)(2,1)S(1)}, bf16[128,1024]{1,0:T(8,128)(2,1)S(1)}, u32[]{:S(2)}, u32[]{:S(2)}) collective-permute-start(bf16[128,1024]{1,0:T(8,128)(2,1)S(1)} %collective-permute-done.refs_2_.x_ref), channel_id=1, source_target_pairs={{0,1},{1,0},{2,3},{3,2},{4,5},{5,4},{6,7},{7,6},{8,9},{9,8},{10,11... | collective-permute-start | bytes 786440 | tf_op jit(solution)/shard_map/ppermute | solution.py:456
  10.9 2.7 %copy-start = (bf16[128,1024]{1,0:T(8,128)(2,1)S(1)}, bf16[128,1024]{1,0:T(8,128)(2,1)}, u32[]{:S(2)}) copy-start(bf16[128,1024]{1,0:T(8,128)(2,1)} %fresh_ref.3) | copy-start | bytes 786436
  11.5 3.8 %collective-permute-start.4 = (bf16[128,128]{1,0:T(8,128)(2,1)S(1)}, bf16[128,128]{1,0:T(8,128)(2,1)S(1)}, u32[]{:S(2)}, u32[]{:S(2)}) collective-permute-start(bf16[128,128]{1,0:T(8,128)(2,1)S(1)} %get-tuple-element.65.piece_ref), channel_id=1, source_target_pairs={{0,3},{1,2},{2,1},{3,0},{4,7},{5,6},{6,5},{7,4},{8,11},{9,10},{10,... | collective-permute-start | bytes 98312 | tf_op jit(solution)/shard_map/ppermute | solution.py:456
  14.1 6.1 %collective-permute-start.6 = (bf16[128,640]{1,0:T(8,128)(2,1)S(1)}, bf16[128,640]{1,0:T(8,128)(2,1)S(1)}, u32[]{:S(2)}, u32[]{:S(2)}) collective-permute-start(bf16[128,640]{1,0:T(8,128)(2,1)S(1)} %get-tuple-element.67), channel_id=1, source_target_pairs={{0,3},{1,2},{2,1},{3,0},{4,7},{5,6},{6,5},{7,4},{8,11},{9,10},{10,... | collective-permute-start | bytes 491528 | tf_op jit(solution)/shard_map/ppermute | solution.py:456
  15.8 8.4 %collective-permute-start.5 = (bf16[128,512]{1,0:T(8,128)(2,1)S(1)}, bf16[128,512]{1,0:T(8,128)(2,1)S(1)}, u32[]{:S(2)}, u32[]{:S(2)}) collective-permute-start(bf16[128,512]{1,0:T(8,128)(2,1)S(1)} %get-tuple-element.66), channel_id=1, source_target_pairs={{0,5},{1,4},{2,7},{3,6},{4,9},{5,8},{6,11},{7,10},{8,13},{9,12},{1... | collective-permute-start | bytes 393224 | tf_op jit(solution)/shard_map/ppermute | solution.py:456
  17.9 9.0 %collective-permute-start.10 = (bf16[128,512]{1,0:T(8,128)(2,1)S(1)}, bf16[128,512]{1,0:T(8,128)(2,1)S(1)}, u32[]{:S(2)}, u32[]{:S(2)}) collective-permute-start(bf16[128,512]{1,0:T(8,128)(2,1)S(1)} %first_attend.3), channel_id=1, source_target_pairs={{0,5},{1,4},{2,7},{3,6},{4,9},{5,8},{6,11},{7,10},{8,13},{9,12},{1... | collective-permute-start | bytes 393224 | tf_op jit(solution)/shard_map/ppermute | solution.py:456
  20.7 9.0 %collective-permute-start.9 = (bf16[128,512]{1,0:T(8,128)(2,1)S(1)}, bf16[128,512]{1,0:T(8,128)(2,1)S(1)}, u32[]{:S(2)}, u32[]{:S(2)}) collective-permute-start(bf16[128,512]{1,0:T(8,128)(2,1)S(1)} %peer_attend.1), channel_id=1, source_target_pairs={{0,5},{1,4},{2,7},{3,6},{4,9},{5,8},{6,11},{7,10},{8,13},{9,12},{1... | collective-permute-start | bytes 393224 | tf_op jit(solution)/shard_map/ppermute | solution.py:456
  24.1 6.1 %collective-permute-start.7 = (bf16[128,512]{1,0:T(8,128)(2,1)S(1)}, bf16[128,512]{1,0:T(8,128)(2,1)S(1)}, u32[]{:S(2)}, u32[]{:S(2)}) collective-permute-start(bf16[128,512]{1,0:T(8,128)(2,1)S(1)} %collective-permute-done.5.refs_0_), channel_id=1, source_target_pairs={{0,3},{1,2},{2,1},{3,0},{4,7},{5,6},{6,5},{7,4},{8,11},{9,10},{10,... | collective-permute-start | bytes 393224 | tf_op jit(solution)/shard_map/ppermute | solution.py:456
  26.3 4.2 %collective-permute-start.12 = (bf16[128,512]{1,0:T(8,128)(2,1)S(1)}, bf16[128,512]{1,0:T(8,128)(2,1)S(1)}, u32[]{:S(2)}, u32[]{:S(2)}) collective-permute-start(bf16[128,512]{1,0:T(8,128)(2,1)S(1)} %collective-permute-done.5.refs_0_), channel_id=1, source_target_pairs={{0,1},{1,0},{2,3},{3,2},{4,5},{5,4},{6,7},{7,6},{8,9},{9,8},{10,11... | collective-permute-start | bytes 393224 | tf_op jit(solution)/shard_map/ppermute | solution.py:456
  29.7 1.3 %collective-permute-start.13 = (bf16[128,512]{1,0:T(8,128)(2,1)S(1)}, bf16[128,512]{1,0:T(8,128)(2,1)S(1)}, u32[]{:S(2)}, u32[]{:S(2)}) collective-permute-start(bf16[128,512]{1,0:T(8,128)(2,1)S(1)} %collective-permute-done.9.refs_2_), channel_id=1, source_target_pairs={{0,1},{1,0},{2,3},{3,2},{4,5},{5,4},{6,7},{7,6},{8,9},{9,8},{10,11... | collective-permute-start | bytes 393224 | tf_op jit(solution)/shard_map/ppermute | solution.py:456
  30.0 2.3 %collective-permute-start.11 = (bf16[128,512]{1,0:T(8,128)(2,1)S(1)}, bf16[128,512]{1,0:T(8,128)(2,1)S(1)}, u32[]{:S(2)}, u32[]{:S(2)}) collective-permute-start(bf16[128,512]{1,0:T(8,128)(2,1)S(1)} %collective-permute-done.10.refs_3_), channel_id=1, source_target_pairs={{0,1},{1,0},{2,3},{3,2},{4,5},{5,4},{6,7},{7,6},{8,9},{9,8},{10,11... | collective-permute-start | bytes 393224 | tf_op jit(solution)/shard_map/ppermute | solution.py:456
  30.3 2.0 %collective-permute-start.8 = (bf16[128,512]{1,0:T(8,128)(2,1)S(1)}, bf16[128,512]{1,0:T(8,128)(2,1)S(1)}, u32[]{:S(2)}, u32[]{:S(2)}) collective-permute-start(bf16[128,512]{1,0:T(8,128)(2,1)S(1)} %collective-permute-done.7.refs_1_), channel_id=1, source_target_pairs={{0,1},{1,0},{2,3},{3,2},{4,5},{5,4},{6,7},{7,6},{8,9},{9,8},{10,11... | collective-permute-start | bytes 393224 | tf_op jit(solution)/shard_map/ppermute | solution.py:456
  32.8 3.4 %collective-permute-start.14 = (bf16[128,128]{1,0:T(8,128)(2,1)S(1)}, bf16[128,128]{1,0:T(8,128)(2,1)S(1)}, u32[]{:S(2)}, u32[]{:S(2)}) collective-permute-start(bf16[128,128]{1,0:T(8,128)(2,1)S(1)} %get-tuple-element.88), channel_id=1, source_target_pairs={{0,3},{1,2},{2,1},{3,0},{4,7},{5,6},{6,5},{7,4},{8,11},{9,10},{10,... | collective-permute-start | bytes 98312 | tf_op jit(solution)/shard_map/ppermute | solution.py:456

commit v9 on v8

--- a/solution.py
+++ b/solution.py
@@ -515,13 +515,14 @@
         a2 = moved(a1, 0, 3)
         a0 = moved(a1, 0, 1)
         state = more_blocks([a1], [place(1)], gain, wq, wkvs, [])
-        b2, b1, *state = lax.optimization_barrier((b2, b1, *state))
+        b1, *state = lax.optimization_barrier((b1, *state))
+        b0 = moved(b1, 0, 1)
+        state = more_blocks([b1], [place(1, split)], gain, wq, wkvs, state)
+        b2, *state = lax.optimization_barrier((b2, *state))
         b3 = moved(b2, 0, 1)
-        b0 = moved(b1, 0, 1)
         a3 = moved(a2, 0, 1)
-        places = [place(0), place(2), *(place(flip, split) for flip in (2, 1, 3))]
-        state = more_blocks([a0, a2, b2, b1, b3], places, gain, wq, wkvs, state)
-        last, places = [a3, b0], [place(3), place(0, split)]
+        state = more_blocks([a0, a2, b2], [place(0), place(2), place(2, split)], gain, wq, wkvs, state)
+        last, places = [a3, b0, b3], [place(3), place(0, split), place(3, split)]
         mine = [a0, b0]
     else:
         mine = [moved(sent, 1, 0)]

time: 37.7 us -> 36.8 us (0.976)
  waiting for transfers between devices: 9.11 us -> 7.23 us
  starting transfers between devices: 15.4 us -> 16.3 us
    ppermute x15, waiting for transfers between devices: 9.11 us -> 7.23 us  [moved(): return lax.ppermute(array, ('section', 'head'), pairs)]
    ppermute x15, starting transfers between devices: 15.4 us -> 16.3 us  [moved(): return lax.ppermute(array, ('section', 'head'), pairs)]
    pallas_call x3 -> x4, Pallas kernels: 2.72 us -> 2.69 us  [more_blocks(): pl.pallas_call(functools.partial(blocks_kernel, len(xs), len(wkvs), len(s...]
  transfers between devices with their start and end apart: 15 -> 15, of which waited for: 9 -> 9; matrix products, arithmetic and copies ran while one was open for 0% -> 0% of each run, Pallas kernels for 28% -> 29%
where the time goes in v9:
time: 36.8 us; the launch traced here: 36.7 us
  starting transfers between devices  16.3 us (44%)
  Pallas kernels  13.1 us (36%)
  waiting for transfers between devices  7.23 us (20%)
    ppermute x15, starting transfers between devices, moved(): return lax.ppermute(array, ('section', 'head'), pairs)  16.3 us
    ppermute x15, waiting for transfers between devices, moved(): return lax.ppermute(array, ('section', 'head'), pairs)  7.23 us
    pallas_call x1, Pallas kernels, load(): pl.pallas_call(functools.partial(load_kernel, n, flips, parts), out_shape...  4.24 us
    pallas_call x4, Pallas kernels, more_blocks(): pl.pallas_call(functools.partial(blocks_kernel, len(xs), len(wkvs), len(s...  2.69 us
    pallas_call x1, Pallas kernels, second_attend(): pl.pallas_call(functools.partial(second_attend_kernel, sections, flips, p...  1.32 us
    pallas_call x2, Pallas kernels, last_kv(): pl.pallas_call(functools.partial(last_kv_kernel, len(xs), len(wkvs), plac...  1.1 us
    pallas_call x2, Pallas kernels, last_q(): pl.pallas_call(functools.partial(last_q_kernel, len(xs), places), out_sha...  1.05 us
    pallas_call x2, Pallas kernels, first_attend(): pl.pallas_call(functools.partial(first_attend_kernel, sections, heads, fl...  0.96 us
  transfers between devices with their start and end apart: 15, of which 9 were waited for; matrix products, arithmetic and copies ran while one was open for 0% of the time, Pallas kernels for 29%

profile of v9, /device:TPU:0, one launch (start us, length us, event | category | flops | bytes accessed | tf_op | source)
XLA Modules:
  0.0 36.7 jit_solution(13549996162694005571)
XLA Ops:
  0.0 2.4 %collective-permute-start = (bf16[128,1024]{1,0:T(8,128)(2,1)}, bf16[128,1024]{1,0:T(8,128)(2,1)S(1)}, u32[]{:S(2)}, u32[]{:S(2)}) collective-permute-start(bf16[128,1024]{1,0:T(8,128)(2,1)} %bitcast.7), channel_id=1, source_target_pairs={{0,3},{1,2},{2,1},{3,0},{4,7},{5,6},{6,5},{7,4},{8,11},{9,10},{10,... | collective-permute-start | bytes 786440 | tf_op jit(solution)/shard_map/ppermute | solution.py:456
  2.4 0.7 %collective-permute-start.2 = (bf16[128,1024]{1,0:T(8,128)(2,1)}, bf16[128,1024]{1,0:T(8,128)(2,1)S(1)}, u32[]{:S(2)}, u32[]{:S(2)}) collective-permute-start(bf16[128,1024]{1,0:T(8,128)(2,1)} %bitcast.8), channel_id=1, source_target_pairs={{0,1},{1,0},{2,3},{3,2},{4,5},{5,4},{6,7},{7,6},{8,9},{9,8},{10,11... | collective-permute-start | bytes 786440 | tf_op jit(solution)/shard_map/ppermute | solution.py:456
  3.1 0.0 collective-permute-start.3
  3.1 0.0 copy-start.1
  3.1 4.2 %load_and_own_queries.1 = (f32[128,1024]{1,0:T(8,128)S(1)}, bf16[128,1024]{1,0:T(8,128)(2,1)S(1)}, f32[1,4096]{1,0:T(1,128)S(1)}, bf16[4096,1024]{1,0:T(8,128)(2...) custom-call(bf16[128,1024]{1,0:T(8,128)(2,1)} %bitcast.9, f32[1,4096]{1,0:T(1,128)} %gain_hbm.1, ...), custom_call_target="tpu_custom_call" | custom-call | flops 99999997952 | bytes 1000000000 | tf_op jit(solution)/shard_map/load_and_own_queries/pallas_call | solution.py:114
  7.3 0.0 copy-done.1
  7.3 0.6 %openings.1 = (s32[128,128]{1,0:T(8,128)S(1)}, s32[128,128]{1,0:T(8,128)S(1)}) custom-call(s32[9]{0:T(128)S(1)} %copy-done.1), custom_call_target="tpu_custom_call" | custom-call | tf_op jit(solution)/shard_map/openings/pallas_call | solution.py:268
  8.0 1.4 %collective-permute-done.refs_2_.x_ref = bf16[128,1024]{1,0:T(8,128)(2,1)S(1)} collective-permute-done((bf16[128,1024]{1,0:T(8,128)(2,1)}, bf16[128,1024]{1,0:T(8,128)(2,1)S(1)}, u32[]{:S(2)}, u32[]{:S(2)}) %collective-permute-start) | collective-permute-done | bytes 262176 | tf_op jit(solution)/shard_map/ppermute | solution.py:456
  9.4 0.1 collective-permute-start.1
  9.5 0.0 collective-permute-done.2.refs_1_
  9.5 0.0 collective-permute-done.3.refs_6_.refs_3_.refs_4_.refs_5_
  9.5 1.1 %more_blocks.4 = (f32[128,1024]{1,0:T(8,128)S(1)}, f32[128,512]{1,0:T(8,128)S(1)}, f32[128,128]{1,0:T(8,128)S(1)}) custom-call(bf16[128,1024]{1,0:T(8,128)(2,1)S(1)} %get-tuple-element.62.refs_0_.x_ref, bf16[128,1024]{1,0:T(8,128)(2,1)S(1)} %collective-permute-done.2.refs_1_, bf16[128,1024]{1,0:T(8,128)(2,1)S(1)} %collective-permute-done.refs_2_.x_ref, ...), custom_call_target="tpu_custom_call" | custom-call | flops 1207959552 | bytes 786432 | tf_op jit(solution)/shard_map/more_blocks/pallas_call | solution.py:166
  10.7 0.3 collective-permute-done.1.refs_0_
  10.9 0.0 copy-start
  10.9 0.5 %last_keys_values.2 = (f32[128,128]{1,0:T(8,128)S(1)}, bf16[128,128]{1,0:T(8,128)(2,1)S(1)}, bf16[128,128]{1,0:T(8,128)(2,1)S(1)}) custom-call(bf16[128,1024]{1,0:T(8,128)(2,1)S(1)} %collective-permute-done.1.refs_0_, f32[1,4096]{1,0:T(1,128)S(1)} %get-tuple-element.60.refs_3_.refs_1_, ...), custom_call_target="tpu_custom_call" | custom-call | flops 134217728 | bytes 262144 | tf_op jit(solution)/shard_map/last_keys_values/pallas_call | solution.py:204
  11.5 2.2 %collective-permute-start.4 = (bf16[128,128]{1,0:T(8,128)(2,1)S(1)}, bf16[128,128]{1,0:T(8,128)(2,1)S(1)}, u32[]{:S(2)}, u32[]{:S(2)}) collective-permute-start(bf16[128,128]{1,0:T(8,128)(2,1)S(1)} %get-tuple-element.71.piece_ref), channel_id=1, source_target_pairs={{0,3},{1,2},{2,1},{3,0},{4,7},{5,6},{6,5},{7,4},{8,11},{9,10},{10,... | collective-permute-start | bytes 98312 | tf_op jit(solution)/shard_map/ppermute | solution.py:456
  13.7 0.0 copy-done
  13.7 0.5 %last_queries.2 = (bf16[128,1024]{1,0:T(8,128)(2,1)S(1)}, bf16[128,640]{1,0:T(8,128)(2,1)S(1)}) custom-call(bf16[128,1024]{1,0:T(8,128)(2,1)S(1)} %collective-permute-done.1.refs_0_, f32[1,4096]{1,0:T(1,128)S(1)} %get-tuple-element.60.refs_3_.refs_1_, bf16[4096,1024]{1,0:T(8,128)(2,1)S(1)} %get-tuple-element.61.refs_4_.refs_2_, ...), custom_call_target="tpu_custom_call" | custom-call | flops 268435456 | bytes 262144 | tf_op jit(solution)/shard_map/last_queries/pallas_call | solution.py:243
  14.1 0.4 %collective-permute-start.6 = (bf16[128,640]{1,0:T(8,128)(2,1)S(1)}, bf16[128,640]{1,0:T(8,128)(2,1)S(1)}, u32[]{:S(2)}, u32[]{:S(2)}) collective-permute-start(bf16[128,640]{1,0:T(8,128)(2,1)S(1)} %get-tuple-element.73), channel_id=1, source_target_pairs={{0,3},{1,2},{2,1},{3,0},{4,7},{5,6},{6,5},{7,4},{8,11},{9,10},{10,... | collective-permute-start | bytes 491528 | tf_op jit(solution)/shard_map/ppermute | solution.py:456
  14.6 0.7 %collective-permute-done.4.refs_1_ = bf16[128,128]{1,0:T(8,128)(2,1)S(1)} collective-permute-done((bf16[128,128]{1,0:T(8,128)(2,1)S(1)}, bf16[128,128]{1,0:T(8,128)(2,1)S(1)}, u32[]{:S(2)}, u32[]{:S(2)}) %collective-permute-start.4) | collective-permute-done | bytes 32800 | tf_op jit(solution)/shard_map/ppermute | solution.py:456
  15.3 0.5 %first_attend.2 = (bf16[128,512]{1,0:T(8,128)(2,1)S(1)}, bf16[128,128]{1,0:T(8,128)(2,1)S(1)}, bf16[128,128]{1,0:T(8,128)(2,1)S(1)}) custom-call(s32[128,128]{1,0:T(8,128)S(1)} %get-tuple-element.58.opened_ref, bf16[128,1024]{1,0:T(8,128)(2,1)S(1)} %get-tuple-element.70.q_ref, bf16[128,1024]{1,0:T(8,128)(2,1)S(1)} %get-tuple-element.62.refs_0_.x_ref, ...), custom_call_target="tpu_custom_call" | custom-call | flops 10000000000 | bytes 1000 | tf_op jit(solution)/shard_map/first_attend/pallas_call | solution.py:370
  15.8 1.7 %collective-permute-start.5 = (bf16[128,512]{1,0:T(8,128)(2,1)S(1)}, bf16[128,512]{1,0:T(8,128)(2,1)S(1)}, u32[]{:S(2)}, u32[]{:S(2)}) collective-permute-start(bf16[128,512]{1,0:T(8,128)(2,1)S(1)} %get-tuple-element.72), channel_id=1, source_target_pairs={{0,5},{1,4},{2,7},{3,6},{4,9},{5,8},{6,11},{7,10},{8,13},{9,12},{1... | collective-permute-start | bytes 393224 | tf_op jit(solution)/shard_map/ppermute | solution.py:456
  17.5 0.5 %first_attend.3 = bf16[128,512]{1,0:T(8,128)(2,1)S(1)} custom-call(s32[128,128]{1,0:T(8,128)S(1)} %get-tuple-element.58.opened_ref, bf16[128,1024]{1,0:T(8,128)(2,1)S(1)} %get-tuple-element.70.q_ref, bf16[128,1024]{1,0:T(8,128)(2,1)S(1)} %get-tuple-element.62.refs_0_.x_ref, bf16[128,1024]{1,0:T(8,128)(2,1)S(1)} %copy-done, ...), custom_call_target="tpu_custom_call" | custom-call | flops 10000000000 | bytes 1000 | tf_op jit(solution)/shard_map/first_attend/pallas_call | solution.py:370
  17.9 1.6 %collective-permute-start.9 = (bf16[128,512]{1,0:T(8,128)(2,1)S(1)}, bf16[128,512]{1,0:T(8,128)(2,1)S(1)}, u32[]{:S(2)}, u32[]{:S(2)}) collective-permute-start(bf16[128,512]{1,0:T(8,128)(2,1)S(1)} %first_attend.3), channel_id=1, source_target_pairs={{0,5},{1,4},{2,7},{3,6},{4,9},{5,8},{6,11},{7,10},{8,13},{9,12},{1... | collective-permute-start | bytes 393224 | tf_op jit(solution)/shard_map/ppermute | solution.py:456
  19.5 0.7 %collective-permute-done.6.bundle_ref = bf16[128,640]{1,0:T(8,128)(2,1)S(1)} collective-permute-done((bf16[128,640]{1,0:T(8,128)(2,1)S(1)}, bf16[128,640]{1,0:T(8,128)(2,1)S(1)}, u32[]{:S(2)}, u32[]{:S(2)}) %collective-permute-start.6) | collective-permute-done | bytes 163872 | tf_op jit(solution)/shard_map/ppermute | solution.py:456
  20.2 0.5 %peer_attend.1 = bf16[128,512]{1,0:T(8,128)(2,1)S(1)} custom-call(s32[128,128]{1,0:T(8,128)S(1)} %get-tuple-element.58.opened_ref, bf16[128,640]{1,0:T(8,128)(2,1)S(1)} %collective-permute-done.6.bundle_ref, bf16[128,1024]{1,0:T(8,128)(2,1)S(1)} %collective-permute-done.refs_2_.x_ref, bf16[128,128]{1,0:T(8,128)(2,1)S(1)} %get-tuple-element.71.piece_ref), custom_call_target="tpu_custom_call" | custom-call | flops 1000 | bytes 1000 | tf_op jit(solution)/shard_map/peer_attend/pallas_call | solution.py:328
  20.7 1.7 %collective-permute-start.11 = (bf16[128,512]{1,0:T(8,128)(2,1)S(1)}, bf16[128,512]{1,0:T(8,128)(2,1)S(1)}, u32[]{:S(2)}, u32[]{:S(2)}) collective-permute-start(bf16[128,512]{1,0:T(8,128)(2,1)S(1)} %peer_attend.1), channel_id=1, source_target_pairs={{0,5},{1,4},{2,7},{3,6},{4,9},{5,8},{6,11},{7,10},{8,13},{9,12},{1... | collective-permute-start | bytes 393224 | tf_op jit(solution)/shard_map/ppermute | solution.py:456
  22.5 1.6 %collective-permute-done.5.refs_0_ = bf16[128,512]{1,0:T(8,128)(2,1)S(1)} collective-permute-done((bf16[128,512]{1,0:T(8,128)(2,1)S(1)}, bf16[128,512]{1,0:T(8,128)(2,1)S(1)}, u32[]{:S(2)}, u32[]{:S(2)}) %collective-permute-start.5) | collective-permute-done | bytes 131104 | tf_op jit(solution)/shard_map/ppermute | solution.py:456
  24.1 2.2 %collective-permute-start.7 = (bf16[128,512]{1,0:T(8,128)(2,1)S(1)}, bf16[128,512]{1,0:T(8,128)(2,1)S(1)}, u32[]{:S(2)}, u32[]{:S(2)}) collective-permute-start(bf16[128,512]{1,0:T(8,128)(2,1)S(1)} %collective-permute-done.5.refs_0_), channel_id=1, source_target_pairs={{0,3},{1,2},{2,1},{3,0},{4,7},{5,6},{6,5},{7,4},{8,11},{9,10},{10,... | collective-permute-start | bytes 393224 | tf_op jit(solution)/shard_map/ppermute | solution.py:456
  26.3 0.0 collective-permute-start.13
  26.3 0.4 %more_blocks.5 = (f32[128,1024]{1,0:T(8,128)S(1)}, f32[128,512]{1,0:T(8,128)S(1)}, f32[128,128]{1,0:T(8,128)S(1)}) custom-call(bf16[128,512]{1,0:T(8,128)(2,1)S(1)} %collective-permute-done.5.refs_0_, f32[1,4096]{1,0:T(1,128)S(1)} %get-tuple-element.60.refs_3_.refs_1_, bf16[4096,1024]{1,0:T(8,128)(2,1)S(1)} %get-tuple-element.61.refs_4_.refs_2_, ...), custom_call_target="tpu_custom_call" | custom-call | flops 201326592 | bytes 131072 | tf_op jit(solution)/shard_map/more_blocks/pallas_call | solution.py:166
  26.7 0.2 collective-permute-done.9.refs_0_
  26.9 1.0 %collective-permute-start.10 = (bf16[128,512]{1,0:T(8,128)(2,1)S(1)}, bf16[128,512]{1,0:T(8,128)(2,1)S(1)}, u32[]{:S(2)}, u32[]{:S(2)}) collective-permute-start(bf16[128,512]{1,0:T(8,128)(2,1)S(1)} %collective-permute-done.9.refs_0_), channel_id=1, source_target_pairs={{0,1},{1,0},{2,3},{3,2},{4,5},{5,4},{6,7},{7,6},{8,9},{9,8},{10,11... | collective-permute-start | bytes 393224 | tf_op jit(solution)/shard_map/ppermute | solution.py:456
  28.0 0.4 %more_blocks.6 = (f32[128,1024]{1,0:T(8,128)S(1)}, f32[128,512]{1,0:T(8,128)S(1)}, f32[128,128]{1,0:T(8,128)S(1)}) custom-call(bf16[128,512]{1,0:T(8,128)(2,1)S(1)} %collective-permute-done.9.refs_0_, f32[1,4096]{1,0:T(1,128)S(1)} %get-tuple-element.60.refs_3_.refs_1_, bf16[4096,1024]{1,0:T(8,128)(2,1)S(1)} %get-tuple-element.61.refs_4_.refs_2_, ...), custom_call_target="tpu_custom_call" | custom-call | flops 201326592 | bytes 131072 | tf_op jit(solution)/shard_map/more_blocks/pallas_call | solution.py:166
  28.3 1.4 %collective-permute-done.11.refs_2_ = bf16[128,512]{1,0:T(8,128)(2,1)S(1)} collective-permute-done((bf16[128,512]{1,0:T(8,128)(2,1)S(1)}, bf16[128,512]{1,0:T(8,128)(2,1)S(1)}, u32[]{:S(2)}, u32[]{:S(2)}) %collective-permute-start.11) | collective-permute-done | bytes 131104 | tf_op jit(solution)/shard_map/ppermute | solution.py:456
  29.7 0.3 collective-permute-start.12
  30.0 0.0 collective-permute-done.7.refs_1_
  30.0 0.2 collective-permute-start.8
  30.3 0.0 collective-permute-done.13.refs_0_
  30.3 0.8 %more_blocks.7 = (f32[128,1024]{1,0:T(8,128)S(1)}, f32[128,512]{1,0:T(8,128)S(1)}, f32[128,128]{1,0:T(8,128)S(1)}) custom-call(bf16[128,512]{1,0:T(8,128)(2,1)S(1)} %collective-permute-done.13.refs_0_, bf16[128,512]{1,0:T(8,128)(2,1)S(1)} %collective-permute-done.7.refs_1_, bf16[128,512]{1,0:T(8,128)(2,1)S(1)} %collective-permute-done.11.refs_2_, ...), custom_call_target="tpu_custom_call" | custom-call | flops 603979776 | bytes 393216 | tf_op jit(solution)/shard_map/more_blocks/pallas_call | solution.py:166
  31.1 0.0 collective-permute-done.10.refs_1_
  31.1 0.0 collective-permute-done.12.refs_2_
  31.1 0.3 collective-permute-done.8.refs_0_
  31.4 0.6 %last_keys_values.3 = (f32[128,128]{1,0:T(8,128)S(1)}, bf16[128,128]{1,0:T(8,128)(2,1)S(1)}, bf16[128,128]{1,0:T(8,128)(2,1)S(1)}) custom-call(bf16[128,512]{1,0:T(8,128)(2,1)S(1)} %collective-permute-done.8.refs_0_, bf16[128,512]{1,0:T(8,128)(2,1)S(1)} %collective-permute-done.10.refs_1_, bf16[128,512]{1,0:T(8,128)(2,1)S(1)} %collective-permute-done.12.refs_2_, ...), custom_call_target="tpu_custom_call" | custom-call | flops 201326592 | bytes 393216 | tf_op jit(solution)/shard_map/last_keys_values/pallas_call | solution.py:204
  32.0 1.8 %collective-permute-start.14 = (bf16[128,128]{1,0:T(8,128)(2,1)S(1)}, bf16[128,128]{1,0:T(8,128)(2,1)S(1)}, u32[]{:S(2)}, u32[]{:S(2)}) collective-permute-start(bf16[128,128]{1,0:T(8,128)(2,1)S(1)} %get-tuple-element.100), channel_id=1, source_target_pairs={{0,3},{1,2},{2,1},{3,0},{4,7},{5,6},{6,5},{7,4},{8,11},{9,10},{10,... | collective-permute-start | bytes 98312 | tf_op jit(solution)/shard_map/ppermute | solution.py:456
  33.7 0.6 %last_queries.3.q_ref = bf16[128,1024]{1,0:T(8,128)(2,1)S(1)} custom-call(bf16[128,512]{1,0:T(8,128)(2,1)S(1)} %collective-permute-done.8.refs_0_, bf16[128,512]{1,0:T(8,128)(2,1)S(1)} %collective-permute-done.10.refs_1_, bf16[128,512]{1,0:T(8,128)(2,1)S(1)} %collective-permute-done.12.refs_2_, f32[1,4096]{1,0:T(1,128)S(1)} %get-tuple-element.60.refs_3_.refs_1_, ...), custom_call_target="tpu_custom_call" | custom-call | flops 402653184 | bytes 393216 | tf_op jit(solution)/shard_map/last_queries/pallas_call | solution.py:243
  34.3 0.6 %resident_attend.1 = (f32[1024,128]{1,0:T(8,128)S(1)}, f32[1024,128]{1,0:T(8,128)S(1)}, f32[1024,128]{1,0:T(8,128)S(1)}) custom-call(s32[128,128]{1,0:T(8,128)S(1)} %get-tuple-element.57.opened_ref, bf16[128,1024]{1,0:T(8,128)(2,1)S(1)} %last_queries.3.q_ref, bf16[128,128]{1,0:T(8,128)(2,1)S(1)} %get-tuple-element.74.refs_0_.keys_ref, ...), custom_call_target="tpu_custom_call" | custom-call | flops 1000 | bytes 1000 | tf_op jit(solution)/shard_map/resident_attend/pallas_call | solution.py:395
  34.9 0.5 %collective-permute-done.14.refs_3_ = bf16[128,128]{1,0:T(8,128)(2,1)S(1)} collective-permute-done((bf16[128,128]{1,0:T(8,128)(2,1)S(1)}, bf16[128,128]{1,0:T(8,128)(2,1)S(1)}, u32[]{:S(2)}, u32[]{:S(2)}) %collective-permute-start.14) | collective-permute-done | bytes 32800 | tf_op jit(solution)/shard_map/ppermute | solution.py:456
  35.4 1.3 %second_attend.1 = bf16[128,1024]{1,0:T(8,128)(2,1)} custom-call(s32[128,128]{1,0:T(8,128)S(1)} %get-tuple-element.57.opened_ref, bf16[128,1024]{1,0:T(8,128)(2,1)S(1)} %last_queries.3.q_ref, f32[1024,128]{1,0:T(8,128)S(1)} %get-tuple-element.96.max_ref, f32[1024,128]{1,0:T(8,128)S(1)} %get-tuple-element.97.sum_ref, ...), custom_call_target="tpu_custom_call" | custom-call | flops 1000 | bytes 1000 | tf_op jit(solution)/shard_map/second_attend/pallas_call | solution.py:429
Async XLA Ops:
  0.0 9.4 %collective-permute-start = (bf16[128,1024]{1,0:T(8,128)(2,1)}, bf16[128,1024]{1,0:T(8,128)(2,1)S(1)}, u32[]{:S(2)}, u32[]{:S(2)}) collective-permute-start(bf16[128,1024]{1,0:T(8,128)(2,1)} %bitcast.7), channel_id=1, source_target_pairs={{0,3},{1,2},{2,1},{3,0},{4,7},{5,6},{6,5},{7,4},{8,11},{9,10},{10,... | collective-permute-start | bytes 786440 | tf_op jit(solution)/shard_map/ppermute | solution.py:456
  2.4 7.1 %collective-permute-start.2 = (bf16[128,1024]{1,0:T(8,128)(2,1)}, bf16[128,1024]{1,0:T(8,128)(2,1)S(1)}, u32[]{:S(2)}, u32[]{:S(2)}) collective-permute-start(bf16[128,1024]{1,0:T(8,128)(2,1)} %bitcast.8), channel_id=1, source_target_pairs={{0,1},{1,0},{2,3},{3,2},{4,5},{5,4},{6,7},{7,6},{8,9},{9,8},{10,11... | collective-permute-start | bytes 786440 | tf_op jit(solution)/shard_map/ppermute | solution.py:456
  3.1 6.4 %collective-permute-start.3 = (bf16[4096,256]{1,0:T(8,128)(2,1)}, bf16[4096,256]{1,0:T(8,128)(2,1)S(1)}, u32[]{:S(2)}, u32[]{:S(2)}) collective-permute-start(bf16[4096,256]{1,0:T(8,128)(2,1)} %bitcast.5), channel_id=1, source_target_pairs={{0,1},{1,0},{2,3},{3,2},{4,5},{5,4},{6,7},{7,6},{8,9},{9,8},{10,11... | collective-permute-start | bytes 6291464 | tf_op jit(solution)/shard_map/ppermute | solution.py:456
  3.1 4.3 %copy-start.1 = (s32[9]{0:T(128)S(1)}, s32[9]{0:T(128)}, u32[]{:S(2)}) copy-start(s32[9]{0:T(128)} %doc_ref) | copy-start | bytes 112
  9.4 1.5 %collective-permute-start.1 = (bf16[128,1024]{1,0:T(8,128)(2,1)S(1)}, bf16[128,1024]{1,0:T(8,128)(2,1)S(1)}, u32[]{:S(2)}, u32[]{:S(2)}) collective-permute-start(bf16[128,1024]{1,0:T(8,128)(2,1)S(1)} %collective-permute-done.refs_2_.x_ref), channel_id=1, source_target_pairs={{0,1},{1,0},{2,3},{3,2},{4,5},{5,4},{6,7},{7,6},{8,9},{9,8},{10,11... | collective-permute-start | bytes 786440 | tf_op jit(solution)/shard_map/ppermute | solution.py:456
  10.9 2.7 %copy-start = (bf16[128,1024]{1,0:T(8,128)(2,1)S(1)}, bf16[128,1024]{1,0:T(8,128)(2,1)}, u32[]{:S(2)}) copy-start(bf16[128,1024]{1,0:T(8,128)(2,1)} %fresh_ref.3) | copy-start | bytes 786436
  11.5 3.8 %collective-permute-start.4 = (bf16[128,128]{1,0:T(8,128)(2,1)S(1)}, bf16[128,128]{1,0:T(8,128)(2,1)S(1)}, u32[]{:S(2)}, u32[]{:S(2)}) collective-permute-start(bf16[128,128]{1,0:T(8,128)(2,1)S(1)} %get-tuple-element.71.piece_ref), channel_id=1, source_target_pairs={{0,3},{1,2},{2,1},{3,0},{4,7},{5,6},{6,5},{7,4},{8,11},{9,10},{10,... | collective-permute-start | bytes 98312 | tf_op jit(solution)/shard_map/ppermute | solution.py:456
  14.1 6.1 %collective-permute-start.6 = (bf16[128,640]{1,0:T(8,128)(2,1)S(1)}, bf16[128,640]{1,0:T(8,128)(2,1)S(1)}, u32[]{:S(2)}, u32[]{:S(2)}) collective-permute-start(bf16[128,640]{1,0:T(8,128)(2,1)S(1)} %get-tuple-element.73), channel_id=1, source_target_pairs={{0,3},{1,2},{2,1},{3,0},{4,7},{5,6},{6,5},{7,4},{8,11},{9,10},{10,... | collective-permute-start | bytes 491528 | tf_op jit(solution)/shard_map/ppermute | solution.py:456
  15.8 8.4 %collective-permute-start.5 = (bf16[128,512]{1,0:T(8,128)(2,1)S(1)}, bf16[128,512]{1,0:T(8,128)(2,1)S(1)}, u32[]{:S(2)}, u32[]{:S(2)}) collective-permute-start(bf16[128,512]{1,0:T(8,128)(2,1)S(1)} %get-tuple-element.72), channel_id=1, source_target_pairs={{0,5},{1,4},{2,7},{3,6},{4,9},{5,8},{6,11},{7,10},{8,13},{9,12},{1... | collective-permute-start | bytes 393224 | tf_op jit(solution)/shard_map/ppermute | solution.py:456
  17.9 9.0 %collective-permute-start.9 = (bf16[128,512]{1,0:T(8,128)(2,1)S(1)}, bf16[128,512]{1,0:T(8,128)(2,1)S(1)}, u32[]{:S(2)}, u32[]{:S(2)}) collective-permute-start(bf16[128,512]{1,0:T(8,128)(2,1)S(1)} %first_attend.3), channel_id=1, source_target_pairs={{0,5},{1,4},{2,7},{3,6},{4,9},{5,8},{6,11},{7,10},{8,13},{9,12},{1... | collective-permute-start | bytes 393224 | tf_op jit(solution)/shard_map/ppermute | solution.py:456
  20.7 9.0 %collective-permute-start.11 = (bf16[128,512]{1,0:T(8,128)(2,1)S(1)}, bf16[128,512]{1,0:T(8,128)(2,1)S(1)}, u32[]{:S(2)}, u32[]{:S(2)}) collective-permute-start(bf16[128,512]{1,0:T(8,128)(2,1)S(1)} %peer_attend.1), channel_id=1, source_target_pairs={{0,5},{1,4},{2,7},{3,6},{4,9},{5,8},{6,11},{7,10},{8,13},{9,12},{1... | collective-permute-start | bytes 393224 | tf_op jit(solution)/shard_map/ppermute | solution.py:456
  24.1 5.9 %collective-permute-start.7 = (bf16[128,512]{1,0:T(8,128)(2,1)S(1)}, bf16[128,512]{1,0:T(8,128)(2,1)S(1)}, u32[]{:S(2)}, u32[]{:S(2)}) collective-permute-start(bf16[128,512]{1,0:T(8,128)(2,1)S(1)} %collective-permute-done.5.refs_0_), channel_id=1, source_target_pairs={{0,3},{1,2},{2,1},{3,0},{4,7},{5,6},{6,5},{7,4},{8,11},{9,10},{10,... | collective-permute-start | bytes 393224 | tf_op jit(solution)/shard_map/ppermute | solution.py:456
  26.3 4.0 %collective-permute-start.13 = (bf16[128,512]{1,0:T(8,128)(2,1)S(1)}, bf16[128,512]{1,0:T(8,128)(2,1)S(1)}, u32[]{:S(2)}, u32[]{:S(2)}) collective-permute-start(bf16[128,512]{1,0:T(8,128)(2,1)S(1)} %collective-permute-done.5.refs_0_), channel_id=1, source_target_pairs={{0,1},{1,0},{2,3},{3,2},{4,5},{5,4},{6,7},{7,6},{8,9},{9,8},{10,11... | collective-permute-start | bytes 393224 | tf_op jit(solution)/shard_map/ppermute | solution.py:456
  26.9 4.1 %collective-permute-start.10 = (bf16[128,512]{1,0:T(8,128)(2,1)S(1)}, bf16[128,512]{1,0:T(8,128)(2,1)S(1)}, u32[]{:S(2)}, u32[]{:S(2)}) collective-permute-start(bf16[128,512]{1,0:T(8,128)(2,1)S(1)} %collective-permute-done.9.refs_0_), channel_id=1, source_target_pairs={{0,1},{1,0},{2,3},{3,2},{4,5},{5,4},{6,7},{7,6},{8,9},{9,8},{10,11... | collective-permute-start | bytes 393224 | tf_op jit(solution)/shard_map/ppermute | solution.py:456
  29.7 1.3 %collective-permute-start.12 = (bf16[128,512]{1,0:T(8,128)(2,1)S(1)}, bf16[128,512]{1,0:T(8,128)(2,1)S(1)}, u32[]{:S(2)}, u32[]{:S(2)}) collective-permute-start(bf16[128,512]{1,0:T(8,128)(2,1)S(1)} %collective-permute-done.11.refs_2_), channel_id=1, source_target_pairs={{0,1},{1,0},{2,3},{3,2},{4,5},{5,4},{6,7},{7,6},{8,9},{9,8},{10,11... | collective-permute-start | bytes 393224 | tf_op jit(solution)/shard_map/ppermute | solution.py:456
  30.0 1.3 %collective-permute-start.8 = (bf16[128,512]{1,0:T(8,128)(2,1)S(1)}, bf16[128,512]{1,0:T(8,128)(2,1)S(1)}, u32[]{:S(2)}, u32[]{:S(2)}) collective-permute-start(bf16[128,512]{1,0:T(8,128)(2,1)S(1)} %collective-permute-done.7.refs_1_), channel_id=1, source_target_pairs={{0,1},{1,0},{2,3},{3,2},{4,5},{5,4},{6,7},{7,6},{8,9},{9,8},{10,11... | collective-permute-start | bytes 393224 | tf_op jit(solution)/shard_map/ppermute | solution.py:456
  32.0 3.4 %collective-permute-start.14 = (bf16[128,128]{1,0:T(8,128)(2,1)S(1)}, bf16[128,128]{1,0:T(8,128)(2,1)S(1)}, u32[]{:S(2)}, u32[]{:S(2)}) collective-permute-start(bf16[128,128]{1,0:T(8,128)(2,1)S(1)} %get-tuple-element.100), channel_id=1, source_target_pairs={{0,3},{1,2},{2,1},{3,0},{4,7},{5,6},{6,5},{7,4},{8,11},{9,10},{10,... | collective-permute-start | bytes 98312 | tf_op jit(solution)/shard_map/ppermute | solution.py:456

commit v10 on v9

--- a/solution.py
+++ b/solution.py
@@ -76,9 +76,52 @@
                 choose_ref[i, first : first + features, :] = jnp.where(offset == wanted, 1.0, 0.0)
 
 
+def paired_selection(me, columns):
+    row = lax.broadcasted_iota(jnp.int32, (columns, columns // 2), 0)
+    col = lax.broadcasted_iota(jnp.int32, (columns, columns // 2), 1)
+    quarter = columns // 8
+    piece, which = col // (2 * quarter), col // quarter % 2
+    group = lax.bitwise_xor(3 * piece, jnp.broadcast_to(me, col.shape))
+    return jnp.where(row == col % quarter * (2 * KVH) + group * 2 + which, 1.0, 0.0).astype(bf16)
+
+
+def select_into(out_ref, wkv_ref, me):
+    select = paired_selection(me, wkv_ref.shape[1])
+    size = wkv_ref.shape[0] // 4
+    for first in range(0, wkv_ref.shape[0], size):
+        out_ref[first : first + size, :] = dot(wkv_ref[first : first + size, :], select).astype(bf16)
+
+
+def select_kernel(wkv_ref, out_ref):
+    select_into(out_ref, wkv_ref, lax.axis_index("head"))
+
+
+def selected(wkv):
+    return pl.pallas_call(
+        select_kernel,
+        out_shape=VMEM((wkv.shape[0], wkv.shape[1] // 2), bf16),
+        in_specs=[vmem],
+        out_specs=vmem,
+        cost_estimate=cost(1000, 1000),
+        compiler_params=params,
+        name="selected_columns",
+    )(*resident_in(wkv))
+
+
+def paired_turn(me, side):
+    row = lax.broadcasted_iota(jnp.int32, (side, side), 0)
+    col = lax.broadcasted_iota(jnp.int32, (side, side), 1)
+    quarter = side // 8
+    piece, which, core = row // (4 * quarter), row // (2 * quarter) % 2, row // quarter % 2
+    whose = lax.bitwise_xor(core, jnp.broadcast_to(lax.rem(me, jnp.int32(2)), core.shape))
+    wanted = whose * (4 * quarter) + piece * (2 * quarter) + which * quarter + row % quarter
+    return jnp.where(col == wanted, 1.0, 0.0)
+
+
 def load_kernel(
-    n, flips, parts, x_hbm, gain_hbm, wq_hbm, wkv_hbm, accq_ref, x_ref, gain_ref, wq_ref, wkv_ref, choose_ref, sems
+    n, flips, parts, x_hbm, gain_hbm, wq_hbm, wkv_hbm, accq_ref, x_ref, gain_ref, wq_ref, choose_ref, *rest
 ):
+    selected_ref, wkv_ref, sems = rest if parts == 2 else (None, *rest)
     width = x_hbm.shape[1]
     me = lax.axis_index("head")
 
@@ -93,18 +136,24 @@
     keys_values = pltpu.make_async_copy(wkv_hbm, wkv_ref, sems.at[n + 2])
     for copy in small:
         copy.start()
+    keys_values.start()
     for step in range(n):
         part(step).start()
-    keys_values.start()
-    choose_rows(choose_ref, me, n, flips, parts)
+    columns = wkv_hbm.shape[1]
+    if parts == 2:
+        choose_ref[0] = paired_turn(me, columns)
+    else:
+        choose_rows(choose_ref, me, n, flips, parts)
     for copy in small:
         copy.wait()
-    normed, _ = gained(x_ref[...], gain_ref, me * width)
+    normed, _ = gained(x_ref[...].astype(f32), gain_ref, me * width)
+    keys_values.wait()
+    if parts == 2:
+        select_into(selected_ref, wkv_ref, me)
     part(0).wait()
     accq_ref[...] = dot(normed, wq_ref[rows_of(me, width), :])
     for step in range(1, n):
         part(step).wait()
-    keys_values.wait()
 
 
 def load(x, gain, wq, wkv, n, flips, parts):
@@ -118,12 +167,12 @@
             VMEM(x.shape, bf16),
             VMEM(gain.shape, f32),
             VMEM(wq.shape, bf16),
-            VMEM(wkv.shape, bf16),
-            VMEM((len(flips), parts * columns // KVH, parts * columns), f32),
-        ),
+            VMEM((1, columns, columns) if parts == 2 else (len(flips), columns // KVH, columns), f32),
+        )
+        + (VMEM((wkv.shape[0], columns // parts), bf16),),
         in_specs=[in_hbm] * 4,
         out_specs=(vmem,) * 6,
-        scratch_shapes=[pltpu.SemaphoreType.DMA((n + 3,))],
+        scratch_shapes=[VMEM(wkv.shape, bf16)] * (parts - 1) + [pltpu.SemaphoreType.DMA((n + 3,))],
         cost_estimate=cost(10**11, 10**9),
         compiler_params=params,
         name="load_and_own_queries",
@@ -192,6 +241,10 @@
     scale = lax.rsqrt(jnp.sum(ssq, axis=1, keepdims=True) / gain_ref.shape[1] + epsilon)
     scale_ref[...] = jnp.broadcast_to(scale, scale_ref.shape)
     kv = jnp.concatenate([(kv * scale).astype(bf16) for kv in kvs], axis=1)
+    if wkv_count == 2:
+        turned = dot_turned(choose_ref[0].astype(bf16), kv).astype(bf16)
+        pieces[0][...], pieces[1][...] = turned[: kv.shape[1] // 2], turned[kv.shape[1] // 2 :]
+        return
     for i, piece in enumerate(pieces):
         piece[...] = dot_turned(choose_ref[i].astype(bf16), kv).astype(bf16)
 
@@ -200,10 +253,10 @@
     tokens = xs[0].shape[0]
     columns = len(wkvs) * wkvs[0].shape[1]
     operands = [*xs, *resident_in(gain, *wkvs, choose), acckv, ssq]
-    count = choose.shape[0]
+    count, size = (2, columns // 2) if len(wkvs) == 2 else choose.shape[:2]
     return pl.pallas_call(
         functools.partial(last_kv_kernel, len(xs), len(wkvs), places),
-        out_shape=(VMEM((tokens, HD), f32),) + (VMEM((columns // KVH, tokens), bf16),) * count,
+        out_shape=(VMEM((tokens, HD), f32),) + (VMEM((size, tokens), bf16),) * count,
         in_specs=[vmem] * len(operands),
         out_specs=(vmem,) * (1 + count),
         cost_estimate=cost(sum(2 * x.size * columns for x in xs), sum(2 * x.size for x in xs)),
@@ -477,11 +530,11 @@
         over = moved(own, 0, 3)
         beside = moved(own, 0, 1)
         w_kv_beside = moved(w_kv, 0, 1)
-    accq, own, gain, wq, wkv, choose = load(own, norm_gain, w_q, w_kv, n, flips, parts)
+    accq, own, gain, wq, choose, wkv = load(own, norm_gain, w_q, w_kv, n, flips, parts)
     opened = openings(after(doc_lengths, accq), tokens, sections)
     if paired:
-        wkvs = [wkv, w_kv_beside]
-        over, *opened = lax.optimization_barrier((over, *opened))
+        wkvs = [wkv, selected(after(w_kv_beside, accq))]
+        over, wkvs[1], *opened = lax.optimization_barrier((over, wkvs[1], *opened))
         passed = moved(over, 0, 1)
         xs, places, with_q = [own, beside, over], [place(0), place(1), place(3)], [False, True, True]
         state = more_blocks(xs, places, gain, wq, wkvs, [accq], with_q)

time: 36.8 us -> 37.4 us (1.016)
  starting transfers between devices: 16.3 us -> 15.1 us
  waiting for transfers between devices: 7.23 us -> 8.22 us
  Pallas kernels: 13.1 us -> 13.8 us
    ppermute x15, starting transfers between devices: 16.3 us -> 15.1 us  [moved(): return lax.ppermute(array, ('section', 'head'), pairs)]
    ppermute x15, waiting for transfers between devices: 7.23 us -> 8.22 us  [moved(): return lax.ppermute(array, ('section', 'head'), pairs)]
    pallas_call x0 -> x1, Pallas kernels: none -> 0.72 us  [selected(): pl.pallas_call(select_kernel, out_shape=VMEM((wkv.shape[0], wkv.shape[1]...]
  transfers between devices with their start and end apart: 15 -> 15, of which waited for: 9 -> 9; matrix products, arithmetic and copies ran while one was open for 0% -> 0% of each run, Pallas kernels for 29% -> 31%
where the time goes in v10:
time: 37.4 us; the launch traced here: 37.3 us
  starting transfers between devices  15.1 us (40%)
  Pallas kernels  13.8 us (37%)
  waiting for transfers between devices  8.22 us (22%)
    ppermute x15, starting transfers between devices, moved(): return lax.ppermute(array, ('section', 'head'), pairs)  15.1 us
    ppermute x15, waiting for transfers between devices, moved(): return lax.ppermute(array, ('section', 'head'), pairs)  8.22 us
    pallas_call x1, Pallas kernels, load(): pl.pallas_call(functools.partial(load_kernel, n, flips, parts), out_shape...  4.24 us
    pallas_call x4, Pallas kernels, more_blocks(): pl.pallas_call(functools.partial(blocks_kernel, len(xs), len(wkvs), len(s...  2.73 us
    pallas_call x1, Pallas kernels, second_attend(): pl.pallas_call(functools.partial(second_attend_kernel, sections, flips, p...  1.32 us
    pallas_call x2, Pallas kernels, last_kv(): pl.pallas_call(functools.partial(last_kv_kernel, len(xs), len(wkvs), plac...  1.07 us
    pallas_call x2, Pallas kernels, last_q(): pl.pallas_call(functools.partial(last_q_kernel, len(xs), places), out_sha...  1.06 us
    pallas_call x2, Pallas kernels, first_attend(): pl.pallas_call(functools.partial(first_attend_kernel, sections, heads, fl...  0.95 us
  transfers between devices with their start and end apart: 15, of which 9 were waited for; matrix products, arithmetic and copies ran while one was open for 0% of the time, Pallas kernels for 31%

profile of v10, /device:TPU:0, one launch (start us, length us, event | category | flops | bytes accessed | tf_op | source)
XLA Modules:
  0.0 37.3 jit_solution(4954257709449602735)
XLA Ops:
  0.0 2.4 %collective-permute-start = (bf16[128,1024]{1,0:T(8,128)(2,1)}, bf16[128,1024]{1,0:T(8,128)(2,1)S(1)}, u32[]{:S(2)}, u32[]{:S(2)}) collective-permute-start(bf16[128,1024]{1,0:T(8,128)(2,1)} %bitcast.7), channel_id=1, source_target_pairs={{0,3},{1,2},{2,1},{3,0},{4,7},{5,6},{6,5},{7,4},{8,11},{9,10},{10,... | collective-permute-start | bytes 786440 | tf_op jit(solution)/shard_map/ppermute | solution.py:509
  2.4 0.7 %collective-permute-start.3 = (bf16[128,1024]{1,0:T(8,128)(2,1)}, bf16[128,1024]{1,0:T(8,128)(2,1)S(1)}, u32[]{:S(2)}, u32[]{:S(2)}) collective-permute-start(bf16[128,1024]{1,0:T(8,128)(2,1)} %bitcast.8), channel_id=1, source_target_pairs={{0,1},{1,0},{2,3},{3,2},{4,5},{5,4},{6,7},{7,6},{8,9},{9,8},{10,11... | collective-permute-start | bytes 786440 | tf_op jit(solution)/shard_map/ppermute | solution.py:509
  3.1 0.0 collective-permute-start.1
  3.1 0.0 copy-start.1
  3.1 4.2 %load_and_own_queries.1 = (f32[128,1024]{1,0:T(8,128)S(1)}, bf16[128,1024]{1,0:T(8,128)(2,1)S(1)}, f32[1,4096]{1,0:T(1,128)S(1)}, bf16[4096,1024]{1,0:T(8,128)(2...) custom-call(bf16[128,1024]{1,0:T(8,128)(2,1)} %bitcast.9, f32[1,4096]{1,0:T(1,128)} %gain_hbm.1, ...), custom_call_target="tpu_custom_call" | custom-call | flops 99999997952 | bytes 1000000000 | tf_op jit(solution)/shard_map/load_and_own_queries/pallas_call | solution.py:163
  7.3 0.0 copy-done.1
  7.3 0.6 %openings.1 = (s32[128,128]{1,0:T(8,128)S(1)}, s32[128,128]{1,0:T(8,128)S(1)}) custom-call(s32[9]{0:T(128)S(1)} %copy-done.1), custom_call_target="tpu_custom_call" | custom-call | tf_op jit(solution)/shard_map/openings/pallas_call | solution.py:321
  8.0 0.0 copy-start
  8.0 0.0 collective-permute-done.1.wkv_ref
  8.0 0.7 %selected_columns.1.refs_6_.refs_3_.refs_4_.refs_5_ = bf16[4096,128]{1,0:T(8,128)(2,1)S(1)} custom-call(bf16[4096,256]{1,0:T(8,128)(2,1)S(1)} %collective-permute-done.1.wkv_ref), custom_call_target="tpu_custom_call" | custom-call | flops 1000 | bytes 1000 | tf_op jit(solution)/shard_map/selected_columns/pallas_call | solution.py:100
  8.7 0.7 %collective-permute-done.refs_2_.x_ref = bf16[128,1024]{1,0:T(8,128)(2,1)S(1)} collective-permute-done((bf16[128,1024]{1,0:T(8,128)(2,1)}, bf16[128,1024]{1,0:T(8,128)(2,1)S(1)}, u32[]{:S(2)}, u32[]{:S(2)}) %collective-permute-start) | collective-permute-done | bytes 262176 | tf_op jit(solution)/shard_map/ppermute | solution.py:509
  9.4 0.1 collective-permute-start.2
  9.5 0.0 collective-permute-done.3.refs_1_
  9.5 1.2 %more_blocks.4 = (f32[128,1024]{1,0:T(8,128)S(1)}, f32[128,256]{1,0:T(8,128)S(1)}, f32[128,128]{1,0:T(8,128)S(1)}) custom-call(bf16[128,1024]{1,0:T(8,128)(2,1)S(1)} %get-tuple-element.65.refs_0_.x_ref, bf16[128,1024]{1,0:T(8,128)(2,1)S(1)} %collective-permute-done.3.refs_1_, bf16[128,1024]{1,0:T(8,128)(2,1)S(1)} %collective-permute-done.refs_2_.x_ref, ...), custom_call_target="tpu_custom_call" | custom-call | flops 1006632960 | bytes 786432 | tf_op jit(solution)/shard_map/more_blocks/pallas_call | solution.py:215
  10.7 0.2 collective-permute-done.2.refs_0_
  10.9 0.5 %last_keys_values.2 = (f32[128,128]{1,0:T(8,128)S(1)}, bf16[128,128]{1,0:T(8,128)(2,1)S(1)}, bf16[128,128]{1,0:T(8,128)(2,1)S(1)}) custom-call(bf16[128,1024]{1,0:T(8,128)(2,1)S(1)} %collective-permute-done.2.refs_0_, f32[1,4096]{1,0:T(1,128)S(1)} %get-tuple-element.63.refs_3_.refs_1_, ...), custom_call_target="tpu_custom_call" | custom-call | flops 67108864 | bytes 262144 | tf_op jit(solution)/shard_map/last_keys_values/pallas_call | solution.py:257
  11.5 2.2 %collective-permute-start.4 = (bf16[128,128]{1,0:T(8,128)(2,1)S(1)}, bf16[128,128]{1,0:T(8,128)(2,1)S(1)}, u32[]{:S(2)}, u32[]{:S(2)}) collective-permute-start(bf16[128,128]{1,0:T(8,128)(2,1)S(1)} %get-tuple-element.75.piece_ref), channel_id=1, source_target_pairs={{0,3},{1,2},{2,1},{3,0},{4,7},{5,6},{6,5},{7,4},{8,11},{9,10},{10,... | collective-permute-start | bytes 98312 | tf_op jit(solution)/shard_map/ppermute | solution.py:509
  13.7 0.0 copy-done
  13.7 0.5 %last_queries.2 = (bf16[128,1024]{1,0:T(8,128)(2,1)S(1)}, bf16[128,640]{1,0:T(8,128)(2,1)S(1)}) custom-call(bf16[128,1024]{1,0:T(8,128)(2,1)S(1)} %collective-permute-done.2.refs_0_, f32[1,4096]{1,0:T(1,128)S(1)} %get-tuple-element.63.refs_3_.refs_1_, bf16[4096,1024]{1,0:T(8,128)(2,1)S(1)} %get-tuple-element.64.refs_4_.refs_2_, ...), custom_call_target="tpu_custom_call" | custom-call | flops 268435456 | bytes 262144 | tf_op jit(solution)/shard_map/last_queries/pallas_call | solution.py:296
  14.2 0.1 collective-permute-start.6
  14.3 1.0 %collective-permute-done.4.refs_1_ = bf16[128,128]{1,0:T(8,128)(2,1)S(1)} collective-permute-done((bf16[128,128]{1,0:T(8,128)(2,1)S(1)}, bf16[128,128]{1,0:T(8,128)(2,1)S(1)}, u32[]{:S(2)}, u32[]{:S(2)}) %collective-permute-start.4) | collective-permute-done | bytes 32800 | tf_op jit(solution)/shard_map/ppermute | solution.py:509
  15.3 0.5 %first_attend.2 = (bf16[128,512]{1,0:T(8,128)(2,1)S(1)}, bf16[128,128]{1,0:T(8,128)(2,1)S(1)}, bf16[128,128]{1,0:T(8,128)(2,1)S(1)}) custom-call(s32[128,128]{1,0:T(8,128)S(1)} %get-tuple-element.61.opened_ref, bf16[128,1024]{1,0:T(8,128)(2,1)S(1)} %get-tuple-element.74.q_ref, bf16[128,1024]{1,0:T(8,128)(2,1)S(1)} %get-tuple-element.65.refs_0_.x_ref, ...), custom_call_target="tpu_custom_call" | custom-call | flops 10000000000 | bytes 1000 | tf_op jit(solution)/shard_map/first_attend/pallas_call | solution.py:423
  15.8 1.7 %collective-permute-start.5 = (bf16[128,512]{1,0:T(8,128)(2,1)S(1)}, bf16[128,512]{1,0:T(8,128)(2,1)S(1)}, u32[]{:S(2)}, u32[]{:S(2)}) collective-permute-start(bf16[128,512]{1,0:T(8,128)(2,1)S(1)} %get-tuple-element.76), channel_id=1, source_target_pairs={{0,5},{1,4},{2,7},{3,6},{4,9},{5,8},{6,11},{7,10},{8,13},{9,12},{1... | collective-permute-start | bytes 393224 | tf_op jit(solution)/shard_map/ppermute | solution.py:509
  17.5 0.5 %first_attend.3 = bf16[128,512]{1,0:T(8,128)(2,1)S(1)} custom-call(s32[128,128]{1,0:T(8,128)S(1)} %get-tuple-element.61.opened_ref, bf16[128,1024]{1,0:T(8,128)(2,1)S(1)} %get-tuple-element.74.q_ref, bf16[128,1024]{1,0:T(8,128)(2,1)S(1)} %get-tuple-element.65.refs_0_.x_ref, bf16[128,1024]{1,0:T(8,128)(2,1)S(1)} %copy-done, ...), custom_call_target="tpu_custom_call" | custom-call | flops 10000000000 | bytes 1000 | tf_op jit(solution)/shard_map/first_attend/pallas_call | solution.py:423
  18.0 1.5 %collective-permute-start.9 = (bf16[128,512]{1,0:T(8,128)(2,1)S(1)}, bf16[128,512]{1,0:T(8,128)(2,1)S(1)}, u32[]{:S(2)}, u32[]{:S(2)}) collective-permute-start(bf16[128,512]{1,0:T(8,128)(2,1)S(1)} %first_attend.3), channel_id=1, source_target_pairs={{0,5},{1,4},{2,7},{3,6},{4,9},{5,8},{6,11},{7,10},{8,13},{9,12},{1... | collective-permute-start | bytes 393224 | tf_op jit(solution)/shard_map/ppermute | solution.py:509
  19.5 0.8 %collective-permute-done.6.bundle_ref = bf16[128,640]{1,0:T(8,128)(2,1)S(1)} collective-permute-done((bf16[128,640]{1,0:T(8,128)(2,1)S(1)}, bf16[128,640]{1,0:T(8,128)(2,1)S(1)}, u32[]{:S(2)}, u32[]{:S(2)}) %collective-permute-start.6) | collective-permute-done | bytes 163872 | tf_op jit(solution)/shard_map/ppermute | solution.py:509
  20.3 0.5 %peer_attend.1 = bf16[128,512]{1,0:T(8,128)(2,1)S(1)} custom-call(s32[128,128]{1,0:T(8,128)S(1)} %get-tuple-element.61.opened_ref, bf16[128,640]{1,0:T(8,128)(2,1)S(1)} %collective-permute-done.6.bundle_ref, bf16[128,1024]{1,0:T(8,128)(2,1)S(1)} %collective-permute-done.refs_2_.x_ref, bf16[128,128]{1,0:T(8,128)(2,1)S(1)} %get-tuple-element.75.piece_ref), custom_call_target="tpu_custom_call" | custom-call | flops 1000 | bytes 1000 | tf_op jit(solution)/shard_map/peer_attend/pallas_call | solution.py:381
  20.8 1.7 %collective-permute-start.11 = (bf16[128,512]{1,0:T(8,128)(2,1)S(1)}, bf16[128,512]{1,0:T(8,128)(2,1)S(1)}, u32[]{:S(2)}, u32[]{:S(2)}) collective-permute-start(bf16[128,512]{1,0:T(8,128)(2,1)S(1)} %peer_attend.1), channel_id=1, source_target_pairs={{0,5},{1,4},{2,7},{3,6},{4,9},{5,8},{6,11},{7,10},{8,13},{9,12},{1... | collective-permute-start | bytes 393224 | tf_op jit(solution)/shard_map/ppermute | solution.py:509
  22.5 1.7 %collective-permute-done.5.refs_0_ = bf16[128,512]{1,0:T(8,128)(2,1)S(1)} collective-permute-done((bf16[128,512]{1,0:T(8,128)(2,1)S(1)}, bf16[128,512]{1,0:T(8,128)(2,1)S(1)}, u32[]{:S(2)}, u32[]{:S(2)}) %collective-permute-start.5) | collective-permute-done | bytes 131104 | tf_op jit(solution)/shard_map/ppermute | solution.py:509
  24.2 2.6 %collective-permute-start.7 = (bf16[128,512]{1,0:T(8,128)(2,1)S(1)}, bf16[128,512]{1,0:T(8,128)(2,1)S(1)}, u32[]{:S(2)}, u32[]{:S(2)}) collective-permute-start(bf16[128,512]{1,0:T(8,128)(2,1)S(1)} %collective-permute-done.5.refs_0_), channel_id=1, source_target_pairs={{0,3},{1,2},{2,1},{3,0},{4,7},{5,6},{6,5},{7,4},{8,11},{9,10},{10,... | collective-permute-start | bytes 393224 | tf_op jit(solution)/shard_map/ppermute | solution.py:509
  26.8 0.0 collective-permute-start.13
  26.8 0.4 more_blocks.5
  27.2 0.0 collective-permute-done.9.refs_0_
  27.2 0.8 %collective-permute-start.10 = (bf16[128,512]{1,0:T(8,128)(2,1)S(1)}, bf16[128,512]{1,0:T(8,128)(2,1)S(1)}, u32[]{:S(2)}, u32[]{:S(2)}) collective-permute-start(bf16[128,512]{1,0:T(8,128)(2,1)S(1)} %collective-permute-done.9.refs_0_), channel_id=1, source_target_pairs={{0,1},{1,0},{2,3},{3,2},{4,5},{5,4},{6,7},{7,6},{8,9},{9,8},{10,11... | collective-permute-start | bytes 393224 | tf_op jit(solution)/shard_map/ppermute | solution.py:509
  27.9 0.4 more_blocks.6
  28.3 1.5 %collective-permute-done.11.refs_2_ = bf16[128,512]{1,0:T(8,128)(2,1)S(1)} collective-permute-done((bf16[128,512]{1,0:T(8,128)(2,1)S(1)}, bf16[128,512]{1,0:T(8,128)(2,1)S(1)}, u32[]{:S(2)}, u32[]{:S(2)}) %collective-permute-start.11) | collective-permute-done | bytes 131104 | tf_op jit(solution)/shard_map/ppermute | solution.py:509
  29.8 0.2 collective-permute-start.12
  30.0 0.6 %collective-permute-done.7.refs_1_ = bf16[128,512]{1,0:T(8,128)(2,1)S(1)} collective-permute-done((bf16[128,512]{1,0:T(8,128)(2,1)S(1)}, bf16[128,512]{1,0:T(8,128)(2,1)S(1)}, u32[]{:S(2)}, u32[]{:S(2)}) %collective-permute-start.7) | collective-permute-done | bytes 131104 | tf_op jit(solution)/shard_map/ppermute | solution.py:509
  30.6 0.1 collective-permute-start.8
  30.7 0.0 collective-permute-done.13.refs_0_
  30.7 0.8 %more_blocks.7 = (f32[128,1024]{1,0:T(8,128)S(1)}, f32[128,256]{1,0:T(8,128)S(1)}, f32[128,128]{1,0:T(8,128)S(1)}) custom-call(bf16[128,512]{1,0:T(8,128)(2,1)S(1)} %collective-permute-done.13.refs_0_, bf16[128,512]{1,0:T(8,128)(2,1)S(1)} %collective-permute-done.7.refs_1_, bf16[128,512]{1,0:T(8,128)(2,1)S(1)} %collective-permute-done.11.refs_2_, ...), custom_call_target="tpu_custom_call" | custom-call | flops 503316480 | bytes 393216 | tf_op jit(solution)/shard_map/more_blocks/pallas_call | solution.py:215
  31.5 0.0 collective-permute-done.10.refs_1_
  31.5 0.0 collective-permute-done.12.refs_2_
  31.5 0.4 %collective-permute-done.8.refs_0_ = bf16[128,512]{1,0:T(8,128)(2,1)S(1)} collective-permute-done((bf16[128,512]{1,0:T(8,128)(2,1)S(1)}, bf16[128,512]{1,0:T(8,128)(2,1)S(1)}, u32[]{:S(2)}, u32[]{:S(2)}) %collective-permute-start.8) | collective-permute-done | bytes 131104 | tf_op jit(solution)/shard_map/ppermute | solution.py:509
  31.9 0.6 %last_keys_values.3 = (f32[128,128]{1,0:T(8,128)S(1)}, bf16[128,128]{1,0:T(8,128)(2,1)S(1)}, bf16[128,128]{1,0:T(8,128)(2,1)S(1)}) custom-call(bf16[128,512]{1,0:T(8,128)(2,1)S(1)} %collective-permute-done.8.refs_0_, bf16[128,512]{1,0:T(8,128)(2,1)S(1)} %collective-permute-done.10.refs_1_, bf16[128,512]{1,0:T(8,128)(2,1)S(1)} %collective-permute-done.12.refs_2_, ...), custom_call_target="tpu_custom_call" | custom-call | flops 100663296 | bytes 393216 | tf_op jit(solution)/shard_map/last_keys_values/pallas_call | solution.py:257
  32.5 1.0 %collective-permute-start.14 = (bf16[128,128]{1,0:T(8,128)(2,1)S(1)}, bf16[128,128]{1,0:T(8,128)(2,1)S(1)}, u32[]{:S(2)}, u32[]{:S(2)}) collective-permute-start(bf16[128,128]{1,0:T(8,128)(2,1)S(1)} %get-tuple-element.104), channel_id=1, source_target_pairs={{0,3},{1,2},{2,1},{3,0},{4,7},{5,6},{6,5},{7,4},{8,11},{9,10},{10,... | collective-permute-start | bytes 98312 | tf_op jit(solution)/shard_map/ppermute | solution.py:509
  33.5 0.6 %last_queries.3.q_ref = bf16[128,1024]{1,0:T(8,128)(2,1)S(1)} custom-call(bf16[128,512]{1,0:T(8,128)(2,1)S(1)} %collective-permute-done.8.refs_0_, bf16[128,512]{1,0:T(8,128)(2,1)S(1)} %collective-permute-done.10.refs_1_, bf16[128,512]{1,0:T(8,128)(2,1)S(1)} %collective-permute-done.12.refs_2_, f32[1,4096]{1,0:T(1,128)S(1)} %get-tuple-element.63.refs_3_.refs_1_, ...), custom_call_target="tpu_custom_call" | custom-call | flops 402653184 | bytes 393216 | tf_op jit(solution)/shard_map/last_queries/pallas_call | solution.py:296
  34.1 0.6 %resident_attend.1 = (f32[1024,128]{1,0:T(8,128)S(1)}, f32[1024,128]{1,0:T(8,128)S(1)}, f32[1024,128]{1,0:T(8,128)S(1)}) custom-call(s32[128,128]{1,0:T(8,128)S(1)} %get-tuple-element.60.opened_ref, bf16[128,1024]{1,0:T(8,128)(2,1)S(1)} %last_queries.3.q_ref, bf16[128,128]{1,0:T(8,128)(2,1)S(1)} %get-tuple-element.78.refs_0_.keys_ref, ...), custom_call_target="tpu_custom_call" | custom-call | flops 1000 | bytes 1000 | tf_op jit(solution)/shard_map/resident_attend/pallas_call | solution.py:448
  34.6 1.3 %collective-permute-done.14.refs_3_ = bf16[128,128]{1,0:T(8,128)(2,1)S(1)} collective-permute-done((bf16[128,128]{1,0:T(8,128)(2,1)S(1)}, bf16[128,128]{1,0:T(8,128)(2,1)S(1)}, u32[]{:S(2)}, u32[]{:S(2)}) %collective-permute-start.14) | collective-permute-done | bytes 32800 | tf_op jit(solution)/shard_map/ppermute | solution.py:509
  35.9 1.3 %second_attend.1 = bf16[128,1024]{1,0:T(8,128)(2,1)} custom-call(s32[128,128]{1,0:T(8,128)S(1)} %get-tuple-element.60.opened_ref, bf16[128,1024]{1,0:T(8,128)(2,1)S(1)} %last_queries.3.q_ref, f32[1024,128]{1,0:T(8,128)S(1)} %get-tuple-element.100.max_ref, f32[1024,128]{1,0:T(8,128)S(1)} %get-tuple-element.101.sum_ref, ...), custom_call_target="tpu_custom_call" | custom-call | flops 1000 | bytes 1000 | tf_op jit(solution)/shard_map/second_attend/pallas_call | solution.py:482
Async XLA Ops:
  0.0 9.4 %collective-permute-start = (bf16[128,1024]{1,0:T(8,128)(2,1)}, bf16[128,1024]{1,0:T(8,128)(2,1)S(1)}, u32[]{:S(2)}, u32[]{:S(2)}) collective-permute-start(bf16[128,1024]{1,0:T(8,128)(2,1)} %bitcast.7), channel_id=1, source_target_pairs={{0,3},{1,2},{2,1},{3,0},{4,7},{5,6},{6,5},{7,4},{8,11},{9,10},{10,... | collective-permute-start | bytes 786440 | tf_op jit(solution)/shard_map/ppermute | solution.py:509
  2.4 7.1 %collective-permute-start.3 = (bf16[128,1024]{1,0:T(8,128)(2,1)}, bf16[128,1024]{1,0:T(8,128)(2,1)S(1)}, u32[]{:S(2)}, u32[]{:S(2)}) collective-permute-start(bf16[128,1024]{1,0:T(8,128)(2,1)} %bitcast.8), channel_id=1, source_target_pairs={{0,1},{1,0},{2,3},{3,2},{4,5},{5,4},{6,7},{7,6},{8,9},{9,8},{10,11... | collective-permute-start | bytes 786440 | tf_op jit(solution)/shard_map/ppermute | solution.py:509
  3.1 4.9 %collective-permute-start.1 = (bf16[4096,256]{1,0:T(8,128)(2,1)}, bf16[4096,256]{1,0:T(8,128)(2,1)S(1)}, u32[]{:S(2)}, u32[]{:S(2)}) collective-permute-start(bf16[4096,256]{1,0:T(8,128)(2,1)} %bitcast.5), channel_id=1, source_target_pairs={{0,1},{1,0},{2,3},{3,2},{4,5},{5,4},{6,7},{7,6},{8,9},{9,8},{10,11... | collective-permute-start | bytes 6291464 | tf_op jit(solution)/shard_map/ppermute | solution.py:509
  3.1 4.3 %copy-start.1 = (s32[9]{0:T(128)S(1)}, s32[9]{0:T(128)}, u32[]{:S(2)}) copy-start(s32[9]{0:T(128)} %doc_ref) | copy-start | bytes 112
  8.0 5.7 %copy-start = (bf16[128,1024]{1,0:T(8,128)(2,1)S(1)}, bf16[128,1024]{1,0:T(8,128)(2,1)}, u32[]{:S(2)}) copy-start(bf16[128,1024]{1,0:T(8,128)(2,1)} %fresh_ref.3) | copy-start | bytes 786436
  9.4 1.5 %collective-permute-start.2 = (bf16[128,1024]{1,0:T(8,128)(2,1)S(1)}, bf16[128,1024]{1,0:T(8,128)(2,1)S(1)}, u32[]{:S(2)}, u32[]{:S(2)}) collective-permute-start(bf16[128,1024]{1,0:T(8,128)(2,1)S(1)} %collective-permute-done.refs_2_.x_ref), channel_id=1, source_target_pairs={{0,1},{1,0},{2,3},{3,2},{4,5},{5,4},{6,7},{7,6},{8,9},{9,8},{10,11... | collective-permute-start | bytes 786440 | tf_op jit(solution)/shard_map/ppermute | solution.py:509
  11.5 3.8 %collective-permute-start.4 = (bf16[128,128]{1,0:T(8,128)(2,1)S(1)}, bf16[128,128]{1,0:T(8,128)(2,1)S(1)}, u32[]{:S(2)}, u32[]{:S(2)}) collective-permute-start(bf16[128,128]{1,0:T(8,128)(2,1)S(1)} %get-tuple-element.75.piece_ref), channel_id=1, source_target_pairs={{0,3},{1,2},{2,1},{3,0},{4,7},{5,6},{6,5},{7,4},{8,11},{9,10},{10,... | collective-permute-start | bytes 98312 | tf_op jit(solution)/shard_map/ppermute | solution.py:509
  14.2 6.1 %collective-permute-start.6 = (bf16[128,640]{1,0:T(8,128)(2,1)S(1)}, bf16[128,640]{1,0:T(8,128)(2,1)S(1)}, u32[]{:S(2)}, u32[]{:S(2)}) collective-permute-start(bf16[128,640]{1,0:T(8,128)(2,1)S(1)} %get-tuple-element.77), channel_id=1, source_target_pairs={{0,3},{1,2},{2,1},{3,0},{4,7},{5,6},{6,5},{7,4},{8,11},{9,10},{10,... | collective-permute-start | bytes 491528 | tf_op jit(solution)/shard_map/ppermute | solution.py:509
  15.8 8.4 %collective-permute-start.5 = (bf16[128,512]{1,0:T(8,128)(2,1)S(1)}, bf16[128,512]{1,0:T(8,128)(2,1)S(1)}, u32[]{:S(2)}, u32[]{:S(2)}) collective-permute-start(bf16[128,512]{1,0:T(8,128)(2,1)S(1)} %get-tuple-element.76), channel_id=1, source_target_pairs={{0,5},{1,4},{2,7},{3,6},{4,9},{5,8},{6,11},{7,10},{8,13},{9,12},{1... | collective-permute-start | bytes 393224 | tf_op jit(solution)/shard_map/ppermute | solution.py:509
  18.0 9.2 %collective-permute-start.9 = (bf16[128,512]{1,0:T(8,128)(2,1)S(1)}, bf16[128,512]{1,0:T(8,128)(2,1)S(1)}, u32[]{:S(2)}, u32[]{:S(2)}) collective-permute-start(bf16[128,512]{1,0:T(8,128)(2,1)S(1)} %first_attend.3), channel_id=1, source_target_pairs={{0,5},{1,4},{2,7},{3,6},{4,9},{5,8},{6,11},{7,10},{8,13},{9,12},{1... | collective-permute-start | bytes 393224 | tf_op jit(solution)/shard_map/ppermute | solution.py:509
  20.8 9.0 %collective-permute-start.11 = (bf16[128,512]{1,0:T(8,128)(2,1)S(1)}, bf16[128,512]{1,0:T(8,128)(2,1)S(1)}, u32[]{:S(2)}, u32[]{:S(2)}) collective-permute-start(bf16[128,512]{1,0:T(8,128)(2,1)S(1)} %peer_attend.1), channel_id=1, source_target_pairs={{0,5},{1,4},{2,7},{3,6},{4,9},{5,8},{6,11},{7,10},{8,13},{9,12},{1... | collective-permute-start | bytes 393224 | tf_op jit(solution)/shard_map/ppermute | solution.py:509
  24.2 6.4 %collective-permute-start.7 = (bf16[128,512]{1,0:T(8,128)(2,1)S(1)}, bf16[128,512]{1,0:T(8,128)(2,1)S(1)}, u32[]{:S(2)}, u32[]{:S(2)}) collective-permute-start(bf16[128,512]{1,0:T(8,128)(2,1)S(1)} %collective-permute-done.5.refs_0_), channel_id=1, source_target_pairs={{0,3},{1,2},{2,1},{3,0},{4,7},{5,6},{6,5},{7,4},{8,11},{9,10},{10,... | collective-permute-start | bytes 393224 | tf_op jit(solution)/shard_map/ppermute | solution.py:509
  26.8 3.9 %collective-permute-start.13 = (bf16[128,512]{1,0:T(8,128)(2,1)S(1)}, bf16[128,512]{1,0:T(8,128)(2,1)S(1)}, u32[]{:S(2)}, u32[]{:S(2)}) collective-permute-start(bf16[128,512]{1,0:T(8,128)(2,1)S(1)} %collective-permute-done.5.refs_0_), channel_id=1, source_target_pairs={{0,1},{1,0},{2,3},{3,2},{4,5},{5,4},{6,7},{7,6},{8,9},{9,8},{10,11... | collective-permute-start | bytes 393224 | tf_op jit(solution)/shard_map/ppermute | solution.py:509
  27.2 4.4 %collective-permute-start.10 = (bf16[128,512]{1,0:T(8,128)(2,1)S(1)}, bf16[128,512]{1,0:T(8,128)(2,1)S(1)}, u32[]{:S(2)}, u32[]{:S(2)}) collective-permute-start(bf16[128,512]{1,0:T(8,128)(2,1)S(1)} %collective-permute-done.9.refs_0_), channel_id=1, source_target_pairs={{0,1},{1,0},{2,3},{3,2},{4,5},{5,4},{6,7},{7,6},{8,9},{9,8},{10,11... | collective-permute-start | bytes 393224 | tf_op jit(solution)/shard_map/ppermute | solution.py:509
  29.8 1.7 %collective-permute-start.12 = (bf16[128,512]{1,0:T(8,128)(2,1)S(1)}, bf16[128,512]{1,0:T(8,128)(2,1)S(1)}, u32[]{:S(2)}, u32[]{:S(2)}) collective-permute-start(bf16[128,512]{1,0:T(8,128)(2,1)S(1)} %collective-permute-done.11.refs_2_), channel_id=1, source_target_pairs={{0,1},{1,0},{2,3},{3,2},{4,5},{5,4},{6,7},{7,6},{8,9},{9,8},{10,11... | collective-permute-start | bytes 393224 | tf_op jit(solution)/shard_map/ppermute | solution.py:509
  30.6 1.3 %collective-permute-start.8 = (bf16[128,512]{1,0:T(8,128)(2,1)S(1)}, bf16[128,512]{1,0:T(8,128)(2,1)S(1)}, u32[]{:S(2)}, u32[]{:S(2)}) collective-permute-start(bf16[128,512]{1,0:T(8,128)(2,1)S(1)} %collective-permute-done.7.refs_1_), channel_id=1, source_target_pairs={{0,1},{1,0},{2,3},{3,2},{4,5},{5,4},{6,7},{7,6},{8,9},{9,8},{10,11... | collective-permute-start | bytes 393224 | tf_op jit(solution)/shard_map/ppermute | solution.py:509
  32.5 3.4 %collective-permute-start.14 = (bf16[128,128]{1,0:T(8,128)(2,1)S(1)}, bf16[128,128]{1,0:T(8,128)(2,1)S(1)}, u32[]{:S(2)}, u32[]{:S(2)}) collective-permute-start(bf16[128,128]{1,0:T(8,128)(2,1)S(1)} %get-tuple-element.104), channel_id=1, source_target_pairs={{0,3},{1,2},{2,1},{3,0},{4,7},{5,6},{6,5},{7,4},{8,11},{9,10},{10,... | collective-permute-start | bytes 98312 | tf_op jit(solution)/shard_map/ppermute | solution.py:509

commit v11 on v9

--- a/solution.py
+++ b/solution.py
@@ -49,14 +49,12 @@
     return lax.dot_general(a, b, (((1,), (1,)), ((), ())), preferred_element_type=f32)
 
 
-def gained(x, gain_ref, start):
-    width = x.shape[1]
-    wide = x.astype(f32)
+def squares_by_lane(wide):
     squares = wide * wide
     ssq = squares[:, :HD]
-    for c in range(HD, width, HD):
+    for c in range(HD, wide.shape[1], HD):
         ssq = ssq + squares[:, c : c + HD]
-    return (wide * gain_ref[:, from_start(start, width)]).astype(bf16), ssq
+    return ssq
 
 
 def choose_rows(choose_ref, me, n, flips, parts):
@@ -77,7 +75,7 @@
 
 
 def load_kernel(
-    n, flips, parts, x_hbm, gain_hbm, wq_hbm, wkv_hbm, accq_ref, x_ref, gain_ref, wq_ref, wkv_ref, choose_ref, sems
+    n, flips, parts, x_hbm, gain_hbm, wq_hbm, wkv_hbm, x_ref, gain_ref, wq_ref, wkv_ref, choose_ref, sems
 ):
     width = x_hbm.shape[1]
     me = lax.axis_index("head")
@@ -97,14 +95,10 @@
         part(step).start()
     keys_values.start()
     choose_rows(choose_ref, me, n, flips, parts)
-    for copy in small:
+    for copy in (*small, keys_values):
         copy.wait()
-    normed, _ = gained(x_ref[...], gain_ref, me * width)
-    part(0).wait()
-    accq_ref[...] = dot(normed, wq_ref[rows_of(me, width), :])
-    for step in range(1, n):
+    for step in range(n):
         part(step).wait()
-    keys_values.wait()
 
 
 def load(x, gain, wq, wkv, n, flips, parts):
@@ -114,7 +108,6 @@
     return pl.pallas_call(
         functools.partial(load_kernel, n, flips, parts),
         out_shape=(
-            VMEM((tokens, wq.shape[1]), f32),
             VMEM(x.shape, bf16),
             VMEM(gain.shape, f32),
             VMEM(wq.shape, bf16),
@@ -122,110 +115,65 @@
             VMEM((len(flips), parts * columns // KVH, parts * columns), f32),
         ),
         in_specs=[in_hbm] * 4,
-        out_specs=(vmem,) * 6,
+        out_specs=(vmem,) * 5,
         scratch_shapes=[pltpu.SemaphoreType.DMA((n + 3,))],
         cost_estimate=cost(10**11, 10**9),
         compiler_params=params,
-        name="load_and_own_queries",
+        name="load",
     )(*operands)
 
 
-def blocks_kernel(count, wkv_count, carried, places, with_q, *refs):
-    xs, refs = refs[:count], refs[count:]
-    gain_ref, wq_ref = refs[:2]
-    wkv_refs, refs = refs[2 : 2 + wkv_count], refs[2 + wkv_count :]
-    old, outs = refs[:carried], refs[carried:]
-    me = lax.axis_index("head")
-    columns = wkv_refs[0].shape[1]
-    q = old[0][...] if carried >= 1 else None
-    kvs = [old[1][:, c * columns : (c + 1) * columns] if carried == 3 else None for c in range(wkv_count)]
-    ssq = old[2][...] if carried == 3 else None
-
-    def add(total, term):
-        return term if total is None else total + term
-
-    for i, x_ref in enumerate(xs):
-        start, width = places[i](me), x_ref.shape[1]
-        normed, squares = gained(x_ref[...], gain_ref, start)
-        ssq = add(ssq, squares)
-        rows = from_start(start, width)
-        kvs = [add(kv, dot(normed, w_ref[rows, :])) for kv, w_ref in zip(kvs, wkv_refs)]
-        if with_q[i]:
-            q = add(q, dot(normed, wq_ref[rows, :]))
-    outs[0][...] = q
-    for c, kv in enumerate(kvs):
-        outs[1][:, c * columns : (c + 1) * columns] = kv
-    outs[2][...] = ssq
-
-
-def more_blocks(xs, places, gain, wq, wkvs, state, with_q=None):
-    tokens = xs[0].shape[0]
-    operands = [*xs, *resident_in(gain, wq, *wkvs), *state]
-    columns = len(wkvs) * wkvs[0].shape[1]
-    shapes = ((tokens, wq.shape[1]), (tokens, columns), (tokens, HD))
-    return pl.pallas_call(
-        functools.partial(
-            blocks_kernel, len(xs), len(wkvs), len(state), places, with_q or [True] * len(xs)
-        ),
-        out_shape=tuple(VMEM(s, f32) for s in shapes),
-        in_specs=[vmem] * len(operands),
-        out_specs=(vmem,) * 3,
-        cost_estimate=cost(sum(2 * x.size * (wq.shape[1] + columns) for x in xs), sum(2 * x.size for x in xs)),
-        compiler_params=params,
-        name="more_blocks",
-    )(*operands)
-
-
-def last_kv_kernel(count, wkv_count, places, *refs):
+def keys_values_kernel(count, wkv_count, places, *refs):
     xs, refs = refs[:count], refs[count:]
     gain_ref, wkv_refs, refs = refs[0], refs[1 : 1 + wkv_count], refs[1 + wkv_count :]
-    choose_ref, acckv_ref, ssq_ref, scale_ref, *pieces = refs
+    choose_ref, normed_ref, *pieces = refs
     me = lax.axis_index("head")
-    columns = wkv_refs[0].shape[1]
-    kvs = [acckv_ref[:, c * columns : (c + 1) * columns] for c in range(wkv_count)]
-    ssq = ssq_ref[...]
-    for i, x_ref in enumerate(xs):
-        start, width = places[i](me), x_ref.shape[1]
-        normed, squares = gained(x_ref[...], gain_ref, start)
-        ssq = ssq + squares
-        kvs = [kv + dot(normed, w_ref[from_start(start, width), :]) for kv, w_ref in zip(kvs, wkv_refs)]
+    ssq = squares_by_lane(xs[0][...].astype(f32))
+    for x_ref in xs[1:]:
+        ssq = ssq + squares_by_lane(x_ref[...].astype(f32))
     scale = lax.rsqrt(jnp.sum(ssq, axis=1, keepdims=True) / gain_ref.shape[1] + epsilon)
-    scale_ref[...] = jnp.broadcast_to(scale, scale_ref.shape)
-    kv = jnp.concatenate([(kv * scale).astype(bf16) for kv in kvs], axis=1)
+    kvs, at = [None] * wkv_count, 0
+    for place, x_ref in zip(places, xs):
+        width = x_ref.shape[1]
+        rows = from_start(place(me), width)
+        normed = (x_ref[...].astype(f32) * scale * gain_ref[:, rows]).astype(bf16)
+        normed_ref[:, at : at + width] = normed
+        at += width
+        terms = [dot(normed, w_ref[rows, :]) for w_ref in wkv_refs]
+        kvs = [term if kv is None else kv + term for kv, term in zip(kvs, terms)]
+    kv = jnp.concatenate([kv.astype(bf16) for kv in kvs], axis=1)
     for i, piece in enumerate(pieces):
         piece[...] = dot_turned(choose_ref[i].astype(bf16), kv).astype(bf16)
 
 
-def last_kv(xs, places, gain, wkvs, choose, acckv, ssq):
-    tokens = xs[0].shape[0]
+def keys_values(xs, places, gain, wkvs, choose):
+    tokens, width = xs[0].shape[0], sum(x.shape[1] for x in xs)
     columns = len(wkvs) * wkvs[0].shape[1]
-    operands = [*xs, *resident_in(gain, *wkvs, choose), acckv, ssq]
+    operands = [*xs, *resident_in(gain, *wkvs, choose)]
     count = choose.shape[0]
     return pl.pallas_call(
-        functools.partial(last_kv_kernel, len(xs), len(wkvs), places),
-        out_shape=(VMEM((tokens, HD), f32),) + (VMEM((columns // KVH, tokens), bf16),) * count,
+        functools.partial(keys_values_kernel, len(xs), len(wkvs), places),
+        out_shape=(VMEM((tokens, width), bf16),) + (VMEM((columns // KVH, tokens), bf16),) * count,
         in_specs=[vmem] * len(operands),
         out_specs=(vmem,) * (1 + count),
-        cost_estimate=cost(sum(2 * x.size * columns for x in xs), sum(2 * x.size for x in xs)),
-        compiler_params=params,
-        name="last_keys_values",
+        cost_estimate=cost(2 * tokens * width * columns, 2 * tokens * width),
+        compiler_params=params,
+        name="keys_values",
     )(*operands)
 
 
-def last_q_kernel(count, places, *refs):
-    xs, rest = refs[:count], refs[count:]
-    gain_ref, wq_ref, accq_ref, scale_ref, *rest = rest
+def queries_kernel(widths, places, normed_ref, wq_ref, *refs):
     me = lax.axis_index("head")
-    total = accq_ref[...]
-    for i, x_ref in enumerate(xs):
-        start, width = places[i](me), x_ref.shape[1]
-        normed, _ = gained(x_ref[...], gain_ref, start)
-        total = total + dot(normed, wq_ref[from_start(start, width), :])
-    q = (total * scale_ref[:, 0:1]).astype(bf16)
-    if len(rest) == 1:
-        rest[0][...] = q
+    total, at = None, 0
+    for place, width in zip(places, widths):
+        term = dot(normed_ref[:, at : at + width], wq_ref[from_start(place(me), width), :])
+        total = term if total is None else total + term
+        at += width
+    q = total.astype(bf16)
+    if len(refs) == 1:
+        refs[0][...] = q
         return
-    piece_ref, fresh_ref, q_ref, bundle_ref = rest
+    piece_ref, fresh_ref, q_ref, bundle_ref = refs
     q_ref[...] = q
     late = bundle_ref.shape[1] - HD
     last = lax.axis_index("section") == lax.axis_size("section") - 1
@@ -234,20 +182,20 @@
     bundle_ref[:, late:] = piece_ref[...]
 
 
-def last_q(xs, places, gain, wq, accq, scale, bundled=(), late=0):
-    operands = [*xs, *resident_in(gain, wq), accq, scale, *bundled]
-    tokens = xs[0].shape[0]
+def queries(normed, widths, places, wq, bundled=(), late=0):
+    tokens = normed.shape[0]
+    operands = [normed, *resident_in(wq), *bundled]
     out = [VMEM((tokens, wq.shape[1]), bf16)]
     if bundled:
         out.append(VMEM((tokens, late + HD), bf16))
     return pl.pallas_call(
-        functools.partial(last_q_kernel, len(xs), places),
+        functools.partial(queries_kernel, widths, places),
         out_shape=tuple(out),
         in_specs=[vmem] * len(operands),
         out_specs=(vmem,) * len(out),
-        cost_estimate=cost(sum(2 * x.size * wq.shape[1] for x in xs), sum(2 * x.size for x in xs)),
-        compiler_params=params,
-        name="last_queries",
+        cost_estimate=cost(1000, 1000),
+        compiler_params=params,
+        name="queries",
     )(*operands)
 
 
@@ -458,10 +406,10 @@
     def after(array, *others):
         return lax.optimization_barrier((array, *others))[0]
 
-    def exchanged(xs, places, state):
-        scale, *pieces = last_kv(xs, places, gain, wkvs, choose, state[1], state[2])
+    def exchanged(xs, places):
+        normed, *pieces = keys_values(xs, places, gain, wkvs, choose)
         received = [moved(piece, 0, flip) for piece, flip in zip(pieces[1:], flips[1:])]
-        return scale, [pieces[0], *received], pieces
+        return normed, [pieces[0], *received], pieces, [x.shape[1] for x in xs]
 
     def rest_of(array):
         every = lax.all_gather(array, "head", axis=0)
@@ -477,27 +425,24 @@
         over = moved(own, 0, 3)
         beside = moved(own, 0, 1)
         w_kv_beside = moved(w_kv, 0, 1)
-    accq, own, gain, wq, wkv, choose = load(own, norm_gain, w_q, w_kv, n, flips, parts)
-    opened = openings(after(doc_lengths, accq), tokens, sections)
+    own, gain, wq, wkv, choose = load(own, norm_gain, w_q, w_kv, n, flips, parts)
+    opened = openings(after(doc_lengths, gain), tokens, sections)
     if paired:
         wkvs = [wkv, w_kv_beside]
         over, *opened = lax.optimization_barrier((over, *opened))
         passed = moved(over, 0, 1)
-        xs, places, with_q = [own, beside, over], [place(0), place(1), place(3)], [False, True, True]
-        state = more_blocks(xs, places, gain, wq, wkvs, [accq], with_q)
-        last, places = [passed], [place(2)]
+        xs, places = [own, beside, over, passed], [place(0), place(1), place(3), place(2)]
     else:
         wkvs = [wkv]
-        state = more_blocks([own], following[:1], gain, wq, wkvs, [accq], [False])
-        last, places = rest_of(own), following[1:]
-    scale, pieces, made = exchanged(last, places, state)
+        xs, places = [own, *rest_of(own)], following
+    normed, pieces, made, widths = exchanged(xs, places)
     part = heads // 2 if paired else heads
     split = part * HD
     if paired:
-        q, bundle = last_q(last, places, gain, wq, state[0], scale, [made[0], fresh_slice], width - split)
+        q, bundle = queries(normed, widths, places, wq, [made[0], fresh_slice], width - split)
         bundle = moved(bundle, 0, 3)
     else:
-        (q,) = last_q(last, places, gain, wq, state[0], scale)
+        (q,) = queries(normed, widths, places, wq)
     sent, keys, values = first_attend(
         opened[0], q, own, fresh_slice, pieces, flips, parts, (0, part), sections
     )
@@ -514,22 +459,18 @@
         a1 = after(a1, peers)
         a2 = moved(a1, 0, 3)
         a0 = moved(a1, 0, 1)
-        state = more_blocks([a1], [place(1)], gain, wq, wkvs, [])
-        b1, *state = lax.optimization_barrier((b1, *state))
         b0 = moved(b1, 0, 1)
-        state = more_blocks([b1], [place(1, split)], gain, wq, wkvs, state)
-        b2, *state = lax.optimization_barrier((b2, *state))
         b3 = moved(b2, 0, 1)
         a3 = moved(a2, 0, 1)
-        state = more_blocks([a0, a2, b2], [place(0), place(2), place(2, split)], gain, wq, wkvs, state)
-        last, places = [a3, b0, b3], [place(3), place(0, split), place(3, split)]
+        xs = [a1, a0, b1, b0, a2, b2, a3, b3]
+        places = [place(1), place(0), place(1, split), place(0, split)]
+        places += [place(2), place(2, split), place(3), place(3, split)]
         mine = [a0, b0]
     else:
-        mine = [moved(sent, 1, 0)]
-        state = more_blocks(mine, following[:1], gain, wq, wkvs, [])
-        last, places = rest_of(mine[0]), following[1:]
-    scale, pieces, _ = exchanged(last, places, state)
-    (q,) = last_q(last, places, gain, wq, state[0], scale)
+        mine = [jnp.where(lax.axis_index("section") == 0, fresh_slice, moved(sent, 1, 0))]
+        xs, places = [*mine, *rest_of(mine[0])], following
+    normed, pieces, _, widths = exchanged(xs, places)
+    (q,) = queries(normed, widths, places, wq)
     resident = resident_attend(opened[1], q, keys, values, sections)
     return second_attend(opened[1], q, mine, resident, pieces, flips, parts, sections)[None]
 

time: 36.8 us -> 42.3 us (1.15)
  waiting for transfers between devices: 7.23 us -> 18 us
  starting transfers between devices: 16.3 us -> 10.9 us
    ppermute x15, waiting for transfers between devices: 7.23 us -> 18 us  [moved(): return lax.ppermute(array, ('section', 'head'), pairs)]
    ppermute x15, starting transfers between devices: 16.3 us -> 10.9 us  [moved(): return lax.ppermute(array, ('section', 'head'), pairs)]
    pallas_call x8 -> x4, Pallas kernels: 4.84 us -> 4.87 us  [the longest x2 2.52 us: queries(): pl.pallas_call(functools.partial(queries_kernel, widths, places), out_sha...]
  transfers between devices with their start and end apart: 15 -> 15, of which waited for: 9 -> 10; matrix products, arithmetic and copies ran while one was open for 0% -> 0% of each run, Pallas kernels for 29% -> 22%
where the time goes in v11:
time: 42.3 us; the launch traced here: 42.2 us
  waiting for transfers between devices  18 us (43%)
  Pallas kernels  13.1 us (31%)
  starting transfers between devices  10.9 us (26%)
    ppermute x15, waiting for transfers between devices, moved(): return lax.ppermute(array, ('section', 'head'), pairs)  18 us
    ppermute x15, starting transfers between devices, moved(): return lax.ppermute(array, ('section', 'head'), pairs)  10.9 us
    pallas_call x1, Pallas kernels, load(): pl.pallas_call(functools.partial(load_kernel, n, flips, parts), out_shape...  4.24 us
    pallas_call x2, Pallas kernels, queries(): pl.pallas_call(functools.partial(queries_kernel, widths, places), out_sha...  2.52 us
    pallas_call x2, Pallas kernels, keys_values(): pl.pallas_call(functools.partial(keys_values_kernel, len(xs), len(wkvs),...  2.35 us
    pallas_call x1, Pallas kernels, second_attend(): pl.pallas_call(functools.partial(second_attend_kernel, sections, flips, p...  1.32 us
    pallas_call x2, Pallas kernels, first_attend(): pl.pallas_call(functools.partial(first_attend_kernel, sections, heads, fl...  0.96 us
  transfers between devices with their start and end apart: 15, of which 10 were waited for; matrix products, arithmetic and copies ran while one was open for 0% of the time, Pallas kernels for 22%

profile of v11, /device:TPU:0, one launch (start us, length us, event | category | flops | bytes accessed | tf_op | source)
XLA Modules:
  0.0 42.2 jit_solution(7166333872882421106)
XLA Ops:
  0.0 0.5 %collective-permute-start.1 = (bf16[128,1024]{1,0:T(8,128)(2,1)}, bf16[128,1024]{1,0:T(8,128)(2,1)S(1)}, u32[]{:S(2)}, u32[]{:S(2)}) collective-permute-start(bf16[128,1024]{1,0:T(8,128)(2,1)} %bitcast.7), channel_id=1, source_target_pairs={{0,1},{1,0},{2,3},{3,2},{4,5},{5,4},{6,7},{7,6},{8,9},{9,8},{10,11... | collective-permute-start | bytes 786440 | tf_op jit(solution)/shard_map/ppermute | solution.py:404
  0.5 2.6 %collective-permute-start = (bf16[128,1024]{1,0:T(8,128)(2,1)}, bf16[128,1024]{1,0:T(8,128)(2,1)S(1)}, u32[]{:S(2)}, u32[]{:S(2)}) collective-permute-start(bf16[128,1024]{1,0:T(8,128)(2,1)} %bitcast.8), channel_id=1, source_target_pairs={{0,3},{1,2},{2,1},{3,0},{4,7},{5,6},{6,5},{7,4},{8,11},{9,10},{10,... | collective-permute-start | bytes 786440 | tf_op jit(solution)/shard_map/ppermute | solution.py:404
  3.1 0.0 collective-permute-start.3
  3.1 0.0 copy-start.1
  3.1 4.2 %load.1 = (bf16[128,1024]{1,0:T(8,128)(2,1)S(1)}, f32[1,4096]{1,0:T(1,128)S(1)}, bf16[4096,1024]{1,0:T(8,128)(2,1)S(1)}, bf16[4096,256]{1,0:T(8,128)(2,1)S(1)}, f32[2,128,512]{2,1,0:T(8,128)S(1)}) custom-call(bf16[128,1024]{1,0:T(8,128)(2,1)} %bitcast.9, f32[1,4096]{1,0:T(1,128)} %gain_hbm.1, bf16[4096,1024]{1,0:T(8,128)(2,1)} %bitcast.4, ...), custom_call_target="tpu_custom_call" | custom-call | flops 99999997952 | bytes 1000000000 | tf_op jit(solution)/shard_map/load/pallas_call | solution.py:108
  7.3 0.0 copy-done.1
  7.4 0.6 %openings.1 = (s32[128,128]{1,0:T(8,128)S(1)}, s32[128,128]{1,0:T(8,128)S(1)}) custom-call(s32[9]{0:T(128)S(1)} %copy-done.1), custom_call_target="tpu_custom_call" | custom-call | tf_op jit(solution)/shard_map/openings/pallas_call | solution.py:216
  8.0 2.0 %collective-permute-done.refs_2_.x_ref = bf16[128,1024]{1,0:T(8,128)(2,1)S(1)} collective-permute-done((bf16[128,1024]{1,0:T(8,128)(2,1)}, bf16[128,1024]{1,0:T(8,128)(2,1)S(1)}, u32[]{:S(2)}, u32[]{:S(2)}) %collective-permute-start) | collective-permute-done | bytes 262176 | tf_op jit(solution)/shard_map/ppermute | solution.py:404
  10.0 0.1 collective-permute-start.2
  10.1 0.0 collective-permute-done.1.refs_1_
  10.1 1.4 %collective-permute-done.2.refs_3_ = bf16[128,1024]{1,0:T(8,128)(2,1)S(1)} collective-permute-done((bf16[128,1024]{1,0:T(8,128)(2,1)S(1)}, bf16[128,1024]{1,0:T(8,128)(2,1)S(1)}, u32[]{:S(2)}, u32[]{:S(2)}) %collective-permute-start.2) | collective-permute-done | bytes 262176 | tf_op jit(solution)/shard_map/ppermute | solution.py:404
  11.5 0.0 collective-permute-done.3.refs_6_.refs_10_
  11.5 0.0 copy-start
  11.5 1.2 %keys_values.2 = (bf16[128,4096]{1,0:T(8,128)(2,1)S(1)}, bf16[128,128]{1,0:T(8,128)(2,1)S(1)}, bf16[128,128]{1,0:T(8,128)(2,1)S(1)}) custom-call(bf16[128,1024]{1,0:T(8,128)(2,1)S(1)} %get-tuple-element.38.refs_0_.x_ref, bf16[128,1024]{1,0:T(8,128)(2,1)S(1)} %collective-permute-done.1.refs_1_, bf16[128,1024]{1,0:T(8,128)(2,1)S(1)} %collective-permute-done.refs_2_.x_ref, ...), custom_call_target="tpu_custom_call" | custom-call | flops 536870912 | bytes 1048576 | tf_op jit(solution)/shard_map/keys_values/pallas_call | solution.py:154
  12.7 1.3 %collective-permute-start.4 = (bf16[128,128]{1,0:T(8,128)(2,1)S(1)}, bf16[128,128]{1,0:T(8,128)(2,1)S(1)}, u32[]{:S(2)}, u32[]{:S(2)}) collective-permute-start(bf16[128,128]{1,0:T(8,128)(2,1)S(1)} %get-tuple-element.46.piece_ref), channel_id=1, source_target_pairs={{0,3},{1,2},{2,1},{3,0},{4,7},{5,6},{6,5},{7,4},{8,11},{9,10},{10,... | collective-permute-start | bytes 98312 | tf_op jit(solution)/shard_map/ppermute | solution.py:404
  14.0 0.0 copy-done
  14.0 1.3 %queries.2 = (bf16[128,1024]{1,0:T(8,128)(2,1)S(1)}, bf16[128,640]{1,0:T(8,128)(2,1)S(1)}) custom-call(bf16[128,4096]{1,0:T(8,128)(2,1)S(1)} %get-tuple-element.42.normed_ref, bf16[4096,1024]{1,0:T(8,128)(2,1)S(1)} %get-tuple-element.43.wq_ref, bf16[128,128]{1,0:T(8,128)(2,1)S(1)} %get-tuple-element.44.refs_0_, bf16[128,1024]{1,0:T(8,128)(2,1)S(1)} %copy-done), custom_call_target="tpu_custom_call" | custom-call | flops 1000 | bytes 1000 | tf_op jit(solution)/shard_map/queries/pallas_call | solution.py:191
  15.3 0.6 %collective-permute-start.6 = (bf16[128,640]{1,0:T(8,128)(2,1)S(1)}, bf16[128,640]{1,0:T(8,128)(2,1)S(1)}, u32[]{:S(2)}, u32[]{:S(2)}) collective-permute-start(bf16[128,640]{1,0:T(8,128)(2,1)S(1)} %get-tuple-element.48), channel_id=1, source_target_pairs={{0,3},{1,2},{2,1},{3,0},{4,7},{5,6},{6,5},{7,4},{8,11},{9,10},{10,... | collective-permute-start | bytes 491528 | tf_op jit(solution)/shard_map/ppermute | solution.py:404
  15.8 0.3 collective-permute-done.4.refs_1_
  16.1 0.5 %first_attend.2 = (bf16[128,512]{1,0:T(8,128)(2,1)S(1)}, bf16[128,128]{1,0:T(8,128)(2,1)S(1)}, bf16[128,128]{1,0:T(8,128)(2,1)S(1)}) custom-call(s32[128,128]{1,0:T(8,128)S(1)} %get-tuple-element.37.opened_ref, bf16[128,1024]{1,0:T(8,128)(2,1)S(1)} %get-tuple-element.45.q_ref, bf16[128,1024]{1,0:T(8,128)(2,1)S(1)} %get-tuple-element.38.refs_0_.x_ref, ...), custom_call_target="tpu_custom_call" | custom-call | flops 10000000000 | bytes 1000 | tf_op jit(solution)/shard_map/first_attend/pallas_call | solution.py:318
  16.6 1.2 %collective-permute-start.5 = (bf16[128,512]{1,0:T(8,128)(2,1)S(1)}, bf16[128,512]{1,0:T(8,128)(2,1)S(1)}, u32[]{:S(2)}, u32[]{:S(2)}) collective-permute-start(bf16[128,512]{1,0:T(8,128)(2,1)S(1)} %get-tuple-element.47), channel_id=1, source_target_pairs={{0,5},{1,4},{2,7},{3,6},{4,9},{5,8},{6,11},{7,10},{8,13},{9,12},{1... | collective-permute-start | bytes 393224 | tf_op jit(solution)/shard_map/ppermute | solution.py:404
  17.9 0.5 %first_attend.3 = bf16[128,512]{1,0:T(8,128)(2,1)S(1)} custom-call(s32[128,128]{1,0:T(8,128)S(1)} %get-tuple-element.37.opened_ref, bf16[128,1024]{1,0:T(8,128)(2,1)S(1)} %get-tuple-element.45.q_ref, bf16[128,1024]{1,0:T(8,128)(2,1)S(1)} %get-tuple-element.38.refs_0_.x_ref, bf16[128,1024]{1,0:T(8,128)(2,1)S(1)} %copy-done, ...), custom_call_target="tpu_custom_call" | custom-call | flops 10000000000 | bytes 1000 | tf_op jit(solution)/shard_map/first_attend/pallas_call | solution.py:318
  18.3 1.4 %collective-permute-start.8 = (bf16[128,512]{1,0:T(8,128)(2,1)S(1)}, bf16[128,512]{1,0:T(8,128)(2,1)S(1)}, u32[]{:S(2)}, u32[]{:S(2)}) collective-permute-start(bf16[128,512]{1,0:T(8,128)(2,1)S(1)} %first_attend.3), channel_id=1, source_target_pairs={{0,5},{1,4},{2,7},{3,6},{4,9},{5,8},{6,11},{7,10},{8,13},{9,12},{1... | collective-permute-start | bytes 393224 | tf_op jit(solution)/shard_map/ppermute | solution.py:404
  19.7 1.8 %collective-permute-done.6.bundle_ref = bf16[128,640]{1,0:T(8,128)(2,1)S(1)} collective-permute-done((bf16[128,640]{1,0:T(8,128)(2,1)S(1)}, bf16[128,640]{1,0:T(8,128)(2,1)S(1)}, u32[]{:S(2)}, u32[]{:S(2)}) %collective-permute-start.6) | collective-permute-done | bytes 163872 | tf_op jit(solution)/shard_map/ppermute | solution.py:404
  21.5 0.5 %peer_attend.1 = bf16[128,512]{1,0:T(8,128)(2,1)S(1)} custom-call(s32[128,128]{1,0:T(8,128)S(1)} %get-tuple-element.37.opened_ref, bf16[128,640]{1,0:T(8,128)(2,1)S(1)} %collective-permute-done.6.bundle_ref, bf16[128,1024]{1,0:T(8,128)(2,1)S(1)} %collective-permute-done.refs_2_.x_ref, bf16[128,128]{1,0:T(8,128)(2,1)S(1)} %get-tuple-element.46.piece_ref), custom_call_target="tpu_custom_call" | custom-call | flops 1000 | bytes 1000 | tf_op jit(solution)/shard_map/peer_attend/pallas_call | solution.py:276
  22.0 2.8 %collective-permute-done.5.refs_0_ = bf16[128,512]{1,0:T(8,128)(2,1)S(1)} collective-permute-done((bf16[128,512]{1,0:T(8,128)(2,1)S(1)}, bf16[128,512]{1,0:T(8,128)(2,1)S(1)}, u32[]{:S(2)}, u32[]{:S(2)}) %collective-permute-start.5) | collective-permute-done | bytes 131104 | tf_op jit(solution)/shard_map/ppermute | solution.py:404
  24.9 1.8 %collective-permute-start.10 = (bf16[128,512]{1,0:T(8,128)(2,1)S(1)}, bf16[128,512]{1,0:T(8,128)(2,1)S(1)}, u32[]{:S(2)}, u32[]{:S(2)}) collective-permute-start(bf16[128,512]{1,0:T(8,128)(2,1)S(1)} %collective-permute-done.5.refs_0_), channel_id=1, source_target_pairs={{0,3},{1,2},{2,1},{3,0},{4,7},{5,6},{6,5},{7,4},{8,11},{9,10},{10,... | collective-permute-start | bytes 393224 | tf_op jit(solution)/shard_map/ppermute | solution.py:404
  26.6 0.0 collective-permute-start.11
  26.6 0.0 collective-permute-start.7
  26.6 1.0 %collective-permute-done.8.refs_2_ = bf16[128,512]{1,0:T(8,128)(2,1)S(1)} collective-permute-done((bf16[128,512]{1,0:T(8,128)(2,1)S(1)}, bf16[128,512]{1,0:T(8,128)(2,1)S(1)}, u32[]{:S(2)}, u32[]{:S(2)}) %collective-permute-start.8) | collective-permute-done | bytes 131104 | tf_op jit(solution)/shard_map/ppermute | solution.py:404
  27.7 0.1 collective-permute-start.9
  27.8 1.9 %collective-permute-done.10.refs_4_ = bf16[128,512]{1,0:T(8,128)(2,1)S(1)} collective-permute-done((bf16[128,512]{1,0:T(8,128)(2,1)S(1)}, bf16[128,512]{1,0:T(8,128)(2,1)S(1)}, u32[]{:S(2)}, u32[]{:S(2)}) %collective-permute-start.10) | collective-permute-done | bytes 131104 | tf_op jit(solution)/shard_map/ppermute | solution.py:404
  29.7 0.7 %collective-permute-start.12 = (bf16[128,512]{1,0:T(8,128)(2,1)S(1)}, bf16[128,512]{1,0:T(8,128)(2,1)S(1)}, u32[]{:S(2)}, u32[]{:S(2)}) collective-permute-start(bf16[128,512]{1,0:T(8,128)(2,1)S(1)} %collective-permute-done.10.refs_4_), channel_id=1, source_target_pairs={{0,1},{1,0},{2,3},{3,2},{4,5},{5,4},{6,7},{7,6},{8,9},{9,8},{10,11... | collective-permute-start | bytes 393224 | tf_op jit(solution)/shard_map/ppermute | solution.py:404
  30.5 4.4 %collective-permute-done.11.refs_5_ = bf16[128,512]{1,0:T(8,128)(2,1)S(1)} collective-permute-done((bf16[128,512]{1,0:T(8,128)(2,1)S(1)}, bf16[128,512]{1,0:T(8,128)(2,1)S(1)}, u32[]{:S(2)}, u32[]{:S(2)}) %collective-permute-start.11) | collective-permute-done | bytes 131104 | tf_op jit(solution)/shard_map/ppermute | solution.py:404
  34.9 0.0 collective-permute-start.13
  34.9 0.0 collective-permute-done.9.refs_3_.refs_1_
  34.9 0.0 collective-permute-done.7.refs_1_.refs_0_
  34.9 0.0 collective-permute-done.12.refs_6_
  34.9 1.3 %collective-permute-done.13.refs_7_ = bf16[128,512]{1,0:T(8,128)(2,1)S(1)} collective-permute-done((bf16[128,512]{1,0:T(8,128)(2,1)S(1)}, bf16[128,512]{1,0:T(8,128)(2,1)S(1)}, u32[]{:S(2)}, u32[]{:S(2)}) %collective-permute-start.13) | collective-permute-done | bytes 131104 | tf_op jit(solution)/shard_map/ppermute | solution.py:404
  36.2 1.2 %keys_values.3 = (bf16[128,4096]{1,0:T(8,128)(2,1)S(1)}, bf16[128,128]{1,0:T(8,128)(2,1)S(1)}, bf16[128,128]{1,0:T(8,128)(2,1)S(1)}) custom-call(bf16[128,512]{1,0:T(8,128)(2,1)S(1)} %collective-permute-done.5.refs_0_, bf16[128,512]{1,0:T(8,128)(2,1)S(1)} %collective-permute-done.7.refs_1_.refs_0_, bf16[128,512]{1,0:T(8,128)(2,1)S(1)} %collective-permute-done.8.refs_2_, ...), custom_call_target="tpu_custom_call" | custom-call | flops 536870912 | bytes 1048576 | tf_op jit(solution)/shard_map/keys_values/pallas_call | solution.py:154
  37.4 0.6 %collective-permute-start.14 = (bf16[128,128]{1,0:T(8,128)(2,1)S(1)}, bf16[128,128]{1,0:T(8,128)(2,1)S(1)}, u32[]{:S(2)}, u32[]{:S(2)}) collective-permute-start(bf16[128,128]{1,0:T(8,128)(2,1)S(1)} %get-tuple-element.58), channel_id=1, source_target_pairs={{0,3},{1,2},{2,1},{3,0},{4,7},{5,6},{6,5},{7,4},{8,11},{9,10},{10,... | collective-permute-start | bytes 98312 | tf_op jit(solution)/shard_map/ppermute | solution.py:404
  38.0 1.3 %queries.3.q_ref = bf16[128,1024]{1,0:T(8,128)(2,1)S(1)} custom-call(bf16[128,4096]{1,0:T(8,128)(2,1)S(1)} %get-tuple-element.53.normed_ref, bf16[4096,1024]{1,0:T(8,128)(2,1)S(1)} %get-tuple-element.43.wq_ref), custom_call_target="tpu_custom_call" | custom-call | flops 1000 | bytes 1000 | tf_op jit(solution)/shard_map/queries/pallas_call | solution.py:191
  39.3 0.6 %resident_attend.1 = (f32[1024,128]{1,0:T(8,128)S(1)}, f32[1024,128]{1,0:T(8,128)S(1)}, f32[1024,128]{1,0:T(8,128)S(1)}) custom-call(s32[128,128]{1,0:T(8,128)S(1)} %get-tuple-element.36.opened_ref, bf16[128,1024]{1,0:T(8,128)(2,1)S(1)} %queries.3.q_ref, bf16[128,128]{1,0:T(8,128)(2,1)S(1)} %get-tuple-element.49.refs_0_.keys_ref, ...), custom_call_target="tpu_custom_call" | custom-call | flops 1000 | bytes 1000 | tf_op jit(solution)/shard_map/resident_attend/pallas_call | solution.py:343
  39.9 1.0 %collective-permute-done.14.refs_3_ = bf16[128,128]{1,0:T(8,128)(2,1)S(1)} collective-permute-done((bf16[128,128]{1,0:T(8,128)(2,1)S(1)}, bf16[128,128]{1,0:T(8,128)(2,1)S(1)}, u32[]{:S(2)}, u32[]{:S(2)}) %collective-permute-start.14) | collective-permute-done | bytes 32800 | tf_op jit(solution)/shard_map/ppermute | solution.py:404
  40.8 1.3 %second_attend.1 = bf16[128,1024]{1,0:T(8,128)(2,1)} custom-call(s32[128,128]{1,0:T(8,128)S(1)} %get-tuple-element.36.opened_ref, bf16[128,1024]{1,0:T(8,128)(2,1)S(1)} %queries.3.q_ref, f32[1024,128]{1,0:T(8,128)S(1)} %get-tuple-element.54.max_ref, f32[1024,128]{1,0:T(8,128)S(1)} %get-tuple-element.55.sum_ref, f32[1024,128]{1,0:T(8,128)S(1)} %get-tuple-element.56.mixed_ref, ...), custom_call_target="tpu_custom_call" | custom-call | flops 1000 | bytes 1000 | tf_op jit(solution)/shard_map/second_attend/pallas_call | solution.py:377
Async XLA Ops:
  0.0 10.1 %collective-permute-start.1 = (bf16[128,1024]{1,0:T(8,128)(2,1)}, bf16[128,1024]{1,0:T(8,128)(2,1)S(1)}, u32[]{:S(2)}, u32[]{:S(2)}) collective-permute-start(bf16[128,1024]{1,0:T(8,128)(2,1)} %bitcast.7), channel_id=1, source_target_pairs={{0,1},{1,0},{2,3},{3,2},{4,5},{5,4},{6,7},{7,6},{8,9},{9,8},{10,11... | collective-permute-start | bytes 786440 | tf_op jit(solution)/shard_map/ppermute | solution.py:404
  0.5 9.5 %collective-permute-start = (bf16[128,1024]{1,0:T(8,128)(2,1)}, bf16[128,1024]{1,0:T(8,128)(2,1)S(1)}, u32[]{:S(2)}, u32[]{:S(2)}) collective-permute-start(bf16[128,1024]{1,0:T(8,128)(2,1)} %bitcast.8), channel_id=1, source_target_pairs={{0,3},{1,2},{2,1},{3,0},{4,7},{5,6},{6,5},{7,4},{8,11},{9,10},{10,... | collective-permute-start | bytes 786440 | tf_op jit(solution)/shard_map/ppermute | solution.py:404
  3.1 8.4 %collective-permute-start.3 = (bf16[4096,256]{1,0:T(8,128)(2,1)}, bf16[4096,256]{1,0:T(8,128)(2,1)S(1)}, u32[]{:S(2)}, u32[]{:S(2)}) collective-permute-start(bf16[4096,256]{1,0:T(8,128)(2,1)} %bitcast.5), channel_id=1, source_target_pairs={{0,1},{1,0},{2,3},{3,2},{4,5},{5,4},{6,7},{7,6},{8,9},{9,8},{10,11... | collective-permute-start | bytes 6291464 | tf_op jit(solution)/shard_map/ppermute | solution.py:404
  3.1 4.3 %copy-start.1 = (s32[9]{0:T(128)S(1)}, s32[9]{0:T(128)}, u32[]{:S(2)}) copy-start(s32[9]{0:T(128)} %doc_ref) | copy-start | bytes 112
  10.0 1.5 %collective-permute-start.2 = (bf16[128,1024]{1,0:T(8,128)(2,1)S(1)}, bf16[128,1024]{1,0:T(8,128)(2,1)S(1)}, u32[]{:S(2)}, u32[]{:S(2)}) collective-permute-start(bf16[128,1024]{1,0:T(8,128)(2,1)S(1)} %collective-permute-done.refs_2_.x_ref), channel_id=1, source_target_pairs={{0,1},{1,0},{2,3},{3,2},{4,5},{5,4},{6,7},{7,6},{8,9},{9,8},{10,11... | collective-permute-start | bytes 786440 | tf_op jit(solution)/shard_map/ppermute | solution.py:404
  11.5 2.5 %copy-start = (bf16[128,1024]{1,0:T(8,128)(2,1)S(1)}, bf16[128,1024]{1,0:T(8,128)(2,1)}, u32[]{:S(2)}) copy-start(bf16[128,1024]{1,0:T(8,128)(2,1)} %fresh_ref.3) | copy-start | bytes 786436
  12.7 3.4 %collective-permute-start.4 = (bf16[128,128]{1,0:T(8,128)(2,1)S(1)}, bf16[128,128]{1,0:T(8,128)(2,1)S(1)}, u32[]{:S(2)}, u32[]{:S(2)}) collective-permute-start(bf16[128,128]{1,0:T(8,128)(2,1)S(1)} %get-tuple-element.46.piece_ref), channel_id=1, source_target_pairs={{0,3},{1,2},{2,1},{3,0},{4,7},{5,6},{6,5},{7,4},{8,11},{9,10},{10,... | collective-permute-start | bytes 98312 | tf_op jit(solution)/shard_map/ppermute | solution.py:404
  15.3 6.2 %collective-permute-start.6 = (bf16[128,640]{1,0:T(8,128)(2,1)S(1)}, bf16[128,640]{1,0:T(8,128)(2,1)S(1)}, u32[]{:S(2)}, u32[]{:S(2)}) collective-permute-start(bf16[128,640]{1,0:T(8,128)(2,1)S(1)} %get-tuple-element.48), channel_id=1, source_target_pairs={{0,3},{1,2},{2,1},{3,0},{4,7},{5,6},{6,5},{7,4},{8,11},{9,10},{10,... | collective-permute-start | bytes 491528 | tf_op jit(solution)/shard_map/ppermute | solution.py:404
  16.6 8.2 %collective-permute-start.5 = (bf16[128,512]{1,0:T(8,128)(2,1)S(1)}, bf16[128,512]{1,0:T(8,128)(2,1)S(1)}, u32[]{:S(2)}, u32[]{:S(2)}) collective-permute-start(bf16[128,512]{1,0:T(8,128)(2,1)S(1)} %get-tuple-element.47), channel_id=1, source_target_pairs={{0,5},{1,4},{2,7},{3,6},{4,9},{5,8},{6,11},{7,10},{8,13},{9,12},{1... | collective-permute-start | bytes 393224 | tf_op jit(solution)/shard_map/ppermute | solution.py:404
  18.3 9.3 %collective-permute-start.8 = (bf16[128,512]{1,0:T(8,128)(2,1)S(1)}, bf16[128,512]{1,0:T(8,128)(2,1)S(1)}, u32[]{:S(2)}, u32[]{:S(2)}) collective-permute-start(bf16[128,512]{1,0:T(8,128)(2,1)S(1)} %first_attend.3), channel_id=1, source_target_pairs={{0,5},{1,4},{2,7},{3,6},{4,9},{5,8},{6,11},{7,10},{8,13},{9,12},{1... | collective-permute-start | bytes 393224 | tf_op jit(solution)/shard_map/ppermute | solution.py:404
  24.9 4.9 %collective-permute-start.10 = (bf16[128,512]{1,0:T(8,128)(2,1)S(1)}, bf16[128,512]{1,0:T(8,128)(2,1)S(1)}, u32[]{:S(2)}, u32[]{:S(2)}) collective-permute-start(bf16[128,512]{1,0:T(8,128)(2,1)S(1)} %collective-permute-done.5.refs_0_), channel_id=1, source_target_pairs={{0,3},{1,2},{2,1},{3,0},{4,7},{5,6},{6,5},{7,4},{8,11},{9,10},{10,... | collective-permute-start | bytes 393224 | tf_op jit(solution)/shard_map/ppermute | solution.py:404
  26.6 8.3 %collective-permute-start.11 = (bf16[128,512]{1,0:T(8,128)(2,1)S(1)}, bf16[128,512]{1,0:T(8,128)(2,1)S(1)}, u32[]{:S(2)}, u32[]{:S(2)}) collective-permute-start(bf16[128,512]{1,0:T(8,128)(2,1)S(1)} %peer_attend.1), channel_id=1, source_target_pairs={{0,5},{1,4},{2,7},{3,6},{4,9},{5,8},{6,11},{7,10},{8,13},{9,12},{1... | collective-permute-start | bytes 393224 | tf_op jit(solution)/shard_map/ppermute | solution.py:404
  26.6 8.3 %collective-permute-start.7 = (bf16[128,512]{1,0:T(8,128)(2,1)S(1)}, bf16[128,512]{1,0:T(8,128)(2,1)S(1)}, u32[]{:S(2)}, u32[]{:S(2)}) collective-permute-start(bf16[128,512]{1,0:T(8,128)(2,1)S(1)} %collective-permute-done.5.refs_0_), channel_id=1, source_target_pairs={{0,1},{1,0},{2,3},{3,2},{4,5},{5,4},{6,7},{7,6},{8,9},{9,8},{10,11... | collective-permute-start | bytes 393224 | tf_op jit(solution)/shard_map/ppermute | solution.py:404
  27.7 7.2 %collective-permute-start.9 = (bf16[128,512]{1,0:T(8,128)(2,1)S(1)}, bf16[128,512]{1,0:T(8,128)(2,1)S(1)}, u32[]{:S(2)}, u32[]{:S(2)}) collective-permute-start(bf16[128,512]{1,0:T(8,128)(2,1)S(1)} %collective-permute-done.8.refs_2_), channel_id=1, source_target_pairs={{0,1},{1,0},{2,3},{3,2},{4,5},{5,4},{6,7},{7,6},{8,9},{9,8},{10,11... | collective-permute-start | bytes 393224 | tf_op jit(solution)/shard_map/ppermute | solution.py:404
  29.7 5.1 %collective-permute-start.12 = (bf16[128,512]{1,0:T(8,128)(2,1)S(1)}, bf16[128,512]{1,0:T(8,128)(2,1)S(1)}, u32[]{:S(2)}, u32[]{:S(2)}) collective-permute-start(bf16[128,512]{1,0:T(8,128)(2,1)S(1)} %collective-permute-done.10.refs_4_), channel_id=1, source_target_pairs={{0,1},{1,0},{2,3},{3,2},{4,5},{5,4},{6,7},{7,6},{8,9},{9,8},{10,11... | collective-permute-start | bytes 393224 | tf_op jit(solution)/shard_map/ppermute | solution.py:404
  34.9 1.3 %collective-permute-start.13 = (bf16[128,512]{1,0:T(8,128)(2,1)S(1)}, bf16[128,512]{1,0:T(8,128)(2,1)S(1)}, u32[]{:S(2)}, u32[]{:S(2)}) collective-permute-start(bf16[128,512]{1,0:T(8,128)(2,1)S(1)} %collective-permute-done.11.refs_5_), channel_id=1, source_target_pairs={{0,1},{1,0},{2,3},{3,2},{4,5},{5,4},{6,7},{7,6},{8,9},{9,8},{10,11... | collective-permute-start | bytes 393224 | tf_op jit(solution)/shard_map/ppermute | solution.py:404
  37.4 3.4 %collective-permute-start.14 = (bf16[128,128]{1,0:T(8,128)(2,1)S(1)}, bf16[128,128]{1,0:T(8,128)(2,1)S(1)}, u32[]{:S(2)}, u32[]{:S(2)}) collective-permute-start(bf16[128,128]{1,0:T(8,128)(2,1)S(1)} %get-tuple-element.58), channel_id=1, source_target_pairs={{0,3},{1,2},{2,1},{3,0},{4,7},{5,6},{6,5},{7,4},{8,11},{9,10},{10,... | collective-permute-start | bytes 98312 | tf_op jit(solution)/shard_map/ppermute | solution.py:404

commit v12 on v11

--- a/solution.py
+++ b/solution.py
@@ -123,13 +123,35 @@
     )(*operands)
 
 
-def keys_values_kernel(count, wkv_count, places, *refs):
+def squares_kernel(count, *refs):
+    ssq = squares_by_lane(refs[0][...].astype(f32))
+    for x_ref in refs[1:count]:
+        ssq = ssq + squares_by_lane(x_ref[...].astype(f32))
+    for old_ref in refs[count:-1]:
+        ssq = ssq + old_ref[...]
+    refs[-1][...] = ssq
+
+
+def squares(xs, old=()):
+    operands = [*xs, *old]
+    return pl.pallas_call(
+        functools.partial(squares_kernel, len(xs)),
+        out_shape=VMEM((xs[0].shape[0], HD), f32),
+        in_specs=[vmem] * len(operands),
+        out_specs=vmem,
+        cost_estimate=cost(sum(2560 * x.size for x in xs), sum(2 * x.size for x in xs)),
+        compiler_params=params,
+        name="squares",
+    )(*operands)
+
+
+def keys_values_kernel(count, wkv_count, squared, places, *refs):
     xs, refs = refs[:count], refs[count:]
     gain_ref, wkv_refs, refs = refs[0], refs[1 : 1 + wkv_count], refs[1 + wkv_count :]
-    choose_ref, normed_ref, *pieces = refs
+    choose_ref, ssq_ref, normed_ref, *pieces = refs
     me = lax.axis_index("head")
-    ssq = squares_by_lane(xs[0][...].astype(f32))
-    for x_ref in xs[1:]:
+    ssq = ssq_ref[...]
+    for x_ref in xs[squared:]:
         ssq = ssq + squares_by_lane(x_ref[...].astype(f32))
     scale = lax.rsqrt(jnp.sum(ssq, axis=1, keepdims=True) / gain_ref.shape[1] + epsilon)
     kvs, at = [None] * wkv_count, 0
@@ -146,13 +168,13 @@
         piece[...] = dot_turned(choose_ref[i].astype(bf16), kv).astype(bf16)
 
 
-def keys_values(xs, places, gain, wkvs, choose):
+def keys_values(xs, places, gain, wkvs, choose, ssq, squared):
     tokens, width = xs[0].shape[0], sum(x.shape[1] for x in xs)
     columns = len(wkvs) * wkvs[0].shape[1]
-    operands = [*xs, *resident_in(gain, *wkvs, choose)]
+    operands = [*xs, *resident_in(gain, *wkvs, choose), ssq]
     count = choose.shape[0]
     return pl.pallas_call(
-        functools.partial(keys_values_kernel, len(xs), len(wkvs), places),
+        functools.partial(keys_values_kernel, len(xs), len(wkvs), squared, places),
         out_shape=(VMEM((tokens, width), bf16),) + (VMEM((columns // KVH, tokens), bf16),) * count,
         in_specs=[vmem] * len(operands),
         out_specs=(vmem,) * (1 + count),
@@ -193,7 +215,7 @@
         out_shape=tuple(out),
         in_specs=[vmem] * len(operands),
         out_specs=(vmem,) * len(out),
-        cost_estimate=cost(1000, 1000),
+        cost_estimate=cost(2 * normed.size * wq.shape[1], 2 * normed.size),
         compiler_params=params,
         name="queries",
     )(*operands)
@@ -406,8 +428,8 @@
     def after(array, *others):
         return lax.optimization_barrier((array, *others))[0]
 
-    def exchanged(xs, places):
-        normed, *pieces = keys_values(xs, places, gain, wkvs, choose)
+    def exchanged(xs, places, ssq, squared):
+        normed, *pieces = keys_values(xs, places, gain, wkvs, choose, ssq, squared)
         received = [moved(piece, 0, flip) for piece, flip in zip(pieces[1:], flips[1:])]
         return normed, [pieces[0], *received], pieces, [x.shape[1] for x in xs]
 
@@ -432,10 +454,12 @@
         over, *opened = lax.optimization_barrier((over, *opened))
         passed = moved(over, 0, 1)
         xs, places = [own, beside, over, passed], [place(0), place(1), place(3), place(2)]
+        ssq, squared = squares([own, beside, over]), 3
     else:
         wkvs = [wkv]
         xs, places = [own, *rest_of(own)], following
-    normed, pieces, made, widths = exchanged(xs, places)
+        ssq, squared = squares([own]), 1
+    normed, pieces, made, widths = exchanged(xs, places, ssq, squared)
     part = heads // 2 if paired else heads
     split = part * HD
     if paired:
@@ -459,17 +483,23 @@
         a1 = after(a1, peers)
         a2 = moved(a1, 0, 3)
         a0 = moved(a1, 0, 1)
+        ssq = squares([a1])
+        b1, ssq = lax.optimization_barrier((b1, ssq))
         b0 = moved(b1, 0, 1)
+        ssq = squares([b1], [ssq])
+        b2, ssq = lax.optimization_barrier((b2, ssq))
         b3 = moved(b2, 0, 1)
         a3 = moved(a2, 0, 1)
-        xs = [a1, a0, b1, b0, a2, b2, a3, b3]
-        places = [place(1), place(0), place(1, split), place(0, split)]
-        places += [place(2), place(2, split), place(3), place(3, split)]
+        ssq, squared = squares([a0, a2, b2], [ssq]), 5
+        xs = [a1, b1, a0, a2, b2, a3, b0, b3]
+        places = [place(1), place(1, split), place(0), place(2), place(2, split)]
+        places += [place(3), place(0, split), place(3, split)]
         mine = [a0, b0]
     else:
         mine = [jnp.where(lax.axis_index("section") == 0, fresh_slice, moved(sent, 1, 0))]
         xs, places = [*mine, *rest_of(mine[0])], following
-    normed, pieces, _, widths = exchanged(xs, places)
+        ssq, squared = squares(mine), 1
+    normed, pieces, _, widths = exchanged(xs, places, ssq, squared)
     (q,) = queries(normed, widths, places, wq)
     resident = resident_attend(opened[1], q, keys, values, sections)
     return second_attend(opened[1], q, mine, resident, pieces, flips, parts, sections)[None]

time: 42.3 us -> 38 us (0.90)
  waiting for transfers between devices: 18 us -> 11.6 us
  starting transfers between devices: 10.9 us -> 13 us
    ppermute x15, waiting for transfers between devices: 18 us -> 11.6 us  [moved(): return lax.ppermute(array, ('section', 'head'), pairs)]
    ppermute x15, starting transfers between devices: 10.9 us -> 13 us  [moved(): return lax.ppermute(array, ('section', 'head'), pairs)]
  transfers between devices with their start and end apart: 15 -> 15, of which waited for: 10 -> 10; matrix products, arithmetic and copies ran while one was open for 0% -> 0% of each run, Pallas kernels for 22% -> 26%
where the time goes in v12:
time: 38 us; the launch traced here: 37.8 us
  Pallas kernels  13.1 us (34%)
  starting transfers between devices  13 us (34%)
  waiting for transfers between devices  11.6 us (31%)
    ppermute x15, starting transfers between devices, moved(): return lax.ppermute(array, ('section', 'head'), pairs)  13 us
    ppermute x15, waiting for transfers between devices, moved(): return lax.ppermute(array, ('section', 'head'), pairs)  11.6 us
    pallas_call x1, Pallas kernels, load(): pl.pallas_call(functools.partial(load_kernel, n, flips, parts), out_shape...  4.24 us
    pallas_call x2, Pallas kernels, queries(): pl.pallas_call(functools.partial(queries_kernel, widths, places), out_sha...  2.52 us
    pallas_call x2, Pallas kernels, keys_values(): pl.pallas_call(functools.partial(keys_values_kernel, len(xs), len(wkvs),...  2.06 us
    pallas_call x1, Pallas kernels, second_attend(): pl.pallas_call(functools.partial(second_attend_kernel, sections, flips, p...  1.32 us
    pallas_call x2, Pallas kernels, first_attend(): pl.pallas_call(functools.partial(first_attend_kernel, sections, heads, fl...  0.96 us
  transfers between devices with their start and end apart: 15, of which 10 were waited for; matrix products, arithmetic and copies ran while one was open for 0% of the time, Pallas kernels for 26%

profile of v12, /device:TPU:0, one launch (start us, length us, event | category | flops | bytes accessed | tf_op | source)
XLA Modules:
  0.0 37.8 jit_solution(14268352145666884059)
XLA Ops:
  0.0 0.5 %collective-permute-start.1 = (bf16[128,1024]{1,0:T(8,128)(2,1)}, bf16[128,1024]{1,0:T(8,128)(2,1)S(1)}, u32[]{:S(2)}, u32[]{:S(2)}) collective-permute-start(bf16[128,1024]{1,0:T(8,128)(2,1)} %bitcast.7), channel_id=1, source_target_pairs={{0,1},{1,0},{2,3},{3,2},{4,5},{5,4},{6,7},{7,6},{8,9},{9,8},{10,11... | collective-permute-start | bytes 786440 | tf_op jit(solution)/shard_map/ppermute | solution.py:426
  0.5 2.6 %collective-permute-start = (bf16[128,1024]{1,0:T(8,128)(2,1)}, bf16[128,1024]{1,0:T(8,128)(2,1)S(1)}, u32[]{:S(2)}, u32[]{:S(2)}) collective-permute-start(bf16[128,1024]{1,0:T(8,128)(2,1)} %bitcast.8), channel_id=1, source_target_pairs={{0,3},{1,2},{2,1},{3,0},{4,7},{5,6},{6,5},{7,4},{8,11},{9,10},{10,... | collective-permute-start | bytes 786440 | tf_op jit(solution)/shard_map/ppermute | solution.py:426
  3.1 0.0 collective-permute-start.3
  3.1 0.0 copy-start.1
  3.1 4.2 %load.1 = (bf16[128,1024]{1,0:T(8,128)(2,1)S(1)}, f32[1,4096]{1,0:T(1,128)S(1)}, bf16[4096,1024]{1,0:T(8,128)(2,1)S(1)}, bf16[4096,256]{1,0:T(8,128)(2,1)S(1)}, f32[2,128,512]{2,1,0:T(8,128)S(1)}) custom-call(bf16[128,1024]{1,0:T(8,128)(2,1)} %bitcast.9, f32[1,4096]{1,0:T(1,128)} %gain_hbm.1, bf16[4096,1024]{1,0:T(8,128)(2,1)} %bitcast.4, ...), custom_call_target="tpu_custom_call" | custom-call | flops 99999997952 | bytes 1000000000 | tf_op jit(solution)/shard_map/load/pallas_call | solution.py:108
  7.3 0.0 copy-done.1
  7.4 0.6 %openings.1 = (s32[128,128]{1,0:T(8,128)S(1)}, s32[128,128]{1,0:T(8,128)S(1)}) custom-call(s32[9]{0:T(128)S(1)} %copy-done.1), custom_call_target="tpu_custom_call" | custom-call | tf_op jit(solution)/shard_map/openings/pallas_call | solution.py:238
  8.0 2.0 %collective-permute-done.refs_2_.x_ref = bf16[128,1024]{1,0:T(8,128)(2,1)S(1)} collective-permute-done((bf16[128,1024]{1,0:T(8,128)(2,1)}, bf16[128,1024]{1,0:T(8,128)(2,1)S(1)}, u32[]{:S(2)}, u32[]{:S(2)}) %collective-permute-start) | collective-permute-done | bytes 262176 | tf_op jit(solution)/shard_map/ppermute | solution.py:426
  10.0 0.1 collective-permute-start.2
  10.1 0.0 collective-permute-done.1.refs_1_
  10.1 0.2 squares.4.refs_8_
  10.2 1.3 %collective-permute-done.2.refs_3_ = bf16[128,1024]{1,0:T(8,128)(2,1)S(1)} collective-permute-done((bf16[128,1024]{1,0:T(8,128)(2,1)S(1)}, bf16[128,1024]{1,0:T(8,128)(2,1)S(1)}, u32[]{:S(2)}, u32[]{:S(2)}) %collective-permute-start.2) | collective-permute-done | bytes 262176 | tf_op jit(solution)/shard_map/ppermute | solution.py:426
  11.5 0.0 collective-permute-done.3.refs_6_.refs_10_
  11.5 0.0 copy-start
  11.5 1.0 %keys_values.2 = (bf16[128,4096]{1,0:T(8,128)(2,1)S(1)}, bf16[128,128]{1,0:T(8,128)(2,1)S(1)}, bf16[128,128]{1,0:T(8,128)(2,1)S(1)}) custom-call(bf16[128,1024]{1,0:T(8,128)(2,1)S(1)} %get-tuple-element.42.refs_0_.x_ref, bf16[128,1024]{1,0:T(8,128)(2,1)S(1)} %collective-permute-done.1.refs_1_, bf16[128,1024]{1,0:T(8,128)(2,1)S(1)} %collective-permute-done.refs_2_.x_ref, ...), custom_call_target="tpu_custom_call" | custom-call | flops 536870912 | bytes 1048576 | tf_op jit(solution)/shard_map/keys_values/pallas_call | solution.py:176
  12.5 1.3 %collective-permute-start.4 = (bf16[128,128]{1,0:T(8,128)(2,1)S(1)}, bf16[128,128]{1,0:T(8,128)(2,1)S(1)}, u32[]{:S(2)}, u32[]{:S(2)}) collective-permute-start(bf16[128,128]{1,0:T(8,128)(2,1)S(1)} %get-tuple-element.50.piece_ref), channel_id=1, source_target_pairs={{0,3},{1,2},{2,1},{3,0},{4,7},{5,6},{6,5},{7,4},{8,11},{9,10},{10,... | collective-permute-start | bytes 98312 | tf_op jit(solution)/shard_map/ppermute | solution.py:426
  13.8 0.0 copy-done
  13.8 1.3 %queries.2 = (bf16[128,1024]{1,0:T(8,128)(2,1)S(1)}, bf16[128,640]{1,0:T(8,128)(2,1)S(1)}) custom-call(bf16[128,4096]{1,0:T(8,128)(2,1)S(1)} %get-tuple-element.46.normed_ref, bf16[4096,1024]{1,0:T(8,128)(2,1)S(1)} %get-tuple-element.47.wq_ref, bf16[128,128]{1,0:T(8,128)(2,1)S(1)} %get-tuple-element.48.refs_0_, bf16[128,1024]{1,0:T(8,128)(2,1)S(1)} %copy-done), custom_call_target="tpu_custom_call" | custom-call | flops 1073741824 | bytes 1048576 | tf_op jit(solution)/shard_map/queries/pallas_call | solution.py:213
  15.1 0.6 %collective-permute-start.6 = (bf16[128,640]{1,0:T(8,128)(2,1)S(1)}, bf16[128,640]{1,0:T(8,128)(2,1)S(1)}, u32[]{:S(2)}, u32[]{:S(2)}) collective-permute-start(bf16[128,640]{1,0:T(8,128)(2,1)S(1)} %get-tuple-element.52), channel_id=1, source_target_pairs={{0,3},{1,2},{2,1},{3,0},{4,7},{5,6},{6,5},{7,4},{8,11},{9,10},{10,... | collective-permute-start | bytes 491528 | tf_op jit(solution)/shard_map/ppermute | solution.py:426
  15.7 0.3 collective-permute-done.4.refs_1_
  16.0 0.5 %first_attend.2 = (bf16[128,512]{1,0:T(8,128)(2,1)S(1)}, bf16[128,128]{1,0:T(8,128)(2,1)S(1)}, bf16[128,128]{1,0:T(8,128)(2,1)S(1)}) custom-call(s32[128,128]{1,0:T(8,128)S(1)} %get-tuple-element.41.opened_ref, bf16[128,1024]{1,0:T(8,128)(2,1)S(1)} %get-tuple-element.49.q_ref, bf16[128,1024]{1,0:T(8,128)(2,1)S(1)} %get-tuple-element.42.refs_0_.x_ref, ...), custom_call_target="tpu_custom_call" | custom-call | flops 10000000000 | bytes 1000 | tf_op jit(solution)/shard_map/first_attend/pallas_call | solution.py:340
  16.5 1.2 %collective-permute-start.5 = (bf16[128,512]{1,0:T(8,128)(2,1)S(1)}, bf16[128,512]{1,0:T(8,128)(2,1)S(1)}, u32[]{:S(2)}, u32[]{:S(2)}) collective-permute-start(bf16[128,512]{1,0:T(8,128)(2,1)S(1)} %get-tuple-element.51), channel_id=1, source_target_pairs={{0,5},{1,4},{2,7},{3,6},{4,9},{5,8},{6,11},{7,10},{8,13},{9,12},{1... | collective-permute-start | bytes 393224 | tf_op jit(solution)/shard_map/ppermute | solution.py:426
  17.7 0.5 %first_attend.3 = bf16[128,512]{1,0:T(8,128)(2,1)S(1)} custom-call(s32[128,128]{1,0:T(8,128)S(1)} %get-tuple-element.41.opened_ref, bf16[128,1024]{1,0:T(8,128)(2,1)S(1)} %get-tuple-element.49.q_ref, bf16[128,1024]{1,0:T(8,128)(2,1)S(1)} %get-tuple-element.42.refs_0_.x_ref, bf16[128,1024]{1,0:T(8,128)(2,1)S(1)} %copy-done, ...), custom_call_target="tpu_custom_call" | custom-call | flops 10000000000 | bytes 1000 | tf_op jit(solution)/shard_map/first_attend/pallas_call | solution.py:340
  18.2 1.4 %collective-permute-start.7 = (bf16[128,512]{1,0:T(8,128)(2,1)S(1)}, bf16[128,512]{1,0:T(8,128)(2,1)S(1)}, u32[]{:S(2)}, u32[]{:S(2)}) collective-permute-start(bf16[128,512]{1,0:T(8,128)(2,1)S(1)} %first_attend.3), channel_id=1, source_target_pairs={{0,5},{1,4},{2,7},{3,6},{4,9},{5,8},{6,11},{7,10},{8,13},{9,12},{1... | collective-permute-start | bytes 393224 | tf_op jit(solution)/shard_map/ppermute | solution.py:426
  19.5 1.8 %collective-permute-done.6.bundle_ref = bf16[128,640]{1,0:T(8,128)(2,1)S(1)} collective-permute-done((bf16[128,640]{1,0:T(8,128)(2,1)S(1)}, bf16[128,640]{1,0:T(8,128)(2,1)S(1)}, u32[]{:S(2)}, u32[]{:S(2)}) %collective-permute-start.6) | collective-permute-done | bytes 163872 | tf_op jit(solution)/shard_map/ppermute | solution.py:426
  21.3 0.5 %peer_attend.1 = bf16[128,512]{1,0:T(8,128)(2,1)S(1)} custom-call(s32[128,128]{1,0:T(8,128)S(1)} %get-tuple-element.41.opened_ref, bf16[128,640]{1,0:T(8,128)(2,1)S(1)} %collective-permute-done.6.bundle_ref, bf16[128,1024]{1,0:T(8,128)(2,1)S(1)} %collective-permute-done.refs_2_.x_ref, bf16[128,128]{1,0:T(8,128)(2,1)S(1)} %get-tuple-element.50.piece_ref), custom_call_target="tpu_custom_call" | custom-call | flops 1000 | bytes 1000 | tf_op jit(solution)/shard_map/peer_attend/pallas_call | solution.py:298
  21.8 1.6 %collective-permute-start.10 = (bf16[128,512]{1,0:T(8,128)(2,1)S(1)}, bf16[128,512]{1,0:T(8,128)(2,1)S(1)}, u32[]{:S(2)}, u32[]{:S(2)}) collective-permute-start(bf16[128,512]{1,0:T(8,128)(2,1)S(1)} %peer_attend.1), channel_id=1, source_target_pairs={{0,5},{1,4},{2,7},{3,6},{4,9},{5,8},{6,11},{7,10},{8,13},{9,12},{1... | collective-permute-start | bytes 393224 | tf_op jit(solution)/shard_map/ppermute | solution.py:426
  23.4 1.3 %collective-permute-done.5.refs_0_ = bf16[128,512]{1,0:T(8,128)(2,1)S(1)} collective-permute-done((bf16[128,512]{1,0:T(8,128)(2,1)S(1)}, bf16[128,512]{1,0:T(8,128)(2,1)S(1)}, u32[]{:S(2)}, u32[]{:S(2)}) %collective-permute-start.5) | collective-permute-done | bytes 131104 | tf_op jit(solution)/shard_map/ppermute | solution.py:426
  24.7 1.8 %collective-permute-start.9 = (bf16[128,512]{1,0:T(8,128)(2,1)S(1)}, bf16[128,512]{1,0:T(8,128)(2,1)S(1)}, u32[]{:S(2)}, u32[]{:S(2)}) collective-permute-start(bf16[128,512]{1,0:T(8,128)(2,1)S(1)} %collective-permute-done.5.refs_0_), channel_id=1, source_target_pairs={{0,3},{1,2},{2,1},{3,0},{4,7},{5,6},{6,5},{7,4},{8,11},{9,10},{10,... | collective-permute-start | bytes 393224 | tf_op jit(solution)/shard_map/ppermute | solution.py:426
  26.4 0.0 collective-permute-start.8
  26.5 1.0 %collective-permute-done.7.refs_0_.refs_1_ = bf16[128,512]{1,0:T(8,128)(2,1)S(1)} collective-permute-done((bf16[128,512]{1,0:T(8,128)(2,1)S(1)}, bf16[128,512]{1,0:T(8,128)(2,1)S(1)}, u32[]{:S(2)}, u32[]{:S(2)}) %collective-permute-start.7) | collective-permute-done | bytes 131104 | tf_op jit(solution)/shard_map/ppermute | solution.py:426
  27.5 0.5 %collective-permute-start.12 = (bf16[128,512]{1,0:T(8,128)(2,1)S(1)}, bf16[128,512]{1,0:T(8,128)(2,1)S(1)}, u32[]{:S(2)}, u32[]{:S(2)}) collective-permute-start(bf16[128,512]{1,0:T(8,128)(2,1)S(1)} %collective-permute-done.7.refs_0_.refs_1_), channel_id=1, source_target_pairs={{0,1},{1,0},{2,3},{3,2},{4,5},{5,4},{6,7},{7,6},{8,9},{9,8},{10,11... | collective-permute-start | bytes 393224 | tf_op jit(solution)/shard_map/ppermute | solution.py:426
  28.0 2.5 %collective-permute-done.10.refs_2_.refs_4_ = bf16[128,512]{1,0:T(8,128)(2,1)S(1)} collective-permute-done((bf16[128,512]{1,0:T(8,128)(2,1)S(1)}, bf16[128,512]{1,0:T(8,128)(2,1)S(1)}, u32[]{:S(2)}, u32[]{:S(2)}) %collective-permute-start.10) | collective-permute-done | bytes 131104 | tf_op jit(solution)/shard_map/ppermute | solution.py:426
  30.5 0.0 collective-permute-done.9.refs_1_.refs_3_
  30.5 0.1 collective-permute-start.11
  30.6 0.4 %collective-permute-start.13 = (bf16[128,512]{1,0:T(8,128)(2,1)S(1)}, bf16[128,512]{1,0:T(8,128)(2,1)S(1)}, u32[]{:S(2)}, u32[]{:S(2)}) collective-permute-start(bf16[128,512]{1,0:T(8,128)(2,1)S(1)} %collective-permute-done.10.refs_2_.refs_4_), channel_id=1, source_target_pairs={{0,1},{1,0},{2,3},{3,2},{4,5},{5,4},{6,7},{7,6},{8,9},{9,8},{10,11... | collective-permute-start | bytes 393224 | tf_op jit(solution)/shard_map/ppermute | solution.py:426
  31.0 0.0 collective-permute-done.8.refs_0_.refs_2_
  31.0 0.1 squares.7.refs_12_
  31.1 0.0 collective-permute-done.12.refs_6_.refs_1_
  31.1 0.7 %collective-permute-done.11.refs_5_ = bf16[128,512]{1,0:T(8,128)(2,1)S(1)} collective-permute-done((bf16[128,512]{1,0:T(8,128)(2,1)S(1)}, bf16[128,512]{1,0:T(8,128)(2,1)S(1)}, u32[]{:S(2)}, u32[]{:S(2)}) %collective-permute-start.11) | collective-permute-done | bytes 131104 | tf_op jit(solution)/shard_map/ppermute | solution.py:426
  31.8 0.2 collective-permute-done.13.refs_7_
  32.0 1.1 %keys_values.3 = (bf16[128,4096]{1,0:T(8,128)(2,1)S(1)}, bf16[128,128]{1,0:T(8,128)(2,1)S(1)}, bf16[128,128]{1,0:T(8,128)(2,1)S(1)}) custom-call(bf16[128,512]{1,0:T(8,128)(2,1)S(1)} %collective-permute-done.5.refs_0_, bf16[128,512]{1,0:T(8,128)(2,1)S(1)} %collective-permute-done.7.refs_0_.refs_1_, ...), custom_call_target="tpu_custom_call" | custom-call | flops 536870912 | bytes 1048576 | tf_op jit(solution)/shard_map/keys_values/pallas_call | solution.py:176
  33.1 1.0 %collective-permute-start.14 = (bf16[128,128]{1,0:T(8,128)(2,1)S(1)}, bf16[128,128]{1,0:T(8,128)(2,1)S(1)}, u32[]{:S(2)}, u32[]{:S(2)}) collective-permute-start(bf16[128,128]{1,0:T(8,128)(2,1)S(1)} %get-tuple-element.66), channel_id=1, source_target_pairs={{0,3},{1,2},{2,1},{3,0},{4,7},{5,6},{6,5},{7,4},{8,11},{9,10},{10,... | collective-permute-start | bytes 98312 | tf_op jit(solution)/shard_map/ppermute | solution.py:426
  34.1 1.3 %queries.3.q_ref = bf16[128,1024]{1,0:T(8,128)(2,1)S(1)} custom-call(bf16[128,4096]{1,0:T(8,128)(2,1)S(1)} %get-tuple-element.61.normed_ref, bf16[4096,1024]{1,0:T(8,128)(2,1)S(1)} %get-tuple-element.47.wq_ref), custom_call_target="tpu_custom_call" | custom-call | flops 1073741824 | bytes 1048576 | tf_op jit(solution)/shard_map/queries/pallas_call | solution.py:213
  35.4 0.6 %resident_attend.1 = (f32[1024,128]{1,0:T(8,128)S(1)}, f32[1024,128]{1,0:T(8,128)S(1)}, f32[1024,128]{1,0:T(8,128)S(1)}) custom-call(s32[128,128]{1,0:T(8,128)S(1)} %get-tuple-element.40.opened_ref, bf16[128,1024]{1,0:T(8,128)(2,1)S(1)} %queries.3.q_ref, bf16[128,128]{1,0:T(8,128)(2,1)S(1)} %get-tuple-element.53.refs_0_.keys_ref, ...), custom_call_target="tpu_custom_call" | custom-call | flops 1000 | bytes 1000 | tf_op jit(solution)/shard_map/resident_attend/pallas_call | solution.py:365
  35.9 0.5 %collective-permute-done.14.refs_3_ = bf16[128,128]{1,0:T(8,128)(2,1)S(1)} collective-permute-done((bf16[128,128]{1,0:T(8,128)(2,1)S(1)}, bf16[128,128]{1,0:T(8,128)(2,1)S(1)}, u32[]{:S(2)}, u32[]{:S(2)}) %collective-permute-start.14) | collective-permute-done | bytes 32800 | tf_op jit(solution)/shard_map/ppermute | solution.py:426
  36.5 1.3 %second_attend.1 = bf16[128,1024]{1,0:T(8,128)(2,1)} custom-call(s32[128,128]{1,0:T(8,128)S(1)} %get-tuple-element.40.opened_ref, bf16[128,1024]{1,0:T(8,128)(2,1)S(1)} %queries.3.q_ref, f32[1024,128]{1,0:T(8,128)S(1)} %get-tuple-element.62.max_ref, f32[1024,128]{1,0:T(8,128)S(1)} %get-tuple-element.63.sum_ref, f32[1024,128]{1,0:T(8,128)S(1)} %get-tuple-element.64.mixed_ref, ...), custom_call_target="tpu_custom_call" | custom-call | flops 1000 | bytes 1000 | tf_op jit(solution)/shard_map/second_attend/pallas_call | solution.py:399
  (2 shorter events, 0.1 us)
Async XLA Ops:
  0.0 10.1 %collective-permute-start.1 = (bf16[128,1024]{1,0:T(8,128)(2,1)}, bf16[128,1024]{1,0:T(8,128)(2,1)S(1)}, u32[]{:S(2)}, u32[]{:S(2)}) collective-permute-start(bf16[128,1024]{1,0:T(8,128)(2,1)} %bitcast.7), channel_id=1, source_target_pairs={{0,1},{1,0},{2,3},{3,2},{4,5},{5,4},{6,7},{7,6},{8,9},{9,8},{10,11... | collective-permute-start | bytes 786440 | tf_op jit(solution)/shard_map/ppermute | solution.py:426
  0.5 9.5 %collective-permute-start = (bf16[128,1024]{1,0:T(8,128)(2,1)}, bf16[128,1024]{1,0:T(8,128)(2,1)S(1)}, u32[]{:S(2)}, u32[]{:S(2)}) collective-permute-start(bf16[128,1024]{1,0:T(8,128)(2,1)} %bitcast.8), channel_id=1, source_target_pairs={{0,3},{1,2},{2,1},{3,0},{4,7},{5,6},{6,5},{7,4},{8,11},{9,10},{10,... | collective-permute-start | bytes 786440 | tf_op jit(solution)/shard_map/ppermute | solution.py:426
  3.1 8.4 %collective-permute-start.3 = (bf16[4096,256]{1,0:T(8,128)(2,1)}, bf16[4096,256]{1,0:T(8,128)(2,1)S(1)}, u32[]{:S(2)}, u32[]{:S(2)}) collective-permute-start(bf16[4096,256]{1,0:T(8,128)(2,1)} %bitcast.5), channel_id=1, source_target_pairs={{0,1},{1,0},{2,3},{3,2},{4,5},{5,4},{6,7},{7,6},{8,9},{9,8},{10,11... | collective-permute-start | bytes 6291464 | tf_op jit(solution)/shard_map/ppermute | solution.py:426
  3.1 4.3 %copy-start.1 = (s32[9]{0:T(128)S(1)}, s32[9]{0:T(128)}, u32[]{:S(2)}) copy-start(s32[9]{0:T(128)} %doc_ref) | copy-start | bytes 112
  10.0 1.5 %collective-permute-start.2 = (bf16[128,1024]{1,0:T(8,128)(2,1)S(1)}, bf16[128,1024]{1,0:T(8,128)(2,1)S(1)}, u32[]{:S(2)}, u32[]{:S(2)}) collective-permute-start(bf16[128,1024]{1,0:T(8,128)(2,1)S(1)} %collective-permute-done.refs_2_.x_ref), channel_id=1, source_target_pairs={{0,1},{1,0},{2,3},{3,2},{4,5},{5,4},{6,7},{7,6},{8,9},{9,8},{10,11... | collective-permute-start | bytes 786440 | tf_op jit(solution)/shard_map/ppermute | solution.py:426
  11.5 2.3 %copy-start = (bf16[128,1024]{1,0:T(8,128)(2,1)S(1)}, bf16[128,1024]{1,0:T(8,128)(2,1)}, u32[]{:S(2)}) copy-start(bf16[128,1024]{1,0:T(8,128)(2,1)} %fresh_ref.3) | copy-start | bytes 786436
  12.5 3.4 %collective-permute-start.4 = (bf16[128,128]{1,0:T(8,128)(2,1)S(1)}, bf16[128,128]{1,0:T(8,128)(2,1)S(1)}, u32[]{:S(2)}, u32[]{:S(2)}) collective-permute-start(bf16[128,128]{1,0:T(8,128)(2,1)S(1)} %get-tuple-element.50.piece_ref), channel_id=1, source_target_pairs={{0,3},{1,2},{2,1},{3,0},{4,7},{5,6},{6,5},{7,4},{8,11},{9,10},{10,... | collective-permute-start | bytes 98312 | tf_op jit(solution)/shard_map/ppermute | solution.py:426
  15.1 6.2 %collective-permute-start.6 = (bf16[128,640]{1,0:T(8,128)(2,1)S(1)}, bf16[128,640]{1,0:T(8,128)(2,1)S(1)}, u32[]{:S(2)}, u32[]{:S(2)}) collective-permute-start(bf16[128,640]{1,0:T(8,128)(2,1)S(1)} %get-tuple-element.52), channel_id=1, source_target_pairs={{0,3},{1,2},{2,1},{3,0},{4,7},{5,6},{6,5},{7,4},{8,11},{9,10},{10,... | collective-permute-start | bytes 491528 | tf_op jit(solution)/shard_map/ppermute | solution.py:426
  16.5 8.2 %collective-permute-start.5 = (bf16[128,512]{1,0:T(8,128)(2,1)S(1)}, bf16[128,512]{1,0:T(8,128)(2,1)S(1)}, u32[]{:S(2)}, u32[]{:S(2)}) collective-permute-start(bf16[128,512]{1,0:T(8,128)(2,1)S(1)} %get-tuple-element.51), channel_id=1, source_target_pairs={{0,5},{1,4},{2,7},{3,6},{4,9},{5,8},{6,11},{7,10},{8,13},{9,12},{1... | collective-permute-start | bytes 393224 | tf_op jit(solution)/shard_map/ppermute | solution.py:426
  18.2 9.3 %collective-permute-start.7 = (bf16[128,512]{1,0:T(8,128)(2,1)S(1)}, bf16[128,512]{1,0:T(8,128)(2,1)S(1)}, u32[]{:S(2)}, u32[]{:S(2)}) collective-permute-start(bf16[128,512]{1,0:T(8,128)(2,1)S(1)} %first_attend.3), channel_id=1, source_target_pairs={{0,5},{1,4},{2,7},{3,6},{4,9},{5,8},{6,11},{7,10},{8,13},{9,12},{1... | collective-permute-start | bytes 393224 | tf_op jit(solution)/shard_map/ppermute | solution.py:426
  21.8 8.6 %collective-permute-start.10 = (bf16[128,512]{1,0:T(8,128)(2,1)S(1)}, bf16[128,512]{1,0:T(8,128)(2,1)S(1)}, u32[]{:S(2)}, u32[]{:S(2)}) collective-permute-start(bf16[128,512]{1,0:T(8,128)(2,1)S(1)} %peer_attend.1), channel_id=1, source_target_pairs={{0,5},{1,4},{2,7},{3,6},{4,9},{5,8},{6,11},{7,10},{8,13},{9,12},{1... | collective-permute-start | bytes 393224 | tf_op jit(solution)/shard_map/ppermute | solution.py:426
  24.7 5.8 %collective-permute-start.9 = (bf16[128,512]{1,0:T(8,128)(2,1)S(1)}, bf16[128,512]{1,0:T(8,128)(2,1)S(1)}, u32[]{:S(2)}, u32[]{:S(2)}) collective-permute-start(bf16[128,512]{1,0:T(8,128)(2,1)S(1)} %collective-permute-done.5.refs_0_), channel_id=1, source_target_pairs={{0,3},{1,2},{2,1},{3,0},{4,7},{5,6},{6,5},{7,4},{8,11},{9,10},{10,... | collective-permute-start | bytes 393224 | tf_op jit(solution)/shard_map/ppermute | solution.py:426
  26.4 4.6 %collective-permute-start.8 = (bf16[128,512]{1,0:T(8,128)(2,1)S(1)}, bf16[128,512]{1,0:T(8,128)(2,1)S(1)}, u32[]{:S(2)}, u32[]{:S(2)}) collective-permute-start(bf16[128,512]{1,0:T(8,128)(2,1)S(1)} %collective-permute-done.5.refs_0_), channel_id=1, source_target_pairs={{0,1},{1,0},{2,3},{3,2},{4,5},{5,4},{6,7},{7,6},{8,9},{9,8},{10,11... | collective-permute-start | bytes 393224 | tf_op jit(solution)/shard_map/ppermute | solution.py:426
  27.5 3.6 %collective-permute-start.12 = (bf16[128,512]{1,0:T(8,128)(2,1)S(1)}, bf16[128,512]{1,0:T(8,128)(2,1)S(1)}, u32[]{:S(2)}, u32[]{:S(2)}) collective-permute-start(bf16[128,512]{1,0:T(8,128)(2,1)S(1)} %collective-permute-done.7.refs_0_.refs_1_), channel_id=1, source_target_pairs={{0,1},{1,0},{2,3},{3,2},{4,5},{5,4},{6,7},{7,6},{8,9},{9,8},{10,11... | collective-permute-start | bytes 393224 | tf_op jit(solution)/shard_map/ppermute | solution.py:426
  30.5 1.3 %collective-permute-start.11 = (bf16[128,512]{1,0:T(8,128)(2,1)S(1)}, bf16[128,512]{1,0:T(8,128)(2,1)S(1)}, u32[]{:S(2)}, u32[]{:S(2)}) collective-permute-start(bf16[128,512]{1,0:T(8,128)(2,1)S(1)} %collective-permute-done.9.refs_1_.refs_3_), channel_id=1, source_target_pairs={{0,1},{1,0},{2,3},{3,2},{4,5},{5,4},{6,7},{7,6},{8,9},{9,8},{10,11... | collective-permute-start | bytes 393224 | tf_op jit(solution)/shard_map/ppermute | solution.py:426
  30.6 1.4 %collective-permute-start.13 = (bf16[128,512]{1,0:T(8,128)(2,1)S(1)}, bf16[128,512]{1,0:T(8,128)(2,1)S(1)}, u32[]{:S(2)}, u32[]{:S(2)}) collective-permute-start(bf16[128,512]{1,0:T(8,128)(2,1)S(1)} %collective-permute-done.10.refs_2_.refs_4_), channel_id=1, source_target_pairs={{0,1},{1,0},{2,3},{3,2},{4,5},{5,4},{6,7},{7,6},{8,9},{9,8},{10,11... | collective-permute-start | bytes 393224 | tf_op jit(solution)/shard_map/ppermute | solution.py:426
  33.1 3.4 %collective-permute-start.14 = (bf16[128,128]{1,0:T(8,128)(2,1)S(1)}, bf16[128,128]{1,0:T(8,128)(2,1)S(1)}, u32[]{:S(2)}, u32[]{:S(2)}) collective-permute-start(bf16[128,128]{1,0:T(8,128)(2,1)S(1)} %get-tuple-element.66), channel_id=1, source_target_pairs={{0,3},{1,2},{2,1},{3,0},{4,7},{5,6},{6,5},{7,4},{8,11},{9,10},{10,... | collective-permute-start | bytes 98312 | tf_op jit(solution)/shard_map/ppermute | solution.py:426
